TPU v7x, 32 devices: a whole 2x2x4 slice. The times are simulated.
32 devices in a mesh: band: 4 (over y, x), loc: 8 (over z, core).
Axes of the slice: x: 2, y: 2, z: 4, core: 2. Of those that a mesh axis runs over, the one named last changes fastest.
Arguments:
- tokens: bfloat16 [2048, 16, 768], P('loc', 'band'), may hold values from -6 to 6
- band_index: int32 [16], replicated, may hold values from 0 to 15, each once
- band_table: float32 [16, 768], replicated, may hold values from -3 to 3
- window_ids: int32 [2048], replicated, may hold values from 0 to 1, as said below
- spatial_qkv: bfloat16 [768, 2304], replicated
- spatial_out: bfloat16 [768, 768], replicated, may hold values from -0.21875 to 0.21875
- channel_qkv: bfloat16 [768, 2304], replicated
- channel_out: bfloat16 [768, 768], replicated, may hold values from -0.21875 to 0.21875
- up_weight: bfloat16 [768, 3072], replicated, may hold values from -0.21875 to 0.21875
- down_weight: bfloat16 [3072, 768], replicated, may hold values from -0.109375 to 0.109375
Outputs:
- joined: bfloat16 [2048, 16, 768], P('loc', 'band')
Inputs may be any that keep to these rules, and one draw needn't show every extreme that they name: `window_ids`: each of the 2 windows holds exactly 1024 locations, and each aligned block of 256 locations holds exactly 128 locations of each window. `band_index`: each of the 16 band numbers once.
All inputs are finite; a program needn't handle non-finite values.
Results may differ from a plain program's by a relative error of at most 0.014.
Values may be sent and summed in bfloat16 or wider, within the bound.
No kernel may reach another device: no remote copies, remote signals or barrier semaphores. Data moves between devices by JAX's collectives and lax.ppermute only.
A program may use at most 128 MiB of HBM per device.

v0:
```python
import functools

import jax
import jax.numpy as jnp
from jax import lax
from jax.experimental import pallas as pl
from jax.experimental.pallas import tpu as pltpu
from jax.sharding import PartitionSpec as P

HEADS = 12
HEAD_DIM = 64
WINDOWS = 2
CHUNKS = 2
LATE_SLOTS = 2
TILE_LOCS = 16
NORM_ROWS = 128
COLUMNS = 256
UNIT_ROWS = 128
UNITS_STEP = 2
CHANNEL_PAIRS = 2
MLP_BLOCKS = 2
LANES = 128
QUERY_SCALE = HEAD_DIM ** (-0.5) * 1.4426950408889634
VMEM_LIMIT = 40 * 1024 * 1024

F32 = jnp.float32
BF16 = jnp.bfloat16


def dot(left, right):
    return jnp.dot(left, right, preferred_element_type=F32)


def dot_t(left, right):
    return lax.dot_general(left, right, (((1,), (1,)), ((), ())), preferred_element_type=F32)


def norm_rows(values):
    centre = values - jnp.mean(values, axis=-1, keepdims=True)
    spread = jnp.mean(centre * centre, axis=-1, keepdims=True)
    return centre * lax.rsqrt(spread + 1e-05)


def gelu(values):
    inner = values * (0.7978845608028654 + 0.035677408136300125 * (values * values))
    return (0.5 * values) * (1.0 + jnp.tanh(inner))


def call(kernel, out_shape, flops, nbytes, **kwargs):
    return pl.pallas_call(
        kernel,
        out_shape=out_shape,
        compiler_params=pltpu.CompilerParams(vmem_limit_bytes=VMEM_LIMIT),
        cost_estimate=pl.CostEstimate(flops=flops, bytes_accessed=nbytes, transcendentals=0),
        **kwargs,
    )


def exchange(value, axis, step):
    if step == 0:
        return value
    return lax.ppermute(value, axis, [(i, i ^ step) for i in range(lax.axis_size(axis))])


class Plan:
    def __init__(self, tokens):
        self.loc_dev, self.band_dev, self.width = tokens.shape
        self.locs = lax.axis_size("loc")
        self.groups = lax.axis_size("band")
        self.share = self.locs // (self.band_dev * WINDOWS)
        assert self.share * self.band_dev * WINDOWS == self.locs
        self.block = self.loc_dev // WINDOWS
        self.rows = self.block // self.share
        self.chunks = CHUNKS
        self.chunk_rows = self.rows // self.chunks
        self.part_rows = self.chunk_rows // self.groups
        assert self.part_rows * self.groups * self.chunks * self.share == self.block


def location_keys(plan, ids):
    size = plan.loc_dev
    row = jnp.broadcast_to(ids.astype(F32), (size, size))
    first = lax.broadcasted_iota(jnp.int32, (size, size), 0)
    second = lax.broadcasted_iota(jnp.int32, (size, size), 1)
    column = jnp.sum(jnp.where(first == second, row, 0.0), axis=1, keepdims=True)
    before = jnp.where((column == row) & (first < second), 1.0, 0.0)
    rank = jnp.sum(before, axis=0, keepdims=True)
    return ids.astype(F32) * plan.block + rank


def arrange(plan, tokens, ids):
    def kernel(ids_ref, x_ref, *rest):
        outs, bands = rest[: plan.locs], rest[plan.locs]
        me = lax.axis_index("loc")
        group = lax.axis_index("band")
        keys = location_keys(plan, ids_ref[pl.ds(me, 1), :])
        for band in range(plan.band_dev):
            bands[band] = x_ref[:, band, :]
        place = lax.broadcasted_iota(jnp.int32, (plan.rows, plan.loc_dev), 0)
        chunk = place // plan.chunk_rows
        owner = (place // plan.part_rows) % plan.groups
        rank = chunk * plan.chunk_rows + (owner ^ group) * plan.part_rows + place % plan.part_rows
        for slot in range(plan.locs):
            peer = me ^ slot
            window = peer % WINDOWS
            part = (peer // WINDOWS) % plan.share
            band = peer // (WINDOWS * plan.share)
            wanted = rank + (window * plan.block + part * plan.rows)
            pick = jnp.where(wanted.astype(F32) == keys, 1.0, 0.0).astype(BF16)
            outs[slot][...] = dot(pick, bands[band]).astype(BF16)

    shape = jax.ShapeDtypeStruct((plan.rows, plan.width), BF16)
    return call(
        kernel,
        [shape] * plan.locs,
        2 * plan.loc_dev * tokens.size,
        4 * tokens.size,
        scratch_shapes=[pltpu.VMEM((plan.band_dev, plan.loc_dev, plan.width), BF16)],
    )(ids, tokens)


def embed_row(plan, index_ref, table_ref):
    band = lax.axis_index("loc") // (WINDOWS * plan.share)
    number = index_ref[lax.axis_index("band") * plan.band_dev + band]
    return table_ref[pl.ds(number, 1), :]


SMEM = pl.BlockSpec(memory_space=pltpu.SMEM)
VMEM = pl.BlockSpec(memory_space=pltpu.VMEM)
ANY = pl.BlockSpec(memory_space=pl.ANY)


def loop(count, step):
    lax.fori_loop(0, count, lambda i, _: (step(i), 0)[1], 0)


def aligned(index, size):
    return pl.ds(pl.multiple_of(index * size, size), size)


def norm_into(target, rows_of, rows):
    tile = min(rows, NORM_ROWS)

    def step(index):
        here = aligned(index, tile)
        target[here, :] = norm_rows(rows_of(here)).astype(BF16)

    loop(rows // tile, step)


def project(plan, slots, index, table, weights, after=()):
    count = len(slots)
    width = plan.width
    rows = count * plan.rows
    blocks = width // COLUMNS

    def kernel(index_ref, table_ref, w_ref, *rest):
        ins, (q_ref, k_ref, v_ref, joined, normed) = rest[:count], rest[count + len(after) :]
        embed = embed_row(plan, index_ref, table_ref)
        for slot in range(count):
            joined[pl.ds(slot * plan.rows, plan.rows), :] = ins[slot][...]
        norm_into(normed, lambda here: joined[here, :].astype(F32) + embed, rows)
        for number, (ref, factor) in enumerate(((q_ref, QUERY_SCALE), (k_ref, 1.0), (v_ref, 1.0))):

            def step(block):
                here = aligned(block, COLUMNS)
                there = pl.ds(
                    pl.multiple_of(number * width + block * COLUMNS, COLUMNS), COLUMNS
                )
                ref[:, here] = (dot(normed[...], w_ref[:, there]) * factor).astype(BF16)

            loop(blocks, step)

    shape = jax.ShapeDtypeStruct((rows, width), BF16)
    return call(
        kernel,
        [shape] * 3,
        2 * rows * width * 3 * width,
        2 * (4 * rows * width + 3 * width * width),
        in_specs=[SMEM, VMEM, VMEM] + [VMEM] * count + [ANY] * len(after),
        out_specs=[VMEM] * 3,
        scratch_shapes=[pltpu.VMEM((rows, width), BF16)] * 2,
    )(index, table, weights, *slots, *after)


def head_masks(rows):
    lane = lax.broadcasted_iota(jnp.int32, (rows, LANES), 1)
    return [(lane // HEAD_DIM) == head for head in range(LANES // HEAD_DIM)]


def stack_heads(query):
    return jnp.concatenate(
        [jnp.where(inside, query, jnp.zeros_like(query)) for inside in head_masks(query.shape[0])],
        axis=0,
    )


def join_heads(stacked):
    heads = LANES // HEAD_DIM
    rows = stacked.shape[0] // heads
    joined = stacked[:rows]
    for head, inside in list(enumerate(head_masks(rows)))[1:]:
        joined = jnp.where(inside, stacked[head * rows : (head + 1) * rows], joined)
    return joined.astype(BF16)


def with_ones(value):
    return jnp.concatenate([value, jnp.ones(value.shape, BF16)], axis=1)


def run_units(units, mask=None):
    def scores_of(unit):
        query, keys, _ = unit
        scores = [dot_t(query, piece) for piece in keys]
        if mask is not None:
            scores = [jnp.where(mask, piece, -1e30) for piece in scores]
        return scores

    results = []
    ahead = scores_of(units[0])
    for number, (_, _, values) in enumerate(units):
        scores = ahead
        if number + 1 < len(units):
            ahead = scores_of(units[number + 1])
        peak = functools.reduce(
            jnp.maximum, [jnp.max(piece, axis=-1, keepdims=True) for piece in scores]
        )
        total = None
        for piece, value in zip(scores, values):
            part = dot(jnp.exp2(piece - peak).astype(BF16), value)
            total = part if total is None else total + part
        results.append(join_heads(total[:, :LANES] / total[:, LANES:]))
    return results


def attend(plan, chunk, query, keys, values, slots, index, table, spatial_out):
    width, rows = plan.width, plan.chunk_rows
    pieces, sources = len(keys), len(query)
    total = plan.locs * rows
    pairs = width // LANES
    unit = min(total, UNIT_ROWS)
    per_step = min(UNITS_STEP, total // unit)
    key_counts = [piece.shape[0] for piece in keys]

    def kernel(index_ref, table_ref, w_ref, *rest):
        q_refs, rest = rest[:sources], rest[sources:]
        k_refs, rest = rest[:pieces], rest[pieces:]
        v_refs, rest = rest[:pieces], rest[pieces:]
        slot_refs, rest = rest[: plan.locs], rest[plan.locs :]
        outs, (asked, result, added, *ones_refs) = rest[: plan.locs], rest[plan.locs :]
        at = 0
        for ref in q_refs:
            for slot in range(ref.shape[0] // plan.rows):
                asked[pl.ds(at, rows), :] = ref[pl.ds(slot * plan.rows + chunk * rows, rows), :]
                at += rows
        for ref in ones_refs:
            ref[:, LANES:] = jnp.ones((ref.shape[0], LANES), BF16)

        def pair_step(pair):
            here = aligned(pair, LANES)
            for ref, v_ref in zip(ones_refs, v_refs):
                ref[:, :LANES] = v_ref[:, here]
            pair_keys = [ref[:, here] for ref in k_refs]
            pair_values = [ref[...] for ref in ones_refs]

            def row_step(step):
                places = [
                    pl.ds(pl.multiple_of((step * per_step + i) * unit, unit), unit)
                    for i in range(per_step)
                ]
                units = [
                    (stack_heads(asked[place, here]), pair_keys, pair_values) for place in places
                ]
                for place, done in zip(places, run_units(units)):
                    result[place, here] = done

            loop(total // (unit * per_step), row_step)

        loop(pairs, pair_step)

        def out_step(block):
            here = aligned(block, COLUMNS)
            added[:, here] = dot(result[...], w_ref[:, here])

        loop(width // COLUMNS, out_step)
        embed = embed_row(plan, index_ref, table_ref)
        for slot in range(plan.locs):
            start = slot_refs[slot][pl.ds(chunk * rows, rows), :].astype(F32) + embed
            outs[slot][...] = (start + added[pl.ds(slot * rows, rows), :]).astype(BF16)

    key_rows = sum(key_counts)
    return call(
        kernel,
        [jax.ShapeDtypeStruct((rows, width), BF16)] * plan.locs,
        16 * total * key_rows * width,
        2 * width * (2 * key_rows + 3 * total + width),
        in_specs=[SMEM] + [VMEM] * (2 + sources + 2 * pieces + plan.locs),
        out_specs=[VMEM] * plan.locs,
        scratch_shapes=[
            pltpu.VMEM((total, width), BF16),
            pltpu.VMEM((total, width), BF16),
            pltpu.VMEM((total, width), F32),
        ]
        + [pltpu.VMEM((count, 2 * LANES), BF16) for count in key_counts],
    )(index, table, spatial_out, *query, *keys, *values, *slots)


def regroup(plan, slots, after=()):
    rows = plan.part_rows
    if rows % 16:
        stacked = jnp.stack(slots).reshape(plan.locs, plan.groups, rows, plan.width)
        return [stacked[:, owner] for owner in range(plan.groups)]

    def kernel(*refs):
        ins, outs = refs[: plan.locs], refs[plan.locs + len(after) :]
        for slot in range(plan.locs):
            for owner in range(plan.groups):
                outs[owner][slot] = ins[slot][owner * rows : (owner + 1) * rows, :]

    shape = jax.ShapeDtypeStruct((plan.locs, rows, plan.width), BF16)
    return call(
        kernel,
        [shape] * plan.groups,
        0,
        4 * plan.locs * plan.chunk_rows * plan.width,
        in_specs=[VMEM] * plan.locs + [ANY] * len(after),
        out_specs=[VMEM] * plan.groups,
    )(*slots, *after)


def channel(plan, parts, channel_qkv, channel_out, up_weight, down_weight):
    groups, width = plan.groups, plan.width
    bands, locations, _ = parts[0].shape
    tile = TILE_LOCS
    assert locations % tile == 0
    tiles = locations // tile
    rows = groups * bands * tile

    def kernel(qkv_hbm, out_hbm, up_hbm, down_hbm, *refs):
        ins, refs = refs[:groups], refs[groups:]
        outs, refs = refs[:groups], refs[groups:]
        qkv_ref, out_ref, up_ref, down_ref, mid, normed, packed, attended, sems = refs
        copies = [
            pltpu.make_async_copy(source, target, sems.at[number])
            for number, (source, target) in enumerate(
                (
                    (qkv_hbm, qkv_ref),
                    (out_hbm, out_ref),
                    (up_hbm, up_ref),
                    (down_hbm, down_ref),
                )
            )
        ]
        for copy in copies:
            copy.start()
        for index in range(tiles):
            for owner in range(groups):
                at = index * rows + owner * bands * tile
                mid[pl.ds(at, bands * tile), :] = (
                    ins[owner][:, index * tile : (index + 1) * tile, :]
                    .reshape(bands * tile, width)
                    .astype(F32)
                )
        norm_into(normed, lambda here: mid[here, :], tiles * rows)
        copies[0].wait()

        def packed_step(block):
            here = aligned(block, COLUMNS)
            factor = jnp.where(block < width // COLUMNS, QUERY_SCALE, 1.0)
            packed[:, here] = (dot(normed[...], qkv_ref[:, here]) * factor).astype(BF16)

        loop(3 * width // COLUMNS, packed_step)
        pairs = width // LANES
        stacked = rows * (LANES // HEAD_DIM)
        first = lax.broadcasted_iota(jnp.int32, (stacked, rows), 0)
        second = lax.broadcasted_iota(jnp.int32, (stacked, rows), 1)
        mask = (first % tile) == (second % tile)

        def attention_step(number):
            index = number // (pairs // CHANNEL_PAIRS)
            mine = aligned(index, rows)
            units = []
            places = []
            for i in range(CHANNEL_PAIRS):
                pair = number % (pairs // CHANNEL_PAIRS) * CHANNEL_PAIRS + i
                query = packed[mine, aligned(pair, LANES)]
                keys = packed[mine, aligned(pair + pairs, LANES)]
                values = packed[mine, aligned(pair + 2 * pairs, LANES)]
                units.append((stack_heads(query), [keys], [with_ones(values)]))
                places.append(aligned(pair, LANES))
            for place, done in zip(places, run_units(units, mask)):
                attended[mine, place] = done

        loop(tiles * pairs // CHANNEL_PAIRS, attention_step)
        copies[1].wait()

        def out_step(block):
            here = aligned(block, COLUMNS)
            mid[:, here] += dot(attended[...], out_ref[:, here])

        loop(width // COLUMNS, out_step)
        norm_into(normed, lambda here: mid[here, :], tiles * rows)
        copies[2].wait()
        copies[3].wait()

        def mlp_step(block):
            places = [aligned(block * MLP_BLOCKS + i, COLUMNS) for i in range(MLP_BLOCKS)]
            raised = [dot(normed[...], up_ref[:, place]) for place in places]
            for place, value in zip(places, raised):
                mid[...] += dot(gelu(value).astype(BF16), down_ref[place, :])

        loop(up_weight.shape[1] // (COLUMNS * MLP_BLOCKS), mlp_step)
        for index in range(tiles):
            for owner in range(groups):
                at = index * rows + owner * bands * tile
                outs[owner][:, index * tile : (index + 1) * tile, :] = (
                    mid[pl.ds(at, bands * tile), :].astype(BF16).reshape(bands, tile, width)
                )

    weights = [channel_qkv, channel_out, up_weight, down_weight]
    size = sum(weight.size for weight in weights)
    count = groups * bands * locations
    return call(
        kernel,
        [jax.ShapeDtypeStruct((bands, locations, width), BF16)] * groups,
        2 * count * size,
        2 * (2 * count * width + size),
        in_specs=[ANY] * 4 + [VMEM] * groups,
        out_specs=[VMEM] * groups,
        scratch_shapes=[pltpu.VMEM(weight.shape, BF16) for weight in weights]
        + [
            pltpu.VMEM((tiles * rows, width), F32),
            pltpu.VMEM((tiles * rows, width), BF16),
            pltpu.VMEM((tiles * rows, 3 * width), BF16),
            pltpu.VMEM((tiles * rows, width), BF16),
            pltpu.SemaphoreType.DMA((len(weights),)),
        ],
    )(*weights, *parts)


def restore(plan, ids, returned):
    locations = plan.loc_dev // (plan.chunks * plan.groups)

    def kernel(ids_ref, *refs):
        ins, out_ref = refs[:-1], refs[-1]
        me = lax.axis_index("loc")
        group = lax.axis_index("band")
        keys = location_keys(plan, ids_ref[pl.ds(me, 1), :])
        place = lax.broadcasted_iota(jnp.int32, (plan.loc_dev, plan.loc_dev), 0)
        inner = place % plan.part_rows
        window = (place // plan.part_rows) % WINDOWS ^ (me % WINDOWS)
        part = (place // (plan.part_rows * WINDOWS)) % plan.share ^ (me // WINDOWS) % plan.share
        owner = (place // locations) % plan.groups ^ group
        chunk = place // (locations * plan.groups)
        wanted = (
            window * plan.block
            + part * plan.rows
            + chunk * plan.chunk_rows
            + owner * plan.part_rows
            + inner
        )
        pick = jnp.where(wanted.astype(F32) == keys, 1.0, 0.0).astype(BF16)
        mine = me // (WINDOWS * plan.share)
        for band in range(plan.band_dev):
            rows = jnp.concatenate([ref[band ^ mine] for ref in ins], axis=0)
            out_ref[:, band, :] = lax.dot_general(
                pick, rows, (((0,), (0,)), ((), ())), preferred_element_type=F32
            ).astype(BF16)

    arrays = [array for chunk in returned for array in chunk]
    size = plan.loc_dev * plan.band_dev * plan.width
    return call(
        kernel,
        jax.ShapeDtypeStruct((plan.loc_dev, plan.band_dev, plan.width), BF16),
        2 * plan.loc_dev * size,
        4 * size,
    )(ids, *arrays)


def body(
    tokens,
    band_index,
    band_table,
    window_ids,
    spatial_qkv,
    spatial_out,
    channel_qkv,
    channel_out,
    up_weight,
    down_weight,
):
    plan = Plan(tokens)
    ids = window_ids.reshape(plan.locs, plan.loc_dev)
    sent = arrange(plan, tokens, ids)
    slots = [exchange(value, "loc", step) for step, value in enumerate(sent)]
    split = plan.locs - LATE_SLOTS
    early = project(plan, slots[:split], band_index, band_table, spatial_qkv)
    late = project(plan, slots[split:], band_index, band_table, spatial_qkv, early[:1])
    query, keys, values = zip(early, late)
    if plan.share > 1:
        same = [
            [(band * plan.share + part) * WINDOWS + window for part in range(plan.share)]
            for band in range(plan.band_dev)
            for window in range(WINDOWS)
        ]
        gather = functools.partial(
            lax.all_gather, axis_name="loc", axis_index_groups=same, axis=0, tiled=True
        )
        keys = [gather(jnp.concatenate(keys, axis=0))]
        values = [gather(jnp.concatenate(values, axis=0))]
    returned = []
    done = []
    for chunk in range(plan.chunks):
        mid = attend(
            plan, chunk, query, keys, values, slots, band_index, band_table, spatial_out
        )
        back = [exchange(value, "loc", step) for step, value in enumerate(mid)]
        parts = regroup(plan, back, done[:1])
        parts = [exchange(value, "band", step) for step, value in enumerate(parts)]
        parts = [part.reshape(plan.band_dev, -1, plan.width) for part in parts]
        done = channel(plan, parts, channel_qkv, channel_out, up_weight, down_weight)
        returned.append([exchange(value, "band", step) for step, value in enumerate(done)])
    return restore(plan, ids, returned)


def solution(mesh):
    placed = (P("loc", "band", None), P(), P(), P(), P(), P(), P(), P(), P(), P())
    return jax.shard_map(
        body, mesh=mesh, in_specs=placed, out_specs=P("loc", "band", None), check_vma=False
    )
```

profile of v0, /device:TPU:0, one launch (start us, length us, event | category | flops | bytes accessed | tf_op | source)
XLA Modules:
  0.0 176.5 jit_solution(9246639774371713621)
XLA Ops:
  2.1 4.2 %shard_map.100 = (bf16[128,768]{1,0:T(8,128)(2,1)S(1)}, bf16[128,768]{1,0:T(8,128)(2,1)S(1)}, bf16[128,768]{1,0:T(8,128)(2,1)S(1)}, bf16[128,768]{1,0:T(8,128)(2...) custom-call(s32[8,256]{1,0:T(8,128)S(1)} %reshape.27.ids_ref, ...), custom_call_target="tpu_custom_call" | custom-call | flops 402653184 | bytes 3145728 | tf_op jit(solution)/shard_map/pallas_call | solution.py:113
  6.9 2.7 %collective-permute-start.1 = (bf16[128,768]{1,0:T(8,128)(2,1)S(1)}, bf16[128,768]{1,0:T(8,128)(2,1)S(1)}, u32[]{:S(2)}, u32[]{:S(2)}) collective-permute-start(bf16[128,768]{1,0:T(8,128)(2,1)S(1)} %get-tuple-element.53), channel_id=1, source_target_pairs={{0,2},{1,3},{2,0},{3,1},{4,6},{5,7},{6,4},{7,5},{8,10},{9,11},{10,... | collective-permute-start | bytes 589832 | tf_op jit(solution)/shard_map/ppermute | solution.py:62
  9.6 2.8 %collective-permute-start.3 = (bf16[128,768]{1,0:T(8,128)(2,1)S(1)}, bf16[128,768]{1,0:T(8,128)(2,1)S(1)}, u32[]{:S(2)}, u32[]{:S(2)}) collective-permute-start(bf16[128,768]{1,0:T(8,128)(2,1)S(1)} %get-tuple-element.55), channel_id=1, source_target_pairs={{0,4},{1,5},{2,6},{3,7},{4,0},{5,1},{6,2},{7,3},{8,12},{9,13},{10,... | collective-permute-start | bytes 589832 | tf_op jit(solution)/shard_map/ppermute | solution.py:62
  12.3 3.6 %collective-permute-start.5 = (bf16[128,768]{1,0:T(8,128)(2,1)S(1)}, bf16[128,768]{1,0:T(8,128)(2,1)S(1)}, u32[]{:S(2)}, u32[]{:S(2)}) collective-permute-start(bf16[128,768]{1,0:T(8,128)(2,1)S(1)} %get-tuple-element.58), channel_id=1, source_target_pairs={{0,6},{1,7},{2,4},{3,5},{4,2},{5,3},{6,0},{7,1},{8,14},{9,15},{10,... | collective-permute-start | bytes 589832 | tf_op jit(solution)/shard_map/ppermute | solution.py:62
  15.9 7.3 %collective-permute-done.1.rest_2_.rest_8_ = bf16[128,768]{1,0:T(8,128)(2,1)S(1)} collective-permute-done((bf16[128,768]{1,0:T(8,128)(2,1)S(1)}, bf16[128,768]{1,0:T(8,128)(2,1)S(1)}, u32[]{:S(2)}, u32[]{:S(2)}) %collective-permute-start.1) | collective-permute-done | bytes 196640 | tf_op jit(solution)/shard_map/ppermute | solution.py:62
  23.7 3.2 %collective-permute-done.2.rest_3_.rest_9_ = bf16[128,768]{1,0:T(8,128)(2,1)S(1)} collective-permute-done((bf16[128,768]{1,0:T(8,128)(2,1)S(1)}, bf16[128,768]{1,0:T(8,128)(2,1)S(1)}, u32[]{:S(2)}, u32[]{:S(2)}) %collective-permute-start.2) | collective-permute-done | bytes 196640 | tf_op jit(solution)/shard_map/ppermute | solution.py:62
  27.4 2.0 %copy-done = bf16[768,2304]{1,0:T(8,128)(2,1)S(1)} copy-done((bf16[768,2304]{1,0:T(8,128)(2,1)S(1)}, bf16[768,2304]{1,0:T(8,128)(2,1)}, u32[]{:S(2)}) %copy-start) | copy-done | bytes 3538968
  29.4 6.4 %shard_map.101 = (bf16[768,768]{1,0:T(8,128)(2,1)S(1)}, bf16[768,768]{1,0:T(8,128)(2,1)S(1)}, bf16[768,768]{1,0:T(8,128)(2,1)S(1)}) custom-call(s32[16]{0:T(128)S(1)} %copy-done.4, f32[16,768]{1,0:T(8,128)S(1)} %copy-done.3, bf16[768,2304]{1,0:T(8,128)(2,1)S(1)} %copy-done, bf16[128,768]{1,0:T(8,128)(2,1)S(1)} %get-tuple-element.51.rest_0_.rest_6_, ...), custom_call_target="tpu_custom_call" | custom-call | flops 2717908992 | bytes 8257536 | tf_op jit(solution)/shard_map/pallas_call | solution.py:175
  35.9 2.1 %collective-permute-done.6.rest_1_.rest_13_ = bf16[128,768]{1,0:T(8,128)(2,1)S(1)} collective-permute-done((bf16[128,768]{1,0:T(8,128)(2,1)S(1)}, bf16[128,768]{1,0:T(8,128)(2,1)S(1)}, u32[]{:S(2)}, u32[]{:S(2)}) %collective-permute-start.6) | collective-permute-done | bytes 196640 | tf_op jit(solution)/shard_map/ppermute | solution.py:62
  37.9 3.5 %shard_map.102 = (bf16[256,768]{1,0:T(8,128)(2,1)S(1)}, bf16[256,768]{1,0:T(8,128)(2,1)S(1)}, bf16[256,768]{1,0:T(8,128)(2,1)S(1)}) custom-call(s32[16]{0:T(128)S(1)} %copy-done.4, f32[16,768]{1,0:T(8,128)S(1)} %copy-done.3, bf16[768,2304]{1,0:T(8,128)(2,1)S(1)} %copy-done.1, bf16[128,768]{1,0:T(8,128)(2,1)S(1)} %collective-permute-done.5.rest_0_.rest_12_, ...), custom_call_target="tpu_custom_call" | custom-call | flops 905969664 | bytes 5111808 | tf_op jit(solution)/shard_map/pallas_call | solution.py:175
  41.4 13.5 %shard_map.103 = (bf16[64,768]{1,0:T(8,128)(2,1)S(1)}, bf16[64,768]{1,0:T(8,128)(2,1)S(1)}, bf16[64,768]{1,0:T(8,128)(2,1)S(1)}, bf16[64,768]{1,0:T(8,128)(2,1)S...) custom-call(s32[16]{0:T(128)S(1)} %copy-done.4, ...), custom_call_target="tpu_custom_call" | custom-call | flops 6442450944 | bytes 6684672 | tf_op jit(solution)/shard_map/pallas_call | solution.py:292
  54.9 11.6 %collective-permute-start.10 = (bf16[64,768]{1,0:T(8,128)(2,1)S(1)}, bf16[64,768]{1,0:T(8,128)(2,1)S(1)}, u32[]{:S(2)}, u32[]{:S(2)}) collective-permute-start(bf16[64,768]{1,0:T(8,128)(2,1)S(1)} %get-tuple-element.69), channel_id=1, source_target_pairs={{0,4},{1,5},{2,6},{3,7},{4,0},{5,1},{6,2},{7,3},{8,12},{9,13},{10,... | collective-permute-start | bytes 294920 | tf_op jit(solution)/shard_map/ppermute | solution.py:62
  66.9 3.8 %collective-permute-start.12 = (bf16[64,768]{1,0:T(8,128)(2,1)S(1)}, bf16[64,768]{1,0:T(8,128)(2,1)S(1)}, u32[]{:S(2)}, u32[]{:S(2)}) collective-permute-start(bf16[64,768]{1,0:T(8,128)(2,1)S(1)} %get-tuple-element.71), channel_id=1, source_target_pairs={{0,6},{1,7},{2,4},{3,5},{4,2},{5,3},{6,0},{7,1},{8,14},{9,15},{10,... | collective-permute-start | bytes 294920 | tf_op jit(solution)/shard_map/ppermute | solution.py:62
  70.9 7.6 %collective-permute-done.10.refs_4_ = bf16[64,768]{1,0:T(8,128)(2,1)S(1)} collective-permute-done((bf16[64,768]{1,0:T(8,128)(2,1)S(1)}, bf16[64,768]{1,0:T(8,128)(2,1)S(1)}, u32[]{:S(2)}, u32[]{:S(2)}) %collective-permute-start.10) | collective-permute-done | bytes 98336 | tf_op jit(solution)/shard_map/ppermute | solution.py:62
  79.0 1.8 %collective-permute-done.11.refs_5_ = bf16[64,768]{1,0:T(8,128)(2,1)S(1)} collective-permute-done((bf16[64,768]{1,0:T(8,128)(2,1)S(1)}, bf16[64,768]{1,0:T(8,128)(2,1)S(1)}, u32[]{:S(2)}, u32[]{:S(2)}) %collective-permute-start.11) | collective-permute-done | bytes 98336 | tf_op jit(solution)/shard_map/ppermute | solution.py:62
  80.9 2.5 %collective-permute-done.8.refs_2_ = bf16[64,768]{1,0:T(8,128)(2,1)S(1)} collective-permute-done((bf16[64,768]{1,0:T(8,128)(2,1)S(1)}, bf16[64,768]{1,0:T(8,128)(2,1)S(1)}, u32[]{:S(2)}, u32[]{:S(2)}) %collective-permute-start.8) | collective-permute-done | bytes 98336 | tf_op jit(solution)/shard_map/ppermute | solution.py:62
  83.3 2.5 %collective-permute-done.9.refs_3_ = bf16[64,768]{1,0:T(8,128)(2,1)S(1)} collective-permute-done((bf16[64,768]{1,0:T(8,128)(2,1)S(1)}, bf16[64,768]{1,0:T(8,128)(2,1)S(1)}, u32[]{:S(2)}, u32[]{:S(2)}) %collective-permute-start.9) | collective-permute-done | bytes 98336 | tf_op jit(solution)/shard_map/ppermute | solution.py:62
  85.8 1.6 collective-permute-start.14
  91.0 13.5 %shard_map.106 = (bf16[64,768]{1,0:T(8,128)(2,1)S(1)}, bf16[64,768]{1,0:T(8,128)(2,1)S(1)}, bf16[64,768]{1,0:T(8,128)(2,1)S(1)}, bf16[64,768]{1,0:T(8,128)(2,1)S...) custom-call(s32[16]{0:T(128)S(1)} %copy-done.4, ...), custom_call_target="tpu_custom_call" | custom-call | flops 6442450944 | bytes 6684672 | tf_op jit(solution)/shard_map/pallas_call | solution.py:292
  106.4 3.8 %collective-permute-done.21.refs_2_ = bf16[64,768]{1,0:T(8,128)(2,1)S(1)} collective-permute-done((bf16[64,768]{1,0:T(8,128)(2,1)S(1)}, bf16[64,768]{1,0:T(8,128)(2,1)S(1)}, u32[]{:S(2)}, u32[]{:S(2)}) %collective-permute-start.21) | collective-permute-done | bytes 98336 | tf_op jit(solution)/shard_map/ppermute | solution.py:62
  110.2 1.6 collective-permute-start.23
  111.9 2.8 %collective-permute-start.25 = (bf16[64,768]{1,0:T(8,128)(2,1)S(1)}, bf16[64,768]{1,0:T(8,128)(2,1)S(1)}, u32[]{:S(2)}, u32[]{:S(2)}) collective-permute-start(bf16[64,768]{1,0:T(8,128)(2,1)S(1)} %get-tuple-element.87), channel_id=1, source_target_pairs={{0,6},{1,7},{2,4},{3,5},{4,2},{5,3},{6,0},{7,1},{8,14},{9,15},{10,... | collective-permute-start | bytes 294920 | tf_op jit(solution)/shard_map/ppermute | solution.py:62
  114.7 1.7 collective-permute-start.26
  116.5 17.1 %shard_map.105 = (bf16[4,32,768]{2,1,0:T(8,128)(2,1)S(1)}, bf16[4,32,768]{2,1,0:T(8,128)(2,1)S(1)}, bf16[4,32,768]{2,1,0:T(8,128)(2,1)S(1)}, bf16[4,32,768]{2,1,0:T(8,128)(2,1)S(1)}) custom-call(bf16[768,2304]{1,0:T(8,128)(2,1)S(1)} %copy-done.5, bf16[768,768]{1,0:T(8,128)(2,1)S(1)} %copy-done.7, bf16[768,3072]{1,0:T(8,128)(2,1)S(1)} %bitcast.9, ...), custom_call_target="tpu_custom_call" | custom-call | flops 7247757312 | bytes 15728640 | tf_op jit(solution)/shard_map/pallas_call | solution.py:423
  133.6 2.1 %collective-permute-start.27 = (bf16[8,16,768]{2,1,0:T(8,128)(2,1)S(1)}, bf16[8,16,768]{2,1,0:T(8,128)(2,1)S(1)}, u32[]{:S(2)}, u32[]{:S(2)}) collective-permute-start(bf16[8,16,768]{2,1,0:T(8,128)(2,1)S(1)} %get-tuple-element.90), channel_id=1, source_target_pairs={{0,8},{8,0},{16,24},{24,16},{1,9},{9,1},{17,25},{25,17},{2,10},{10... | collective-permute-start | bytes 589832 | tf_op jit(solution)/shard_map/ppermute | solution.py:62
  137.3 1.9 %collective-permute-start.17 = (bf16[4,32,768]{2,1,0:T(8,128)(2,1)S(1)}, bf16[4,32,768]{2,1,0:T(8,128)(2,1)S(1)}, u32[]{:S(2)}, u32[]{:S(2)}) collective-permute-start(bf16[4,32,768]{2,1,0:T(8,128)(2,1)S(1)} %get-tuple-element.78), channel_id=1, source_target_pairs={{0,8},{8,0},{16,24},{24,16},{1,9},{9,1},{17,25},{25,17},{2,10},{10... | collective-permute-start | bytes 589832 | tf_op jit(solution)/shard_map/ppermute | solution.py:62
  141.5 2.5 %collective-permute-start.19 = (bf16[4,32,768]{2,1,0:T(8,128)(2,1)S(1)}, bf16[4,32,768]{2,1,0:T(8,128)(2,1)S(1)}, u32[]{:S(2)}, u32[]{:S(2)}) collective-permute-start(bf16[4,32,768]{2,1,0:T(8,128)(2,1)S(1)} %get-tuple-element.80), channel_id=1, source_target_pairs={{0,24},{8,16},{16,8},{24,0},{1,25},{9,17},{17,9},{25,1},{2,26},{10... | collective-permute-start | bytes 589832 | tf_op jit(solution)/shard_map/ppermute | solution.py:62
  144.0 3.7 %collective-permute-done.28 = bf16[8,16,768]{2,1,0:T(8,128)(2,1)S(1)} collective-permute-done((bf16[8,16,768]{2,1,0:T(8,128)(2,1)S(1)}, bf16[8,16,768]{2,1,0:T(8,128)(2,1)S(1)}, u32[]{:S(2)}, u32[]{:S(2)}) %collective-permute-start.28) | collective-permute-done | bytes 196640 | tf_op jit(solution)/shard_map/ppermute | solution.py:62
  147.6 17.3 %shard_map.108 = (bf16[4,32,768]{2,1,0:T(8,128)(2,1)S(1)}, bf16[4,32,768]{2,1,0:T(8,128)(2,1)S(1)}, bf16[4,32,768]{2,1,0:T(8,128)(2,1)S(1)}, bf16[4,32,768]{2,1,0:T(8,128)(2,1)S(1)}) custom-call(bf16[768,2304]{1,0:T(8,128)(2,1)S(1)} %copy-done.5, bf16[768,768]{1,0:T(8,128)(2,1)S(1)} %copy-done.7, bf16[768,3072]{1,0:T(8,128)(2,1)S(1)} %bitcast.9, ...), custom_call_target="tpu_custom_call" | custom-call | flops 7247757312 | bytes 15728640 | tf_op jit(solution)/shard_map/pallas_call | solution.py:423
  168.5 2.2 %collective-permute-done.30.refs_5_ = bf16[4,32,768]{2,1,0:T(8,128)(2,1)S(1)} collective-permute-done((bf16[4,32,768]{2,1,0:T(8,128)(2,1)S(1)}, bf16[4,32,768]{2,1,0:T(8,128)(2,1)S(1)}, u32[]{:S(2)}, u32[]{:S(2)}) %collective-permute-start.30) | collective-permute-done | bytes 196640 | tf_op jit(solution)/shard_map/ppermute | solution.py:62
  170.7 1.8 %collective-permute-done.31.refs_6_ = bf16[4,32,768]{2,1,0:T(8,128)(2,1)S(1)} collective-permute-done((bf16[4,32,768]{2,1,0:T(8,128)(2,1)S(1)}, bf16[4,32,768]{2,1,0:T(8,128)(2,1)S(1)}, u32[]{:S(2)}, u32[]{:S(2)}) %collective-permute-start.31) | collective-permute-done | bytes 196640 | tf_op jit(solution)/shard_map/ppermute | solution.py:62
  173.7 2.8 %shard_map.109 = bf16[256,4,768]{2,1,0:T(4,128)(2,1)} custom-call(s32[8,256]{1,0:T(8,128)S(1)} %reshape.27.ids_ref, bf16[4,32,768]{2,1,0:T(8,128)(2,1)S(1)} %get-tuple-element.77.refs_8_.refs_0_, bf16[4,32,768]{2,1,0:T(8,128)(2,1)S(1)} %collective-permute-done.17.refs_1_, bf16[4,32,768]{2,1,0:T(8,128)(2,1)S(1)} %collective-permute-done.18.refs_2_, ...), custom_call_target="tpu_custom_call" | custom-call | flops 402653184 | bytes 3145728 | tf_op jit(solution)/shard_map/pallas_call | solution.py:472
  (70 shorter events, 19.1 us)
Async XLA Ops:
  6.3 6.0 %collective-permute-start = (bf16[128,768]{1,0:T(8,128)(2,1)S(1)}, bf16[128,768]{1,0:T(8,128)(2,1)S(1)}, u32[]{:S(2)}, u32[]{:S(2)}) collective-permute-start(bf16[128,768]{1,0:T(8,128)(2,1)S(1)} %get-tuple-element.52), channel_id=1, source_target_pairs={{0,1},{1,0},{2,3},{3,2},{4,5},{5,4},{6,7},{7,6},{8,9},{9,8},{10,11... | collective-permute-start | bytes 589832 | tf_op jit(solution)/shard_map/ppermute | solution.py:62
  6.9 16.4 %collective-permute-start.1 = (bf16[128,768]{1,0:T(8,128)(2,1)S(1)}, bf16[128,768]{1,0:T(8,128)(2,1)S(1)}, u32[]{:S(2)}, u32[]{:S(2)}) collective-permute-start(bf16[128,768]{1,0:T(8,128)(2,1)S(1)} %get-tuple-element.53), channel_id=1, source_target_pairs={{0,2},{1,3},{2,0},{3,1},{4,6},{5,7},{6,4},{7,5},{8,10},{9,11},{10,... | collective-permute-start | bytes 589832 | tf_op jit(solution)/shard_map/ppermute | solution.py:62
  9.5 17.4 %collective-permute-start.2 = (bf16[128,768]{1,0:T(8,128)(2,1)S(1)}, bf16[128,768]{1,0:T(8,128)(2,1)S(1)}, u32[]{:S(2)}, u32[]{:S(2)}) collective-permute-start(bf16[128,768]{1,0:T(8,128)(2,1)S(1)} %get-tuple-element.54), channel_id=1, source_target_pairs={{0,3},{1,2},{2,1},{3,0},{4,7},{5,6},{6,5},{7,4},{8,11},{9,10},{10,... | collective-permute-start | bytes 589832 | tf_op jit(solution)/shard_map/ppermute | solution.py:62
  9.6 17.3 %collective-permute-start.3 = (bf16[128,768]{1,0:T(8,128)(2,1)S(1)}, bf16[128,768]{1,0:T(8,128)(2,1)S(1)}, u32[]{:S(2)}, u32[]{:S(2)}) collective-permute-start(bf16[128,768]{1,0:T(8,128)(2,1)S(1)} %get-tuple-element.55), channel_id=1, source_target_pairs={{0,4},{1,5},{2,6},{3,7},{4,0},{5,1},{6,2},{7,3},{8,12},{9,13},{10,... | collective-permute-start | bytes 589832 | tf_op jit(solution)/shard_map/ppermute | solution.py:62
  12.3 15.1 %collective-permute-start.4 = (bf16[128,768]{1,0:T(8,128)(2,1)S(1)}, bf16[128,768]{1,0:T(8,128)(2,1)S(1)}, u32[]{:S(2)}, u32[]{:S(2)}) collective-permute-start(bf16[128,768]{1,0:T(8,128)(2,1)S(1)} %get-tuple-element.56), channel_id=1, source_target_pairs={{0,5},{1,4},{2,7},{3,6},{4,1},{5,0},{6,3},{7,2},{8,13},{9,12},{10,... | collective-permute-start | bytes 589832 | tf_op jit(solution)/shard_map/ppermute | solution.py:62
  12.3 23.5 %collective-permute-start.5 = (bf16[128,768]{1,0:T(8,128)(2,1)S(1)}, bf16[128,768]{1,0:T(8,128)(2,1)S(1)}, u32[]{:S(2)}, u32[]{:S(2)}) collective-permute-start(bf16[128,768]{1,0:T(8,128)(2,1)S(1)} %get-tuple-element.58), channel_id=1, source_target_pairs={{0,6},{1,7},{2,4},{3,5},{4,2},{5,3},{6,0},{7,1},{8,14},{9,15},{10,... | collective-permute-start | bytes 589832 | tf_op jit(solution)/shard_map/ppermute | solution.py:62
  23.2 14.7 %collective-permute-start.6 = (bf16[128,768]{1,0:T(8,128)(2,1)S(1)}, bf16[128,768]{1,0:T(8,128)(2,1)S(1)}, u32[]{:S(2)}, u32[]{:S(2)}) collective-permute-start(bf16[128,768]{1,0:T(8,128)(2,1)S(1)} %get-tuple-element.59), channel_id=1, source_target_pairs={{0,7},{1,6},{2,5},{3,4},{4,3},{5,2},{6,1},{7,0},{8,15},{9,14},{10,... | collective-permute-start | bytes 589832 | tf_op jit(solution)/shard_map/ppermute | solution.py:62
  54.9 23.6 %collective-permute-start.10 = (bf16[64,768]{1,0:T(8,128)(2,1)S(1)}, bf16[64,768]{1,0:T(8,128)(2,1)S(1)}, u32[]{:S(2)}, u32[]{:S(2)}) collective-permute-start(bf16[64,768]{1,0:T(8,128)(2,1)S(1)} %get-tuple-element.69), channel_id=1, source_target_pairs={{0,4},{1,5},{2,6},{3,7},{4,0},{5,1},{6,2},{7,3},{8,12},{9,13},{10,... | collective-permute-start | bytes 294920 | tf_op jit(solution)/shard_map/ppermute | solution.py:62
  66.6 14.2 %collective-permute-start.11 = (bf16[64,768]{1,0:T(8,128)(2,1)S(1)}, bf16[64,768]{1,0:T(8,128)(2,1)S(1)}, u32[]{:S(2)}, u32[]{:S(2)}) collective-permute-start(bf16[64,768]{1,0:T(8,128)(2,1)S(1)} %get-tuple-element.70), channel_id=1, source_target_pairs={{0,5},{1,4},{2,7},{3,6},{4,1},{5,0},{6,3},{7,2},{8,13},{9,12},{10,... | collective-permute-start | bytes 294920 | tf_op jit(solution)/shard_map/ppermute | solution.py:62
  66.9 13.9 %collective-permute-start.12 = (bf16[64,768]{1,0:T(8,128)(2,1)S(1)}, bf16[64,768]{1,0:T(8,128)(2,1)S(1)}, u32[]{:S(2)}, u32[]{:S(2)}) collective-permute-start(bf16[64,768]{1,0:T(8,128)(2,1)S(1)} %get-tuple-element.71), channel_id=1, source_target_pairs={{0,6},{1,7},{2,4},{3,5},{4,2},{5,3},{6,0},{7,1},{8,14},{9,15},{10,... | collective-permute-start | bytes 294920 | tf_op jit(solution)/shard_map/ppermute | solution.py:62
  70.7 10.2 %collective-permute-start.13 = (bf16[64,768]{1,0:T(8,128)(2,1)S(1)}, bf16[64,768]{1,0:T(8,128)(2,1)S(1)}, u32[]{:S(2)}, u32[]{:S(2)}) collective-permute-start(bf16[64,768]{1,0:T(8,128)(2,1)S(1)} %get-tuple-element.72), channel_id=1, source_target_pairs={{0,7},{1,6},{2,5},{3,4},{4,3},{5,2},{6,1},{7,0},{8,15},{9,14},{10,... | collective-permute-start | bytes 294920 | tf_op jit(solution)/shard_map/ppermute | solution.py:62
  70.7 10.2 %collective-permute-start.7 = (bf16[64,768]{1,0:T(8,128)(2,1)S(1)}, bf16[64,768]{1,0:T(8,128)(2,1)S(1)}, u32[]{:S(2)}, u32[]{:S(2)}) collective-permute-start(bf16[64,768]{1,0:T(8,128)(2,1)S(1)} %get-tuple-element.66), channel_id=1, source_target_pairs={{0,1},{1,0},{2,3},{3,2},{4,5},{5,4},{6,7},{7,6},{8,9},{9,8},{10,11... | collective-permute-start | bytes 294920 | tf_op jit(solution)/shard_map/ppermute | solution.py:62
  78.5 4.8 %collective-permute-start.8 = (bf16[64,768]{1,0:T(8,128)(2,1)S(1)}, bf16[64,768]{1,0:T(8,128)(2,1)S(1)}, u32[]{:S(2)}, u32[]{:S(2)}) collective-permute-start(bf16[64,768]{1,0:T(8,128)(2,1)S(1)} %get-tuple-element.67), channel_id=1, source_target_pairs={{0,2},{1,3},{2,0},{3,1},{4,6},{5,7},{6,4},{7,5},{8,10},{9,11},{10,... | collective-permute-start | bytes 294920 | tf_op jit(solution)/shard_map/ppermute | solution.py:62
  80.8 5.0 %collective-permute-start.9 = (bf16[64,768]{1,0:T(8,128)(2,1)S(1)}, bf16[64,768]{1,0:T(8,128)(2,1)S(1)}, u32[]{:S(2)}, u32[]{:S(2)}) collective-permute-start(bf16[64,768]{1,0:T(8,128)(2,1)S(1)} %get-tuple-element.68), channel_id=1, source_target_pairs={{0,3},{1,2},{2,1},{3,0},{4,7},{5,6},{6,5},{7,4},{8,11},{9,10},{10,... | collective-permute-start | bytes 294920 | tf_op jit(solution)/shard_map/ppermute | solution.py:62
  85.8 26.0 %collective-permute-start.14 = (bf16[8,16,768]{2,1,0:T(8,128)(2,1)S(1)}, bf16[8,16,768]{2,1,0:T(8,128)(2,1)S(1)}, u32[]{:S(2)}, u32[]{:S(2)}) collective-permute-start(bf16[8,16,768]{2,1,0:T(8,128)(2,1)S(1)} %get-tuple-element.74), channel_id=1, source_target_pairs={{0,8},{8,0},{16,24},{24,16},{1,9},{9,1},{17,25},{25,17},{2,10},{10... | collective-permute-start | bytes 589832 | tf_op jit(solution)/shard_map/ppermute | solution.py:62
  87.5 24.4 %collective-permute-start.15 = (bf16[8,16,768]{2,1,0:T(8,128)(2,1)S(1)}, bf16[8,16,768]{2,1,0:T(8,128)(2,1)S(1)}, u32[]{:S(2)}, u32[]{:S(2)}) collective-permute-start(bf16[8,16,768]{2,1,0:T(8,128)(2,1)S(1)} %get-tuple-element.75), channel_id=1, source_target_pairs={{0,16},{8,24},{16,0},{24,8},{1,17},{9,25},{17,1},{25,9},{2,18},{10... | collective-permute-start | bytes 589832 | tf_op jit(solution)/shard_map/ppermute | solution.py:62
  89.0 25.7 %collective-permute-start.16 = (bf16[8,16,768]{2,1,0:T(8,128)(2,1)S(1)}, bf16[8,16,768]{2,1,0:T(8,128)(2,1)S(1)}, u32[]{:S(2)}, u32[]{:S(2)}) collective-permute-start(bf16[8,16,768]{2,1,0:T(8,128)(2,1)S(1)} %get-tuple-element.76), channel_id=1, source_target_pairs={{0,24},{8,16},{16,8},{24,0},{1,25},{9,17},{17,9},{25,1},{2,26},{10... | collective-permute-start | bytes 589832 | tf_op jit(solution)/shard_map/ppermute | solution.py:62
  104.6 5.7 %collective-permute-start.21 = (bf16[64,768]{1,0:T(8,128)(2,1)S(1)}, bf16[64,768]{1,0:T(8,128)(2,1)S(1)}, u32[]{:S(2)}, u32[]{:S(2)}) collective-permute-start(bf16[64,768]{1,0:T(8,128)(2,1)S(1)} %get-tuple-element.83), channel_id=1, source_target_pairs={{0,2},{1,3},{2,0},{3,1},{4,6},{5,7},{6,4},{7,5},{8,10},{9,11},{10,... | collective-permute-start | bytes 294920 | tf_op jit(solution)/shard_map/ppermute | solution.py:62
  105.9 27.7 %collective-permute-start.22 = (bf16[64,768]{1,0:T(8,128)(2,1)S(1)}, bf16[64,768]{1,0:T(8,128)(2,1)S(1)}, u32[]{:S(2)}, u32[]{:S(2)}) collective-permute-start(bf16[64,768]{1,0:T(8,128)(2,1)S(1)} %get-tuple-element.84), channel_id=1, source_target_pairs={{0,3},{1,2},{2,1},{3,0},{4,7},{5,6},{6,5},{7,4},{8,11},{9,10},{10,... | collective-permute-start | bytes 294920 | tf_op jit(solution)/shard_map/ppermute | solution.py:62
  110.2 23.3 %collective-permute-start.23 = (bf16[64,768]{1,0:T(8,128)(2,1)S(1)}, bf16[64,768]{1,0:T(8,128)(2,1)S(1)}, u32[]{:S(2)}, u32[]{:S(2)}) collective-permute-start(bf16[64,768]{1,0:T(8,128)(2,1)S(1)} %get-tuple-element.85), channel_id=1, source_target_pairs={{0,4},{1,5},{2,6},{3,7},{4,0},{5,1},{6,2},{7,3},{8,12},{9,13},{10,... | collective-permute-start | bytes 294920 | tf_op jit(solution)/shard_map/ppermute | solution.py:62
  111.8 21.7 %collective-permute-start.24 = (bf16[64,768]{1,0:T(8,128)(2,1)S(1)}, bf16[64,768]{1,0:T(8,128)(2,1)S(1)}, u32[]{:S(2)}, u32[]{:S(2)}) collective-permute-start(bf16[64,768]{1,0:T(8,128)(2,1)S(1)} %get-tuple-element.86), channel_id=1, source_target_pairs={{0,5},{1,4},{2,7},{3,6},{4,1},{5,0},{6,3},{7,2},{8,13},{9,12},{10,... | collective-permute-start | bytes 294920 | tf_op jit(solution)/shard_map/ppermute | solution.py:62
  111.9 21.7 %collective-permute-start.25 = (bf16[64,768]{1,0:T(8,128)(2,1)S(1)}, bf16[64,768]{1,0:T(8,128)(2,1)S(1)}, u32[]{:S(2)}, u32[]{:S(2)}) collective-permute-start(bf16[64,768]{1,0:T(8,128)(2,1)S(1)} %get-tuple-element.87), channel_id=1, source_target_pairs={{0,6},{1,7},{2,4},{3,5},{4,2},{5,3},{6,0},{7,1},{8,14},{9,15},{10,... | collective-permute-start | bytes 294920 | tf_op jit(solution)/shard_map/ppermute | solution.py:62
  114.7 18.9 %collective-permute-start.26 = (bf16[64,768]{1,0:T(8,128)(2,1)S(1)}, bf16[64,768]{1,0:T(8,128)(2,1)S(1)}, u32[]{:S(2)}, u32[]{:S(2)}) collective-permute-start(bf16[64,768]{1,0:T(8,128)(2,1)S(1)} %get-tuple-element.88), channel_id=1, source_target_pairs={{0,7},{1,6},{2,5},{3,4},{4,3},{5,2},{6,1},{7,0},{8,15},{9,14},{10,... | collective-permute-start | bytes 294920 | tf_op jit(solution)/shard_map/ppermute | solution.py:62
  133.6 7.9 %collective-permute-start.27 = (bf16[8,16,768]{2,1,0:T(8,128)(2,1)S(1)}, bf16[8,16,768]{2,1,0:T(8,128)(2,1)S(1)}, u32[]{:S(2)}, u32[]{:S(2)}) collective-permute-start(bf16[8,16,768]{2,1,0:T(8,128)(2,1)S(1)} %get-tuple-element.90), channel_id=1, source_target_pairs={{0,8},{8,0},{16,24},{24,16},{1,9},{9,1},{17,25},{25,17},{2,10},{10... | collective-permute-start | bytes 589832 | tf_op jit(solution)/shard_map/ppermute | solution.py:62
  135.7 11.9 %collective-permute-start.28 = (bf16[8,16,768]{2,1,0:T(8,128)(2,1)S(1)}, bf16[8,16,768]{2,1,0:T(8,128)(2,1)S(1)}, u32[]{:S(2)}, u32[]{:S(2)}) collective-permute-start(bf16[8,16,768]{2,1,0:T(8,128)(2,1)S(1)} %get-tuple-element.91), channel_id=1, source_target_pairs={{0,16},{8,24},{16,0},{24,8},{1,17},{9,25},{17,1},{25,9},{2,18},{10... | collective-permute-start | bytes 589832 | tf_op jit(solution)/shard_map/ppermute | solution.py:62
  136.7 10.9 %collective-permute-start.29 = (bf16[8,16,768]{2,1,0:T(8,128)(2,1)S(1)}, bf16[8,16,768]{2,1,0:T(8,128)(2,1)S(1)}, u32[]{:S(2)}, u32[]{:S(2)}) collective-permute-start(bf16[8,16,768]{2,1,0:T(8,128)(2,1)S(1)} %get-tuple-element.92), channel_id=1, source_target_pairs={{0,24},{8,16},{16,8},{24,0},{1,25},{9,17},{17,9},{25,1},{2,26},{10... | collective-permute-start | bytes 589832 | tf_op jit(solution)/shard_map/ppermute | solution.py:62
  137.3 29.9 %collective-permute-start.17 = (bf16[4,32,768]{2,1,0:T(8,128)(2,1)S(1)}, bf16[4,32,768]{2,1,0:T(8,128)(2,1)S(1)}, u32[]{:S(2)}, u32[]{:S(2)}) collective-permute-start(bf16[4,32,768]{2,1,0:T(8,128)(2,1)S(1)} %get-tuple-element.78), channel_id=1, source_target_pairs={{0,8},{8,0},{16,24},{24,16},{1,9},{9,1},{17,25},{25,17},{2,10},{10... | collective-permute-start | bytes 589832 | tf_op jit(solution)/shard_map/ppermute | solution.py:62
  139.2 29.3 %collective-permute-start.18 = (bf16[4,32,768]{2,1,0:T(8,128)(2,1)S(1)}, bf16[4,32,768]{2,1,0:T(8,128)(2,1)S(1)}, u32[]{:S(2)}, u32[]{:S(2)}) collective-permute-start(bf16[4,32,768]{2,1,0:T(8,128)(2,1)S(1)} %get-tuple-element.79), channel_id=1, source_target_pairs={{0,16},{8,24},{16,0},{24,8},{1,17},{9,25},{17,1},{25,9},{2,18},{10... | collective-permute-start | bytes 589832 | tf_op jit(solution)/shard_map/ppermute | solution.py:62
  141.5 27.0 %collective-permute-start.19 = (bf16[4,32,768]{2,1,0:T(8,128)(2,1)S(1)}, bf16[4,32,768]{2,1,0:T(8,128)(2,1)S(1)}, u32[]{:S(2)}, u32[]{:S(2)}) collective-permute-start(bf16[4,32,768]{2,1,0:T(8,128)(2,1)S(1)} %get-tuple-element.80), channel_id=1, source_target_pairs={{0,24},{8,16},{16,8},{24,0},{1,25},{9,17},{17,9},{25,1},{2,26},{10... | collective-permute-start | bytes 589832 | tf_op jit(solution)/shard_map/ppermute | solution.py:62
  164.9 5.7 %collective-permute-start.30 = (bf16[4,32,768]{2,1,0:T(8,128)(2,1)S(1)}, bf16[4,32,768]{2,1,0:T(8,128)(2,1)S(1)}, u32[]{:S(2)}, u32[]{:S(2)}) collective-permute-start(bf16[4,32,768]{2,1,0:T(8,128)(2,1)S(1)} %get-tuple-element.94), channel_id=1, source_target_pairs={{0,8},{8,0},{16,24},{24,16},{1,9},{9,1},{17,25},{25,17},{2,10},{10... | collective-permute-start | bytes 589832 | tf_op jit(solution)/shard_map/ppermute | solution.py:62
  165.6 6.9 %collective-permute-start.31 = (bf16[4,32,768]{2,1,0:T(8,128)(2,1)S(1)}, bf16[4,32,768]{2,1,0:T(8,128)(2,1)S(1)}, u32[]{:S(2)}, u32[]{:S(2)}) collective-permute-start(bf16[4,32,768]{2,1,0:T(8,128)(2,1)S(1)} %get-tuple-element.95), channel_id=1, source_target_pairs={{0,16},{8,24},{16,0},{24,8},{1,17},{9,25},{17,1},{25,9},{2,18},{10... | collective-permute-start | bytes 589832 | tf_op jit(solution)/shard_map/ppermute | solution.py:62
  167.1 6.6 %collective-permute-start.32 = (bf16[4,32,768]{2,1,0:T(8,128)(2,1)S(1)}, bf16[4,32,768]{2,1,0:T(8,128)(2,1)S(1)}, u32[]{:S(2)}, u32[]{:S(2)}) collective-permute-start(bf16[4,32,768]{2,1,0:T(8,128)(2,1)S(1)} %get-tuple-element.96), channel_id=1, source_target_pairs={{0,24},{8,16},{16,8},{24,0},{1,25},{9,17},{17,9},{25,1},{2,26},{10... | collective-permute-start | bytes 589832 | tf_op jit(solution)/shard_map/ppermute | solution.py:62
  (13 other events, 186.4 us)
where the time goes:
time: 177 us; the launch traced here: 176 us
  Pallas kernels  78.3 us (44%)
  starting transfers between devices  49.9 us (28%)
  waiting for transfers between devices  42.4 us (24%)
  local copies, waits for them, and re-layouts  5.67 us (3%)
    ppermute x33, starting transfers between devices, exchange(): lax.ppermute(value, axis, [(i, i ^ step) for i in range(lax.axis_size(axi...  49.9 us
    ppermute x33, waiting for transfers between devices, exchange(): lax.ppermute(value, axis, [(i, i ^ step) for i in range(lax.axis_size(axi...  42.4 us
    pallas_call x2, Pallas kernels, channel(): call(kernel, [jax.ShapeDtypeStruct((bands, locations, width), BF16)] * gr...  34.3 us
    pallas_call x2, Pallas kernels, attend(): call(kernel, [jax.ShapeDtypeStruct((rows, width), BF16)] * plan.locs, 16...  27 us
    pallas_call x2, Pallas kernels, project(): call(kernel, [shape] * 3, 2 * rows * width * 3 * width, 2 * (4 * rows * w...  9.86 us
    unnamed x24, local copies, waits for them, and re-layouts  4.96 us
    pallas_call x1, Pallas kernels, arrange(): call(kernel, [shape] * plan.locs, 2 * plan.loc_dev * tokens.size, 4 * tok...  4.21 us
  transfers between devices with their start and end apart: 33, of which 15 were waited for; matrix products, arithmetic and copies ran while one was open for 0% of the time, Pallas kernels for 31%

commit v1 on v0

--- a/solution.py
+++ b/solution.py
@@ -11,17 +11,16 @@
 HEAD_DIM = 64
 WINDOWS = 2
 CHUNKS = 2
-LATE_SLOTS = 2
+LATE_SLOTS = 4
 TILE_LOCS = 16
+GROUP_LOCS = 8
 NORM_ROWS = 128
-COLUMNS = 256
 UNIT_ROWS = 128
-UNITS_STEP = 2
-CHANNEL_PAIRS = 2
-MLP_BLOCKS = 2
+STEP_PAIRS = 2
+ROW_TILE = 256
 LANES = 128
-QUERY_SCALE = HEAD_DIM ** (-0.5) * 1.4426950408889634
-VMEM_LIMIT = 40 * 1024 * 1024
+QUERY_SCALE = HEAD_DIM ** (-0.5)
+VMEM_LIMIT = 28 * 1024 * 1024
 
 F32 = jnp.float32
 BF16 = jnp.bfloat16
@@ -60,6 +59,13 @@
     if step == 0:
         return value
     return lax.ppermute(value, axis, [(i, i ^ step) for i in range(lax.axis_size(axis))])
+
+
+def exchange_all(values):
+    got = list(values)
+    for step in reversed(range(len(values))):
+        got[step] = exchange(values[step], "loc", step)
+    return got
 
 
 class Plan:
@@ -151,26 +157,20 @@
 def project(plan, slots, index, table, weights, after=()):
     count = len(slots)
     width = plan.width
+
+    def kernel(index_ref, table_ref, w_ref, *rest):
+        ins, (q_ref, k_ref, v_ref) = rest[:count], rest[count + len(after) :]
+        embed = embed_row(plan, index_ref, table_ref)
+        for first in range(0, count, 2):
+            some = ins[first : first + 2]
+            rows = jnp.concatenate([ref[...].astype(F32) for ref in some], axis=0) + embed
+            normed = norm_rows(rows).astype(BF16)
+            here = pl.ds(first * plan.rows, len(some) * plan.rows)
+            q_ref[here, :] = (dot(normed, w_ref[:, :width]) * QUERY_SCALE).astype(BF16)
+            k_ref[here, :] = dot(normed, w_ref[:, width : 2 * width]).astype(BF16)
+            v_ref[here, :] = dot(normed, w_ref[:, 2 * width :]).astype(BF16)
+
     rows = count * plan.rows
-    blocks = width // COLUMNS
-
-    def kernel(index_ref, table_ref, w_ref, *rest):
-        ins, (q_ref, k_ref, v_ref, joined, normed) = rest[:count], rest[count + len(after) :]
-        embed = embed_row(plan, index_ref, table_ref)
-        for slot in range(count):
-            joined[pl.ds(slot * plan.rows, plan.rows), :] = ins[slot][...]
-        norm_into(normed, lambda here: joined[here, :].astype(F32) + embed, rows)
-        for number, (ref, factor) in enumerate(((q_ref, QUERY_SCALE), (k_ref, 1.0), (v_ref, 1.0))):
-
-            def step(block):
-                here = aligned(block, COLUMNS)
-                there = pl.ds(
-                    pl.multiple_of(number * width + block * COLUMNS, COLUMNS), COLUMNS
-                )
-                ref[:, here] = (dot(normed[...], w_ref[:, there]) * factor).astype(BF16)
-
-            loop(blocks, step)
-
     shape = jax.ShapeDtypeStruct((rows, width), BF16)
     return call(
         kernel,
@@ -179,7 +179,6 @@
         2 * (4 * rows * width + 3 * width * width),
         in_specs=[SMEM, VMEM, VMEM] + [VMEM] * count + [ANY] * len(after),
         out_specs=[VMEM] * 3,
-        scratch_shapes=[pltpu.VMEM((rows, width), BF16)] * 2,
     )(index, table, weights, *slots, *after)
 
 
@@ -201,7 +200,7 @@
     joined = stacked[:rows]
     for head, inside in list(enumerate(head_masks(rows)))[1:]:
         joined = jnp.where(inside, stacked[head * rows : (head + 1) * rows], joined)
-    return joined.astype(BF16)
+    return joined
 
 
 def with_ones(value):
@@ -227,9 +226,11 @@
         )
         total = None
         for piece, value in zip(scores, values):
-            part = dot(jnp.exp2(piece - peak).astype(BF16), value)
+            part = dot(jnp.exp(piece - peak).astype(BF16), value)
             total = part if total is None else total + part
-        results.append(join_heads(total[:, :LANES] / total[:, LANES:]))
+        results.append(
+            (join_heads(total[:, :LANES]) / join_heads(total[:, LANES:])).astype(BF16)
+        )
     return results
 
 
@@ -239,56 +240,39 @@
     total = plan.locs * rows
     pairs = width // LANES
     unit = min(total, UNIT_ROWS)
-    per_step = min(UNITS_STEP, total // unit)
-    key_counts = [piece.shape[0] for piece in keys]
 
     def kernel(index_ref, table_ref, w_ref, *rest):
         q_refs, rest = rest[:sources], rest[sources:]
         k_refs, rest = rest[:pieces], rest[pieces:]
         v_refs, rest = rest[:pieces], rest[pieces:]
         slot_refs, rest = rest[: plan.locs], rest[plan.locs :]
-        outs, (asked, result, added, *ones_refs) = rest[: plan.locs], rest[plan.locs :]
+        outs, (asked, result, added) = rest[: plan.locs], rest[plan.locs :]
         at = 0
         for ref in q_refs:
             for slot in range(ref.shape[0] // plan.rows):
                 asked[pl.ds(at, rows), :] = ref[pl.ds(slot * plan.rows + chunk * rows, rows), :]
                 at += rows
-        for ref in ones_refs:
-            ref[:, LANES:] = jnp.ones((ref.shape[0], LANES), BF16)
-
-        def pair_step(pair):
-            here = aligned(pair, LANES)
-            for ref, v_ref in zip(ones_refs, v_refs):
-                ref[:, :LANES] = v_ref[:, here]
-            pair_keys = [ref[:, here] for ref in k_refs]
-            pair_values = [ref[...] for ref in ones_refs]
-
-            def row_step(step):
-                places = [
-                    pl.ds(pl.multiple_of((step * per_step + i) * unit, unit), unit)
-                    for i in range(per_step)
-                ]
-                units = [
-                    (stack_heads(asked[place, here]), pair_keys, pair_values) for place in places
-                ]
-                for place, done in zip(places, run_units(units)):
-                    result[place, here] = done
-
-            loop(total // (unit * per_step), row_step)
-
-        loop(pairs, pair_step)
-
-        def out_step(block):
-            here = aligned(block, COLUMNS)
-            added[:, here] = dot(result[...], w_ref[:, here])
-
-        loop(width // COLUMNS, out_step)
+        def step(number):
+            units, places = [], []
+            for i in range(STEP_PAIRS):
+                here = aligned(number * STEP_PAIRS + i, LANES)
+                pair_keys = [ref[:, here] for ref in k_refs]
+                pair_values = [with_ones(ref[:, here]) for ref in v_refs]
+                for first in range(0, total, unit):
+                    place = (pl.ds(first, unit), here)
+                    units.append((stack_heads(asked[place]), pair_keys, pair_values))
+                    places.append(place)
+            for place, done in zip(places, run_units(units)):
+                result[place] = done
+
+        loop(pairs // STEP_PAIRS, step)
+        added[...] = dot(result[...], w_ref[...])
         embed = embed_row(plan, index_ref, table_ref)
         for slot in range(plan.locs):
             start = slot_refs[slot][pl.ds(chunk * rows, rows), :].astype(F32) + embed
             outs[slot][...] = (start + added[pl.ds(slot * rows, rows), :]).astype(BF16)
 
-    key_rows = sum(key_counts)
+    key_rows = sum(piece.shape[0] for piece in keys)
     return call(
         kernel,
         [jax.ShapeDtypeStruct((rows, width), BF16)] * plan.locs,
@@ -300,8 +284,7 @@
             pltpu.VMEM((total, width), BF16),
             pltpu.VMEM((total, width), BF16),
             pltpu.VMEM((total, width), F32),
-        ]
-        + [pltpu.VMEM((count, 2 * LANES), BF16) for count in key_counts],
+        ],
     )(index, table, spatial_out, *query, *keys, *values, *slots)
 
 
@@ -331,109 +314,90 @@
 def channel(plan, parts, channel_qkv, channel_out, up_weight, down_weight):
     groups, width = plan.groups, plan.width
     bands, locations, _ = parts[0].shape
-    tile = TILE_LOCS
+    tile, small = TILE_LOCS, GROUP_LOCS
     assert locations % tile == 0
-    tiles = locations // tile
-    rows = groups * bands * tile
-
-    def kernel(qkv_hbm, out_hbm, up_hbm, down_hbm, *refs):
+    group_rows = groups * bands * small
+    rows = groups * bands * locations
+    row_tile = min(rows, ROW_TILE)
+
+    def kernel(qkv_ref, out_ref, up_ref, down_ref, *refs):
         ins, refs = refs[:groups], refs[groups:]
-        outs, refs = refs[:groups], refs[groups:]
-        qkv_ref, out_ref, up_ref, down_ref, mid, normed, packed, attended, sems = refs
-        copies = [
-            pltpu.make_async_copy(source, target, sems.at[number])
-            for number, (source, target) in enumerate(
-                (
-                    (qkv_hbm, qkv_ref),
-                    (out_hbm, out_ref),
-                    (up_hbm, up_ref),
-                    (down_hbm, down_ref),
-                )
-            )
+        outs, (mid, normed, packed, attended) = refs[:groups], refs[groups:]
+        pieces = [
+            (owner, band, first)
+            for owner in range(groups)
+            for band in range(bands)
+            for first in range(0, locations, tile)
         ]
-        for copy in copies:
-            copy.start()
-        for index in range(tiles):
-            for owner in range(groups):
-                at = index * rows + owner * bands * tile
-                mid[pl.ds(at, bands * tile), :] = (
-                    ins[owner][:, index * tile : (index + 1) * tile, :]
-                    .reshape(bands * tile, width)
-                    .astype(F32)
-                )
-        norm_into(normed, lambda here: mid[here, :], tiles * rows)
-        copies[0].wait()
+
+        def places(owner, band, first):
+            return [
+                pl.ds((at // small) * group_rows + (owner * bands + band) * small, small)
+                for at in range(first, first + tile, small)
+            ]
+
+        for owner, band, first in pieces:
+            piece = ins[owner][band, first : first + tile, :].astype(F32)
+            for number, place in enumerate(places(owner, band, first)):
+                mid[place, :] = piece[number * small : (number + 1) * small]
+        norm_into(normed, lambda here: mid[here, :], rows)
 
         def packed_step(block):
-            here = aligned(block, COLUMNS)
-            factor = jnp.where(block < width // COLUMNS, QUERY_SCALE, 1.0)
+            here = aligned(block, width)
+            factor = jnp.where(block == 0, QUERY_SCALE, 1.0)
             packed[:, here] = (dot(normed[...], qkv_ref[:, here]) * factor).astype(BF16)
 
-        loop(3 * width // COLUMNS, packed_step)
+        loop(3, packed_step)
         pairs = width // LANES
-        stacked = rows * (LANES // HEAD_DIM)
-        first = lax.broadcasted_iota(jnp.int32, (stacked, rows), 0)
-        second = lax.broadcasted_iota(jnp.int32, (stacked, rows), 1)
-        mask = (first % tile) == (second % tile)
-
-        def attention_step(number):
-            index = number // (pairs // CHANNEL_PAIRS)
-            mine = aligned(index, rows)
-            units = []
-            places = []
-            for i in range(CHANNEL_PAIRS):
-                pair = number % (pairs // CHANNEL_PAIRS) * CHANNEL_PAIRS + i
+        stacked = group_rows * (LANES // HEAD_DIM)
+        one = lax.broadcasted_iota(jnp.int32, (stacked, group_rows), 0)
+        other = lax.broadcasted_iota(jnp.int32, (stacked, group_rows), 1)
+        mask = (one % small) == (other % small)
+
+        def attention_step(pair):
+            units, spots = [], []
+            for first in range(0, rows, group_rows):
+                mine = pl.ds(first, group_rows)
                 query = packed[mine, aligned(pair, LANES)]
                 keys = packed[mine, aligned(pair + pairs, LANES)]
                 values = packed[mine, aligned(pair + 2 * pairs, LANES)]
                 units.append((stack_heads(query), [keys], [with_ones(values)]))
-                places.append(aligned(pair, LANES))
-            for place, done in zip(places, run_units(units, mask)):
-                attended[mine, place] = done
-
-        loop(tiles * pairs // CHANNEL_PAIRS, attention_step)
-        copies[1].wait()
-
-        def out_step(block):
-            here = aligned(block, COLUMNS)
-            mid[:, here] += dot(attended[...], out_ref[:, here])
-
-        loop(width // COLUMNS, out_step)
-        norm_into(normed, lambda here: mid[here, :], tiles * rows)
-        copies[2].wait()
-        copies[3].wait()
+                spots.append((mine, aligned(pair, LANES)))
+            for spot, done in zip(spots, run_units(units, mask)):
+                attended[spot] = done
+
+        loop(pairs, attention_step)
+        mid[...] += dot(attended[...], out_ref[...])
+        norm_into(normed, lambda here: mid[here, :], rows)
 
         def mlp_step(block):
-            places = [aligned(block * MLP_BLOCKS + i, COLUMNS) for i in range(MLP_BLOCKS)]
-            raised = [dot(normed[...], up_ref[:, place]) for place in places]
-            for place, value in zip(places, raised):
-                mid[...] += dot(gelu(value).astype(BF16), down_ref[place, :])
-
-        loop(up_weight.shape[1] // (COLUMNS * MLP_BLOCKS), mlp_step)
-        for index in range(tiles):
-            for owner in range(groups):
-                at = index * rows + owner * bands * tile
-                outs[owner][:, index * tile : (index + 1) * tile, :] = (
-                    mid[pl.ds(at, bands * tile), :].astype(BF16).reshape(bands, tile, width)
-                )
+            here = aligned(block, width)
+            tiles = [pl.ds(first, row_tile) for first in range(0, rows, row_tile)]
+            raised = [dot(normed[mine, :], up_ref[:, here]) for mine in tiles]
+            for mine, value in zip(tiles, raised):
+                mid[mine, :] += dot(gelu(value).astype(BF16), down_ref[here, :])
+
+        loop(up_weight.shape[1] // width, mlp_step)
+        for owner, band, first in pieces:
+            piece = jnp.concatenate(
+                [mid[place, :] for place in places(owner, band, first)], axis=0
+            )
+            outs[owner][band, first : first + tile, :] = piece.astype(BF16)
 
     weights = [channel_qkv, channel_out, up_weight, down_weight]
     size = sum(weight.size for weight in weights)
-    count = groups * bands * locations
     return call(
         kernel,
         [jax.ShapeDtypeStruct((bands, locations, width), BF16)] * groups,
-        2 * count * size,
-        2 * (2 * count * width + size),
-        in_specs=[ANY] * 4 + [VMEM] * groups,
+        2 * rows * size,
+        2 * (2 * rows * width + size),
+        in_specs=[VMEM] * (4 + groups),
         out_specs=[VMEM] * groups,
-        scratch_shapes=[pltpu.VMEM(weight.shape, BF16) for weight in weights]
-        + [
-            pltpu.VMEM((tiles * rows, width), F32),
-            pltpu.VMEM((tiles * rows, width), BF16),
-            pltpu.VMEM((tiles * rows, 3 * width), BF16),
-            pltpu.VMEM((tiles * rows, width), BF16),
-            pltpu.SemaphoreType.DMA((len(weights),)),
+        scratch_shapes=[
+            pltpu.VMEM((rows, width), F32),
+            pltpu.VMEM((rows, width), BF16),
+            pltpu.VMEM((rows, 3 * width), BF16),
+            pltpu.VMEM((rows, width), BF16),
         ],
     )(*weights, *parts)
 
@@ -492,7 +456,7 @@
     plan = Plan(tokens)
     ids = window_ids.reshape(plan.locs, plan.loc_dev)
     sent = arrange(plan, tokens, ids)
-    slots = [exchange(value, "loc", step) for step, value in enumerate(sent)]
+    slots = exchange_all(sent)
     split = plan.locs - LATE_SLOTS
     early = project(plan, slots[:split], band_index, band_table, spatial_qkv)
     late = project(plan, slots[split:], band_index, band_table, spatial_qkv, early[:1])
@@ -508,14 +472,16 @@
         )
         keys = [gather(jnp.concatenate(keys, axis=0))]
         values = [gather(jnp.concatenate(values, axis=0))]
+    mids = [
+        attend(plan, chunk, query, keys, values, slots, band_index, band_table, spatial_out)
+        for chunk in range(plan.chunks)
+    ]
+    backs = [exchange_all(mid) for mid in mids]
     returned = []
     done = []
     for chunk in range(plan.chunks):
-        mid = attend(
-            plan, chunk, query, keys, values, slots, band_index, band_table, spatial_out
-        )
-        back = [exchange(value, "loc", step) for step, value in enumerate(mid)]
-        parts = regroup(plan, back, done[:1])
+        ahead = [mid[0] for mid in mids[chunk + 1 : chunk + 2]] + list(done[:1])
+        parts = regroup(plan, backs[chunk], ahead)
         parts = [exchange(value, "band", step) for step, value in enumerate(parts)]
         parts = [part.reshape(plan.band_dev, -1, plan.width) for part in parts]
         done = channel(plan, parts, channel_qkv, channel_out, up_weight, down_weight)

time: 177 us -> 154 us (0.87)
  Pallas kernels: 78.3 us -> 63.5 us
  waiting for transfers between devices: 42.4 us -> 28.8 us
  starting transfers between devices: 49.9 us -> 55.1 us
    ppermute x33, waiting for transfers between devices: 42.4 us -> 28.8 us  [exchange(): lax.ppermute(value, axis, [(i, i ^ step) for i in range(lax.axis_size(axi...]
    pallas_call x2, Pallas kernels: 27 us -> 20.2 us  [attend(): call(kernel, [jax.ShapeDtypeStruct((rows, width), BF16)] * plan.locs, 16...]
    ppermute x33, starting transfers between devices: 49.9 us -> 55.1 us  [exchange(): lax.ppermute(value, axis, [(i, i ^ step) for i in range(lax.axis_size(axi...]
    pallas_call x2, Pallas kernels: 9.86 us -> 5.65 us  [project(): call(kernel, [shape] * 3, 2 * rows * width * 3 * width, 2 * (4 * rows * w...]
    pallas_call x2, Pallas kernels: 34.3 us -> 30.5 us  [channel(): call(kernel, [jax.ShapeDtypeStruct((bands, locations, width), BF16)] * gr...]
    unnamed x24 -> x26, local copies, waits for them, and re-layouts: 4.96 us -> 4.91 us
  transfers between devices with their start and end apart: 33 -> 33, of which waited for: 15 -> 10; matrix products, arithmetic and copies ran while one was open for 0% -> 0% of each run, Pallas kernels for 31% -> 28%
where the time goes in v1:
time: 154 us; the launch traced here: 153 us
  Pallas kernels  63.5 us (41%)
  starting transfers between devices  55.1 us (36%)
  waiting for transfers between devices  28.8 us (19%)
  local copies, waits for them, and re-layouts  5.6 us (4%)
    ppermute x33, starting transfers between devices, exchange(): lax.ppermute(value, axis, [(i, i ^ step) for i in range(lax.axis_size(axi...  55.1 us
    pallas_call x2, Pallas kernels, channel(): call(kernel, [jax.ShapeDtypeStruct((bands, locations, width), BF16)] * gr...  30.5 us
    ppermute x33, waiting for transfers between devices, exchange(): lax.ppermute(value, axis, [(i, i ^ step) for i in range(lax.axis_size(axi...  28.8 us
    pallas_call x2, Pallas kernels, attend(): call(kernel, [jax.ShapeDtypeStruct((rows, width), BF16)] * plan.locs, 16...  20.2 us
    pallas_call x2, Pallas kernels, project(): call(kernel, [shape] * 3, 2 * rows * width * 3 * width, 2 * (4 * rows * w...  5.65 us
    unnamed x26, local copies, waits for them, and re-layouts  4.91 us
    pallas_call x1, Pallas kernels, arrange(): call(kernel, [shape] * plan.locs, 2 * plan.loc_dev * tokens.size, 4 * tok...  4.21 us
  transfers between devices with their start and end apart: 33, of which 10 were waited for; matrix products, arithmetic and copies ran while one was open for 0% of the time, Pallas kernels for 28%

profile of v1, /device:TPU:0, one launch (start us, length us, event | category | flops | bytes accessed | tf_op | source)
XLA Modules:
  0.0 153.2 jit_solution(7588646717850380587)
XLA Ops:
  2.1 4.2 %shard_map.100 = (bf16[128,768]{1,0:T(8,128)(2,1)S(1)}, bf16[128,768]{1,0:T(8,128)(2,1)S(1)}, bf16[128,768]{1,0:T(8,128)(2,1)S(1)}, bf16[128,768]{1,0:T(8,128)(2...) custom-call(s32[8,256]{1,0:T(8,128)S(1)} %reshape.27.ids_ref, ...), custom_call_target="tpu_custom_call" | custom-call | flops 402653184 | bytes 3145728 | tf_op jit(solution)/shard_map/pallas_call | solution.py:119
  6.8 2.7 %collective-permute-start.1 = (bf16[128,768]{1,0:T(8,128)(2,1)S(1)}, bf16[128,768]{1,0:T(8,128)(2,1)S(1)}, u32[]{:S(2)}, u32[]{:S(2)}) collective-permute-start(bf16[128,768]{1,0:T(8,128)(2,1)S(1)} %get-tuple-element.53), channel_id=1, source_target_pairs={{0,2},{1,3},{2,0},{3,1},{4,6},{5,7},{6,4},{7,5},{8,10},{9,11},{10,... | collective-permute-start | bytes 589832 | tf_op jit(solution)/shard_map/ppermute | solution.py:61
  9.6 2.8 %collective-permute-start.3 = (bf16[128,768]{1,0:T(8,128)(2,1)S(1)}, bf16[128,768]{1,0:T(8,128)(2,1)S(1)}, u32[]{:S(2)}, u32[]{:S(2)}) collective-permute-start(bf16[128,768]{1,0:T(8,128)(2,1)S(1)} %get-tuple-element.56), channel_id=1, source_target_pairs={{0,4},{1,5},{2,6},{3,7},{4,0},{5,1},{6,2},{7,3},{8,12},{9,13},{10,... | collective-permute-start | bytes 589832 | tf_op jit(solution)/shard_map/ppermute | solution.py:61
  12.3 3.6 %collective-permute-start.5 = (bf16[128,768]{1,0:T(8,128)(2,1)S(1)}, bf16[128,768]{1,0:T(8,128)(2,1)S(1)}, u32[]{:S(2)}, u32[]{:S(2)}) collective-permute-start(bf16[128,768]{1,0:T(8,128)(2,1)S(1)} %get-tuple-element.58), channel_id=1, source_target_pairs={{0,6},{1,7},{2,4},{3,5},{4,2},{5,3},{6,0},{7,1},{8,14},{9,15},{10,... | collective-permute-start | bytes 589832 | tf_op jit(solution)/shard_map/ppermute | solution.py:61
  15.9 7.3 %collective-permute-done.1.rest_2_.rest_8_ = bf16[128,768]{1,0:T(8,128)(2,1)S(1)} collective-permute-done((bf16[128,768]{1,0:T(8,128)(2,1)S(1)}, bf16[128,768]{1,0:T(8,128)(2,1)S(1)}, u32[]{:S(2)}, u32[]{:S(2)}) %collective-permute-start.1) | collective-permute-done | bytes 196640 | tf_op jit(solution)/shard_map/ppermute | solution.py:61
  23.7 3.2 %collective-permute-done.2.rest_3_.rest_9_ = bf16[128,768]{1,0:T(8,128)(2,1)S(1)} collective-permute-done((bf16[128,768]{1,0:T(8,128)(2,1)S(1)}, bf16[128,768]{1,0:T(8,128)(2,1)S(1)}, u32[]{:S(2)}, u32[]{:S(2)}) %collective-permute-start.2) | collective-permute-done | bytes 196640 | tf_op jit(solution)/shard_map/ppermute | solution.py:61
  26.9 2.0 %copy-done.1 = bf16[768,2304]{1,0:T(8,128)(2,1)S(1)} copy-done((bf16[768,2304]{1,0:T(8,128)(2,1)S(1)}, bf16[768,2304]{1,0:T(8,128)(2,1)}, u32[]{:S(2)}) %copy-start.1) | copy-done | bytes 3538968
  30.4 2.8 %shard_map.101 = (bf16[512,768]{1,0:T(8,128)(2,1)S(1)}, bf16[512,768]{1,0:T(8,128)(2,1)S(1)}, bf16[512,768]{1,0:T(8,128)(2,1)S(1)}) custom-call(s32[16]{0:T(128)S(1)} %copy-done.7, f32[16,768]{1,0:T(8,128)S(1)} %copy-done.6, bf16[768,2304]{1,0:T(8,128)(2,1)S(1)} %copy-done.1, bf16[128,768]{1,0:T(8,128)(2,1)S(1)} %get-tuple-element.51.rest_0_.rest_6_, ...), custom_call_target="tpu_custom_call" | custom-call | flops 1811939328 | bytes 6684672 | tf_op jit(solution)/shard_map/pallas_call | solution.py:175
  34.6 3.3 %collective-permute-done.6.rest_3_.rest_13_ = bf16[128,768]{1,0:T(8,128)(2,1)S(1)} collective-permute-done((bf16[128,768]{1,0:T(8,128)(2,1)S(1)}, bf16[128,768]{1,0:T(8,128)(2,1)S(1)}, u32[]{:S(2)}, u32[]{:S(2)}) %collective-permute-start.6) | collective-permute-done | bytes 196640 | tf_op jit(solution)/shard_map/ppermute | solution.py:61
  37.9 2.8 %shard_map.102 = (bf16[512,768]{1,0:T(8,128)(2,1)S(1)}, bf16[512,768]{1,0:T(8,128)(2,1)S(1)}, bf16[512,768]{1,0:T(8,128)(2,1)S(1)}) custom-call(s32[16]{0:T(128)S(1)} %copy-done.7, f32[16,768]{1,0:T(8,128)S(1)} %copy-done.6, bf16[768,2304]{1,0:T(8,128)(2,1)S(1)} %copy-done.2, bf16[128,768]{1,0:T(8,128)(2,1)S(1)} %collective-permute-done.3.rest_0_.rest_10_, ...), custom_call_target="tpu_custom_call" | custom-call | flops 1811939328 | bytes 6684672 | tf_op jit(solution)/shard_map/pallas_call | solution.py:175
  40.8 10.2 %shard_map.103 = (bf16[64,768]{1,0:T(8,128)(2,1)S(1)}, bf16[64,768]{1,0:T(8,128)(2,1)S(1)}, bf16[64,768]{1,0:T(8,128)(2,1)S(1)}, bf16[64,768]{1,0:T(8,128)(2,1)S...) custom-call(s32[16]{0:T(128)S(1)} %copy-done.8, ...), custom_call_target="tpu_custom_call" | custom-call | flops 6442450944 | bytes 6684672 | tf_op jit(solution)/shard_map/pallas_call | solution.py:276
  52.3 9.0 %collective-permute-start.8 = (bf16[64,768]{1,0:T(8,128)(2,1)S(1)}, bf16[64,768]{1,0:T(8,128)(2,1)S(1)}, u32[]{:S(2)}, u32[]{:S(2)}) collective-permute-start(bf16[64,768]{1,0:T(8,128)(2,1)S(1)} %get-tuple-element.67), channel_id=1, source_target_pairs={{0,2},{1,3},{2,0},{3,1},{4,6},{5,7},{6,4},{7,5},{8,10},{9,11},{10,... | collective-permute-start | bytes 294920 | tf_op jit(solution)/shard_map/ppermute | solution.py:61
  61.4 3.1 %collective-permute-start.10 = (bf16[64,768]{1,0:T(8,128)(2,1)S(1)}, bf16[64,768]{1,0:T(8,128)(2,1)S(1)}, u32[]{:S(2)}, u32[]{:S(2)}) collective-permute-start(bf16[64,768]{1,0:T(8,128)(2,1)S(1)} %get-tuple-element.69), channel_id=1, source_target_pairs={{0,4},{1,5},{2,6},{3,7},{4,0},{5,1},{6,2},{7,3},{8,12},{9,13},{10,... | collective-permute-start | bytes 294920 | tf_op jit(solution)/shard_map/ppermute | solution.py:61
  64.8 2.1 %collective-permute-start.12 = (bf16[64,768]{1,0:T(8,128)(2,1)S(1)}, bf16[64,768]{1,0:T(8,128)(2,1)S(1)}, u32[]{:S(2)}, u32[]{:S(2)}) collective-permute-start(bf16[64,768]{1,0:T(8,128)(2,1)S(1)} %get-tuple-element.71), channel_id=1, source_target_pairs={{0,6},{1,7},{2,4},{3,5},{4,2},{5,3},{6,0},{7,1},{8,14},{9,15},{10,... | collective-permute-start | bytes 294920 | tf_op jit(solution)/shard_map/ppermute | solution.py:61
  68.1 10.0 %shard_map.104 = (bf16[64,768]{1,0:T(8,128)(2,1)S(1)}, bf16[64,768]{1,0:T(8,128)(2,1)S(1)}, bf16[64,768]{1,0:T(8,128)(2,1)S(1)}, bf16[64,768]{1,0:T(8,128)(2,1)S...) custom-call(s32[16]{0:T(128)S(1)} %copy-done.8, ...), custom_call_target="tpu_custom_call" | custom-call | flops 6442450944 | bytes 6684672 | tf_op jit(solution)/shard_map/pallas_call | solution.py:276
  78.7 1.5 collective-permute-start.14
  80.2 1.5 collective-permute-start.15
  82.3 4.7 %collective-permute-start.21 = (bf16[64,768]{1,0:T(8,128)(2,1)S(1)}, bf16[64,768]{1,0:T(8,128)(2,1)S(1)}, u32[]{:S(2)}, u32[]{:S(2)}) collective-permute-start(bf16[64,768]{1,0:T(8,128)(2,1)S(1)} %get-tuple-element.83), channel_id=1, source_target_pairs={{0,2},{1,3},{2,0},{3,1},{4,6},{5,7},{6,4},{7,5},{8,10},{9,11},{10,... | collective-permute-start | bytes 294920 | tf_op jit(solution)/shard_map/ppermute | solution.py:61
  88.1 2.6 %collective-permute-done.21.refs_2_ = bf16[64,768]{1,0:T(8,128)(2,1)S(1)} collective-permute-done((bf16[64,768]{1,0:T(8,128)(2,1)S(1)}, bf16[64,768]{1,0:T(8,128)(2,1)S(1)}, u32[]{:S(2)}, u32[]{:S(2)}) %collective-permute-start.21) | collective-permute-done | bytes 98336 | tf_op jit(solution)/shard_map/ppermute | solution.py:61
  90.6 1.8 %collective-permute-start.23 = (bf16[64,768]{1,0:T(8,128)(2,1)S(1)}, bf16[64,768]{1,0:T(8,128)(2,1)S(1)}, u32[]{:S(2)}, u32[]{:S(2)}) collective-permute-start(bf16[64,768]{1,0:T(8,128)(2,1)S(1)} %get-tuple-element.85), channel_id=1, source_target_pairs={{0,4},{1,5},{2,6},{3,7},{4,0},{5,1},{6,2},{7,3},{8,12},{9,13},{10,... | collective-permute-start | bytes 294920 | tf_op jit(solution)/shard_map/ppermute | solution.py:61
  92.7 2.4 %collective-permute-start.25 = (bf16[64,768]{1,0:T(8,128)(2,1)S(1)}, bf16[64,768]{1,0:T(8,128)(2,1)S(1)}, u32[]{:S(2)}, u32[]{:S(2)}) collective-permute-start(bf16[64,768]{1,0:T(8,128)(2,1)S(1)} %get-tuple-element.87), channel_id=1, source_target_pairs={{0,6},{1,7},{2,4},{3,5},{4,2},{5,3},{6,0},{7,1},{8,14},{9,15},{10,... | collective-permute-start | bytes 294920 | tf_op jit(solution)/shard_map/ppermute | solution.py:61
  95.0 1.8 %collective-permute-start.26 = (bf16[64,768]{1,0:T(8,128)(2,1)S(1)}, bf16[64,768]{1,0:T(8,128)(2,1)S(1)}, u32[]{:S(2)}, u32[]{:S(2)}) collective-permute-start(bf16[64,768]{1,0:T(8,128)(2,1)S(1)} %get-tuple-element.88), channel_id=1, source_target_pairs={{0,7},{1,6},{2,5},{3,4},{4,3},{5,2},{6,1},{7,0},{8,15},{9,14},{10,... | collective-permute-start | bytes 294920 | tf_op jit(solution)/shard_map/ppermute | solution.py:61
  96.9 15.4 %shard_map.106 = (bf16[4,32,768]{2,1,0:T(8,128)(2,1)S(1)}, bf16[4,32,768]{2,1,0:T(8,128)(2,1)S(1)}, bf16[4,32,768]{2,1,0:T(8,128)(2,1)S(1)}, bf16[4,32,768]{2,1,0:T(8,128)(2,1)S(1)}) custom-call(bf16[768,2304]{1,0:T(8,128)(2,1)S(1)} %copy-done.3, bf16[768,768]{1,0:T(8,128)(2,1)S(1)} %copy-done.5, bf16[768,3072]{1,0:T(8,128)(2,1)S(1)} %bitcast.9, ...), custom_call_target="tpu_custom_call" | custom-call | flops 7247757312 | bytes 15728640 | tf_op jit(solution)/shard_map/pallas_call | solution.py:389
  112.4 1.5 collective-permute-start.27
  113.9 1.5 collective-permute-start.28
  117.4 1.5 collective-permute-start.18
  120.3 2.4 %collective-permute-start.19 = (bf16[4,32,768]{2,1,0:T(8,128)(2,1)S(1)}, bf16[4,32,768]{2,1,0:T(8,128)(2,1)S(1)}, u32[]{:S(2)}, u32[]{:S(2)}) collective-permute-start(bf16[4,32,768]{2,1,0:T(8,128)(2,1)S(1)} %get-tuple-element.81), channel_id=1, source_target_pairs={{0,24},{8,16},{16,8},{24,0},{1,25},{9,17},{17,9},{25,1},{2,26},{10... | collective-permute-start | bytes 589832 | tf_op jit(solution)/shard_map/ppermute | solution.py:61
  122.6 3.3 %collective-permute-done.28 = bf16[8,16,768]{2,1,0:T(8,128)(2,1)S(1)} collective-permute-done((bf16[8,16,768]{2,1,0:T(8,128)(2,1)S(1)}, bf16[8,16,768]{2,1,0:T(8,128)(2,1)S(1)}, u32[]{:S(2)}, u32[]{:S(2)}) %collective-permute-start.28) | collective-permute-done | bytes 196640 | tf_op jit(solution)/shard_map/ppermute | solution.py:61
  125.9 15.1 %shard_map.108 = (bf16[4,32,768]{2,1,0:T(8,128)(2,1)S(1)}, bf16[4,32,768]{2,1,0:T(8,128)(2,1)S(1)}, bf16[4,32,768]{2,1,0:T(8,128)(2,1)S(1)}, bf16[4,32,768]{2,1,0:T(8,128)(2,1)S(1)}) custom-call(bf16[768,2304]{1,0:T(8,128)(2,1)S(1)} %copy-done.3, bf16[768,768]{1,0:T(8,128)(2,1)S(1)} %copy-done.5, bf16[768,3072]{1,0:T(8,128)(2,1)S(1)} %bitcast.9, ...), custom_call_target="tpu_custom_call" | custom-call | flops 7247757312 | bytes 15728640 | tf_op jit(solution)/shard_map/pallas_call | solution.py:389
  144.6 2.8 %collective-permute-done.30.refs_5_ = bf16[4,32,768]{2,1,0:T(8,128)(2,1)S(1)} collective-permute-done((bf16[4,32,768]{2,1,0:T(8,128)(2,1)S(1)}, bf16[4,32,768]{2,1,0:T(8,128)(2,1)S(1)}, u32[]{:S(2)}, u32[]{:S(2)}) %collective-permute-start.30) | collective-permute-done | bytes 196640 | tf_op jit(solution)/shard_map/ppermute | solution.py:61
  147.4 3.0 %collective-permute-done.31.refs_6_ = bf16[4,32,768]{2,1,0:T(8,128)(2,1)S(1)} collective-permute-done((bf16[4,32,768]{2,1,0:T(8,128)(2,1)S(1)}, bf16[4,32,768]{2,1,0:T(8,128)(2,1)S(1)}, u32[]{:S(2)}, u32[]{:S(2)}) %collective-permute-start.31) | collective-permute-done | bytes 196640 | tf_op jit(solution)/shard_map/ppermute | solution.py:61
  150.5 2.8 %shard_map.109 = bf16[256,4,768]{2,1,0:T(4,128)(2,1)} custom-call(s32[8,256]{1,0:T(8,128)S(1)} %reshape.27.ids_ref, bf16[4,32,768]{2,1,0:T(8,128)(2,1)S(1)} %get-tuple-element.78.refs_8_.refs_0_, bf16[4,32,768]{2,1,0:T(8,128)(2,1)S(1)} %collective-permute-done.17.refs_1_, bf16[4,32,768]{2,1,0:T(8,128)(2,1)S(1)} %collective-permute-done.18.refs_2_, ...), custom_call_target="tpu_custom_call" | custom-call | flops 402653184 | bytes 3145728 | tf_op jit(solution)/shard_map/pallas_call | solution.py:436
  (73 shorter events, 18.2 us)
Async XLA Ops:
  6.3 6.0 %collective-permute-start = (bf16[128,768]{1,0:T(8,128)(2,1)S(1)}, bf16[128,768]{1,0:T(8,128)(2,1)S(1)}, u32[]{:S(2)}, u32[]{:S(2)}) collective-permute-start(bf16[128,768]{1,0:T(8,128)(2,1)S(1)} %get-tuple-element.52), channel_id=1, source_target_pairs={{0,1},{1,0},{2,3},{3,2},{4,5},{5,4},{6,7},{7,6},{8,9},{9,8},{10,11... | collective-permute-start | bytes 589832 | tf_op jit(solution)/shard_map/ppermute | solution.py:61
  6.8 16.4 %collective-permute-start.1 = (bf16[128,768]{1,0:T(8,128)(2,1)S(1)}, bf16[128,768]{1,0:T(8,128)(2,1)S(1)}, u32[]{:S(2)}, u32[]{:S(2)}) collective-permute-start(bf16[128,768]{1,0:T(8,128)(2,1)S(1)} %get-tuple-element.53), channel_id=1, source_target_pairs={{0,2},{1,3},{2,0},{3,1},{4,6},{5,7},{6,4},{7,5},{8,10},{9,11},{10,... | collective-permute-start | bytes 589832 | tf_op jit(solution)/shard_map/ppermute | solution.py:61
  9.5 17.4 %collective-permute-start.2 = (bf16[128,768]{1,0:T(8,128)(2,1)S(1)}, bf16[128,768]{1,0:T(8,128)(2,1)S(1)}, u32[]{:S(2)}, u32[]{:S(2)}) collective-permute-start(bf16[128,768]{1,0:T(8,128)(2,1)S(1)} %get-tuple-element.54), channel_id=1, source_target_pairs={{0,3},{1,2},{2,1},{3,0},{4,7},{5,6},{6,5},{7,4},{8,11},{9,10},{10,... | collective-permute-start | bytes 589832 | tf_op jit(solution)/shard_map/ppermute | solution.py:61
  9.6 23.7 %collective-permute-start.3 = (bf16[128,768]{1,0:T(8,128)(2,1)S(1)}, bf16[128,768]{1,0:T(8,128)(2,1)S(1)}, u32[]{:S(2)}, u32[]{:S(2)}) collective-permute-start(bf16[128,768]{1,0:T(8,128)(2,1)S(1)} %get-tuple-element.56), channel_id=1, source_target_pairs={{0,4},{1,5},{2,6},{3,7},{4,0},{5,1},{6,2},{7,3},{8,12},{9,13},{10,... | collective-permute-start | bytes 589832 | tf_op jit(solution)/shard_map/ppermute | solution.py:61
  12.3 20.9 %collective-permute-start.4 = (bf16[128,768]{1,0:T(8,128)(2,1)S(1)}, bf16[128,768]{1,0:T(8,128)(2,1)S(1)}, u32[]{:S(2)}, u32[]{:S(2)}) collective-permute-start(bf16[128,768]{1,0:T(8,128)(2,1)S(1)} %get-tuple-element.57), channel_id=1, source_target_pairs={{0,5},{1,4},{2,7},{3,6},{4,1},{5,0},{6,3},{7,2},{8,13},{9,12},{10,... | collective-permute-start | bytes 589832 | tf_op jit(solution)/shard_map/ppermute | solution.py:61
  12.3 22.3 %collective-permute-start.5 = (bf16[128,768]{1,0:T(8,128)(2,1)S(1)}, bf16[128,768]{1,0:T(8,128)(2,1)S(1)}, u32[]{:S(2)}, u32[]{:S(2)}) collective-permute-start(bf16[128,768]{1,0:T(8,128)(2,1)S(1)} %get-tuple-element.58), channel_id=1, source_target_pairs={{0,6},{1,7},{2,4},{3,5},{4,2},{5,3},{6,0},{7,1},{8,14},{9,15},{10,... | collective-permute-start | bytes 589832 | tf_op jit(solution)/shard_map/ppermute | solution.py:61
  23.2 14.7 %collective-permute-start.6 = (bf16[128,768]{1,0:T(8,128)(2,1)S(1)}, bf16[128,768]{1,0:T(8,128)(2,1)S(1)}, u32[]{:S(2)}, u32[]{:S(2)}) collective-permute-start(bf16[128,768]{1,0:T(8,128)(2,1)S(1)} %get-tuple-element.59), channel_id=1, source_target_pairs={{0,7},{1,6},{2,5},{3,4},{4,3},{5,2},{6,1},{7,0},{8,15},{9,14},{10,... | collective-permute-start | bytes 589832 | tf_op jit(solution)/shard_map/ppermute | solution.py:61
  51.0 13.8 %collective-permute-start.7 = (bf16[64,768]{1,0:T(8,128)(2,1)S(1)}, bf16[64,768]{1,0:T(8,128)(2,1)S(1)}, u32[]{:S(2)}, u32[]{:S(2)}) collective-permute-start(bf16[64,768]{1,0:T(8,128)(2,1)S(1)} %get-tuple-element.66), channel_id=1, source_target_pairs={{0,1},{1,0},{2,3},{3,2},{4,5},{5,4},{6,7},{7,6},{8,9},{9,8},{10,11... | collective-permute-start | bytes 294920 | tf_op jit(solution)/shard_map/ppermute | solution.py:61
  52.3 14.6 %collective-permute-start.8 = (bf16[64,768]{1,0:T(8,128)(2,1)S(1)}, bf16[64,768]{1,0:T(8,128)(2,1)S(1)}, u32[]{:S(2)}, u32[]{:S(2)}) collective-permute-start(bf16[64,768]{1,0:T(8,128)(2,1)S(1)} %get-tuple-element.67), channel_id=1, source_target_pairs={{0,2},{1,3},{2,0},{3,1},{4,6},{5,7},{6,4},{7,5},{8,10},{9,11},{10,... | collective-permute-start | bytes 294920 | tf_op jit(solution)/shard_map/ppermute | solution.py:61
  61.3 16.8 %collective-permute-start.9 = (bf16[64,768]{1,0:T(8,128)(2,1)S(1)}, bf16[64,768]{1,0:T(8,128)(2,1)S(1)}, u32[]{:S(2)}, u32[]{:S(2)}) collective-permute-start(bf16[64,768]{1,0:T(8,128)(2,1)S(1)} %get-tuple-element.68), channel_id=1, source_target_pairs={{0,3},{1,2},{2,1},{3,0},{4,7},{5,6},{6,5},{7,4},{8,11},{9,10},{10,... | collective-permute-start | bytes 294920 | tf_op jit(solution)/shard_map/ppermute | solution.py:61
  61.4 16.8 %collective-permute-start.10 = (bf16[64,768]{1,0:T(8,128)(2,1)S(1)}, bf16[64,768]{1,0:T(8,128)(2,1)S(1)}, u32[]{:S(2)}, u32[]{:S(2)}) collective-permute-start(bf16[64,768]{1,0:T(8,128)(2,1)S(1)} %get-tuple-element.69), channel_id=1, source_target_pairs={{0,4},{1,5},{2,6},{3,7},{4,0},{5,1},{6,2},{7,3},{8,12},{9,13},{10,... | collective-permute-start | bytes 294920 | tf_op jit(solution)/shard_map/ppermute | solution.py:61
  64.5 14.2 %collective-permute-start.11 = (bf16[64,768]{1,0:T(8,128)(2,1)S(1)}, bf16[64,768]{1,0:T(8,128)(2,1)S(1)}, u32[]{:S(2)}, u32[]{:S(2)}) collective-permute-start(bf16[64,768]{1,0:T(8,128)(2,1)S(1)} %get-tuple-element.70), channel_id=1, source_target_pairs={{0,5},{1,4},{2,7},{3,6},{4,1},{5,0},{6,3},{7,2},{8,13},{9,12},{10,... | collective-permute-start | bytes 294920 | tf_op jit(solution)/shard_map/ppermute | solution.py:61
  64.8 13.9 %collective-permute-start.12 = (bf16[64,768]{1,0:T(8,128)(2,1)S(1)}, bf16[64,768]{1,0:T(8,128)(2,1)S(1)}, u32[]{:S(2)}, u32[]{:S(2)}) collective-permute-start(bf16[64,768]{1,0:T(8,128)(2,1)S(1)} %get-tuple-element.71), channel_id=1, source_target_pairs={{0,6},{1,7},{2,4},{3,5},{4,2},{5,3},{6,0},{7,1},{8,14},{9,15},{10,... | collective-permute-start | bytes 294920 | tf_op jit(solution)/shard_map/ppermute | solution.py:61
  66.9 11.7 %collective-permute-start.13 = (bf16[64,768]{1,0:T(8,128)(2,1)S(1)}, bf16[64,768]{1,0:T(8,128)(2,1)S(1)}, u32[]{:S(2)}, u32[]{:S(2)}) collective-permute-start(bf16[64,768]{1,0:T(8,128)(2,1)S(1)} %get-tuple-element.72), channel_id=1, source_target_pairs={{0,7},{1,6},{2,5},{3,4},{4,3},{5,2},{6,1},{7,0},{8,15},{9,14},{10,... | collective-permute-start | bytes 294920 | tf_op jit(solution)/shard_map/ppermute | solution.py:61
  78.7 13.8 %collective-permute-start.14 = (bf16[8,16,768]{2,1,0:T(8,128)(2,1)S(1)}, bf16[8,16,768]{2,1,0:T(8,128)(2,1)S(1)}, u32[]{:S(2)}, u32[]{:S(2)}) collective-permute-start(bf16[8,16,768]{2,1,0:T(8,128)(2,1)S(1)} %get-tuple-element.75), channel_id=1, source_target_pairs={{0,8},{8,0},{16,24},{24,16},{1,9},{9,1},{17,25},{25,17},{2,10},{10... | collective-permute-start | bytes 589832 | tf_op jit(solution)/shard_map/ppermute | solution.py:61
  80.2 12.5 %collective-permute-start.15 = (bf16[8,16,768]{2,1,0:T(8,128)(2,1)S(1)}, bf16[8,16,768]{2,1,0:T(8,128)(2,1)S(1)}, u32[]{:S(2)}, u32[]{:S(2)}) collective-permute-start(bf16[8,16,768]{2,1,0:T(8,128)(2,1)S(1)} %get-tuple-element.76), channel_id=1, source_target_pairs={{0,16},{8,24},{16,0},{24,8},{1,17},{9,25},{17,1},{25,9},{2,18},{10... | collective-permute-start | bytes 589832 | tf_op jit(solution)/shard_map/ppermute | solution.py:61
  81.7 13.4 %collective-permute-start.16 = (bf16[8,16,768]{2,1,0:T(8,128)(2,1)S(1)}, bf16[8,16,768]{2,1,0:T(8,128)(2,1)S(1)}, u32[]{:S(2)}, u32[]{:S(2)}) collective-permute-start(bf16[8,16,768]{2,1,0:T(8,128)(2,1)S(1)} %get-tuple-element.77), channel_id=1, source_target_pairs={{0,24},{8,16},{16,8},{24,0},{1,25},{9,17},{17,9},{25,1},{2,26},{10... | collective-permute-start | bytes 589832 | tf_op jit(solution)/shard_map/ppermute | solution.py:61
  82.3 8.4 %collective-permute-start.21 = (bf16[64,768]{1,0:T(8,128)(2,1)S(1)}, bf16[64,768]{1,0:T(8,128)(2,1)S(1)}, u32[]{:S(2)}, u32[]{:S(2)}) collective-permute-start(bf16[64,768]{1,0:T(8,128)(2,1)S(1)} %get-tuple-element.83), channel_id=1, source_target_pairs={{0,2},{1,3},{2,0},{3,1},{4,6},{5,7},{6,4},{7,5},{8,10},{9,11},{10,... | collective-permute-start | bytes 294920 | tf_op jit(solution)/shard_map/ppermute | solution.py:61
  87.0 25.3 %collective-permute-start.22 = (bf16[64,768]{1,0:T(8,128)(2,1)S(1)}, bf16[64,768]{1,0:T(8,128)(2,1)S(1)}, u32[]{:S(2)}, u32[]{:S(2)}) collective-permute-start(bf16[64,768]{1,0:T(8,128)(2,1)S(1)} %get-tuple-element.84), channel_id=1, source_target_pairs={{0,3},{1,2},{2,1},{3,0},{4,7},{5,6},{6,5},{7,4},{8,11},{9,10},{10,... | collective-permute-start | bytes 294920 | tf_op jit(solution)/shard_map/ppermute | solution.py:61
  90.6 21.6 %collective-permute-start.23 = (bf16[64,768]{1,0:T(8,128)(2,1)S(1)}, bf16[64,768]{1,0:T(8,128)(2,1)S(1)}, u32[]{:S(2)}, u32[]{:S(2)}) collective-permute-start(bf16[64,768]{1,0:T(8,128)(2,1)S(1)} %get-tuple-element.85), channel_id=1, source_target_pairs={{0,4},{1,5},{2,6},{3,7},{4,0},{5,1},{6,2},{7,3},{8,12},{9,13},{10,... | collective-permute-start | bytes 294920 | tf_op jit(solution)/shard_map/ppermute | solution.py:61
  92.5 19.8 %collective-permute-start.24 = (bf16[64,768]{1,0:T(8,128)(2,1)S(1)}, bf16[64,768]{1,0:T(8,128)(2,1)S(1)}, u32[]{:S(2)}, u32[]{:S(2)}) collective-permute-start(bf16[64,768]{1,0:T(8,128)(2,1)S(1)} %get-tuple-element.86), channel_id=1, source_target_pairs={{0,5},{1,4},{2,7},{3,6},{4,1},{5,0},{6,3},{7,2},{8,13},{9,12},{10,... | collective-permute-start | bytes 294920 | tf_op jit(solution)/shard_map/ppermute | solution.py:61
  92.7 19.7 %collective-permute-start.25 = (bf16[64,768]{1,0:T(8,128)(2,1)S(1)}, bf16[64,768]{1,0:T(8,128)(2,1)S(1)}, u32[]{:S(2)}, u32[]{:S(2)}) collective-permute-start(bf16[64,768]{1,0:T(8,128)(2,1)S(1)} %get-tuple-element.87), channel_id=1, source_target_pairs={{0,6},{1,7},{2,4},{3,5},{4,2},{5,3},{6,0},{7,1},{8,14},{9,15},{10,... | collective-permute-start | bytes 294920 | tf_op jit(solution)/shard_map/ppermute | solution.py:61
  95.0 17.3 %collective-permute-start.26 = (bf16[64,768]{1,0:T(8,128)(2,1)S(1)}, bf16[64,768]{1,0:T(8,128)(2,1)S(1)}, u32[]{:S(2)}, u32[]{:S(2)}) collective-permute-start(bf16[64,768]{1,0:T(8,128)(2,1)S(1)} %get-tuple-element.88), channel_id=1, source_target_pairs={{0,7},{1,6},{2,5},{3,4},{4,3},{5,2},{6,1},{7,0},{8,15},{9,14},{10,... | collective-permute-start | bytes 294920 | tf_op jit(solution)/shard_map/ppermute | solution.py:61
  112.4 7.9 %collective-permute-start.27 = (bf16[8,16,768]{2,1,0:T(8,128)(2,1)S(1)}, bf16[8,16,768]{2,1,0:T(8,128)(2,1)S(1)}, u32[]{:S(2)}, u32[]{:S(2)}) collective-permute-start(bf16[8,16,768]{2,1,0:T(8,128)(2,1)S(1)} %get-tuple-element.90), channel_id=1, source_target_pairs={{0,8},{8,0},{16,24},{24,16},{1,9},{9,1},{17,25},{25,17},{2,10},{10... | collective-permute-start | bytes 589832 | tf_op jit(solution)/shard_map/ppermute | solution.py:61
  113.9 12.0 %collective-permute-start.28 = (bf16[8,16,768]{2,1,0:T(8,128)(2,1)S(1)}, bf16[8,16,768]{2,1,0:T(8,128)(2,1)S(1)}, u32[]{:S(2)}, u32[]{:S(2)}) collective-permute-start(bf16[8,16,768]{2,1,0:T(8,128)(2,1)S(1)} %get-tuple-element.91), channel_id=1, source_target_pairs={{0,16},{8,24},{16,0},{24,8},{1,17},{9,25},{17,1},{25,9},{2,18},{10... | collective-permute-start | bytes 589832 | tf_op jit(solution)/shard_map/ppermute | solution.py:61
  115.4 10.5 %collective-permute-start.29 = (bf16[8,16,768]{2,1,0:T(8,128)(2,1)S(1)}, bf16[8,16,768]{2,1,0:T(8,128)(2,1)S(1)}, u32[]{:S(2)}, u32[]{:S(2)}) collective-permute-start(bf16[8,16,768]{2,1,0:T(8,128)(2,1)S(1)} %get-tuple-element.92), channel_id=1, source_target_pairs={{0,24},{8,16},{16,8},{24,0},{1,25},{9,17},{17,9},{25,1},{2,26},{10... | collective-permute-start | bytes 589832 | tf_op jit(solution)/shard_map/ppermute | solution.py:61
  115.9 27.3 %collective-permute-start.17 = (bf16[4,32,768]{2,1,0:T(8,128)(2,1)S(1)}, bf16[4,32,768]{2,1,0:T(8,128)(2,1)S(1)}, u32[]{:S(2)}, u32[]{:S(2)}) collective-permute-start(bf16[4,32,768]{2,1,0:T(8,128)(2,1)S(1)} %get-tuple-element.79), channel_id=1, source_target_pairs={{0,8},{8,0},{16,24},{24,16},{1,9},{9,1},{17,25},{25,17},{2,10},{10... | collective-permute-start | bytes 589832 | tf_op jit(solution)/shard_map/ppermute | solution.py:61
  117.4 27.3 %collective-permute-start.18 = (bf16[4,32,768]{2,1,0:T(8,128)(2,1)S(1)}, bf16[4,32,768]{2,1,0:T(8,128)(2,1)S(1)}, u32[]{:S(2)}, u32[]{:S(2)}) collective-permute-start(bf16[4,32,768]{2,1,0:T(8,128)(2,1)S(1)} %get-tuple-element.80), channel_id=1, source_target_pairs={{0,16},{8,24},{16,0},{24,8},{1,17},{9,25},{17,1},{25,9},{2,18},{10... | collective-permute-start | bytes 589832 | tf_op jit(solution)/shard_map/ppermute | solution.py:61
  120.3 24.4 %collective-permute-start.19 = (bf16[4,32,768]{2,1,0:T(8,128)(2,1)S(1)}, bf16[4,32,768]{2,1,0:T(8,128)(2,1)S(1)}, u32[]{:S(2)}, u32[]{:S(2)}) collective-permute-start(bf16[4,32,768]{2,1,0:T(8,128)(2,1)S(1)} %get-tuple-element.81), channel_id=1, source_target_pairs={{0,24},{8,16},{16,8},{24,0},{1,25},{9,17},{17,9},{25,1},{2,26},{10... | collective-permute-start | bytes 589832 | tf_op jit(solution)/shard_map/ppermute | solution.py:61
  141.1 6.4 %collective-permute-start.30 = (bf16[4,32,768]{2,1,0:T(8,128)(2,1)S(1)}, bf16[4,32,768]{2,1,0:T(8,128)(2,1)S(1)}, u32[]{:S(2)}, u32[]{:S(2)}) collective-permute-start(bf16[4,32,768]{2,1,0:T(8,128)(2,1)S(1)} %get-tuple-element.94), channel_id=1, source_target_pairs={{0,8},{8,0},{16,24},{24,16},{1,9},{9,1},{17,25},{25,17},{2,10},{10... | collective-permute-start | bytes 589832 | tf_op jit(solution)/shard_map/ppermute | solution.py:61
  142.1 8.4 %collective-permute-start.31 = (bf16[4,32,768]{2,1,0:T(8,128)(2,1)S(1)}, bf16[4,32,768]{2,1,0:T(8,128)(2,1)S(1)}, u32[]{:S(2)}, u32[]{:S(2)}) collective-permute-start(bf16[4,32,768]{2,1,0:T(8,128)(2,1)S(1)} %get-tuple-element.95), channel_id=1, source_target_pairs={{0,16},{8,24},{16,0},{24,8},{1,17},{9,25},{17,1},{25,9},{2,18},{10... | collective-permute-start | bytes 589832 | tf_op jit(solution)/shard_map/ppermute | solution.py:61
  143.3 7.2 %collective-permute-start.32 = (bf16[4,32,768]{2,1,0:T(8,128)(2,1)S(1)}, bf16[4,32,768]{2,1,0:T(8,128)(2,1)S(1)}, u32[]{:S(2)}, u32[]{:S(2)}) collective-permute-start(bf16[4,32,768]{2,1,0:T(8,128)(2,1)S(1)} %get-tuple-element.96), channel_id=1, source_target_pairs={{0,24},{8,16},{16,8},{24,0},{1,25},{9,17},{17,9},{25,1},{2,26},{10... | collective-permute-start | bytes 589832 | tf_op jit(solution)/shard_map/ppermute | solution.py:61
  (14 other events, 212.3 us)

commit v2 on v1

--- a/solution.py
+++ b/solution.py
@@ -98,14 +98,13 @@
     def kernel(ids_ref, x_ref, *rest):
         outs, bands = rest[: plan.locs], rest[plan.locs]
         me = lax.axis_index("loc")
-        group = lax.axis_index("band")
         keys = location_keys(plan, ids_ref[pl.ds(me, 1), :])
         for band in range(plan.band_dev):
             bands[band] = x_ref[:, band, :]
         place = lax.broadcasted_iota(jnp.int32, (plan.rows, plan.loc_dev), 0)
         chunk = place // plan.chunk_rows
         owner = (place // plan.part_rows) % plan.groups
-        rank = chunk * plan.chunk_rows + (owner ^ group) * plan.part_rows + place % plan.part_rows
+        rank = chunk * plan.chunk_rows + owner * plan.part_rows + place % plan.part_rows
         for slot in range(plan.locs):
             peer = me ^ slot
             window = peer % WINDOWS
@@ -246,7 +245,8 @@
         k_refs, rest = rest[:pieces], rest[pieces:]
         v_refs, rest = rest[:pieces], rest[pieces:]
         slot_refs, rest = rest[: plan.locs], rest[plan.locs :]
-        outs, (asked, result, added) = rest[: plan.locs], rest[plan.locs :]
+        out_ref, asked, result, added = rest
+        me = lax.axis_index("loc")
         at = 0
         for ref in q_refs:
             for slot in range(ref.shape[0] // plan.rows):
@@ -270,16 +270,19 @@
         embed = embed_row(plan, index_ref, table_ref)
         for slot in range(plan.locs):
             start = slot_refs[slot][pl.ds(chunk * rows, rows), :].astype(F32) + embed
-            outs[slot][...] = (start + added[pl.ds(slot * rows, rows), :]).astype(BF16)
+            mid = (start + added[pl.ds(slot * rows, rows), :]).astype(BF16)
+            for owner in range(plan.groups):
+                part = mid[owner * plan.part_rows : (owner + 1) * plan.part_rows]
+                out_ref[owner, me ^ slot] = part
 
     key_rows = sum(piece.shape[0] for piece in keys)
     return call(
         kernel,
-        [jax.ShapeDtypeStruct((rows, width), BF16)] * plan.locs,
+        jax.ShapeDtypeStruct((plan.groups, plan.locs, plan.part_rows, width), BF16),
         16 * total * key_rows * width,
         2 * width * (2 * key_rows + 3 * total + width),
         in_specs=[SMEM] + [VMEM] * (2 + sources + 2 * pieces + plan.locs),
-        out_specs=[VMEM] * plan.locs,
+        out_specs=VMEM,
         scratch_shapes=[
             pltpu.VMEM((total, width), BF16),
             pltpu.VMEM((total, width), BF16),
@@ -288,32 +291,9 @@
     )(index, table, spatial_out, *query, *keys, *values, *slots)
 
 
-def regroup(plan, slots, after=()):
-    rows = plan.part_rows
-    if rows % 16:
-        stacked = jnp.stack(slots).reshape(plan.locs, plan.groups, rows, plan.width)
-        return [stacked[:, owner] for owner in range(plan.groups)]
-
-    def kernel(*refs):
-        ins, outs = refs[: plan.locs], refs[plan.locs + len(after) :]
-        for slot in range(plan.locs):
-            for owner in range(plan.groups):
-                outs[owner][slot] = ins[slot][owner * rows : (owner + 1) * rows, :]
-
-    shape = jax.ShapeDtypeStruct((plan.locs, rows, plan.width), BF16)
-    return call(
-        kernel,
-        [shape] * plan.groups,
-        0,
-        4 * plan.locs * plan.chunk_rows * plan.width,
-        in_specs=[VMEM] * plan.locs + [ANY] * len(after),
-        out_specs=[VMEM] * plan.groups,
-    )(*slots, *after)
-
-
 def channel(plan, parts, channel_qkv, channel_out, up_weight, down_weight):
     groups, width = plan.groups, plan.width
-    bands, locations, _ = parts[0].shape
+    _, bands, locations, _ = parts.shape
     tile, small = TILE_LOCS, GROUP_LOCS
     assert locations % tile == 0
     group_rows = groups * bands * small
@@ -321,8 +301,9 @@
     row_tile = min(rows, ROW_TILE)
 
     def kernel(qkv_ref, out_ref, up_ref, down_ref, *refs):
-        ins, refs = refs[:groups], refs[groups:]
+        in_ref, *refs = refs
         outs, (mid, normed, packed, attended) = refs[:groups], refs[groups:]
+        me = lax.axis_index("band")
         pieces = [
             (owner, band, first)
             for owner in range(groups)
@@ -337,7 +318,7 @@
             ]
 
         for owner, band, first in pieces:
-            piece = ins[owner][band, first : first + tile, :].astype(F32)
+            piece = in_ref[me ^ owner, band, first : first + tile, :].astype(F32)
             for number, place in enumerate(places(owner, band, first)):
                 mid[place, :] = piece[number * small : (number + 1) * small]
         norm_into(normed, lambda here: mid[here, :], rows)
@@ -391,7 +372,7 @@
         [jax.ShapeDtypeStruct((bands, locations, width), BF16)] * groups,
         2 * rows * size,
         2 * (2 * rows * width + size),
-        in_specs=[VMEM] * (4 + groups),
+        in_specs=[VMEM] * 5,
         out_specs=[VMEM] * groups,
         scratch_shapes=[
             pltpu.VMEM((rows, width), F32),
@@ -399,7 +380,7 @@
             pltpu.VMEM((rows, 3 * width), BF16),
             pltpu.VMEM((rows, width), BF16),
         ],
-    )(*weights, *parts)
+    )(*weights, parts)
 
 
 def restore(plan, ids, returned):
@@ -412,8 +393,8 @@
         keys = location_keys(plan, ids_ref[pl.ds(me, 1), :])
         place = lax.broadcasted_iota(jnp.int32, (plan.loc_dev, plan.loc_dev), 0)
         inner = place % plan.part_rows
-        window = (place // plan.part_rows) % WINDOWS ^ (me % WINDOWS)
-        part = (place // (plan.part_rows * WINDOWS)) % plan.share ^ (me // WINDOWS) % plan.share
+        window = (place // plan.part_rows) % WINDOWS
+        part = (place // (plan.part_rows * WINDOWS)) % plan.share
         owner = (place // locations) % plan.groups ^ group
         chunk = place // (locations * plan.groups)
         wanted = (
@@ -424,9 +405,8 @@
             + inner
         )
         pick = jnp.where(wanted.astype(F32) == keys, 1.0, 0.0).astype(BF16)
-        mine = me // (WINDOWS * plan.share)
         for band in range(plan.band_dev):
-            rows = jnp.concatenate([ref[band ^ mine] for ref in ins], axis=0)
+            rows = jnp.concatenate([ref[band] for ref in ins], axis=0)
             out_ref[:, band, :] = lax.dot_general(
                 pick, rows, (((0,), (0,)), ((), ())), preferred_element_type=F32
             ).astype(BF16)
@@ -476,14 +456,12 @@
         attend(plan, chunk, query, keys, values, slots, band_index, band_table, spatial_out)
         for chunk in range(plan.chunks)
     ]
-    backs = [exchange_all(mid) for mid in mids]
     returned = []
-    done = []
-    for chunk in range(plan.chunks):
-        ahead = [mid[0] for mid in mids[chunk + 1 : chunk + 2]] + list(done[:1])
-        parts = regroup(plan, backs[chunk], ahead)
-        parts = [exchange(value, "band", step) for step, value in enumerate(parts)]
-        parts = [part.reshape(plan.band_dev, -1, plan.width) for part in parts]
+    for mid in mids:
+        parts = lax.all_to_all(
+            mid.reshape(-1, plan.part_rows, plan.width), ("band", "loc"), 0, 0, tiled=True
+        )
+        parts = parts.reshape(plan.groups, plan.band_dev, -1, plan.width)
         done = channel(plan, parts, channel_qkv, channel_out, up_weight, down_weight)
         returned.append([exchange(value, "band", step) for step, value in enumerate(done)])
     return restore(plan, ids, returned)

time: 154 us -> 160 us (1.039)
  local copies, waits for them, and re-layouts: 5.6 us -> 27.8 us
  starting transfers between devices: 55.1 us -> 33.6 us
  waiting for transfers between devices: 28.8 us -> 32.7 us
    ppermute x33 -> x13, starting transfers between devices: 55.1 us -> 17.2 us  [exchange(): lax.ppermute(value, axis, [(i, i ^ step) for i in range(lax.axis_size(axi...]
    unnamed x26 -> x56, local copies, waits for them, and re-layouts: 4.91 us -> 27.1 us
    all_to_all x0 -> x2, starting transfers between devices: none -> 16.4 us  [body(): lax.all_to_all(mid.reshape(-1, plan.part_rows, plan.width), ('band', 'loc...]
    all_to_all x0 -> x2, waiting for transfers between devices: none -> 3.53 us  [body(): lax.all_to_all(mid.reshape(-1, plan.part_rows, plan.width), ('band', 'loc...]
    pallas_call x4 -> x2, Pallas kernels: 20.3 us -> 21.8 us  [attend(): call(kernel, jax.ShapeDtypeStruct((plan.groups, plan.locs, plan.part_rows...]
    ppermute x33 -> x13, waiting for transfers between devices: 28.8 us -> 29.1 us  [exchange(): lax.ppermute(value, axis, [(i, i ^ step) for i in range(lax.axis_size(axi...]
  transfers between devices with their start and end apart: 33 -> 15, of which waited for: 10 -> 8; matrix products, arithmetic and copies ran while one was open for 0% -> 0% of each run, Pallas kernels for 28% -> 28%
where the time goes in v2:
time: 160 us; the launch traced here: 159 us
  Pallas kernels  64.6 us (40%)
  starting transfers between devices  33.6 us (21%)
  waiting for transfers between devices  32.7 us (20%)
  local copies, waits for them, and re-layouts  27.8 us (17%)
    pallas_call x2, Pallas kernels, channel(): call(kernel, [jax.ShapeDtypeStruct((bands, locations, width), BF16)] * gr...  30.3 us
    ppermute x13, waiting for transfers between devices, exchange(): lax.ppermute(value, axis, [(i, i ^ step) for i in range(lax.axis_size(axi...  29.1 us
    unnamed x56, local copies, waits for them, and re-layouts  27.1 us
    pallas_call x2, Pallas kernels, attend(): call(kernel, jax.ShapeDtypeStruct((plan.groups, plan.locs, plan.part_rows...  21.8 us
    ppermute x13, starting transfers between devices, exchange(): lax.ppermute(value, axis, [(i, i ^ step) for i in range(lax.axis_size(axi...  17.2 us
    all_to_all x2, starting transfers between devices, body(): lax.all_to_all(mid.reshape(-1, plan.part_rows, plan.width), ('band', 'loc...  16.4 us
    pallas_call x2, Pallas kernels, project(): call(kernel, [shape] * 3, 2 * rows * width * 3 * width, 2 * (4 * rows * w...  5.64 us
    pallas_call x1, Pallas kernels, arrange(): call(kernel, [shape] * plan.locs, 2 * plan.loc_dev * tokens.size, 4 * tok...  4.19 us
  transfers between devices with their start and end apart: 15, of which 8 were waited for; matrix products, arithmetic and copies ran while one was open for 0% of the time, Pallas kernels for 28%

profile of v2, /device:TPU:0, one launch (start us, length us, event | category | flops | bytes accessed | tf_op | source)
XLA Modules:
  0.0 158.9 jit_solution(12552728196550904431)
XLA Ops:
  0.7 1.4 copy-done
  2.1 4.2 %shard_map.100 = (bf16[128,768]{1,0:T(8,128)(2,1)S(1)}, bf16[128,768]{1,0:T(8,128)(2,1)S(1)}, bf16[128,768]{1,0:T(8,128)(2,1)S(1)}, bf16[128,768]{1,0:T(8,128)(2...) custom-call(s32[8,256]{1,0:T(8,128)S(1)} %reshape.15.ids_ref, ...), custom_call_target="tpu_custom_call" | custom-call | flops 402653184 | bytes 3145728 | tf_op jit(solution)/shard_map/pallas_call | solution.py:118
  6.8 2.7 %collective-permute-start.1 = (bf16[128,768]{1,0:T(8,128)(2,1)S(1)}, bf16[128,768]{1,0:T(8,128)(2,1)S(1)}, u32[]{:S(2)}, u32[]{:S(2)}) collective-permute-start(bf16[128,768]{1,0:T(8,128)(2,1)S(1)} %get-tuple-element.29), channel_id=1, source_target_pairs={{0,2},{1,3},{2,0},{3,1},{4,6},{5,7},{6,4},{7,5},{8,10},{9,11},{10,... | collective-permute-start | bytes 589832 | tf_op jit(solution)/shard_map/ppermute | solution.py:61
  9.5 2.8 %collective-permute-start.3 = (bf16[128,768]{1,0:T(8,128)(2,1)S(1)}, bf16[128,768]{1,0:T(8,128)(2,1)S(1)}, u32[]{:S(2)}, u32[]{:S(2)}) collective-permute-start(bf16[128,768]{1,0:T(8,128)(2,1)S(1)} %get-tuple-element.32), channel_id=1, source_target_pairs={{0,4},{1,5},{2,6},{3,7},{4,0},{5,1},{6,2},{7,3},{8,12},{9,13},{10,... | collective-permute-start | bytes 589832 | tf_op jit(solution)/shard_map/ppermute | solution.py:61
  12.3 3.6 %collective-permute-start.5 = (bf16[128,768]{1,0:T(8,128)(2,1)S(1)}, bf16[128,768]{1,0:T(8,128)(2,1)S(1)}, u32[]{:S(2)}, u32[]{:S(2)}) collective-permute-start(bf16[128,768]{1,0:T(8,128)(2,1)S(1)} %get-tuple-element.34), channel_id=1, source_target_pairs={{0,6},{1,7},{2,4},{3,5},{4,2},{5,3},{6,0},{7,1},{8,14},{9,15},{10,... | collective-permute-start | bytes 589832 | tf_op jit(solution)/shard_map/ppermute | solution.py:61
  15.9 7.3 %collective-permute-done.1.rest_2_.rest_8_ = bf16[128,768]{1,0:T(8,128)(2,1)S(1)} collective-permute-done((bf16[128,768]{1,0:T(8,128)(2,1)S(1)}, bf16[128,768]{1,0:T(8,128)(2,1)S(1)}, u32[]{:S(2)}, u32[]{:S(2)}) %collective-permute-start.1) | collective-permute-done | bytes 196640 | tf_op jit(solution)/shard_map/ppermute | solution.py:61
  23.7 3.2 %collective-permute-done.2.rest_3_.rest_9_ = bf16[128,768]{1,0:T(8,128)(2,1)S(1)} collective-permute-done((bf16[128,768]{1,0:T(8,128)(2,1)S(1)}, bf16[128,768]{1,0:T(8,128)(2,1)S(1)}, u32[]{:S(2)}, u32[]{:S(2)}) %collective-permute-start.2) | collective-permute-done | bytes 196640 | tf_op jit(solution)/shard_map/ppermute | solution.py:61
  26.9 2.0 %copy-done.5 = bf16[768,2304]{1,0:T(8,128)(2,1)S(1)} copy-done((bf16[768,2304]{1,0:T(8,128)(2,1)S(1)}, bf16[768,2304]{1,0:T(8,128)(2,1)}, u32[]{:S(2)}) %copy-start.5) | copy-done | bytes 3538968
  30.3 2.8 %shard_map.101 = (bf16[512,768]{1,0:T(8,128)(2,1)S(1)}, bf16[512,768]{1,0:T(8,128)(2,1)S(1)}, bf16[512,768]{1,0:T(8,128)(2,1)S(1)}) custom-call(s32[16]{0:T(128)S(1)} %copy-done.14, f32[16,768]{1,0:T(8,128)S(1)} %copy-done.12, bf16[768,2304]{1,0:T(8,128)(2,1)S(1)} %copy-done.5, bf16[128,768]{1,0:T(8,128)(2,1)S(1)} %get-tuple-element.27.rest_0_.rest_6_, ...), custom_call_target="tpu_custom_call" | custom-call | flops 1811939328 | bytes 6684672 | tf_op jit(solution)/shard_map/pallas_call | solution.py:174
  33.2 1.3 collective-permute-done.5.rest_2_.rest_12_
  34.6 3.3 %collective-permute-done.6.rest_3_.rest_13_ = bf16[128,768]{1,0:T(8,128)(2,1)S(1)} collective-permute-done((bf16[128,768]{1,0:T(8,128)(2,1)S(1)}, bf16[128,768]{1,0:T(8,128)(2,1)S(1)}, u32[]{:S(2)}, u32[]{:S(2)}) %collective-permute-start.6) | collective-permute-done | bytes 196640 | tf_op jit(solution)/shard_map/ppermute | solution.py:61
  37.9 2.8 %shard_map.102 = (bf16[512,768]{1,0:T(8,128)(2,1)S(1)}, bf16[512,768]{1,0:T(8,128)(2,1)S(1)}, bf16[512,768]{1,0:T(8,128)(2,1)S(1)}) custom-call(s32[16]{0:T(128)S(1)} %copy-done.14, f32[16,768]{1,0:T(8,128)S(1)} %copy-done.12, bf16[768,2304]{1,0:T(8,128)(2,1)S(1)} %copy-done.6, bf16[128,768]{1,0:T(8,128)(2,1)S(1)} %collective-permute-done.3.rest_0_.rest_10_, ...), custom_call_target="tpu_custom_call" | custom-call | flops 1811939328 | bytes 6684672 | tf_op jit(solution)/shard_map/pallas_call | solution.py:174
  40.8 10.9 %shard_map.103 = bf16[4,8,16,768]{3,2,1,0:T(8,128)(2,1)} custom-call(s32[16]{0:T(128)S(1)} %copy-done.14, f32[16,768]{1,0:T(8,128)S(1)} %copy-done.12, bf16[768,768]{1,0:T(8,128)(2,1)S(1)} %copy-done.9, bf16[512,768]{1,0:T(8,128)(2,1)S(1)} %get-tuple-element.31.rest_4_.rest_0_, bf16[512,768]{1,0:T(8,128)(2,1)S(1)} %get-tuple-element.36.rest_1_, ...), custom_call_target="tpu_custom_call" | custom-call | flops 6442450944 | bytes 6684672 | tf_op jit(solution)/shard_map/pallas_call | solution.py:279
  51.7 13.8 %all-to-all-start = ((bf16[32,16,768]{2,1,0:T(8,128)(2,1)}), bf16[32,16,768]{2,1,0:T(8,128)(2,1)S(1)}, u32[]{:S(2)}, u32[]{:S(2)}) async-start(bf16[32,16,768]{2,1,0:T(8,128)(2,1)} %bitcast), calls=%async_computation | async-start | bytes 1572864 | tf_op jit(solution)/shard_map/all_to_all | solution.py:461
  73.2 10.8 %shard_map.105 = bf16[4,8,16,768]{3,2,1,0:T(8,128)(2,1)} custom-call(s32[16]{0:T(128)S(1)} %copy-done.15, f32[16,768]{1,0:T(8,128)S(1)} %copy-done.13, bf16[768,768]{1,0:T(8,128)(2,1)S(1)} %copy-done.9, bf16[512,768]{1,0:T(8,128)(2,1)S(1)} %copy-done.17, bf16[512,768]{1,0:T(8,128)(2,1)S(1)} %copy-done.19, bf16[512,768]{1,0:T(8,128)(2,1)S(1)} %copy-done.25, ...), custom_call_target="tpu_custom_call" | custom-call | flops 6442450944 | bytes 6684672 | tf_op jit(solution)/shard_map/pallas_call | solution.py:279
  84.0 3.5 %all-to-all-done = bf16[32,16,768]{2,1,0:T(8,128)(2,1)S(1)} async-done(((bf16[32,16,768]{2,1,0:T(8,128)(2,1)}), bf16[32,16,768]{2,1,0:T(8,128)(2,1)S(1)}, u32[]{:S(2)}, u32[]{:S(2)}) %all-to-all-start) | async-done | bytes 786464 | tf_op jit(solution)/shard_map/all_to_all | solution.py:461
  87.5 2.6 %all-to-all-start.1 = ((bf16[32,16,768]{2,1,0:T(8,128)(2,1)}), bf16[32,16,768]{2,1,0:T(8,128)(2,1)S(1)}, u32[]{:S(2)}, u32[]{:S(2)}) async-start(bf16[32,16,768]{2,1,0:T(8,128)(2,1)} %bitcast.2), calls=%async_computation.1 | async-start | bytes 1572864 | tf_op jit(solution)/shard_map/all_to_all | solution.py:461
  90.2 2.3 %copy-done.1 = bf16[768,3072]{1,0:T(8,128)(2,1)S(1)} copy-done((bf16[768,3072]{1,0:T(8,128)(2,1)S(1)}, bf16[768,3072]{1,0:T(8,128)(2,1)}, u32[]{:S(2)}) %copy-start.1) | copy-done | bytes 4718616
  92.5 2.3 %copy-done.3 = bf16[3072,768]{1,0:T(8,128)(2,1)S(1)} copy-done((bf16[3072,768]{1,0:T(8,128)(2,1)S(1)}, bf16[3072,768]{1,0:T(8,128)(2,1)}, u32[]{:S(2)}) %copy-start.3) | copy-done | bytes 4718616
  94.8 2.0 %copy-done.7 = bf16[768,2304]{1,0:T(8,128)(2,1)S(1)} copy-done((bf16[768,2304]{1,0:T(8,128)(2,1)S(1)}, bf16[768,2304]{1,0:T(8,128)(2,1)}, u32[]{:S(2)}) %copy-start.7) | copy-done | bytes 3538968
  98.1 15.1 %shard_map.104 = (bf16[4,32,768]{2,1,0:T(8,128)(2,1)S(1)}, bf16[4,32,768]{2,1,0:T(8,128)(2,1)S(1)}, bf16[4,32,768]{2,1,0:T(8,128)(2,1)S(1)}, bf16[4,32,768]{2,1,0:T(8,128)(2,1)S(1)}) custom-call(bf16[768,2304]{1,0:T(8,128)(2,1)S(1)} %copy-done.7, bf16[768,768]{1,0:T(8,128)(2,1)S(1)} %copy-done.10, bf16[768,3072]{1,0:T(8,128)(2,1)S(1)} %copy-done.1, ...), custom_call_target="tpu_custom_call" | custom-call | flops 7247757312 | bytes 15728640 | tf_op jit(solution)/shard_map/pallas_call | solution.py:370
  113.3 1.7 %collective-permute-start.7 = (bf16[4,32,768]{2,1,0:T(8,128)(2,1)S(1)}, bf16[4,32,768]{2,1,0:T(8,128)(2,1)S(1)}, u32[]{:S(2)}, u32[]{:S(2)}) collective-permute-start(bf16[4,32,768]{2,1,0:T(8,128)(2,1)S(1)} %get-tuple-element.42), channel_id=1, source_target_pairs={{0,8},{8,0},{16,24},{24,16},{1,9},{9,1},{17,25},{25,17},{2,10},{10... | collective-permute-start | bytes 589832 | tf_op jit(solution)/shard_map/ppermute | solution.py:61
  115.0 2.3 %copy-done.2 = bf16[768,3072]{1,0:T(8,128)(2,1)S(1)} copy-done((bf16[768,3072]{1,0:T(8,128)(2,1)S(1)}, bf16[768,3072]{1,0:T(8,128)(2,1)}, u32[]{:S(2)}) %copy-start.2) | copy-done | bytes 4718616
  117.3 2.3 %copy-done.4 = bf16[3072,768]{1,0:T(8,128)(2,1)S(1)} copy-done((bf16[3072,768]{1,0:T(8,128)(2,1)S(1)}, bf16[3072,768]{1,0:T(8,128)(2,1)}, u32[]{:S(2)}) %copy-start.4) | copy-done | bytes 4718616
  119.6 2.0 %copy-done.8 = bf16[768,2304]{1,0:T(8,128)(2,1)S(1)} copy-done((bf16[768,2304]{1,0:T(8,128)(2,1)S(1)}, bf16[768,2304]{1,0:T(8,128)(2,1)}, u32[]{:S(2)}) %copy-start.8) | copy-done | bytes 3538968
  121.6 15.1 %shard_map.106 = (bf16[4,32,768]{2,1,0:T(8,128)(2,1)S(1)}, bf16[4,32,768]{2,1,0:T(8,128)(2,1)S(1)}, bf16[4,32,768]{2,1,0:T(8,128)(2,1)S(1)}, bf16[4,32,768]{2,1,0:T(8,128)(2,1)S(1)}) custom-call(bf16[768,2304]{1,0:T(8,128)(2,1)S(1)} %copy-done.8, bf16[768,768]{1,0:T(8,128)(2,1)S(1)} %copy-done.11, bf16[768,3072]{1,0:T(8,128)(2,1)S(1)} %copy-done.2, ...), custom_call_target="tpu_custom_call" | custom-call | flops 7247757312 | bytes 15728640 | tf_op jit(solution)/shard_map/pallas_call | solution.py:370
  136.8 1.6 collective-permute-start.8
  138.7 1.6 %collective-permute-start.10 = (bf16[4,32,768]{2,1,0:T(8,128)(2,1)S(1)}, bf16[4,32,768]{2,1,0:T(8,128)(2,1)S(1)}, u32[]{:S(2)}, u32[]{:S(2)}) collective-permute-start(bf16[4,32,768]{2,1,0:T(8,128)(2,1)S(1)} %get-tuple-element.46), channel_id=1, source_target_pairs={{0,8},{8,0},{16,24},{24,16},{1,9},{9,1},{17,25},{25,17},{2,10},{10... | collective-permute-start | bytes 589832 | tf_op jit(solution)/shard_map/ppermute | solution.py:61
  140.4 1.5 collective-permute-start.11
  142.2 7.0 %collective-permute-done.8.refs_2_ = bf16[4,32,768]{2,1,0:T(8,128)(2,1)S(1)} collective-permute-done((bf16[4,32,768]{2,1,0:T(8,128)(2,1)S(1)}, bf16[4,32,768]{2,1,0:T(8,128)(2,1)S(1)}, u32[]{:S(2)}, u32[]{:S(2)}) %collective-permute-start.8) | collective-permute-done | bytes 196640 | tf_op jit(solution)/shard_map/ppermute | solution.py:61
  150.4 5.8 %collective-permute-done.11.refs_6_ = bf16[4,32,768]{2,1,0:T(8,128)(2,1)S(1)} collective-permute-done((bf16[4,32,768]{2,1,0:T(8,128)(2,1)S(1)}, bf16[4,32,768]{2,1,0:T(8,128)(2,1)S(1)}, u32[]{:S(2)}, u32[]{:S(2)}) %collective-permute-start.11) | collective-permute-done | bytes 196640 | tf_op jit(solution)/shard_map/ppermute | solution.py:61
  156.2 2.8 %shard_map.107 = bf16[256,4,768]{2,1,0:T(4,128)(2,1)} custom-call(s32[8,256]{1,0:T(8,128)S(1)} %reshape.15.ids_ref, bf16[4,32,768]{2,1,0:T(8,128)(2,1)S(1)} %get-tuple-element.41.refs_0_, bf16[4,32,768]{2,1,0:T(8,128)(2,1)S(1)} %collective-permute-done.7.refs_1_, bf16[4,32,768]{2,1,0:T(8,128)(2,1)S(1)} %collective-permute-done.8.refs_2_, ...), custom_call_target="tpu_custom_call" | custom-call | flops 402653184 | bytes 3145728 | tf_op jit(solution)/shard_map/pallas_call | solution.py:416
  (63 shorter events, 14.0 us)
Async XLA Ops:
  6.3 6.0 %collective-permute-start = (bf16[128,768]{1,0:T(8,128)(2,1)S(1)}, bf16[128,768]{1,0:T(8,128)(2,1)S(1)}, u32[]{:S(2)}, u32[]{:S(2)}) collective-permute-start(bf16[128,768]{1,0:T(8,128)(2,1)S(1)} %get-tuple-element.28), channel_id=1, source_target_pairs={{0,1},{1,0},{2,3},{3,2},{4,5},{5,4},{6,7},{7,6},{8,9},{9,8},{10,11... | collective-permute-start | bytes 589832 | tf_op jit(solution)/shard_map/ppermute | solution.py:61
  6.8 16.4 %collective-permute-start.1 = (bf16[128,768]{1,0:T(8,128)(2,1)S(1)}, bf16[128,768]{1,0:T(8,128)(2,1)S(1)}, u32[]{:S(2)}, u32[]{:S(2)}) collective-permute-start(bf16[128,768]{1,0:T(8,128)(2,1)S(1)} %get-tuple-element.29), channel_id=1, source_target_pairs={{0,2},{1,3},{2,0},{3,1},{4,6},{5,7},{6,4},{7,5},{8,10},{9,11},{10,... | collective-permute-start | bytes 589832 | tf_op jit(solution)/shard_map/ppermute | solution.py:61
  9.5 17.4 %collective-permute-start.2 = (bf16[128,768]{1,0:T(8,128)(2,1)S(1)}, bf16[128,768]{1,0:T(8,128)(2,1)S(1)}, u32[]{:S(2)}, u32[]{:S(2)}) collective-permute-start(bf16[128,768]{1,0:T(8,128)(2,1)S(1)} %get-tuple-element.30), channel_id=1, source_target_pairs={{0,3},{1,2},{2,1},{3,0},{4,7},{5,6},{6,5},{7,4},{8,11},{9,10},{10,... | collective-permute-start | bytes 589832 | tf_op jit(solution)/shard_map/ppermute | solution.py:61
  9.5 23.7 %collective-permute-start.3 = (bf16[128,768]{1,0:T(8,128)(2,1)S(1)}, bf16[128,768]{1,0:T(8,128)(2,1)S(1)}, u32[]{:S(2)}, u32[]{:S(2)}) collective-permute-start(bf16[128,768]{1,0:T(8,128)(2,1)S(1)} %get-tuple-element.32), channel_id=1, source_target_pairs={{0,4},{1,5},{2,6},{3,7},{4,0},{5,1},{6,2},{7,3},{8,12},{9,13},{10,... | collective-permute-start | bytes 589832 | tf_op jit(solution)/shard_map/ppermute | solution.py:61
  12.3 20.9 %collective-permute-start.4 = (bf16[128,768]{1,0:T(8,128)(2,1)S(1)}, bf16[128,768]{1,0:T(8,128)(2,1)S(1)}, u32[]{:S(2)}, u32[]{:S(2)}) collective-permute-start(bf16[128,768]{1,0:T(8,128)(2,1)S(1)} %get-tuple-element.33), channel_id=1, source_target_pairs={{0,5},{1,4},{2,7},{3,6},{4,1},{5,0},{6,3},{7,2},{8,13},{9,12},{10,... | collective-permute-start | bytes 589832 | tf_op jit(solution)/shard_map/ppermute | solution.py:61
  12.3 22.3 %collective-permute-start.5 = (bf16[128,768]{1,0:T(8,128)(2,1)S(1)}, bf16[128,768]{1,0:T(8,128)(2,1)S(1)}, u32[]{:S(2)}, u32[]{:S(2)}) collective-permute-start(bf16[128,768]{1,0:T(8,128)(2,1)S(1)} %get-tuple-element.34), channel_id=1, source_target_pairs={{0,6},{1,7},{2,4},{3,5},{4,2},{5,3},{6,0},{7,1},{8,14},{9,15},{10,... | collective-permute-start | bytes 589832 | tf_op jit(solution)/shard_map/ppermute | solution.py:61
  23.2 14.7 %collective-permute-start.6 = (bf16[128,768]{1,0:T(8,128)(2,1)S(1)}, bf16[128,768]{1,0:T(8,128)(2,1)S(1)}, u32[]{:S(2)}, u32[]{:S(2)}) collective-permute-start(bf16[128,768]{1,0:T(8,128)(2,1)S(1)} %get-tuple-element.35), channel_id=1, source_target_pairs={{0,7},{1,6},{2,5},{3,4},{4,3},{5,2},{6,1},{7,0},{8,15},{9,14},{10,... | collective-permute-start | bytes 589832 | tf_op jit(solution)/shard_map/ppermute | solution.py:61
  26.9 2.0 %copy-start.5 = (bf16[768,2304]{1,0:T(8,128)(2,1)S(1)}, bf16[768,2304]{1,0:T(8,128)(2,1)}, u32[]{:S(2)}) copy-start(bf16[768,2304]{1,0:T(8,128)(2,1)} %w_ref.5) | copy-start | bytes 10616836
  30.3 7.5 %copy-start.6 = (bf16[768,2304]{1,0:T(8,128)(2,1)S(1)}, bf16[768,2304]{1,0:T(8,128)(2,1)}, u32[]{:S(2)}) copy-start(bf16[768,2304]{1,0:T(8,128)(2,1)} %w_ref.5) | copy-start | bytes 10616836
  33.2 18.5 %copy-start.16 = (bf16[512,768]{1,0:T(8,128)(2,1)}, bf16[512,768]{1,0:T(8,128)(2,1)S(1)}, u32[]{:S(2)}) copy-start(bf16[512,768]{1,0:T(8,128)(2,1)S(1)} %get-tuple-element.31.rest_4_.rest_0_) | copy-start | bytes 2359300
  33.2 18.5 %copy-start.24 = (bf16[512,768]{1,0:T(8,128)(2,1)}, bf16[512,768]{1,0:T(8,128)(2,1)S(1)}, u32[]{:S(2)}) copy-start(bf16[512,768]{1,0:T(8,128)(2,1)S(1)} %get-tuple-element.37.rest_2_) | copy-start | bytes 2359300
  33.2 18.5 %copy-start.26 = (bf16[512,768]{1,0:T(8,128)(2,1)}, bf16[512,768]{1,0:T(8,128)(2,1)S(1)}, u32[]{:S(2)}) copy-start(bf16[512,768]{1,0:T(8,128)(2,1)S(1)} %get-tuple-element.39.rest_4_) | copy-start | bytes 2359300
  33.2 7.6 %copy-start.9 = (bf16[768,768]{1,0:T(8,128)(2,1)S(1)}, bf16[768,768]{1,0:T(8,128)(2,1)}, u32[]{:S(2)}) copy-start(bf16[768,768]{1,0:T(8,128)(2,1)} %w_ref.7) | copy-start | bytes 3538948
  40.7 11.0 %copy-start.18 = (bf16[512,768]{1,0:T(8,128)(2,1)}, bf16[512,768]{1,0:T(8,128)(2,1)S(1)}, u32[]{:S(2)}) copy-start(bf16[512,768]{1,0:T(8,128)(2,1)S(1)} %get-tuple-element.36.rest_1_) | copy-start | bytes 2359300
  40.7 11.0 %copy-start.20 = (bf16[512,768]{1,0:T(8,128)(2,1)}, bf16[512,768]{1,0:T(8,128)(2,1)S(1)}, u32[]{:S(2)}) copy-start(bf16[512,768]{1,0:T(8,128)(2,1)S(1)} %get-tuple-element.38.rest_3_) | copy-start | bytes 2359300
  40.7 11.0 %copy-start.22 = (bf16[512,768]{1,0:T(8,128)(2,1)}, bf16[512,768]{1,0:T(8,128)(2,1)S(1)}, u32[]{:S(2)}) copy-start(bf16[512,768]{1,0:T(8,128)(2,1)S(1)} %get-tuple-element.40.rest_5_) | copy-start | bytes 2359300
  40.8 24.8 %copy-start.15 = (s32[16]{0:T(128)S(1)}, s32[16]{0:T(128)}, u32[]{:S(2)}) copy-start(s32[16]{0:T(128)} %index_ref.7) | copy-start | bytes 196
  51.7 35.8 %all-to-all-start = ((bf16[32,16,768]{2,1,0:T(8,128)(2,1)}), bf16[32,16,768]{2,1,0:T(8,128)(2,1)S(1)}, u32[]{:S(2)}, u32[]{:S(2)}) async-start(bf16[32,16,768]{2,1,0:T(8,128)(2,1)} %bitcast), calls=%async_computation | async-start | bytes 1572864 | tf_op jit(solution)/shard_map/all_to_all | solution.py:461
  87.5 27.4 %all-to-all-start.1 = ((bf16[32,16,768]{2,1,0:T(8,128)(2,1)}), bf16[32,16,768]{2,1,0:T(8,128)(2,1)S(1)}, u32[]{:S(2)}, u32[]{:S(2)}) async-start(bf16[32,16,768]{2,1,0:T(8,128)(2,1)} %bitcast.2), calls=%async_computation.1 | async-start | bytes 1572864 | tf_op jit(solution)/shard_map/all_to_all | solution.py:461
  90.2 2.3 %copy-start.1 = (bf16[768,3072]{1,0:T(8,128)(2,1)S(1)}, bf16[768,3072]{1,0:T(8,128)(2,1)}, u32[]{:S(2)}) copy-start(bf16[768,3072]{1,0:T(8,128)(2,1)} %up_ref.3) | copy-start | bytes 14155780
  92.5 2.3 %copy-start.3 = (bf16[3072,768]{1,0:T(8,128)(2,1)S(1)}, bf16[3072,768]{1,0:T(8,128)(2,1)}, u32[]{:S(2)}) copy-start(bf16[3072,768]{1,0:T(8,128)(2,1)} %down_ref.3) | copy-start | bytes 14155780
  94.8 2.0 %copy-start.7 = (bf16[768,2304]{1,0:T(8,128)(2,1)S(1)}, bf16[768,2304]{1,0:T(8,128)(2,1)}, u32[]{:S(2)}) copy-start(bf16[768,2304]{1,0:T(8,128)(2,1)} %qkv_ref.3) | copy-start | bytes 10616836
  98.1 16.8 %copy-start.11 = (bf16[768,768]{1,0:T(8,128)(2,1)S(1)}, bf16[768,768]{1,0:T(8,128)(2,1)}, u32[]{:S(2)}) copy-start(bf16[768,768]{1,0:T(8,128)(2,1)} %out_ref.3) | copy-start | bytes 3538948
  113.3 28.6 %collective-permute-start.7 = (bf16[4,32,768]{2,1,0:T(8,128)(2,1)S(1)}, bf16[4,32,768]{2,1,0:T(8,128)(2,1)S(1)}, u32[]{:S(2)}, u32[]{:S(2)}) collective-permute-start(bf16[4,32,768]{2,1,0:T(8,128)(2,1)S(1)} %get-tuple-element.42), channel_id=1, source_target_pairs={{0,8},{8,0},{16,24},{24,16},{1,9},{9,1},{17,25},{25,17},{2,10},{10... | collective-permute-start | bytes 589832 | tf_op jit(solution)/shard_map/ppermute | solution.py:61
  115.0 2.3 %copy-start.2 = (bf16[768,3072]{1,0:T(8,128)(2,1)S(1)}, bf16[768,3072]{1,0:T(8,128)(2,1)}, u32[]{:S(2)}) copy-start(bf16[768,3072]{1,0:T(8,128)(2,1)} %up_ref.3) | copy-start | bytes 14155780
  117.3 2.3 %copy-start.4 = (bf16[3072,768]{1,0:T(8,128)(2,1)S(1)}, bf16[3072,768]{1,0:T(8,128)(2,1)}, u32[]{:S(2)}) copy-start(bf16[3072,768]{1,0:T(8,128)(2,1)} %down_ref.3) | copy-start | bytes 14155780
  119.6 2.0 %copy-start.8 = (bf16[768,2304]{1,0:T(8,128)(2,1)S(1)}, bf16[768,2304]{1,0:T(8,128)(2,1)}, u32[]{:S(2)}) copy-start(bf16[768,2304]{1,0:T(8,128)(2,1)} %qkv_ref.3) | copy-start | bytes 10616836
  136.8 12.4 %collective-permute-start.8 = (bf16[4,32,768]{2,1,0:T(8,128)(2,1)S(1)}, bf16[4,32,768]{2,1,0:T(8,128)(2,1)S(1)}, u32[]{:S(2)}, u32[]{:S(2)}) collective-permute-start(bf16[4,32,768]{2,1,0:T(8,128)(2,1)S(1)} %get-tuple-element.43), channel_id=1, source_target_pairs={{0,16},{8,24},{16,0},{24,8},{1,17},{9,25},{17,1},{25,9},{2,18},{10... | collective-permute-start | bytes 589832 | tf_op jit(solution)/shard_map/ppermute | solution.py:61
  138.4 10.8 %collective-permute-start.9 = (bf16[4,32,768]{2,1,0:T(8,128)(2,1)S(1)}, bf16[4,32,768]{2,1,0:T(8,128)(2,1)S(1)}, u32[]{:S(2)}, u32[]{:S(2)}) collective-permute-start(bf16[4,32,768]{2,1,0:T(8,128)(2,1)S(1)} %get-tuple-element.44), channel_id=1, source_target_pairs={{0,24},{8,16},{16,8},{24,0},{1,25},{9,17},{17,9},{25,1},{2,26},{10... | collective-permute-start | bytes 589832 | tf_op jit(solution)/shard_map/ppermute | solution.py:61
  138.7 11.7 %collective-permute-start.10 = (bf16[4,32,768]{2,1,0:T(8,128)(2,1)S(1)}, bf16[4,32,768]{2,1,0:T(8,128)(2,1)S(1)}, u32[]{:S(2)}, u32[]{:S(2)}) collective-permute-start(bf16[4,32,768]{2,1,0:T(8,128)(2,1)S(1)} %get-tuple-element.46), channel_id=1, source_target_pairs={{0,8},{8,0},{16,24},{24,16},{1,9},{9,1},{17,25},{25,17},{2,10},{10... | collective-permute-start | bytes 589832 | tf_op jit(solution)/shard_map/ppermute | solution.py:61
  140.4 15.8 %collective-permute-start.11 = (bf16[4,32,768]{2,1,0:T(8,128)(2,1)S(1)}, bf16[4,32,768]{2,1,0:T(8,128)(2,1)S(1)}, u32[]{:S(2)}, u32[]{:S(2)}) collective-permute-start(bf16[4,32,768]{2,1,0:T(8,128)(2,1)S(1)} %get-tuple-element.47), channel_id=1, source_target_pairs={{0,16},{8,24},{16,0},{24,8},{1,17},{9,25},{17,1},{25,9},{2,18},{10... | collective-permute-start | bytes 589832 | tf_op jit(solution)/shard_map/ppermute | solution.py:61
  141.8 14.3 %collective-permute-start.12 = (bf16[4,32,768]{2,1,0:T(8,128)(2,1)S(1)}, bf16[4,32,768]{2,1,0:T(8,128)(2,1)S(1)}, u32[]{:S(2)}, u32[]{:S(2)}) collective-permute-start(bf16[4,32,768]{2,1,0:T(8,128)(2,1)S(1)} %get-tuple-element.48), channel_id=1, source_target_pairs={{0,24},{8,16},{16,8},{24,0},{1,25},{9,17},{17,9},{25,1},{2,26},{10... | collective-permute-start | bytes 589832 | tf_op jit(solution)/shard_map/ppermute | solution.py:61
  (11 other events, 11.7 us)

commit v3 on v2

v3 whole, which is shorter than its diff:
```python
import functools

import jax
import jax.numpy as jnp
from jax import lax
from jax.experimental import pallas as pl
from jax.experimental.pallas import tpu as pltpu
from jax.sharding import PartitionSpec as P

HEADS = 12
HEAD_DIM = 64
WINDOWS = 2
CORES = 2
TILE_LOCS = 16
GROUP_LOCS = 8
NORM_ROWS = 128
UNIT_ROWS = 128
STEP_PAIRS = 2
ROW_TILE = 256
LANES = 128
QUERY_SCALE = HEAD_DIM ** (-0.5)
VMEM_LIMIT = 28 * 1024 * 1024
WIDE_LIMIT = 52 * 1024 * 1024

F32 = jnp.float32
BF16 = jnp.bfloat16


def dot(left, right):
    return jnp.dot(left, right, preferred_element_type=F32)


def dot_t(left, right):
    return lax.dot_general(left, right, (((1,), (1,)), ((), ())), preferred_element_type=F32)


def norm_rows(values):
    centre = values - jnp.mean(values, axis=-1, keepdims=True)
    spread = jnp.mean(centre * centre, axis=-1, keepdims=True)
    return centre * lax.rsqrt(spread + 1e-05)


def gelu(values):
    inner = values * (0.7978845608028654 + 0.035677408136300125 * (values * values))
    return (0.5 * values) * (1.0 + jnp.tanh(inner))


def call(kernel, out_shape, flops, nbytes, limit=VMEM_LIMIT, **kwargs):
    return pl.pallas_call(
        kernel,
        out_shape=out_shape,
        compiler_params=pltpu.CompilerParams(vmem_limit_bytes=limit),
        cost_estimate=pl.CostEstimate(flops=flops, bytes_accessed=nbytes, transcendentals=0),
        **kwargs,
    )


def exchange(value, axis, step):
    if step == 0:
        return value
    return lax.ppermute(value, axis, [(i, i ^ step) for i in range(lax.axis_size(axis))])


class Plan:
    def __init__(self, tokens):
        self.loc_dev, self.band_dev, self.width = tokens.shape
        self.locs = lax.axis_size("loc")
        self.groups = lax.axis_size("band")
        self.rows_count = self.locs // CORES
        self.share = self.rows_count // self.band_dev
        assert self.share * self.band_dev * CORES == self.locs
        self.block = self.loc_dev // WINDOWS
        self.rows = self.block // self.share
        self.part_rows = self.rows // self.groups
        assert self.part_rows * self.groups * self.share * WINDOWS == self.loc_dev


def location_keys(plan, ids_ref):
    size = plan.loc_dev
    lines = size // LANES
    first = lax.axis_index("loc") * lines
    ids = jnp.concatenate([ids_ref[pl.ds(first + i, 1), :] for i in range(lines)], axis=1)
    ids = ids.astype(F32)
    row = jnp.broadcast_to(ids, (size, size))
    first = lax.broadcasted_iota(jnp.int32, (size, size), 0)
    second = lax.broadcasted_iota(jnp.int32, (size, size), 1)
    column = jnp.sum(jnp.where(first == second, row, 0.0), axis=1, keepdims=True)
    before = jnp.where((column == row) & (first < second), 1.0, 0.0)
    rank = jnp.sum(before, axis=0, keepdims=True)
    return ids * plan.block + rank


SMEM = pl.BlockSpec(memory_space=pltpu.SMEM)
VMEM = pl.BlockSpec(memory_space=pltpu.VMEM)
ANY = pl.BlockSpec(memory_space=pl.ANY)


def pick_rows(plan, window, keys, bands, outs):
    row = lax.axis_index("loc") // CORES
    place = lax.broadcasted_iota(jnp.int32, (plan.rows, plan.loc_dev), 0)
    for slot in range(plan.rows_count):
        peer = row ^ slot
        wanted = place + (window * plan.block + (peer % plan.share) * plan.rows)
        pick = jnp.where(wanted.astype(F32) == keys, 1.0, 0.0).astype(BF16)
        outs[slot][...] = dot(pick, bands[peer // plan.share]).astype(BF16)


def arrange_first(plan, tokens, ids):
    count = plan.rows_count

    def kernel(ids_ref, x_ref, *rest):
        outs, (bands, keys_ref) = rest[:count], rest[count:]
        keys = location_keys(plan, ids_ref)
        keys_ref[...] = keys
        for band in range(plan.band_dev):
            bands[band] = x_ref[:, band, :]
        pick_rows(plan, 0, keys, bands, outs)

    return call(
        kernel,
        [jax.ShapeDtypeStruct((plan.rows, plan.width), BF16)] * count
        + [
            jax.ShapeDtypeStruct((plan.band_dev, plan.loc_dev, plan.width), BF16),
            jax.ShapeDtypeStruct((1, plan.loc_dev), F32),
        ],
        2 * plan.loc_dev * tokens.size,
        4 * tokens.size,
        in_specs=[VMEM] * 2,
        out_specs=[VMEM] * (count + 2),
    )(ids, tokens)


def arrange_next(plan, window, bands, keys, after):
    count = plan.rows_count

    def kernel(bands_ref, keys_ref, *rest):
        pick_rows(plan, window, keys_ref[...], bands_ref, rest[len(after) :])

    return call(
        kernel,
        [jax.ShapeDtypeStruct((plan.rows, plan.width), BF16)] * count,
        2 * plan.loc_dev * bands.size,
        4 * bands.size,
        in_specs=[VMEM] * 2 + [ANY] * len(after),
        out_specs=[VMEM] * count,
    )(bands, keys, *after)


def join_slots(plan, slots, after):
    def kernel(*refs):
        for slot in range(len(slots)):
            refs[-1][pl.ds(slot * plan.rows, plan.rows), :] = refs[slot][...]

    return call(
        kernel,
        jax.ShapeDtypeStruct((len(slots) * plan.rows, plan.width), BF16),
        0,
        4 * len(slots) * plan.rows * plan.width,
        in_specs=[VMEM] * len(slots) + [ANY] * len(after),
        out_specs=VMEM,
    )(*slots, *after)


def embed_row(plan, index_ref, table_ref):
    band = lax.axis_index("loc") // (CORES * plan.share)
    number = index_ref[lax.axis_index("band") * plan.band_dev + band]
    return table_ref[pl.ds(number, 1), :]


def loop(count, step):
    lax.fori_loop(0, count, lambda i, _: (step(i), 0)[1], 0)


def aligned(index, size):
    return pl.ds(pl.multiple_of(index * size, size), size)


def norm_into(target, rows_of, rows):
    tile = min(rows, NORM_ROWS)

    def step(index):
        here = aligned(index, tile)
        target[here, :] = norm_rows(rows_of(here)).astype(BF16)

    loop(rows // tile, step)


def project(plan, tokens, index, table, weights, queries, after=()):
    rows, width = tokens.shape
    tile = min(rows, ROW_TILE)
    names = range(3) if queries else range(1, 3)

    def kernel(index_ref, table_ref, w_ref, x_ref, *rest):
        outs = rest[len(after) :]
        embed = embed_row(plan, index_ref, table_ref)
        for first in range(0, rows, tile):
            here = pl.ds(first, tile)
            normed = norm_rows(x_ref[here, :].astype(F32) + embed).astype(BF16)
            for ref, name in zip(outs, names):
                value = dot(normed, w_ref[:, name * width : (name + 1) * width])
                ref[here, :] = (value * QUERY_SCALE if name == 0 else value).astype(BF16)

    return call(
        kernel,
        [jax.ShapeDtypeStruct((rows, width), BF16)] * len(names),
        2 * rows * width * len(names) * width,
        2 * ((1 + len(names)) * rows * width + 3 * width * width),
        in_specs=[SMEM, VMEM, VMEM, VMEM] + [ANY] * len(after),
        out_specs=[VMEM] * len(names),
    )(index, table, weights, tokens, *after)


def head_masks(rows):
    lane = lax.broadcasted_iota(jnp.int32, (rows, LANES), 1)
    return [(lane // HEAD_DIM) == head for head in range(LANES // HEAD_DIM)]


def stack_heads(query):
    return jnp.concatenate(
        [jnp.where(inside, query, jnp.zeros_like(query)) for inside in head_masks(query.shape[0])],
        axis=0,
    )


def join_heads(stacked):
    heads = LANES // HEAD_DIM
    rows = stacked.shape[0] // heads
    joined = stacked[:rows]
    for head, inside in list(enumerate(head_masks(rows)))[1:]:
        joined = jnp.where(inside, stacked[head * rows : (head + 1) * rows], joined)
    return joined


def with_ones(value):
    return jnp.concatenate([value, jnp.ones(value.shape, BF16)], axis=1)


def run_units(units, mask=None):
    def scores_of(unit):
        query, keys, _ = unit
        scores = [dot_t(query, piece) for piece in keys]
        if mask is not None:
            scores = [jnp.where(mask, piece, -1e30) for piece in scores]
        return scores

    results = []
    ahead = scores_of(units[0])
    for number, (_, _, values) in enumerate(units):
        scores = ahead
        if number + 1 < len(units):
            ahead = scores_of(units[number + 1])
        peak = functools.reduce(
            jnp.maximum, [jnp.max(piece, axis=-1, keepdims=True) for piece in scores]
        )
        total = None
        for piece, value in zip(scores, values):
            part = dot(jnp.exp(piece - peak).astype(BF16), value)
            total = part if total is None else total + part
        results.append(
            (join_heads(total[:, :LANES]) / join_heads(total[:, LANES:])).astype(BF16)
        )
    return results


def attend(plan, query, keys, values, tokens, index, table, spatial_out):
    total, width = query.shape
    rows = plan.rows
    pieces = len(keys)
    pairs = width // LANES
    unit = min(total, UNIT_ROWS)

    def kernel(index_ref, table_ref, w_ref, x_ref, q_ref, *rest):
        k_refs, rest = rest[:pieces], rest[pieces:]
        v_refs, (out_ref, result, added) = rest[:pieces], rest[pieces:]

        def step(number):
            units, places = [], []
            for i in range(STEP_PAIRS):
                here = aligned(number * STEP_PAIRS + i, LANES)
                pair_keys = [ref[:, here] for ref in k_refs]
                pair_values = [with_ones(ref[:, here]) for ref in v_refs]
                for first in range(0, total, unit):
                    place = (pl.ds(first, unit), here)
                    units.append((stack_heads(q_ref[place]), pair_keys, pair_values))
                    places.append(place)
            for place, done in zip(places, run_units(units)):
                result[place] = done

        loop(pairs // STEP_PAIRS, step)
        added[...] = dot(result[...], w_ref[...])
        embed = embed_row(plan, index_ref, table_ref)
        row = lax.axis_index("loc") // CORES
        for slot in range(plan.rows_count):
            here = pl.ds(slot * rows, rows)
            mid = (x_ref[here, :].astype(F32) + embed + added[here, :]).astype(BF16)
            for owner in range(plan.groups):
                part = mid[owner * plan.part_rows : (owner + 1) * plan.part_rows]
                out_ref[owner, row ^ slot] = part

    key_rows = sum(piece.shape[0] for piece in keys)
    return call(
        kernel,
        jax.ShapeDtypeStruct((plan.groups, plan.rows_count, plan.part_rows, width), BF16),
        16 * total * key_rows * width,
        2 * width * (2 * key_rows + 3 * total + width),
        in_specs=[SMEM] + [VMEM] * (4 + 2 * pieces),
        out_specs=VMEM,
        scratch_shapes=[pltpu.VMEM((total, width), BF16), pltpu.VMEM((total, width), F32)],
    )(index, table, spatial_out, tokens, query, *keys, *values)


def channel(plan, parts, channel_qkv, channel_out, up_weight, down_weight):
    groups, width = plan.groups, plan.width
    _, bands, locations, _ = parts.shape
    tile, small = TILE_LOCS, GROUP_LOCS
    assert locations % tile == 0
    group_rows = groups * bands * small
    rows = groups * bands * locations
    row_tile = min(rows, ROW_TILE)

    def kernel(qkv_hbm, out_hbm, up_hbm, down_hbm, *refs):
        in_ref, *refs = refs
        outs, refs = refs[:groups], refs[groups:]
        mid, normed, packed, attended, qkv_ref, out_ref, up_ref, down_ref, sems = refs
        me = lax.axis_index("band")
        columns = [pl.ds(first, width) for first in range(0, 3 * width, width)]
        copies = []
        for source, target, spots in (
            (qkv_hbm, qkv_ref, [(slice(None), spot) for spot in columns]),
            (out_hbm, out_ref, [(slice(None), slice(None))]),
            (up_hbm, up_ref, [(slice(None), slice(None))]),
            (down_hbm, down_ref, [(slice(None), slice(None))]),
        ):
            for spot in spots:
                copies.append(
                    pltpu.make_async_copy(
                        source.at[spot], target.at[spot], sems.at[len(copies)]
                    )
                )
        for copy in copies:
            copy.start()
        pieces = [
            (owner, band, first)
            for owner in range(groups)
            for band in range(bands)
            for first in range(0, locations, tile)
        ]

        def places(owner, band, first):
            return [
                pl.ds((at // small) * group_rows + (owner * bands + band) * small, small)
                for at in range(first, first + tile, small)
            ]

        for owner, band, first in pieces:
            piece = in_ref[me ^ owner, band, first : first + tile, :].astype(F32)
            for number, place in enumerate(places(owner, band, first)):
                mid[place, :] = piece[number * small : (number + 1) * small]
        norm_into(normed, lambda here: mid[here, :], rows)

        for number, here in enumerate(columns):
            copies[number].wait()
            factor = QUERY_SCALE if number == 0 else 1.0
            packed[:, here] = (dot(normed[...], qkv_ref[:, here]) * factor).astype(BF16)
        pairs = width // LANES
        stacked = group_rows * (LANES // HEAD_DIM)
        one = lax.broadcasted_iota(jnp.int32, (stacked, group_rows), 0)
        other = lax.broadcasted_iota(jnp.int32, (stacked, group_rows), 1)
        mask = (one % small) == (other % small)

        def attention_step(pair):
            units, spots = [], []
            for first in range(0, rows, group_rows):
                mine = pl.ds(first, group_rows)
                query = packed[mine, aligned(pair, LANES)]
                keys = packed[mine, aligned(pair + pairs, LANES)]
                values = packed[mine, aligned(pair + 2 * pairs, LANES)]
                units.append((stack_heads(query), [keys], [with_ones(values)]))
                spots.append((mine, aligned(pair, LANES)))
            for spot, done in zip(spots, run_units(units, mask)):
                attended[spot] = done

        loop(pairs, attention_step)
        copies[3].wait()
        mid[...] += dot(attended[...], out_ref[...])
        norm_into(normed, lambda here: mid[here, :], rows)

        copies[4].wait()
        copies[5].wait()

        def mlp_step(block):
            here = aligned(block, width)
            tiles = [pl.ds(first, row_tile) for first in range(0, rows, row_tile)]
            raised = [dot(normed[mine, :], up_ref[:, here]) for mine in tiles]
            for mine, value in zip(tiles, raised):
                mid[mine, :] += dot(gelu(value).astype(BF16), down_ref[here, :])

        loop(up_weight.shape[1] // width, mlp_step)
        for owner, band, first in pieces:
            piece = jnp.concatenate(
                [mid[place, :] for place in places(owner, band, first)], axis=0
            )
            outs[owner][band, first : first + tile, :] = piece.astype(BF16)

    weights = [channel_qkv, channel_out, up_weight, down_weight]
    size = sum(weight.size for weight in weights)
    return call(
        kernel,
        [jax.ShapeDtypeStruct((bands, locations, width), BF16)] * groups,
        2 * rows * size,
        2 * (2 * rows * width + size),
        limit=WIDE_LIMIT,
        in_specs=[ANY] * 4 + [VMEM],
        out_specs=[VMEM] * groups,
        scratch_shapes=[
            pltpu.VMEM((rows, width), F32),
            pltpu.VMEM((rows, width), BF16),
            pltpu.VMEM((rows, 3 * width), BF16),
            pltpu.VMEM((rows, width), BF16),
        ]
        + [pltpu.VMEM(weight.shape, BF16) for weight in weights]
        + [pltpu.SemaphoreType.DMA((6,))],
    )(*weights, parts)


def restore(plan, keys, returned):
    def kernel(keys_ref, *refs):
        ins, out_ref = refs[:-1], refs[-1]
        group = lax.axis_index("band")
        place = lax.broadcasted_iota(jnp.int32, (plan.loc_dev, plan.loc_dev), 0)
        inner = place % plan.part_rows
        part = (place // plan.part_rows) % plan.share
        owner = (place // (plan.part_rows * plan.share)) % plan.groups ^ group
        window = place // plan.block
        wanted = window * plan.block + part * plan.rows + owner * plan.part_rows + inner
        pick = jnp.where(wanted.astype(F32) == keys_ref[...], 1.0, 0.0).astype(BF16)
        for band in range(plan.band_dev):
            rows = jnp.concatenate([ref[band] for ref in ins], axis=0)
            out_ref[:, band, :] = lax.dot_general(
                pick, rows, (((0,), (0,)), ((), ())), preferred_element_type=F32
            ).astype(BF16)

    arrays = [array for chunk in returned for array in chunk]
    size = plan.loc_dev * plan.band_dev * plan.width
    return call(
        kernel,
        jax.ShapeDtypeStruct((plan.loc_dev, plan.band_dev, plan.width), BF16),
        2 * plan.loc_dev * size,
        4 * size,
    )(keys, *arrays)


def body(
    tokens,
    band_index,
    band_table,
    window_ids,
    spatial_qkv,
    spatial_out,
    channel_qkv,
    channel_out,
    up_weight,
    down_weight,
):
    plan = Plan(tokens)
    ids = window_ids.reshape(-1, LANES)
    *sent, bands, place_keys = arrange_first(plan, tokens, ids)
    mids, behind, began = [], (), ()
    for window in range(WINDOWS):
        if window > 0:
            sent = arrange_next(plan, window, bands, place_keys, began)
        slots = [exchange(value, "loc", CORES * step) for step, value in enumerate(sent)]
        began = slots[1:2]
        own = join_slots(plan, slots, behind)
        if plan.share == 1:
            other = exchange(own, "loc", 1)
            query, *mine = project(plan, own, band_index, band_table, spatial_qkv, True)
            theirs = project(plan, other, band_index, band_table, spatial_qkv, False, mine[:1])
            keys, values = zip(mine, theirs)
        else:
            step = CORES * plan.share
            same = [list(range(at, at + step)) for at in range(0, plan.locs, step)]
            every = lax.all_gather(own, "loc", axis_index_groups=same, tiled=True)
            query, _, _ = project(plan, own, band_index, band_table, spatial_qkv, True)
            keys, values = zip(
                project(plan, every, band_index, band_table, spatial_qkv, False)
            )
        mid = attend(plan, query, keys, values, own, band_index, band_table, spatial_out)
        behind = (mid,)
        mids.append(mid)
    same = [
        [(g * plan.rows_count + r) * CORES + core for g in range(plan.groups) for r in range(plan.rows_count)]
        for core in range(CORES)
    ]
    returned = []
    for mid in mids:
        parts = lax.all_to_all(
            mid.reshape(-1, plan.part_rows, plan.width),
            ("band", "loc"),
            0,
            0,
            axis_index_groups=same,
            tiled=True,
        )
        parts = parts.reshape(plan.groups, plan.band_dev, -1, plan.width)
        done = channel(plan, parts, channel_qkv, channel_out, up_weight, down_weight)
        returned.append([exchange(value, "band", step) for step, value in enumerate(done)])
    return restore(plan, place_keys, returned)


def solution(mesh):
    placed = (P("loc", "band", None), P(), P(), P(), P(), P(), P(), P(), P(), P())
    return jax.shard_map(
        body, mesh=mesh, in_specs=placed, out_specs=P("loc", "band", None), check_vma=False
    )
```

time: 160 us -> 134 us (0.84)
  local copies, waits for them, and re-layouts: 27.8 us -> 2.99 us
  Pallas kernels: 64.6 us -> 73.5 us
  waiting for transfers between devices: 32.7 us -> 25.9 us
  starting transfers between devices: 33.6 us -> 30.5 us
    unnamed x56 -> x18, local copies, waits for them, and re-layouts: 27.1 us -> 2.99 us
    ppermute x13 -> x14, waiting for transfers between devices: 29.1 us -> 21.1 us  [exchange(): lax.ppermute(value, axis, [(i, i ^ step) for i in range(lax.axis_size(axi...]
    pallas_call x5 -> x10, Pallas kernels: 31.6 us -> 37.9 us  [the longest x2 21.3 us: attend(): call(kernel, jax.ShapeDtypeStruct((plan.groups, plan.rows_count, plan.par...]
    all_to_all x2, starting transfers between devices: 16.4 us -> 11.7 us  [body(): lax.all_to_all(mid.reshape(-1, plan.part_rows, plan.width), ('band', 'loc...]
    pallas_call x2, Pallas kernels: 30.3 us -> 32.9 us  [channel(): call(kernel, [jax.ShapeDtypeStruct((bands, locations, width), BF16)] * gr...]
    ppermute x13 -> x14, starting transfers between devices: 17.2 us -> 18.8 us  [exchange(): lax.ppermute(value, axis, [(i, i ^ step) for i in range(lax.axis_size(axi...]
  transfers between devices with their start and end apart: 15 -> 16, of which waited for: 8 -> 6; matrix products, arithmetic and copies ran while one was open for 0% -> 0% of each run, Pallas kernels for 28% -> 49%
where the time goes in v3:
time: 134 us; the launch traced here: 133 us
  Pallas kernels  73.5 us (55%)
  starting transfers between devices  30.5 us (23%)
  waiting for transfers between devices  25.9 us (19%)
  local copies, waits for them, and re-layouts  2.99 us (2%)
    pallas_call x2, Pallas kernels, channel(): call(kernel, [jax.ShapeDtypeStruct((bands, locations, width), BF16)] * gr...  32.9 us
    pallas_call x2, Pallas kernels, attend(): call(kernel, jax.ShapeDtypeStruct((plan.groups, plan.rows_count, plan.par...  21.3 us
    ppermute x14, waiting for transfers between devices, exchange(): lax.ppermute(value, axis, [(i, i ^ step) for i in range(lax.axis_size(axi...  21.1 us
    ppermute x14, starting transfers between devices, exchange(): lax.ppermute(value, axis, [(i, i ^ step) for i in range(lax.axis_size(axi...  18.8 us
    all_to_all x2, starting transfers between devices, body(): lax.all_to_all(mid.reshape(-1, plan.part_rows, plan.width), ('band', 'loc...  11.7 us
    pallas_call x4, Pallas kernels, project(): call(kernel, [jax.ShapeDtypeStruct((rows, width), BF16)] * len(names), 2...  11.2 us
    all_to_all x2, waiting for transfers between devices, body(): lax.all_to_all(mid.reshape(-1, plan.part_rows, plan.width), ('band', 'loc...  4.81 us
    pallas_call x1, Pallas kernels, arrange_first(): call(kernel, [jax.ShapeDtypeStruct((plan.rows, plan.width), BF16)] * coun...  3.97 us
  transfers between devices with their start and end apart: 16, of which 6 were waited for; matrix products, arithmetic and copies ran while one was open for 0% of the time, Pallas kernels for 49%

profile of v3, /device:TPU:0, one launch (start us, length us, event | category | flops | bytes accessed | tf_op | source)
XLA Modules:
  0.0 133.0 jit_solution(584387081195260196)
XLA Ops:
  0.0 1.4 %copy-done.2 = bf16[256,4,768]{2,1,0:T(4,128)(2,1)S(1)} copy-done((bf16[256,4,768]{2,1,0:T(4,128)(2,1)S(1)}, bf16[256,4,768]{2,1,0:T(4,128)(2,1)}, u32[]{:S(2)}) %copy-start.2) | copy-done | bytes 1572888
  1.4 0.7 copy-done.5
  2.1 4.0 %shard_map.100 = (bf16[128,768]{1,0:T(8,128)(2,1)S(1)}, bf16[128,768]{1,0:T(8,128)(2,1)S(1)}, bf16[128,768]{1,0:T(8,128)(2,1)S(1)}, bf16[128,768]{1,0:T(8,128)(2...) custom-call(s32[16,128]{1,0:T(8,128)S(1)} %bitcast.7, bf16[256,4,768]{2,1,0:T(4,128)(2,1)S(1)} %copy-done.2), custom_call_target="tpu_custom_call" | custom-call | flops 402653184 | bytes 3145728 | tf_op jit(solution)/shard_map/pallas_call | solution.py:119
  6.1 3.1 %collective-permute-start = (bf16[128,768]{1,0:T(8,128)(2,1)S(1)}, bf16[128,768]{1,0:T(8,128)(2,1)S(1)}, u32[]{:S(2)}, u32[]{:S(2)}) collective-permute-start(bf16[128,768]{1,0:T(8,128)(2,1)S(1)} %get-tuple-element.35), channel_id=1, source_target_pairs={{0,2},{1,3},{2,0},{3,1},{4,6},{5,7},{6,4},{7,5},{8,10},{9,11},{10,... | collective-permute-start | bytes 589832 | tf_op jit(solution)/shard_map/ppermute | solution.py:61
  9.2 2.6 %collective-permute-start.1 = (bf16[128,768]{1,0:T(8,128)(2,1)S(1)}, bf16[128,768]{1,0:T(8,128)(2,1)S(1)}, u32[]{:S(2)}, u32[]{:S(2)}) collective-permute-start(bf16[128,768]{1,0:T(8,128)(2,1)S(1)} %get-tuple-element.36), channel_id=1, source_target_pairs={{0,4},{1,5},{2,6},{3,7},{4,0},{5,1},{6,2},{7,3},{8,12},{9,13},{10,... | collective-permute-start | bytes 589832 | tf_op jit(solution)/shard_map/ppermute | solution.py:61
  11.8 5.7 %collective-permute-done.refs_1_.rest_0_ = bf16[128,768]{1,0:T(8,128)(2,1)S(1)} collective-permute-done((bf16[128,768]{1,0:T(8,128)(2,1)S(1)}, bf16[128,768]{1,0:T(8,128)(2,1)S(1)}, u32[]{:S(2)}, u32[]{:S(2)}) %collective-permute-start) | collective-permute-done | bytes 196640 | tf_op jit(solution)/shard_map/ppermute | solution.py:61
  17.5 8.8 %collective-permute-done.1.refs_2_ = bf16[128,768]{1,0:T(8,128)(2,1)S(1)} collective-permute-done((bf16[128,768]{1,0:T(8,128)(2,1)S(1)}, bf16[128,768]{1,0:T(8,128)(2,1)S(1)}, u32[]{:S(2)}, u32[]{:S(2)}) %collective-permute-start.1) | collective-permute-done | bytes 196640 | tf_op jit(solution)/shard_map/ppermute | solution.py:61
  26.9 3.4 %collective-permute-start.7 = (bf16[128,768]{1,0:T(8,128)(2,1)S(1)}, bf16[128,768]{1,0:T(8,128)(2,1)S(1)}, u32[]{:S(2)}, u32[]{:S(2)}) collective-permute-start(bf16[128,768]{1,0:T(8,128)(2,1)S(1)} %get-tuple-element.49), channel_id=1, source_target_pairs={{0,2},{1,3},{2,0},{3,1},{4,6},{5,7},{6,4},{7,5},{8,10},{9,11},{10,... | collective-permute-start | bytes 589832 | tf_op jit(solution)/shard_map/ppermute | solution.py:61
  30.3 1.1 collective-permute-start.8
  31.4 1.4 %collective-permute-start.9 = (bf16[128,768]{1,0:T(8,128)(2,1)S(1)}, bf16[128,768]{1,0:T(8,128)(2,1)S(1)}, u32[]{:S(2)}, u32[]{:S(2)}) collective-permute-start(bf16[128,768]{1,0:T(8,128)(2,1)S(1)} %get-tuple-element.51), channel_id=1, source_target_pairs={{0,6},{1,7},{2,4},{3,5},{4,2},{5,3},{6,0},{7,1},{8,14},{9,15},{10,... | collective-permute-start | bytes 589832 | tf_op jit(solution)/shard_map/ppermute | solution.py:61
  32.8 2.8 %shard_map.102 = (bf16[512,768]{1,0:T(8,128)(2,1)S(1)}, bf16[512,768]{1,0:T(8,128)(2,1)S(1)}, bf16[512,768]{1,0:T(8,128)(2,1)S(1)}) custom-call(s32[16]{0:T(128)S(1)} %copy-done.6, f32[16,768]{1,0:T(8,128)S(1)} %copy-done.3, bf16[768,2304]{1,0:T(8,128)(2,1)S(1)} %copy-done, bf16[512,768]{1,0:T(8,128)(2,1)S(1)} %shard_map.101.x_ref), custom_call_target="tpu_custom_call" | custom-call | flops 1811939328 | bytes 6684672 | tf_op jit(solution)/shard_map/pallas_call | solution.py:203
  35.6 2.2 %shard_map.103 = (bf16[512,768]{1,0:T(8,128)(2,1)S(1)}, bf16[512,768]{1,0:T(8,128)(2,1)S(1)}) custom-call(s32[16]{0:T(128)S(1)} %copy-done.6, f32[16,768]{1,0:T(8,128)S(1)} %copy-done.3, bf16[768,2304]{1,0:T(8,128)(2,1)S(1)} %copy-done, bf16[512,768]{1,0:T(8,128)(2,1)S(1)} %collective-permute-done.3.x_ref, bf16[512,768]{1,0:T(8,128)(2,1)S(1)} %get-tuple-element.39.rest_0_), custom_call_target="tpu_custom_call" | custom-call | flops 1207959552 | bytes 5898240 | tf_op jit(solution)/shard_map/pallas_call | solution.py:203
  37.8 9.9 %shard_map.104.refs_4_ = bf16[4,4,32,768]{3,2,1,0:T(8,128)(2,1)S(1)} custom-call(s32[16]{0:T(128)S(1)} %copy-done.6, f32[16,768]{1,0:T(8,128)S(1)} %copy-done.3, bf16[768,768]{1,0:T(8,128)(2,1)S(1)} %copy-done.7, bf16[512,768]{1,0:T(8,128)(2,1)S(1)} %shard_map.101.x_ref, bf16[512,768]{1,0:T(8,128)(2,1)S(1)} %get-tuple-element.38.q_ref, ...), custom_call_target="tpu_custom_call" | custom-call | flops 6442450944 | bytes 6684672 | tf_op jit(solution)/shard_map/pallas_call | solution.py:301
  47.7 1.0 shard_map.107.x_ref
  48.8 7.9 %all-to-all-start = ((bf16[16,32,768]{2,1,0:T(8,128)(2,1)}), bf16[16,32,768]{2,1,0:T(8,128)(2,1)}, u32[]{:S(2)}, u32[]{:S(2)}) async-start(bf16[16,32,768]{2,1,0:T(8,128)(2,1)} %bitcast.5), calls=%async_computation | async-start | bytes 1572864 | tf_op jit(solution)/shard_map/all_to_all | solution.py:497
  56.8 0.8 copy-done.4
  57.5 3.4 %shard_map.108 = (bf16[512,768]{1,0:T(8,128)(2,1)S(1)}, bf16[512,768]{1,0:T(8,128)(2,1)S(1)}, bf16[512,768]{1,0:T(8,128)(2,1)S(1)}) custom-call(s32[16]{0:T(128)S(1)} %copy-done.6, f32[16,768]{1,0:T(8,128)S(1)} %copy-done.4, bf16[768,2304]{1,0:T(8,128)(2,1)S(1)} %copy-done, bf16[512,768]{1,0:T(8,128)(2,1)} %shard_map.107.x_ref), custom_call_target="tpu_custom_call" | custom-call | flops 1811939328 | bytes 6684672 | tf_op jit(solution)/shard_map/pallas_call | solution.py:203
  61.0 2.9 %shard_map.109 = (bf16[512,768]{1,0:T(8,128)(2,1)S(1)}, bf16[512,768]{1,0:T(8,128)(2,1)S(1)}) custom-call(s32[16]{0:T(128)S(1)} %copy-done.6, f32[16,768]{1,0:T(8,128)S(1)} %copy-done.4, bf16[768,2304]{1,0:T(8,128)(2,1)S(1)} %copy-done, bf16[512,768]{1,0:T(8,128)(2,1)} %collective-permute-done.10.x_ref, bf16[512,768]{1,0:T(8,128)(2,1)S(1)} %get-tuple-element.53.rest_0_), custom_call_target="tpu_custom_call" | custom-call | flops 1207959552 | bytes 5898240 | tf_op jit(solution)/shard_map/pallas_call | solution.py:203
  63.8 11.4 %shard_map.110 = bf16[4,4,32,768]{3,2,1,0:T(8,128)(2,1)} custom-call(s32[16]{0:T(128)S(1)} %copy-done.6, f32[16,768]{1,0:T(8,128)S(1)} %copy-done.4, bf16[768,768]{1,0:T(8,128)(2,1)S(1)} %copy-done.8, bf16[512,768]{1,0:T(8,128)(2,1)} %shard_map.107.x_ref, bf16[512,768]{1,0:T(8,128)(2,1)S(1)} %get-tuple-element.52.q_ref, ...), custom_call_target="tpu_custom_call" | custom-call | flops 6442450944 | bytes 6684672 | tf_op jit(solution)/shard_map/pallas_call | solution.py:301
  75.2 4.1 %all-to-all-done = bf16[16,32,768]{2,1,0:T(8,128)(2,1)} async-done(((bf16[16,32,768]{2,1,0:T(8,128)(2,1)}), bf16[16,32,768]{2,1,0:T(8,128)(2,1)}, u32[]{:S(2)}, u32[]{:S(2)}) %all-to-all-start) | async-done | bytes 786464 | tf_op jit(solution)/shard_map/all_to_all | solution.py:497
  79.3 3.8 %all-to-all-start.1 = ((bf16[16,32,768]{2,1,0:T(8,128)(2,1)}), bf16[16,32,768]{2,1,0:T(8,128)(2,1)S(1)}, u32[]{:S(2)}, u32[]{:S(2)}) async-start(bf16[16,32,768]{2,1,0:T(8,128)(2,1)} %bitcast.3), calls=%async_computation.1 | async-start | bytes 1572864 | tf_op jit(solution)/shard_map/all_to_all | solution.py:497
  83.2 17.0 %shard_map.105 = (bf16[4,32,768]{2,1,0:T(8,128)(2,1)S(1)}, bf16[4,32,768]{2,1,0:T(8,128)(2,1)S(1)}, bf16[4,32,768]{2,1,0:T(8,128)(2,1)S(1)}, bf16[4,32,768]{2,1,0:T(8,128)(2,1)S(1)}) custom-call(bf16[768,2304]{1,0:T(8,128)(2,1)} %qkv_hbm.3, bf16[768,768]{1,0:T(8,128)(2,1)} %out_hbm.3, bf16[768,3072]{1,0:T(8,128)(2,1)} %up_hbm.3, bf16[3072,768]{1,0:T(8,128)(2,1)} %down_hbm.3, ...), custom_call_target="tpu_custom_call" | custom-call | flops 7247757312 | bytes 15728640 | tf_op jit(solution)/shard_map/pallas_call | solution.py:407
  100.2 1.7 %collective-permute-start.4 = (bf16[4,32,768]{2,1,0:T(8,128)(2,1)S(1)}, bf16[4,32,768]{2,1,0:T(8,128)(2,1)S(1)}, u32[]{:S(2)}, u32[]{:S(2)}) collective-permute-start(bf16[4,32,768]{2,1,0:T(8,128)(2,1)S(1)} %get-tuple-element.44), channel_id=1, source_target_pairs={{0,8},{8,0},{16,24},{24,16},{1,9},{9,1},{17,25},{25,17},{2,10},{10... | collective-permute-start | bytes 589832 | tf_op jit(solution)/shard_map/ppermute | solution.py:61
  101.9 1.5 %collective-permute-start.5 = (bf16[4,32,768]{2,1,0:T(8,128)(2,1)S(1)}, bf16[4,32,768]{2,1,0:T(8,128)(2,1)S(1)}, u32[]{:S(2)}, u32[]{:S(2)}) collective-permute-start(bf16[4,32,768]{2,1,0:T(8,128)(2,1)S(1)} %get-tuple-element.45), channel_id=1, source_target_pairs={{0,16},{8,24},{16,0},{24,8},{1,17},{9,25},{17,1},{25,9},{2,18},{10... | collective-permute-start | bytes 589832 | tf_op jit(solution)/shard_map/ppermute | solution.py:61
  103.8 0.7 all-to-all-done.1
  104.4 15.9 %shard_map.111 = (bf16[4,32,768]{2,1,0:T(8,128)(2,1)S(1)}, bf16[4,32,768]{2,1,0:T(8,128)(2,1)S(1)}, bf16[4,32,768]{2,1,0:T(8,128)(2,1)S(1)}, bf16[4,32,768]{2,1,0:T(8,128)(2,1)S(1)}) custom-call(bf16[768,2304]{1,0:T(8,128)(2,1)} %qkv_hbm.3, bf16[768,768]{1,0:T(8,128)(2,1)} %out_hbm.3, bf16[768,3072]{1,0:T(8,128)(2,1)} %up_hbm.3, bf16[3072,768]{1,0:T(8,128)(2,1)} %down_hbm.3, ...), custom_call_target="tpu_custom_call" | custom-call | flops 7247757312 | bytes 15728640 | tf_op jit(solution)/shard_map/pallas_call | solution.py:407
  120.3 1.0 collective-permute-start.11
  121.3 1.5 %collective-permute-start.12 = (bf16[4,32,768]{2,1,0:T(8,128)(2,1)S(1)}, bf16[4,32,768]{2,1,0:T(8,128)(2,1)S(1)}, u32[]{:S(2)}, u32[]{:S(2)}) collective-permute-start(bf16[4,32,768]{2,1,0:T(8,128)(2,1)S(1)} %get-tuple-element.59), channel_id=1, source_target_pairs={{0,16},{8,24},{16,0},{24,8},{1,17},{9,25},{17,1},{25,9},{2,18},{10... | collective-permute-start | bytes 589832 | tf_op jit(solution)/shard_map/ppermute | solution.py:61
  122.8 1.1 collective-permute-start.13
  123.9 4.0 %collective-permute-done.11.refs_5_ = bf16[4,32,768]{2,1,0:T(8,128)(2,1)S(1)} collective-permute-done((bf16[4,32,768]{2,1,0:T(8,128)(2,1)S(1)}, bf16[4,32,768]{2,1,0:T(8,128)(2,1)S(1)}, u32[]{:S(2)}, u32[]{:S(2)}) %collective-permute-start.11) | collective-permute-done | bytes 196640 | tf_op jit(solution)/shard_map/ppermute | solution.py:61
  127.9 2.5 %collective-permute-done.12.refs_6_ = bf16[4,32,768]{2,1,0:T(8,128)(2,1)S(1)} collective-permute-done((bf16[4,32,768]{2,1,0:T(8,128)(2,1)S(1)}, bf16[4,32,768]{2,1,0:T(8,128)(2,1)S(1)}, u32[]{:S(2)}, u32[]{:S(2)}) %collective-permute-start.12) | collective-permute-done | bytes 196640 | tf_op jit(solution)/shard_map/ppermute | solution.py:61
  130.4 2.7 %shard_map.112 = bf16[256,4,768]{2,1,0:T(4,128)(2,1)} custom-call(f32[1,256]{1,0:T(1,128)S(1)} %get-tuple-element.33.keys_ref, bf16[4,32,768]{2,1,0:T(8,128)(2,1)S(1)} %get-tuple-element.43.refs_0_, bf16[4,32,768]{2,1,0:T(8,128)(2,1)S(1)} %collective-permute-done.4.refs_1_, bf16[4,32,768]{2,1,0:T(8,128)(2,1)S(1)} %collective-permute-done.5.refs_2_, ...), custom_call_target="tpu_custom_call" | custom-call | flops 402653184 | bytes 3145728 | tf_op jit(solution)/shard_map/pallas_call | solution.py:445
  (31 shorter events, 1.0 us)
Async XLA Ops:
  0.0 1.4 %copy-start.2 = (bf16[256,4,768]{2,1,0:T(4,128)(2,1)S(1)}, bf16[256,4,768]{2,1,0:T(4,128)(2,1)}, u32[]{:S(2)}) copy-start(bf16[256,4,768]{2,1,0:T(4,128)(2,1)} %x_ref.1) | copy-start | bytes 4718596
  1.4 0.7 copy-start.5
  2.1 30.7 %copy-start = (bf16[768,2304]{1,0:T(8,128)(2,1)S(1)}, bf16[768,2304]{1,0:T(8,128)(2,1)}, u32[]{:S(2)}) copy-start(bf16[768,2304]{1,0:T(8,128)(2,1)} %w_ref.10) | copy-start | bytes 10616836
  6.1 11.4 %collective-permute-start = (bf16[128,768]{1,0:T(8,128)(2,1)S(1)}, bf16[128,768]{1,0:T(8,128)(2,1)S(1)}, u32[]{:S(2)}, u32[]{:S(2)}) collective-permute-start(bf16[128,768]{1,0:T(8,128)(2,1)S(1)} %get-tuple-element.35), channel_id=1, source_target_pairs={{0,2},{1,3},{2,0},{3,1},{4,6},{5,7},{6,4},{7,5},{8,10},{9,11},{10,... | collective-permute-start | bytes 589832 | tf_op jit(solution)/shard_map/ppermute | solution.py:61
  9.2 17.2 %collective-permute-start.1 = (bf16[128,768]{1,0:T(8,128)(2,1)S(1)}, bf16[128,768]{1,0:T(8,128)(2,1)S(1)}, u32[]{:S(2)}, u32[]{:S(2)}) collective-permute-start(bf16[128,768]{1,0:T(8,128)(2,1)S(1)} %get-tuple-element.36), channel_id=1, source_target_pairs={{0,4},{1,5},{2,6},{3,7},{4,0},{5,1},{6,2},{7,3},{8,12},{9,13},{10,... | collective-permute-start | bytes 589832 | tf_op jit(solution)/shard_map/ppermute | solution.py:61
  11.8 14.6 %collective-permute-start.2 = (bf16[128,768]{1,0:T(8,128)(2,1)S(1)}, bf16[128,768]{1,0:T(8,128)(2,1)S(1)}, u32[]{:S(2)}, u32[]{:S(2)}) collective-permute-start(bf16[128,768]{1,0:T(8,128)(2,1)S(1)} %get-tuple-element.37), channel_id=1, source_target_pairs={{0,6},{1,7},{2,4},{3,5},{4,2},{5,3},{6,0},{7,1},{8,14},{9,15},{10,... | collective-permute-start | bytes 589832 | tf_op jit(solution)/shard_map/ppermute | solution.py:61
  26.3 6.4 %copy-start.3 = (f32[16,768]{1,0:T(8,128)S(1)}, f32[16,768]{1,0:T(8,128)}, u32[]{:S(2)}) copy-start(f32[16,768]{1,0:T(8,128)} %table_ref.11) | copy-start | bytes 147460
  26.3 6.4 %copy-start.6 = (s32[16]{0:T(128)S(1)}, s32[16]{0:T(128)}, u32[]{:S(2)}) copy-start(s32[16]{0:T(128)} %index_ref.11) | copy-start | bytes 196
  26.4 9.2 %collective-permute-start.3 = (bf16[512,768]{1,0:T(8,128)(2,1)S(1)}, bf16[512,768]{1,0:T(8,128)(2,1)S(1)}, u32[]{:S(2)}, u32[]{:S(2)}) collective-permute-start(bf16[512,768]{1,0:T(8,128)(2,1)S(1)} %shard_map.101.x_ref), channel_id=1, source_target_pairs={{0,1},{1,0},{2,3},{3,2},{4,5},{5,4},{6,7},{7,6},{8,9},{9,8},{10,11... | collective-permute-start | bytes 2359304 | tf_op jit(solution)/shard_map/ppermute | solution.py:61
  26.9 20.8 %collective-permute-start.7 = (bf16[128,768]{1,0:T(8,128)(2,1)S(1)}, bf16[128,768]{1,0:T(8,128)(2,1)S(1)}, u32[]{:S(2)}, u32[]{:S(2)}) collective-permute-start(bf16[128,768]{1,0:T(8,128)(2,1)S(1)} %get-tuple-element.49), channel_id=1, source_target_pairs={{0,2},{1,3},{2,0},{3,1},{4,6},{5,7},{6,4},{7,5},{8,10},{9,11},{10,... | collective-permute-start | bytes 589832 | tf_op jit(solution)/shard_map/ppermute | solution.py:61
  30.3 17.4 %collective-permute-start.8 = (bf16[128,768]{1,0:T(8,128)(2,1)S(1)}, bf16[128,768]{1,0:T(8,128)(2,1)S(1)}, u32[]{:S(2)}, u32[]{:S(2)}) collective-permute-start(bf16[128,768]{1,0:T(8,128)(2,1)S(1)} %get-tuple-element.50), channel_id=1, source_target_pairs={{0,4},{1,5},{2,6},{3,7},{4,0},{5,1},{6,2},{7,3},{8,12},{9,13},{10,... | collective-permute-start | bytes 589832 | tf_op jit(solution)/shard_map/ppermute | solution.py:61
  31.4 16.3 %collective-permute-start.9 = (bf16[128,768]{1,0:T(8,128)(2,1)S(1)}, bf16[128,768]{1,0:T(8,128)(2,1)S(1)}, u32[]{:S(2)}, u32[]{:S(2)}) collective-permute-start(bf16[128,768]{1,0:T(8,128)(2,1)S(1)} %get-tuple-element.51), channel_id=1, source_target_pairs={{0,6},{1,7},{2,4},{3,5},{4,2},{5,3},{6,0},{7,1},{8,14},{9,15},{10,... | collective-permute-start | bytes 589832 | tf_op jit(solution)/shard_map/ppermute | solution.py:61
  35.6 2.2 %copy-start.7 = (bf16[768,768]{1,0:T(8,128)(2,1)S(1)}, bf16[768,768]{1,0:T(8,128)(2,1)}, u32[]{:S(2)}) copy-start(bf16[768,768]{1,0:T(8,128)(2,1)} %w_ref.11) | copy-start | bytes 3538948
  47.7 1.1 copy-start.1
  48.8 12.2 %collective-permute-start.10 = (bf16[512,768]{1,0:T(8,128)(2,1)}, bf16[512,768]{1,0:T(8,128)(2,1)}, u32[]{:S(2)}, u32[]{:S(2)}) collective-permute-start(bf16[512,768]{1,0:T(8,128)(2,1)} %shard_map.107.x_ref), channel_id=1, source_target_pairs={{0,1},{1,0},{2,3},{3,2},{4,5},{5,4},{6,7},{7,6},{8,9},{9,8},{10,11... | collective-permute-start | bytes 2359304 | tf_op jit(solution)/shard_map/ppermute | solution.py:61
  48.8 30.5 %all-to-all-start = ((bf16[16,32,768]{2,1,0:T(8,128)(2,1)}), bf16[16,32,768]{2,1,0:T(8,128)(2,1)}, u32[]{:S(2)}, u32[]{:S(2)}) async-start(bf16[16,32,768]{2,1,0:T(8,128)(2,1)} %bitcast.5), calls=%async_computation | async-start | bytes 1572864 | tf_op jit(solution)/shard_map/all_to_all | solution.py:497
  56.7 0.8 copy-start.4
  60.9 2.9 %copy-start.8 = (bf16[768,768]{1,0:T(8,128)(2,1)S(1)}, bf16[768,768]{1,0:T(8,128)(2,1)}, u32[]{:S(2)}) copy-start(bf16[768,768]{1,0:T(8,128)(2,1)} %w_ref.11) | copy-start | bytes 3538948
  79.3 25.1 %all-to-all-start.1 = ((bf16[16,32,768]{2,1,0:T(8,128)(2,1)}), bf16[16,32,768]{2,1,0:T(8,128)(2,1)S(1)}, u32[]{:S(2)}, u32[]{:S(2)}) async-start(bf16[16,32,768]{2,1,0:T(8,128)(2,1)} %bitcast.3), calls=%async_computation.1 | async-start | bytes 1572864 | tf_op jit(solution)/shard_map/all_to_all | solution.py:497
  100.2 22.6 %collective-permute-start.4 = (bf16[4,32,768]{2,1,0:T(8,128)(2,1)S(1)}, bf16[4,32,768]{2,1,0:T(8,128)(2,1)S(1)}, u32[]{:S(2)}, u32[]{:S(2)}) collective-permute-start(bf16[4,32,768]{2,1,0:T(8,128)(2,1)S(1)} %get-tuple-element.44), channel_id=1, source_target_pairs={{0,8},{8,0},{16,24},{24,16},{1,9},{9,1},{17,25},{25,17},{2,10},{10... | collective-permute-start | bytes 589832 | tf_op jit(solution)/shard_map/ppermute | solution.py:61
  101.9 22.0 %collective-permute-start.5 = (bf16[4,32,768]{2,1,0:T(8,128)(2,1)S(1)}, bf16[4,32,768]{2,1,0:T(8,128)(2,1)S(1)}, u32[]{:S(2)}, u32[]{:S(2)}) collective-permute-start(bf16[4,32,768]{2,1,0:T(8,128)(2,1)S(1)} %get-tuple-element.45), channel_id=1, source_target_pairs={{0,16},{8,24},{16,0},{24,8},{1,17},{9,25},{17,1},{25,9},{2,18},{10... | collective-permute-start | bytes 589832 | tf_op jit(solution)/shard_map/ppermute | solution.py:61
  103.4 20.5 %collective-permute-start.6 = (bf16[4,32,768]{2,1,0:T(8,128)(2,1)S(1)}, bf16[4,32,768]{2,1,0:T(8,128)(2,1)S(1)}, u32[]{:S(2)}, u32[]{:S(2)}) collective-permute-start(bf16[4,32,768]{2,1,0:T(8,128)(2,1)S(1)} %get-tuple-element.46), channel_id=1, source_target_pairs={{0,24},{8,16},{16,8},{24,0},{1,25},{9,17},{17,9},{25,1},{2,26},{10... | collective-permute-start | bytes 589832 | tf_op jit(solution)/shard_map/ppermute | solution.py:61
  120.3 7.6 %collective-permute-start.11 = (bf16[4,32,768]{2,1,0:T(8,128)(2,1)S(1)}, bf16[4,32,768]{2,1,0:T(8,128)(2,1)S(1)}, u32[]{:S(2)}, u32[]{:S(2)}) collective-permute-start(bf16[4,32,768]{2,1,0:T(8,128)(2,1)S(1)} %get-tuple-element.58), channel_id=1, source_target_pairs={{0,8},{8,0},{16,24},{24,16},{1,9},{9,1},{17,25},{25,17},{2,10},{10... | collective-permute-start | bytes 589832 | tf_op jit(solution)/shard_map/ppermute | solution.py:61
  121.3 9.1 %collective-permute-start.12 = (bf16[4,32,768]{2,1,0:T(8,128)(2,1)S(1)}, bf16[4,32,768]{2,1,0:T(8,128)(2,1)S(1)}, u32[]{:S(2)}, u32[]{:S(2)}) collective-permute-start(bf16[4,32,768]{2,1,0:T(8,128)(2,1)S(1)} %get-tuple-element.59), channel_id=1, source_target_pairs={{0,16},{8,24},{16,0},{24,8},{1,17},{9,25},{17,1},{25,9},{2,18},{10... | collective-permute-start | bytes 589832 | tf_op jit(solution)/shard_map/ppermute | solution.py:61
  122.8 7.6 %collective-permute-start.13 = (bf16[4,32,768]{2,1,0:T(8,128)(2,1)S(1)}, bf16[4,32,768]{2,1,0:T(8,128)(2,1)S(1)}, u32[]{:S(2)}, u32[]{:S(2)}) collective-permute-start(bf16[4,32,768]{2,1,0:T(8,128)(2,1)S(1)} %get-tuple-element.60), channel_id=1, source_target_pairs={{0,24},{8,16},{16,8},{24,0},{1,25},{9,17},{17,9},{25,1},{2,26},{10... | collective-permute-start | bytes 589832 | tf_op jit(solution)/shard_map/ppermute | solution.py:61

commit v4 on v3

--- a/solution.py
+++ b/solution.py
@@ -13,8 +13,7 @@
 CORES = 2
 TILE_LOCS = 16
 GROUP_LOCS = 8
-NORM_ROWS = 128
-UNIT_ROWS = 128
+UNIT_ROWS = 256
 STEP_PAIRS = 2
 ROW_TILE = 256
 LANES = 128
@@ -95,55 +94,64 @@
 ANY = pl.BlockSpec(memory_space=pl.ANY)
 
 
-def pick_rows(plan, window, keys, bands, outs):
+def pick_rows(plan, window, place_keys, rows, outs):
     row = lax.axis_index("loc") // CORES
-    place = lax.broadcasted_iota(jnp.int32, (plan.rows, plan.loc_dev), 0)
+    place = lax.broadcasted_iota(jnp.int32, (plan.rows, rows.shape[0]), 0)
     for slot in range(plan.rows_count):
         peer = row ^ slot
-        wanted = place + (window * plan.block + (peer % plan.share) * plan.rows)
-        pick = jnp.where(wanted.astype(F32) == keys, 1.0, 0.0).astype(BF16)
-        outs[slot][...] = dot(pick, bands[peer // plan.share]).astype(BF16)
+        band, part = peer // plan.share, peer % plan.share
+        wanted = place + (band * plan.loc_dev + window * plan.block + part * plan.rows)
+        pick = jnp.where(wanted.astype(F32) == place_keys, 1.0, 0.0).astype(BF16)
+        outs[slot][...] = dot(pick, rows[...]).astype(BF16)
 
 
 def arrange_first(plan, tokens, ids):
     count = plan.rows_count
+    total = plan.loc_dev * plan.band_dev
+    assert plan.loc_dev <= 256
 
     def kernel(ids_ref, x_ref, *rest):
-        outs, (bands, keys_ref) = rest[:count], rest[count:]
+        outs, (rows_ref, keys_ref, place_ref) = rest[:count], rest[count:]
         keys = location_keys(plan, ids_ref)
         keys_ref[...] = keys
-        for band in range(plan.band_dev):
-            bands[band] = x_ref[:, band, :]
-        pick_rows(plan, 0, keys, bands, outs)
+        place = lax.broadcasted_iota(jnp.int32, (plan.loc_dev, total), 1)
+        location = lax.broadcasted_iota(jnp.int32, (plan.loc_dev, total), 0)
+        spread = jnp.where(place // plan.band_dev == location, 1.0, 0.0).astype(BF16)
+        wide = dot(jnp.broadcast_to(keys, (16, plan.loc_dev)).astype(BF16), spread)
+        band = lax.broadcasted_iota(jnp.int32, (1, total), 1) % plan.band_dev
+        place_ref[...] = wide[:1] + (band * plan.loc_dev).astype(F32)
+        rows_ref[...] = x_ref[...].reshape(total, plan.width)
+        pick_rows(plan, 0, place_ref[...], rows_ref, outs)
 
     return call(
         kernel,
         [jax.ShapeDtypeStruct((plan.rows, plan.width), BF16)] * count
         + [
-            jax.ShapeDtypeStruct((plan.band_dev, plan.loc_dev, plan.width), BF16),
+            jax.ShapeDtypeStruct((total, plan.width), BF16),
             jax.ShapeDtypeStruct((1, plan.loc_dev), F32),
+            jax.ShapeDtypeStruct((1, total), F32),
         ],
         2 * plan.loc_dev * tokens.size,
         4 * tokens.size,
         in_specs=[VMEM] * 2,
-        out_specs=[VMEM] * (count + 2),
+        out_specs=[VMEM] * (count + 3),
     )(ids, tokens)
 
 
-def arrange_next(plan, window, bands, keys, after):
+def arrange_next(plan, window, rows, place_keys, after):
     count = plan.rows_count
 
-    def kernel(bands_ref, keys_ref, *rest):
-        pick_rows(plan, window, keys_ref[...], bands_ref, rest[len(after) :])
+    def kernel(rows_ref, place_ref, *rest):
+        pick_rows(plan, window, place_ref[...], rows_ref, rest[len(after) :])
 
     return call(
         kernel,
         [jax.ShapeDtypeStruct((plan.rows, plan.width), BF16)] * count,
-        2 * plan.loc_dev * bands.size,
-        4 * bands.size,
+        2 * plan.loc_dev * rows.size,
+        4 * rows.size,
         in_specs=[VMEM] * 2 + [ANY] * len(after),
         out_specs=[VMEM] * count,
-    )(bands, keys, *after)
+    )(rows, place_keys, *after)
 
 
 def join_slots(plan, slots, after):
@@ -167,22 +175,20 @@
     return table_ref[pl.ds(number, 1), :]
 
 
-def loop(count, step):
-    lax.fori_loop(0, count, lambda i, _: (step(i), 0)[1], 0)
+def loop(count, step, unroll=1):
+    lax.fori_loop(0, count, lambda i, _: (step(i), 0)[1], 0, unroll=unroll)
 
 
 def aligned(index, size):
     return pl.ds(pl.multiple_of(index * size, size), size)
 
 
-def norm_into(target, rows_of, rows):
-    tile = min(rows, NORM_ROWS)
-
-    def step(index):
-        here = aligned(index, tile)
-        target[here, :] = norm_rows(rows_of(here)).astype(BF16)
-
-    loop(rows // tile, step)
+def norm_into(target, source):
+    rows = source.shape[0]
+    tile = min(rows, ROW_TILE)
+    for first in range(0, rows, tile):
+        here = pl.ds(first, tile)
+        target[here, :] = norm_rows(source[here, :]).astype(BF16)
 
 
 def project(plan, tokens, index, table, weights, queries, after=()):
@@ -356,7 +362,7 @@
             piece = in_ref[me ^ owner, band, first : first + tile, :].astype(F32)
             for number, place in enumerate(places(owner, band, first)):
                 mid[place, :] = piece[number * small : (number + 1) * small]
-        norm_into(normed, lambda here: mid[here, :], rows)
+        norm_into(normed, mid)
 
         for number, here in enumerate(columns):
             copies[number].wait()
@@ -380,10 +386,10 @@
             for spot, done in zip(spots, run_units(units, mask)):
                 attended[spot] = done
 
-        loop(pairs, attention_step)
+        loop(pairs, attention_step, unroll=2)
         copies[3].wait()
         mid[...] += dot(attended[...], out_ref[...])
-        norm_into(normed, lambda here: mid[here, :], rows)
+        norm_into(normed, mid)
 
         copies[4].wait()
         copies[5].wait()
@@ -464,29 +470,32 @@
 ):
     plan = Plan(tokens)
     ids = window_ids.reshape(-1, LANES)
-    *sent, bands, place_keys = arrange_first(plan, tokens, ids)
-    mids, behind, began = [], (), ()
-    for window in range(WINDOWS):
-        if window > 0:
-            sent = arrange_next(plan, window, bands, place_keys, began)
-        slots = [exchange(value, "loc", CORES * step) for step, value in enumerate(sent)]
-        began = slots[1:2]
+    *sent, rows, keys, place_keys = arrange_first(plan, tokens, ids)
+    arrived = [[exchange(value, "loc", CORES * step) for step, value in enumerate(sent)]]
+    following = []
+    for window in range(1, WINDOWS):
+        following = arrange_next(plan, window, rows, place_keys, arrived[-1][1:2])
+        arrived.append(
+            [exchange(value, "loc", CORES * step) for step, value in enumerate(following)]
+        )
+    mids, behind = [], following[:1]
+    for slots in arrived:
         own = join_slots(plan, slots, behind)
         if plan.share == 1:
             other = exchange(own, "loc", 1)
             query, *mine = project(plan, own, band_index, band_table, spatial_qkv, True)
             theirs = project(plan, other, band_index, band_table, spatial_qkv, False, mine[:1])
-            keys, values = zip(mine, theirs)
+            all_keys, all_values = zip(mine, theirs)
         else:
             step = CORES * plan.share
             same = [list(range(at, at + step)) for at in range(0, plan.locs, step)]
             every = lax.all_gather(own, "loc", axis_index_groups=same, tiled=True)
             query, _, _ = project(plan, own, band_index, band_table, spatial_qkv, True)
-            keys, values = zip(
+            all_keys, all_values = zip(
                 project(plan, every, band_index, band_table, spatial_qkv, False)
             )
-        mid = attend(plan, query, keys, values, own, band_index, band_table, spatial_out)
-        behind = (mid,)
+        mid = attend(plan, query, all_keys, all_values, own, band_index, band_table, spatial_out)
+        behind = [mid]
         mids.append(mid)
     same = [
         [(g * plan.rows_count + r) * CORES + core for g in range(plan.groups) for r in range(plan.rows_count)]
@@ -505,7 +514,7 @@
         parts = parts.reshape(plan.groups, plan.band_dev, -1, plan.width)
         done = channel(plan, parts, channel_qkv, channel_out, up_weight, down_weight)
         returned.append([exchange(value, "band", step) for step, value in enumerate(done)])
-    return restore(plan, place_keys, returned)
+    return restore(plan, keys, returned)
 
 
 def solution(mesh):

time: 134 us -> 129 us (0.963)
  Pallas kernels: 73.5 us -> 67.5 us
    pallas_call x2, Pallas kernels: 32.9 us -> 29.6 us  [channel(): call(kernel, [jax.ShapeDtypeStruct((bands, locations, width), BF16)] * gr...]
    pallas_call x1, Pallas kernels: 3.97 us -> 1.27 us  [arrange_first(): call(kernel, [jax.ShapeDtypeStruct((plan.rows, plan.width), BF16)] * coun...]
    all_to_all x2, waiting for transfers between devices: 4.81 us -> 6.73 us  [body(): lax.all_to_all(mid.reshape(-1, plan.part_rows, plan.width), ('band', 'loc...]
where the time goes in v4:
time: 129 us; the launch traced here: 128 us
  Pallas kernels  67.5 us (52%)
  starting transfers between devices  30.8 us (24%)
  waiting for transfers between devices  26.5 us (21%)
  local copies, waits for them, and re-layouts  2.99 us (2%)
    pallas_call x2, Pallas kernels, channel(): call(kernel, [jax.ShapeDtypeStruct((bands, locations, width), BF16)] * gr...  29.6 us
    pallas_call x2, Pallas kernels, attend(): call(kernel, jax.ShapeDtypeStruct((plan.groups, plan.rows_count, plan.par...  20.7 us
    ppermute x14, waiting for transfers between devices, exchange(): lax.ppermute(value, axis, [(i, i ^ step) for i in range(lax.axis_size(axi...  19.8 us
    ppermute x14, starting transfers between devices, exchange(): lax.ppermute(value, axis, [(i, i ^ step) for i in range(lax.axis_size(axi...  18.7 us
    all_to_all x2, starting transfers between devices, body(): lax.all_to_all(mid.reshape(-1, plan.part_rows, plan.width), ('band', 'loc...  12 us
    pallas_call x4, Pallas kernels, project(): call(kernel, [jax.ShapeDtypeStruct((rows, width), BF16)] * len(names), 2...  11.2 us
    all_to_all x2, waiting for transfers between devices, body(): lax.all_to_all(mid.reshape(-1, plan.part_rows, plan.width), ('band', 'loc...  6.73 us
    unnamed x18, local copies, waits for them, and re-layouts  2.99 us
  transfers between devices with their start and end apart: 16, of which 6 were waited for; matrix products, arithmetic and copies ran while one was open for 0% of the time, Pallas kernels for 49%

profile of v4, /device:TPU:0, one launch (start us, length us, event | category | flops | bytes accessed | tf_op | source)
XLA Modules:
  0.0 128.0 jit_solution(10256380346913871591)
XLA Ops:
  0.0 1.4 %copy-done.2 = bf16[256,4,768]{2,1,0:T(4,128)(2,1)S(1)} copy-done((bf16[256,4,768]{2,1,0:T(4,128)(2,1)S(1)}, bf16[256,4,768]{2,1,0:T(4,128)(2,1)}, u32[]{:S(2)}) %copy-start.2) | copy-done | bytes 1572888
  1.4 0.7 copy-done.5
  2.1 1.3 shard_map.100
  3.4 3.1 %collective-permute-start = (bf16[128,768]{1,0:T(8,128)(2,1)S(1)}, bf16[128,768]{1,0:T(8,128)(2,1)S(1)}, u32[]{:S(2)}, u32[]{:S(2)}) collective-permute-start(bf16[128,768]{1,0:T(8,128)(2,1)S(1)} %get-tuple-element.36), channel_id=1, source_target_pairs={{0,2},{1,3},{2,0},{3,1},{4,6},{5,7},{6,4},{7,5},{8,10},{9,11},{10,... | collective-permute-start | bytes 589832 | tf_op jit(solution)/shard_map/ppermute | solution.py:60
  6.5 2.6 %collective-permute-start.1 = (bf16[128,768]{1,0:T(8,128)(2,1)S(1)}, bf16[128,768]{1,0:T(8,128)(2,1)S(1)}, u32[]{:S(2)}, u32[]{:S(2)}) collective-permute-start(bf16[128,768]{1,0:T(8,128)(2,1)S(1)} %get-tuple-element.37), channel_id=1, source_target_pairs={{0,4},{1,5},{2,6},{3,7},{4,0},{5,1},{6,2},{7,3},{8,12},{9,13},{10,... | collective-permute-start | bytes 589832 | tf_op jit(solution)/shard_map/ppermute | solution.py:60
  9.1 5.7 %collective-permute-done.rest_0_.refs_1_ = bf16[128,768]{1,0:T(8,128)(2,1)S(1)} collective-permute-done((bf16[128,768]{1,0:T(8,128)(2,1)S(1)}, bf16[128,768]{1,0:T(8,128)(2,1)S(1)}, u32[]{:S(2)}, u32[]{:S(2)}) %collective-permute-start) | collective-permute-done | bytes 196640 | tf_op jit(solution)/shard_map/ppermute | solution.py:60
  14.8 1.0 shard_map.101
  15.8 7.8 %collective-permute-done.1.refs_2_ = bf16[128,768]{1,0:T(8,128)(2,1)S(1)} collective-permute-done((bf16[128,768]{1,0:T(8,128)(2,1)S(1)}, bf16[128,768]{1,0:T(8,128)(2,1)S(1)}, u32[]{:S(2)}, u32[]{:S(2)}) %collective-permute-start.1) | collective-permute-done | bytes 196640 | tf_op jit(solution)/shard_map/ppermute | solution.py:60
  23.8 3.4 %collective-permute-start.7 = (bf16[128,768]{1,0:T(8,128)(2,1)S(1)}, bf16[128,768]{1,0:T(8,128)(2,1)S(1)}, u32[]{:S(2)}, u32[]{:S(2)}) collective-permute-start(bf16[128,768]{1,0:T(8,128)(2,1)S(1)} %get-tuple-element.51), channel_id=1, source_target_pairs={{0,2},{1,3},{2,0},{3,1},{4,6},{5,7},{6,4},{7,5},{8,10},{9,11},{10,... | collective-permute-start | bytes 589832 | tf_op jit(solution)/shard_map/ppermute | solution.py:60
  27.2 1.1 collective-permute-start.8
  28.3 1.4 %collective-permute-start.9 = (bf16[128,768]{1,0:T(8,128)(2,1)S(1)}, bf16[128,768]{1,0:T(8,128)(2,1)S(1)}, u32[]{:S(2)}, u32[]{:S(2)}) collective-permute-start(bf16[128,768]{1,0:T(8,128)(2,1)S(1)} %get-tuple-element.53), channel_id=1, source_target_pairs={{0,6},{1,7},{2,4},{3,5},{4,2},{5,3},{6,0},{7,1},{8,14},{9,15},{10,... | collective-permute-start | bytes 589832 | tf_op jit(solution)/shard_map/ppermute | solution.py:60
  29.7 2.8 %shard_map.103 = (bf16[512,768]{1,0:T(8,128)(2,1)S(1)}, bf16[512,768]{1,0:T(8,128)(2,1)S(1)}, bf16[512,768]{1,0:T(8,128)(2,1)S(1)}) custom-call(s32[16]{0:T(128)S(1)} %copy-done.6, f32[16,768]{1,0:T(8,128)S(1)} %copy-done.3, bf16[768,2304]{1,0:T(8,128)(2,1)S(1)} %copy-done, bf16[512,768]{1,0:T(8,128)(2,1)S(1)} %shard_map.102.x_ref), custom_call_target="tpu_custom_call" | custom-call | flops 1811939328 | bytes 6684672 | tf_op jit(solution)/shard_map/pallas_call | solution.py:209
  32.5 2.2 %shard_map.104 = (bf16[512,768]{1,0:T(8,128)(2,1)S(1)}, bf16[512,768]{1,0:T(8,128)(2,1)S(1)}) custom-call(s32[16]{0:T(128)S(1)} %copy-done.6, f32[16,768]{1,0:T(8,128)S(1)} %copy-done.3, bf16[768,2304]{1,0:T(8,128)(2,1)S(1)} %copy-done, bf16[512,768]{1,0:T(8,128)(2,1)S(1)} %collective-permute-done.3.x_ref, bf16[512,768]{1,0:T(8,128)(2,1)S(1)} %get-tuple-element.43.rest_0_), custom_call_target="tpu_custom_call" | custom-call | flops 1207959552 | bytes 5898240 | tf_op jit(solution)/shard_map/pallas_call | solution.py:209
  34.7 9.6 %shard_map.105.refs_4_ = bf16[4,4,32,768]{3,2,1,0:T(8,128)(2,1)S(1)} custom-call(s32[16]{0:T(128)S(1)} %copy-done.6, f32[16,768]{1,0:T(8,128)S(1)} %copy-done.3, bf16[768,768]{1,0:T(8,128)(2,1)S(1)} %copy-done.7, bf16[512,768]{1,0:T(8,128)(2,1)S(1)} %shard_map.102.x_ref, bf16[512,768]{1,0:T(8,128)(2,1)S(1)} %get-tuple-element.42.q_ref, ...), custom_call_target="tpu_custom_call" | custom-call | flops 6442450944 | bytes 6684672 | tf_op jit(solution)/shard_map/pallas_call | solution.py:307
  44.3 1.0 shard_map.107.x_ref
  45.4 8.2 %all-to-all-start = ((bf16[16,32,768]{2,1,0:T(8,128)(2,1)}), bf16[16,32,768]{2,1,0:T(8,128)(2,1)}, u32[]{:S(2)}, u32[]{:S(2)}) async-start(bf16[16,32,768]{2,1,0:T(8,128)(2,1)} %bitcast.5), calls=%async_computation | async-start | bytes 1572864 | tf_op jit(solution)/shard_map/all_to_all | solution.py:506
  53.6 0.8 copy-done.4
  54.4 3.4 %shard_map.108 = (bf16[512,768]{1,0:T(8,128)(2,1)S(1)}, bf16[512,768]{1,0:T(8,128)(2,1)S(1)}, bf16[512,768]{1,0:T(8,128)(2,1)S(1)}) custom-call(s32[16]{0:T(128)S(1)} %copy-done.6, f32[16,768]{1,0:T(8,128)S(1)} %copy-done.4, bf16[768,2304]{1,0:T(8,128)(2,1)S(1)} %copy-done, bf16[512,768]{1,0:T(8,128)(2,1)} %shard_map.107.x_ref), custom_call_target="tpu_custom_call" | custom-call | flops 1811939328 | bytes 6684672 | tf_op jit(solution)/shard_map/pallas_call | solution.py:209
  57.8 2.9 %shard_map.109 = (bf16[512,768]{1,0:T(8,128)(2,1)S(1)}, bf16[512,768]{1,0:T(8,128)(2,1)S(1)}) custom-call(s32[16]{0:T(128)S(1)} %copy-done.6, f32[16,768]{1,0:T(8,128)S(1)} %copy-done.4, bf16[768,2304]{1,0:T(8,128)(2,1)S(1)} %copy-done, bf16[512,768]{1,0:T(8,128)(2,1)} %collective-permute-done.10.x_ref, bf16[512,768]{1,0:T(8,128)(2,1)S(1)} %get-tuple-element.55.rest_0_), custom_call_target="tpu_custom_call" | custom-call | flops 1207959552 | bytes 5898240 | tf_op jit(solution)/shard_map/pallas_call | solution.py:209
  60.7 11.1 %shard_map.110 = bf16[4,4,32,768]{3,2,1,0:T(8,128)(2,1)} custom-call(s32[16]{0:T(128)S(1)} %copy-done.6, f32[16,768]{1,0:T(8,128)S(1)} %copy-done.4, bf16[768,768]{1,0:T(8,128)(2,1)S(1)} %copy-done.8, bf16[512,768]{1,0:T(8,128)(2,1)} %shard_map.107.x_ref, bf16[512,768]{1,0:T(8,128)(2,1)S(1)} %get-tuple-element.54.q_ref, ...), custom_call_target="tpu_custom_call" | custom-call | flops 6442450944 | bytes 6684672 | tf_op jit(solution)/shard_map/pallas_call | solution.py:307
  71.8 4.4 %all-to-all-done = bf16[16,32,768]{2,1,0:T(8,128)(2,1)} async-done(((bf16[16,32,768]{2,1,0:T(8,128)(2,1)}), bf16[16,32,768]{2,1,0:T(8,128)(2,1)}, u32[]{:S(2)}, u32[]{:S(2)}) %all-to-all-start) | async-done | bytes 786464 | tf_op jit(solution)/shard_map/all_to_all | solution.py:506
  76.2 3.8 %all-to-all-start.1 = ((bf16[16,32,768]{2,1,0:T(8,128)(2,1)}), bf16[16,32,768]{2,1,0:T(8,128)(2,1)S(1)}, u32[]{:S(2)}, u32[]{:S(2)}) async-start(bf16[16,32,768]{2,1,0:T(8,128)(2,1)} %bitcast.3), calls=%async_computation.1 | async-start | bytes 1572864 | tf_op jit(solution)/shard_map/all_to_all | solution.py:506
  80.0 15.4 %shard_map.106 = (bf16[4,32,768]{2,1,0:T(8,128)(2,1)S(1)}, bf16[4,32,768]{2,1,0:T(8,128)(2,1)S(1)}, bf16[4,32,768]{2,1,0:T(8,128)(2,1)S(1)}, bf16[4,32,768]{2,1,0:T(8,128)(2,1)S(1)}) custom-call(bf16[768,2304]{1,0:T(8,128)(2,1)} %qkv_hbm.3, bf16[768,768]{1,0:T(8,128)(2,1)} %out_hbm.3, bf16[768,3072]{1,0:T(8,128)(2,1)} %up_hbm.3, bf16[3072,768]{1,0:T(8,128)(2,1)} %down_hbm.3, ...), custom_call_target="tpu_custom_call" | custom-call | flops 7247757312 | bytes 15728640 | tf_op jit(solution)/shard_map/pallas_call | solution.py:413
  95.4 1.7 %collective-permute-start.4 = (bf16[4,32,768]{2,1,0:T(8,128)(2,1)S(1)}, bf16[4,32,768]{2,1,0:T(8,128)(2,1)S(1)}, u32[]{:S(2)}, u32[]{:S(2)}) collective-permute-start(bf16[4,32,768]{2,1,0:T(8,128)(2,1)S(1)} %get-tuple-element.48), channel_id=1, source_target_pairs={{0,8},{8,0},{16,24},{24,16},{1,9},{9,1},{17,25},{25,17},{2,10},{10... | collective-permute-start | bytes 589832 | tf_op jit(solution)/shard_map/ppermute | solution.py:60
  97.1 1.5 %collective-permute-start.5 = (bf16[4,32,768]{2,1,0:T(8,128)(2,1)S(1)}, bf16[4,32,768]{2,1,0:T(8,128)(2,1)S(1)}, u32[]{:S(2)}, u32[]{:S(2)}) collective-permute-start(bf16[4,32,768]{2,1,0:T(8,128)(2,1)S(1)} %get-tuple-element.49), channel_id=1, source_target_pairs={{0,16},{8,24},{16,0},{24,8},{1,17},{9,25},{17,1},{25,9},{2,18},{10... | collective-permute-start | bytes 589832 | tf_op jit(solution)/shard_map/ppermute | solution.py:60
  99.0 2.3 %all-to-all-done.1 = bf16[16,32,768]{2,1,0:T(8,128)(2,1)S(1)} async-done(((bf16[16,32,768]{2,1,0:T(8,128)(2,1)}), bf16[16,32,768]{2,1,0:T(8,128)(2,1)S(1)}, u32[]{:S(2)}, u32[]{:S(2)}) %all-to-all-start.1) | async-done | bytes 786464 | tf_op jit(solution)/shard_map/all_to_all | solution.py:506
  101.3 14.2 %shard_map.111 = (bf16[4,32,768]{2,1,0:T(8,128)(2,1)S(1)}, bf16[4,32,768]{2,1,0:T(8,128)(2,1)S(1)}, bf16[4,32,768]{2,1,0:T(8,128)(2,1)S(1)}, bf16[4,32,768]{2,1,0:T(8,128)(2,1)S(1)}) custom-call(bf16[768,2304]{1,0:T(8,128)(2,1)} %qkv_hbm.3, bf16[768,768]{1,0:T(8,128)(2,1)} %out_hbm.3, bf16[768,3072]{1,0:T(8,128)(2,1)} %up_hbm.3, bf16[3072,768]{1,0:T(8,128)(2,1)} %down_hbm.3, ...), custom_call_target="tpu_custom_call" | custom-call | flops 7247757312 | bytes 15728640 | tf_op jit(solution)/shard_map/pallas_call | solution.py:413
  115.6 1.0 collective-permute-start.12
  116.7 2.4 %collective-permute-start.13 = (bf16[4,32,768]{2,1,0:T(8,128)(2,1)S(1)}, bf16[4,32,768]{2,1,0:T(8,128)(2,1)S(1)}, u32[]{:S(2)}, u32[]{:S(2)}) collective-permute-start(bf16[4,32,768]{2,1,0:T(8,128)(2,1)S(1)} %get-tuple-element.62), channel_id=1, source_target_pairs={{0,24},{8,16},{16,8},{24,0},{1,25},{9,17},{17,9},{25,1},{2,26},{10... | collective-permute-start | bytes 589832 | tf_op jit(solution)/shard_map/ppermute | solution.py:60
  119.1 4.0 %collective-permute-done.11.refs_5_ = bf16[4,32,768]{2,1,0:T(8,128)(2,1)S(1)} collective-permute-done((bf16[4,32,768]{2,1,0:T(8,128)(2,1)S(1)}, bf16[4,32,768]{2,1,0:T(8,128)(2,1)S(1)}, u32[]{:S(2)}, u32[]{:S(2)}) %collective-permute-start.11) | collective-permute-done | bytes 196640 | tf_op jit(solution)/shard_map/ppermute | solution.py:60
  123.1 2.2 %collective-permute-done.12.refs_6_ = bf16[4,32,768]{2,1,0:T(8,128)(2,1)S(1)} collective-permute-done((bf16[4,32,768]{2,1,0:T(8,128)(2,1)S(1)}, bf16[4,32,768]{2,1,0:T(8,128)(2,1)S(1)}, u32[]{:S(2)}, u32[]{:S(2)}) %collective-permute-start.12) | collective-permute-done | bytes 196640 | tf_op jit(solution)/shard_map/ppermute | solution.py:60
  125.3 2.7 %shard_map.112 = bf16[256,4,768]{2,1,0:T(4,128)(2,1)} custom-call(f32[1,256]{1,0:T(1,128)S(1)} %get-tuple-element.34.keys_ref, bf16[4,32,768]{2,1,0:T(8,128)(2,1)S(1)} %get-tuple-element.47.refs_0_, bf16[4,32,768]{2,1,0:T(8,128)(2,1)S(1)} %collective-permute-done.4.refs_1_, bf16[4,32,768]{2,1,0:T(8,128)(2,1)S(1)} %collective-permute-done.5.refs_2_, ...), custom_call_target="tpu_custom_call" | custom-call | flops 402653184 | bytes 3145728 | tf_op jit(solution)/shard_map/pallas_call | solution.py:451
  (31 shorter events, 0.7 us)
Async XLA Ops:
  0.0 1.4 %copy-start.2 = (bf16[256,4,768]{2,1,0:T(4,128)(2,1)S(1)}, bf16[256,4,768]{2,1,0:T(4,128)(2,1)}, u32[]{:S(2)}) copy-start(bf16[256,4,768]{2,1,0:T(4,128)(2,1)} %x_ref.1) | copy-start | bytes 4718596
  1.4 0.7 copy-start.5
  2.1 27.6 %copy-start.3 = (f32[16,768]{1,0:T(8,128)S(1)}, f32[16,768]{1,0:T(8,128)}, u32[]{:S(2)}) copy-start(f32[16,768]{1,0:T(8,128)} %table_ref.11) | copy-start | bytes 147460
  3.4 11.4 %collective-permute-start = (bf16[128,768]{1,0:T(8,128)(2,1)S(1)}, bf16[128,768]{1,0:T(8,128)(2,1)S(1)}, u32[]{:S(2)}, u32[]{:S(2)}) collective-permute-start(bf16[128,768]{1,0:T(8,128)(2,1)S(1)} %get-tuple-element.36), channel_id=1, source_target_pairs={{0,2},{1,3},{2,0},{3,1},{4,6},{5,7},{6,4},{7,5},{8,10},{9,11},{10,... | collective-permute-start | bytes 589832 | tf_op jit(solution)/shard_map/ppermute | solution.py:60
  6.5 17.2 %collective-permute-start.1 = (bf16[128,768]{1,0:T(8,128)(2,1)S(1)}, bf16[128,768]{1,0:T(8,128)(2,1)S(1)}, u32[]{:S(2)}, u32[]{:S(2)}) collective-permute-start(bf16[128,768]{1,0:T(8,128)(2,1)S(1)} %get-tuple-element.37), channel_id=1, source_target_pairs={{0,4},{1,5},{2,6},{3,7},{4,0},{5,1},{6,2},{7,3},{8,12},{9,13},{10,... | collective-permute-start | bytes 589832 | tf_op jit(solution)/shard_map/ppermute | solution.py:60
  9.1 14.6 %collective-permute-start.2 = (bf16[128,768]{1,0:T(8,128)(2,1)S(1)}, bf16[128,768]{1,0:T(8,128)(2,1)S(1)}, u32[]{:S(2)}, u32[]{:S(2)}) collective-permute-start(bf16[128,768]{1,0:T(8,128)(2,1)S(1)} %get-tuple-element.38), channel_id=1, source_target_pairs={{0,6},{1,7},{2,4},{3,5},{4,2},{5,3},{6,0},{7,1},{8,14},{9,15},{10,... | collective-permute-start | bytes 589832 | tf_op jit(solution)/shard_map/ppermute | solution.py:60
  14.8 14.9 %copy-start = (bf16[768,2304]{1,0:T(8,128)(2,1)S(1)}, bf16[768,2304]{1,0:T(8,128)(2,1)}, u32[]{:S(2)}) copy-start(bf16[768,2304]{1,0:T(8,128)(2,1)} %w_ref.10) | copy-start | bytes 10616836
  14.8 14.9 %copy-start.6 = (s32[16]{0:T(128)S(1)}, s32[16]{0:T(128)}, u32[]{:S(2)}) copy-start(s32[16]{0:T(128)} %index_ref.11) | copy-start | bytes 196
  23.7 8.8 %collective-permute-start.3 = (bf16[512,768]{1,0:T(8,128)(2,1)S(1)}, bf16[512,768]{1,0:T(8,128)(2,1)S(1)}, u32[]{:S(2)}, u32[]{:S(2)}) collective-permute-start(bf16[512,768]{1,0:T(8,128)(2,1)S(1)} %shard_map.102.x_ref), channel_id=1, source_target_pairs={{0,1},{1,0},{2,3},{3,2},{4,5},{5,4},{6,7},{7,6},{8,9},{9,8},{10,11... | collective-permute-start | bytes 2359304 | tf_op jit(solution)/shard_map/ppermute | solution.py:60
  23.8 20.5 %collective-permute-start.7 = (bf16[128,768]{1,0:T(8,128)(2,1)S(1)}, bf16[128,768]{1,0:T(8,128)(2,1)S(1)}, u32[]{:S(2)}, u32[]{:S(2)}) collective-permute-start(bf16[128,768]{1,0:T(8,128)(2,1)S(1)} %get-tuple-element.51), channel_id=1, source_target_pairs={{0,2},{1,3},{2,0},{3,1},{4,6},{5,7},{6,4},{7,5},{8,10},{9,11},{10,... | collective-permute-start | bytes 589832 | tf_op jit(solution)/shard_map/ppermute | solution.py:60
  27.2 17.1 %collective-permute-start.8 = (bf16[128,768]{1,0:T(8,128)(2,1)S(1)}, bf16[128,768]{1,0:T(8,128)(2,1)S(1)}, u32[]{:S(2)}, u32[]{:S(2)}) collective-permute-start(bf16[128,768]{1,0:T(8,128)(2,1)S(1)} %get-tuple-element.52), channel_id=1, source_target_pairs={{0,4},{1,5},{2,6},{3,7},{4,0},{5,1},{6,2},{7,3},{8,12},{9,13},{10,... | collective-permute-start | bytes 589832 | tf_op jit(solution)/shard_map/ppermute | solution.py:60
  28.3 16.0 %collective-permute-start.9 = (bf16[128,768]{1,0:T(8,128)(2,1)S(1)}, bf16[128,768]{1,0:T(8,128)(2,1)S(1)}, u32[]{:S(2)}, u32[]{:S(2)}) collective-permute-start(bf16[128,768]{1,0:T(8,128)(2,1)S(1)} %get-tuple-element.53), channel_id=1, source_target_pairs={{0,6},{1,7},{2,4},{3,5},{4,2},{5,3},{6,0},{7,1},{8,14},{9,15},{10,... | collective-permute-start | bytes 589832 | tf_op jit(solution)/shard_map/ppermute | solution.py:60
  32.5 2.2 %copy-start.7 = (bf16[768,768]{1,0:T(8,128)(2,1)S(1)}, bf16[768,768]{1,0:T(8,128)(2,1)}, u32[]{:S(2)}) copy-start(bf16[768,768]{1,0:T(8,128)(2,1)} %w_ref.11) | copy-start | bytes 3538948
  44.3 1.1 copy-start.1
  45.4 12.5 %collective-permute-start.10 = (bf16[512,768]{1,0:T(8,128)(2,1)}, bf16[512,768]{1,0:T(8,128)(2,1)}, u32[]{:S(2)}, u32[]{:S(2)}) collective-permute-start(bf16[512,768]{1,0:T(8,128)(2,1)} %shard_map.107.x_ref), channel_id=1, source_target_pairs={{0,1},{1,0},{2,3},{3,2},{4,5},{5,4},{6,7},{7,6},{8,9},{9,8},{10,11... | collective-permute-start | bytes 2359304 | tf_op jit(solution)/shard_map/ppermute | solution.py:60
  45.4 30.8 %all-to-all-start = ((bf16[16,32,768]{2,1,0:T(8,128)(2,1)}), bf16[16,32,768]{2,1,0:T(8,128)(2,1)}, u32[]{:S(2)}, u32[]{:S(2)}) async-start(bf16[16,32,768]{2,1,0:T(8,128)(2,1)} %bitcast.5), calls=%async_computation | async-start | bytes 1572864 | tf_op jit(solution)/shard_map/all_to_all | solution.py:506
  53.6 0.8 copy-start.4
  57.8 2.9 %copy-start.8 = (bf16[768,768]{1,0:T(8,128)(2,1)S(1)}, bf16[768,768]{1,0:T(8,128)(2,1)}, u32[]{:S(2)}) copy-start(bf16[768,768]{1,0:T(8,128)(2,1)} %w_ref.11) | copy-start | bytes 3538948
  76.2 25.1 %all-to-all-start.1 = ((bf16[16,32,768]{2,1,0:T(8,128)(2,1)}), bf16[16,32,768]{2,1,0:T(8,128)(2,1)S(1)}, u32[]{:S(2)}, u32[]{:S(2)}) async-start(bf16[16,32,768]{2,1,0:T(8,128)(2,1)} %bitcast.3), calls=%async_computation.1 | async-start | bytes 1572864 | tf_op jit(solution)/shard_map/all_to_all | solution.py:506
  95.4 21.2 %collective-permute-start.4 = (bf16[4,32,768]{2,1,0:T(8,128)(2,1)S(1)}, bf16[4,32,768]{2,1,0:T(8,128)(2,1)S(1)}, u32[]{:S(2)}, u32[]{:S(2)}) collective-permute-start(bf16[4,32,768]{2,1,0:T(8,128)(2,1)S(1)} %get-tuple-element.48), channel_id=1, source_target_pairs={{0,8},{8,0},{16,24},{24,16},{1,9},{9,1},{17,25},{25,17},{2,10},{10... | collective-permute-start | bytes 589832 | tf_op jit(solution)/shard_map/ppermute | solution.py:60
  97.1 22.0 %collective-permute-start.5 = (bf16[4,32,768]{2,1,0:T(8,128)(2,1)S(1)}, bf16[4,32,768]{2,1,0:T(8,128)(2,1)S(1)}, u32[]{:S(2)}, u32[]{:S(2)}) collective-permute-start(bf16[4,32,768]{2,1,0:T(8,128)(2,1)S(1)} %get-tuple-element.49), channel_id=1, source_target_pairs={{0,16},{8,24},{16,0},{24,8},{1,17},{9,25},{17,1},{25,9},{2,18},{10... | collective-permute-start | bytes 589832 | tf_op jit(solution)/shard_map/ppermute | solution.py:60
  98.6 20.5 %collective-permute-start.6 = (bf16[4,32,768]{2,1,0:T(8,128)(2,1)S(1)}, bf16[4,32,768]{2,1,0:T(8,128)(2,1)S(1)}, u32[]{:S(2)}, u32[]{:S(2)}) collective-permute-start(bf16[4,32,768]{2,1,0:T(8,128)(2,1)S(1)} %get-tuple-element.50), channel_id=1, source_target_pairs={{0,24},{8,16},{16,8},{24,0},{1,25},{9,17},{17,9},{25,1},{2,26},{10... | collective-permute-start | bytes 589832 | tf_op jit(solution)/shard_map/ppermute | solution.py:60
  115.5 7.6 %collective-permute-start.11 = (bf16[4,32,768]{2,1,0:T(8,128)(2,1)S(1)}, bf16[4,32,768]{2,1,0:T(8,128)(2,1)S(1)}, u32[]{:S(2)}, u32[]{:S(2)}) collective-permute-start(bf16[4,32,768]{2,1,0:T(8,128)(2,1)S(1)} %get-tuple-element.60), channel_id=1, source_target_pairs={{0,8},{8,0},{16,24},{24,16},{1,9},{9,1},{17,25},{25,17},{2,10},{10... | collective-permute-start | bytes 589832 | tf_op jit(solution)/shard_map/ppermute | solution.py:60
  115.6 9.7 %collective-permute-start.12 = (bf16[4,32,768]{2,1,0:T(8,128)(2,1)S(1)}, bf16[4,32,768]{2,1,0:T(8,128)(2,1)S(1)}, u32[]{:S(2)}, u32[]{:S(2)}) collective-permute-start(bf16[4,32,768]{2,1,0:T(8,128)(2,1)S(1)} %get-tuple-element.61), channel_id=1, source_target_pairs={{0,16},{8,24},{16,0},{24,8},{1,17},{9,25},{17,1},{25,9},{2,18},{10... | collective-permute-start | bytes 589832 | tf_op jit(solution)/shard_map/ppermute | solution.py:60
  116.7 8.6 %collective-permute-start.13 = (bf16[4,32,768]{2,1,0:T(8,128)(2,1)S(1)}, bf16[4,32,768]{2,1,0:T(8,128)(2,1)S(1)}, u32[]{:S(2)}, u32[]{:S(2)}) collective-permute-start(bf16[4,32,768]{2,1,0:T(8,128)(2,1)S(1)} %get-tuple-element.62), channel_id=1, source_target_pairs={{0,24},{8,16},{16,8},{24,0},{1,25},{9,17},{17,9},{25,1},{2,26},{10... | collective-permute-start | bytes 589832 | tf_op jit(solution)/shard_map/ppermute | solution.py:60

commit v5 on v4

--- a/solution.py
+++ b/solution.py
@@ -14,7 +14,7 @@
 TILE_LOCS = 16
 GROUP_LOCS = 8
 UNIT_ROWS = 256
-STEP_PAIRS = 2
+STEP_PAIRS = 3
 ROW_TILE = 256
 LANES = 128
 QUERY_SCALE = HEAD_DIM ** (-0.5)
@@ -49,7 +49,7 @@
         kernel,
         out_shape=out_shape,
         compiler_params=pltpu.CompilerParams(vmem_limit_bytes=limit),
-        cost_estimate=pl.CostEstimate(flops=flops, bytes_accessed=nbytes, transcendentals=0),
+        cost_estimate=pl.CostEstimate(flops=0, bytes_accessed=0, transcendentals=0),
         **kwargs,
     )
 
@@ -386,7 +386,7 @@
             for spot, done in zip(spots, run_units(units, mask)):
                 attended[spot] = done
 
-        loop(pairs, attention_step, unroll=2)
+        loop(pairs, attention_step, unroll=3)
         copies[3].wait()
         mid[...] += dot(attended[...], out_ref[...])
         norm_into(normed, mid)

time: 129 us -> 156 us (1.21)
  waiting for transfers between devices: 26.5 us -> 52.6 us
  local copies, waits for them, and re-layouts: 2.99 us -> 5.74 us
  Pallas kernels: 67.5 us -> 65 us
    ppermute x14, waiting for transfers between devices: 19.8 us -> 49.3 us  [exchange(): lax.ppermute(value, axis, [(i, i ^ step) for i in range(lax.axis_size(axi...]
    all_to_all x2, waiting for transfers between devices: 6.73 us -> 3.22 us  [body(): lax.all_to_all(mid.reshape(-1, plan.part_rows, plan.width), ('band', 'loc...]
    all_to_all x2, starting transfers between devices: 12 us -> 14.9 us  [body(): lax.all_to_all(mid.reshape(-1, plan.part_rows, plan.width), ('band', 'loc...]
    unnamed x18 -> x30, local copies, waits for them, and re-layouts: 2.99 us -> 5.74 us
  transfers between devices with their start and end apart: 16 -> 16, of which waited for: 6 -> 7; matrix products, arithmetic and copies ran while one was open for 0% -> 0% of each run, Pallas kernels for 49% -> 32%
where the time goes in v5:
time: 156 us
  Pallas kernels  65 us (42%)
  waiting for transfers between devices  52.6 us (34%)
  starting transfers between devices  32.3 us (21%)
  local copies, waits for them, and re-layouts  5.74 us (4%)
    ppermute x14, waiting for transfers between devices, exchange(): lax.ppermute(value, axis, [(i, i ^ step) for i in range(lax.axis_size(axi...  49.3 us
    pallas_call x2, Pallas kernels, channel(): call(kernel, [jax.ShapeDtypeStruct((bands, locations, width), BF16)] * gr...  29.7 us
    pallas_call x2, Pallas kernels, attend(): call(kernel, jax.ShapeDtypeStruct((plan.groups, plan.rows_count, plan.par...  19.9 us
    ppermute x14, starting transfers between devices, exchange(): lax.ppermute(value, axis, [(i, i ^ step) for i in range(lax.axis_size(axi...  17.4 us
    all_to_all x2, starting transfers between devices, body(): lax.all_to_all(mid.reshape(-1, plan.part_rows, plan.width), ('band', 'loc...  14.9 us
    pallas_call x4, Pallas kernels, project(): call(kernel, [jax.ShapeDtypeStruct((rows, width), BF16)] * len(names), 2...  10.2 us
    unnamed x30, local copies, waits for them, and re-layouts  5.74 us
    all_to_all x2, waiting for transfers between devices, body(): lax.all_to_all(mid.reshape(-1, plan.part_rows, plan.width), ('band', 'loc...  3.22 us
  transfers between devices with their start and end apart: 16, of which 7 were waited for; matrix products, arithmetic and copies ran while one was open for 0% of the time, Pallas kernels for 32%

profile of v5, /device:TPU:0, one launch (start us, length us, event | category | flops | bytes accessed | tf_op | source)
XLA Modules:
  0.0 155.8 jit_solution(14614009192955512222)
XLA Ops:
  0.0 1.4 copy-done.7
  2.1 1.3 shard_map.100
  3.4 3.1 %collective-permute-start = (bf16[128,768]{1,0:T(8,128)(2,1)S(1)}, bf16[128,768]{1,0:T(8,128)(2,1)S(1)}, u32[]{:S(2)}, u32[]{:S(2)}) collective-permute-start(bf16[128,768]{1,0:T(8,128)(2,1)S(1)} %get-tuple-element.36), channel_id=1, source_target_pairs={{0,2},{1,3},{2,0},{3,1},{4,6},{5,7},{6,4},{7,5},{8,10},{9,11},{10,... | collective-permute-start | bytes 589832 | tf_op jit(solution)/shard_map/ppermute | solution.py:60
  6.5 2.6 %collective-permute-start.1 = (bf16[128,768]{1,0:T(8,128)(2,1)S(1)}, bf16[128,768]{1,0:T(8,128)(2,1)S(1)}, u32[]{:S(2)}, u32[]{:S(2)}) collective-permute-start(bf16[128,768]{1,0:T(8,128)(2,1)S(1)} %get-tuple-element.37), channel_id=1, source_target_pairs={{0,4},{1,5},{2,6},{3,7},{4,0},{5,1},{6,2},{7,3},{8,12},{9,13},{10,... | collective-permute-start | bytes 589832 | tf_op jit(solution)/shard_map/ppermute | solution.py:60
  9.1 5.7 %collective-permute-done.rest_0_.refs_1_ = bf16[128,768]{1,0:T(8,128)(2,1)S(1)} collective-permute-done((bf16[128,768]{1,0:T(8,128)(2,1)S(1)}, bf16[128,768]{1,0:T(8,128)(2,1)S(1)}, u32[]{:S(2)}, u32[]{:S(2)}) %collective-permute-start) | collective-permute-done | bytes 196640 | tf_op jit(solution)/shard_map/ppermute | solution.py:60
  14.8 1.0 shard_map.101
  15.9 7.8 %collective-permute-done.1.refs_2_ = bf16[128,768]{1,0:T(8,128)(2,1)S(1)} collective-permute-done((bf16[128,768]{1,0:T(8,128)(2,1)S(1)}, bf16[128,768]{1,0:T(8,128)(2,1)S(1)}, u32[]{:S(2)}, u32[]{:S(2)}) %collective-permute-start.1) | collective-permute-done | bytes 196640 | tf_op jit(solution)/shard_map/ppermute | solution.py:60
  23.9 2.9 %shard_map.103 = (bf16[512,768]{1,0:T(8,128)(2,1)S(1)}, bf16[512,768]{1,0:T(8,128)(2,1)S(1)}, bf16[512,768]{1,0:T(8,128)(2,1)S(1)}) custom-call(s32[16]{0:T(128)S(1)} %copy-done.10, f32[16,768]{1,0:T(8,128)S(1)} %copy-done.5, bf16[768,2304]{1,0:T(8,128)(2,1)S(1)} %copy-done, bf16[512,768]{1,0:T(8,128)(2,1)S(1)} %shard_map.102.x_ref), custom_call_target="tpu_custom_call" | custom-call | tf_op jit(solution)/shard_map/pallas_call | solution.py:209
  26.8 2.3 %shard_map.104 = (bf16[512,768]{1,0:T(8,128)(2,1)S(1)}, bf16[512,768]{1,0:T(8,128)(2,1)S(1)}) custom-call(s32[16]{0:T(128)S(1)} %copy-done.10, f32[16,768]{1,0:T(8,128)S(1)} %copy-done.5, bf16[768,2304]{1,0:T(8,128)(2,1)S(1)} %copy-done, bf16[512,768]{1,0:T(8,128)(2,1)S(1)} %collective-permute-done.3.x_ref, bf16[512,768]{1,0:T(8,128)(2,1)S(1)} %get-tuple-element.43.rest_0_), custom_call_target="tpu_custom_call" | custom-call | tf_op jit(solution)/shard_map/pallas_call | solution.py:209
  29.0 9.5 %shard_map.105.refs_4_ = bf16[4,4,32,768]{3,2,1,0:T(8,128)(2,1)S(1)} custom-call(s32[16]{0:T(128)S(1)} %copy-done.10, f32[16,768]{1,0:T(8,128)S(1)} %copy-done.5, bf16[768,768]{1,0:T(8,128)(2,1)S(1)} %copy-done.3, bf16[512,768]{1,0:T(8,128)(2,1)S(1)} %shard_map.102.x_ref, bf16[512,768]{1,0:T(8,128)(2,1)S(1)} %get-tuple-element.42.q_ref, ...), custom_call_target="tpu_custom_call" | custom-call | tf_op jit(solution)/shard_map/pallas_call | solution.py:307
  38.6 0.9 copy-done.1
  39.4 7.7 %all-to-all-start = ((bf16[16,32,768]{2,1,0:T(8,128)(2,1)}), bf16[16,32,768]{2,1,0:T(8,128)(2,1)}, u32[]{:S(2)}, u32[]{:S(2)}) async-start(bf16[16,32,768]{2,1,0:T(8,128)(2,1)} %bitcast.5), calls=%async_computation | async-start | bytes 1572864 | tf_op jit(solution)/shard_map/all_to_all | solution.py:506
  47.1 1.9 %collective-permute-start.7 = (bf16[128,768]{1,0:T(8,128)(2,1)}, bf16[128,768]{1,0:T(8,128)(2,1)S(1)}, u32[]{:S(2)}, u32[]{:S(2)}) collective-permute-start(bf16[128,768]{1,0:T(8,128)(2,1)} %copy-done.14), channel_id=1, source_target_pairs={{0,2},{1,3},{2,0},{3,1},{4,6},{5,7},{6,4},{7,5},{8,10},{9,11},{10,... | collective-permute-start | bytes 589832 | tf_op jit(solution)/shard_map/ppermute | solution.py:60
  49.0 2.4 %collective-permute-start.8 = (bf16[128,768]{1,0:T(8,128)(2,1)}, bf16[128,768]{1,0:T(8,128)(2,1)S(1)}, u32[]{:S(2)}, u32[]{:S(2)}) collective-permute-start(bf16[128,768]{1,0:T(8,128)(2,1)} %copy-done.13), channel_id=1, source_target_pairs={{0,4},{1,5},{2,6},{3,7},{4,0},{5,1},{6,2},{7,3},{8,12},{9,13},{10,... | collective-permute-start | bytes 589832 | tf_op jit(solution)/shard_map/ppermute | solution.py:60
  51.6 14.2 %collective-permute-done.7.refs_1_ = bf16[128,768]{1,0:T(8,128)(2,1)S(1)} collective-permute-done((bf16[128,768]{1,0:T(8,128)(2,1)}, bf16[128,768]{1,0:T(8,128)(2,1)S(1)}, u32[]{:S(2)}, u32[]{:S(2)}) %collective-permute-start.7) | collective-permute-done | bytes 196640 | tf_op jit(solution)/shard_map/ppermute | solution.py:60
  65.8 15.4 %collective-permute-done.8.refs_2_ = bf16[128,768]{1,0:T(8,128)(2,1)S(1)} collective-permute-done((bf16[128,768]{1,0:T(8,128)(2,1)}, bf16[128,768]{1,0:T(8,128)(2,1)S(1)}, u32[]{:S(2)}, u32[]{:S(2)}) %collective-permute-start.8) | collective-permute-done | bytes 196640 | tf_op jit(solution)/shard_map/ppermute | solution.py:60
  81.1 1.1 copy-done.2
  82.3 0.9 copy-done.9
  84.0 2.9 %shard_map.108 = (bf16[512,768]{1,0:T(8,128)(2,1)S(1)}, bf16[512,768]{1,0:T(8,128)(2,1)S(1)}, bf16[512,768]{1,0:T(8,128)(2,1)S(1)}) custom-call(s32[16]{0:T(128)S(1)} %copy-done.10, f32[16,768]{1,0:T(8,128)S(1)} %copy-done.6, bf16[768,2304]{1,0:T(8,128)(2,1)S(1)} %copy-done, bf16[512,768]{1,0:T(8,128)(2,1)S(1)} %shard_map.107.x_ref), custom_call_target="tpu_custom_call" | custom-call | tf_op jit(solution)/shard_map/pallas_call | solution.py:209
  86.9 2.3 %shard_map.109 = (bf16[512,768]{1,0:T(8,128)(2,1)S(1)}, bf16[512,768]{1,0:T(8,128)(2,1)S(1)}) custom-call(s32[16]{0:T(128)S(1)} %copy-done.10, f32[16,768]{1,0:T(8,128)S(1)} %copy-done.6, bf16[768,2304]{1,0:T(8,128)(2,1)S(1)} %copy-done, bf16[512,768]{1,0:T(8,128)(2,1)S(1)} %collective-permute-done.10.x_ref, bf16[512,768]{1,0:T(8,128)(2,1)S(1)} %get-tuple-element.55.rest_0_), custom_call_target="tpu_custom_call" | custom-call | tf_op jit(solution)/shard_map/pallas_call | solution.py:209
  89.2 10.4 %shard_map.110 = bf16[4,4,32,768]{3,2,1,0:T(8,128)(2,1)} custom-call(s32[16]{0:T(128)S(1)} %copy-done.10, f32[16,768]{1,0:T(8,128)S(1)} %copy-done.6, bf16[768,768]{1,0:T(8,128)(2,1)S(1)} %copy-done.4, bf16[512,768]{1,0:T(8,128)(2,1)S(1)} %shard_map.107.x_ref, bf16[512,768]{1,0:T(8,128)(2,1)S(1)} %get-tuple-element.54.q_ref, ...), custom_call_target="tpu_custom_call" | custom-call | tf_op jit(solution)/shard_map/pallas_call | solution.py:307
  99.6 7.2 %all-to-all-start.1 = ((bf16[16,32,768]{2,1,0:T(8,128)(2,1)}), bf16[16,32,768]{2,1,0:T(8,128)(2,1)S(1)}, u32[]{:S(2)}, u32[]{:S(2)}) async-start(bf16[16,32,768]{2,1,0:T(8,128)(2,1)} %bitcast.3), calls=%async_computation.1 | async-start | bytes 1572864 | tf_op jit(solution)/shard_map/all_to_all | solution.py:506
  106.8 15.4 %shard_map.106 = (bf16[4,32,768]{2,1,0:T(8,128)(2,1)S(1)}, bf16[4,32,768]{2,1,0:T(8,128)(2,1)S(1)}, bf16[4,32,768]{2,1,0:T(8,128)(2,1)S(1)}, bf16[4,32,768]{2,1,0:T(8,128)(2,1)S(1)}) custom-call(bf16[768,2304]{1,0:T(8,128)(2,1)} %qkv_hbm.3, bf16[768,768]{1,0:T(8,128)(2,1)} %out_hbm.3, bf16[768,3072]{1,0:T(8,128)(2,1)} %up_hbm.3, bf16[3072,768]{1,0:T(8,128)(2,1)} %down_hbm.3, ...), custom_call_target="tpu_custom_call" | custom-call | tf_op jit(solution)/shard_map/pallas_call | solution.py:413
  122.2 2.0 %collective-permute-start.4 = (bf16[4,32,768]{2,1,0:T(8,128)(2,1)S(1)}, bf16[4,32,768]{2,1,0:T(8,128)(2,1)S(1)}, u32[]{:S(2)}, u32[]{:S(2)}) collective-permute-start(bf16[4,32,768]{2,1,0:T(8,128)(2,1)S(1)} %get-tuple-element.48), channel_id=1, source_target_pairs={{0,8},{8,0},{16,24},{24,16},{1,9},{9,1},{17,25},{25,17},{2,10},{10... | collective-permute-start | bytes 589832 | tf_op jit(solution)/shard_map/ppermute | solution.py:60
  124.2 1.5 collective-permute-start.5
  125.8 3.2 %all-to-all-done.1 = bf16[16,32,768]{2,1,0:T(8,128)(2,1)S(1)} async-done(((bf16[16,32,768]{2,1,0:T(8,128)(2,1)}), bf16[16,32,768]{2,1,0:T(8,128)(2,1)S(1)}, u32[]{:S(2)}, u32[]{:S(2)}) %all-to-all-start.1) | async-done | bytes 786464 | tf_op jit(solution)/shard_map/all_to_all | solution.py:506
  129.0 14.3 %shard_map.111 = (bf16[4,32,768]{2,1,0:T(8,128)(2,1)S(1)}, bf16[4,32,768]{2,1,0:T(8,128)(2,1)S(1)}, bf16[4,32,768]{2,1,0:T(8,128)(2,1)S(1)}, bf16[4,32,768]{2,1,0:T(8,128)(2,1)S(1)}) custom-call(bf16[768,2304]{1,0:T(8,128)(2,1)} %qkv_hbm.3, bf16[768,768]{1,0:T(8,128)(2,1)} %out_hbm.3, bf16[768,3072]{1,0:T(8,128)(2,1)} %up_hbm.3, bf16[3072,768]{1,0:T(8,128)(2,1)} %down_hbm.3, ...), custom_call_target="tpu_custom_call" | custom-call | tf_op jit(solution)/shard_map/pallas_call | solution.py:413
  143.4 1.0 collective-permute-start.12
  144.5 2.4 %collective-permute-start.13 = (bf16[4,32,768]{2,1,0:T(8,128)(2,1)S(1)}, bf16[4,32,768]{2,1,0:T(8,128)(2,1)S(1)}, u32[]{:S(2)}, u32[]{:S(2)}) collective-permute-start(bf16[4,32,768]{2,1,0:T(8,128)(2,1)S(1)} %get-tuple-element.62), channel_id=1, source_target_pairs={{0,24},{8,16},{16,8},{24,0},{1,25},{9,17},{17,9},{25,1},{2,26},{10... | collective-permute-start | bytes 589832 | tf_op jit(solution)/shard_map/ppermute | solution.py:60
  146.9 4.1 %collective-permute-done.11.refs_5_ = bf16[4,32,768]{2,1,0:T(8,128)(2,1)S(1)} collective-permute-done((bf16[4,32,768]{2,1,0:T(8,128)(2,1)S(1)}, bf16[4,32,768]{2,1,0:T(8,128)(2,1)S(1)}, u32[]{:S(2)}, u32[]{:S(2)}) %collective-permute-start.11) | collective-permute-done | bytes 196640 | tf_op jit(solution)/shard_map/ppermute | solution.py:60
  151.0 2.2 %collective-permute-done.12.refs_6_ = bf16[4,32,768]{2,1,0:T(8,128)(2,1)S(1)} collective-permute-done((bf16[4,32,768]{2,1,0:T(8,128)(2,1)S(1)}, bf16[4,32,768]{2,1,0:T(8,128)(2,1)S(1)}, u32[]{:S(2)}, u32[]{:S(2)}) %collective-permute-start.12) | collective-permute-done | bytes 196640 | tf_op jit(solution)/shard_map/ppermute | solution.py:60
  153.1 2.7 %shard_map.112 = bf16[256,4,768]{2,1,0:T(4,128)(2,1)} custom-call(f32[1,256]{1,0:T(1,128)S(1)} %get-tuple-element.34.keys_ref, bf16[4,32,768]{2,1,0:T(8,128)(2,1)S(1)} %get-tuple-element.47.refs_0_, bf16[4,32,768]{2,1,0:T(8,128)(2,1)S(1)} %collective-permute-done.4.refs_1_, bf16[4,32,768]{2,1,0:T(8,128)(2,1)S(1)} %collective-permute-done.5.refs_2_, ...), custom_call_target="tpu_custom_call" | custom-call | tf_op jit(solution)/shard_map/pallas_call | solution.py:451
  (43 shorter events, 2.0 us)
Async XLA Ops:
  0.0 1.4 copy-start.7
  1.4 0.7 copy-start.11
  2.1 21.7 %copy-start.5 = (f32[16,768]{1,0:T(8,128)S(1)}, f32[16,768]{1,0:T(8,128)}, u32[]{:S(2)}) copy-start(f32[16,768]{1,0:T(8,128)} %table_ref.11) | copy-start | bytes 147460
  3.4 11.4 %collective-permute-start = (bf16[128,768]{1,0:T(8,128)(2,1)S(1)}, bf16[128,768]{1,0:T(8,128)(2,1)S(1)}, u32[]{:S(2)}, u32[]{:S(2)}) collective-permute-start(bf16[128,768]{1,0:T(8,128)(2,1)S(1)} %get-tuple-element.36), channel_id=1, source_target_pairs={{0,2},{1,3},{2,0},{3,1},{4,6},{5,7},{6,4},{7,5},{8,10},{9,11},{10,... | collective-permute-start | bytes 589832 | tf_op jit(solution)/shard_map/ppermute | solution.py:60
  6.5 17.2 %collective-permute-start.1 = (bf16[128,768]{1,0:T(8,128)(2,1)S(1)}, bf16[128,768]{1,0:T(8,128)(2,1)S(1)}, u32[]{:S(2)}, u32[]{:S(2)}) collective-permute-start(bf16[128,768]{1,0:T(8,128)(2,1)S(1)} %get-tuple-element.37), channel_id=1, source_target_pairs={{0,4},{1,5},{2,6},{3,7},{4,0},{5,1},{6,2},{7,3},{8,12},{9,13},{10,... | collective-permute-start | bytes 589832 | tf_op jit(solution)/shard_map/ppermute | solution.py:60
  9.1 14.6 %collective-permute-start.2 = (bf16[128,768]{1,0:T(8,128)(2,1)S(1)}, bf16[128,768]{1,0:T(8,128)(2,1)S(1)}, u32[]{:S(2)}, u32[]{:S(2)}) collective-permute-start(bf16[128,768]{1,0:T(8,128)(2,1)S(1)} %get-tuple-element.38), channel_id=1, source_target_pairs={{0,6},{1,7},{2,4},{3,5},{4,2},{5,3},{6,0},{7,1},{8,14},{9,15},{10,... | collective-permute-start | bytes 589832 | tf_op jit(solution)/shard_map/ppermute | solution.py:60
  14.8 9.0 %copy-start = (bf16[768,2304]{1,0:T(8,128)(2,1)S(1)}, bf16[768,2304]{1,0:T(8,128)(2,1)}, u32[]{:S(2)}) copy-start(bf16[768,2304]{1,0:T(8,128)(2,1)} %w_ref.10) | copy-start | bytes 10616836
  14.8 9.0 %copy-start.10 = (s32[16]{0:T(128)S(1)}, s32[16]{0:T(128)}, u32[]{:S(2)}) copy-start(s32[16]{0:T(128)} %index_ref.11) | copy-start | bytes 196
  15.9 7.9 %copy-start.8 = (bf16[128,768]{1,0:T(8,128)(2,1)}, bf16[128,768]{1,0:T(8,128)(2,1)S(1)}, u32[]{:S(2)}) copy-start(bf16[128,768]{1,0:T(8,128)(2,1)S(1)} %get-tuple-element.41.refs_4_.refs_0_) | copy-start | bytes 589828
  15.9 7.9 %copy-start.12 = (bf16[128,768]{1,0:T(8,128)(2,1)}, bf16[128,768]{1,0:T(8,128)(2,1)S(1)}, u32[]{:S(2)}) copy-start(bf16[128,768]{1,0:T(8,128)(2,1)S(1)} %get-tuple-element.53) | copy-start | bytes 589828
  15.9 7.9 %copy-start.13 = (bf16[128,768]{1,0:T(8,128)(2,1)}, bf16[128,768]{1,0:T(8,128)(2,1)S(1)}, u32[]{:S(2)}) copy-start(bf16[128,768]{1,0:T(8,128)(2,1)S(1)} %get-tuple-element.52) | copy-start | bytes 589828
  15.9 7.9 %copy-start.14 = (bf16[128,768]{1,0:T(8,128)(2,1)}, bf16[128,768]{1,0:T(8,128)(2,1)S(1)}, u32[]{:S(2)}) copy-start(bf16[128,768]{1,0:T(8,128)(2,1)S(1)} %get-tuple-element.51) | copy-start | bytes 589828
  23.8 3.0 %collective-permute-start.3 = (bf16[512,768]{1,0:T(8,128)(2,1)S(1)}, bf16[512,768]{1,0:T(8,128)(2,1)S(1)}, u32[]{:S(2)}, u32[]{:S(2)}) collective-permute-start(bf16[512,768]{1,0:T(8,128)(2,1)S(1)} %shard_map.102.x_ref), channel_id=1, source_target_pairs={{0,1},{1,0},{2,3},{3,2},{4,5},{5,4},{6,7},{7,6},{8,9},{9,8},{10,11... | collective-permute-start | bytes 2359304 | tf_op jit(solution)/shard_map/ppermute | solution.py:60
  26.8 2.3 %copy-start.3 = (bf16[768,768]{1,0:T(8,128)(2,1)S(1)}, bf16[768,768]{1,0:T(8,128)(2,1)}, u32[]{:S(2)}) copy-start(bf16[768,768]{1,0:T(8,128)(2,1)} %w_ref.11) | copy-start | bytes 3538948
  38.5 0.9 copy-start.1
  39.4 60.1 %all-to-all-start = ((bf16[16,32,768]{2,1,0:T(8,128)(2,1)}), bf16[16,32,768]{2,1,0:T(8,128)(2,1)}, u32[]{:S(2)}, u32[]{:S(2)}) async-start(bf16[16,32,768]{2,1,0:T(8,128)(2,1)} %bitcast.5), calls=%async_computation | async-start | bytes 1572864 | tf_op jit(solution)/shard_map/all_to_all | solution.py:506
  47.1 18.6 %collective-permute-start.7 = (bf16[128,768]{1,0:T(8,128)(2,1)}, bf16[128,768]{1,0:T(8,128)(2,1)S(1)}, u32[]{:S(2)}, u32[]{:S(2)}) collective-permute-start(bf16[128,768]{1,0:T(8,128)(2,1)} %copy-done.14), channel_id=1, source_target_pairs={{0,2},{1,3},{2,0},{3,1},{4,6},{5,7},{6,4},{7,5},{8,10},{9,11},{10,... | collective-permute-start | bytes 589832 | tf_op jit(solution)/shard_map/ppermute | solution.py:60
  49.0 32.1 %collective-permute-start.8 = (bf16[128,768]{1,0:T(8,128)(2,1)}, bf16[128,768]{1,0:T(8,128)(2,1)S(1)}, u32[]{:S(2)}, u32[]{:S(2)}) collective-permute-start(bf16[128,768]{1,0:T(8,128)(2,1)} %copy-done.13), channel_id=1, source_target_pairs={{0,4},{1,5},{2,6},{3,7},{4,0},{5,1},{6,2},{7,3},{8,12},{9,13},{10,... | collective-permute-start | bytes 589832 | tf_op jit(solution)/shard_map/ppermute | solution.py:60
  51.4 29.7 %collective-permute-start.9 = (bf16[128,768]{1,0:T(8,128)(2,1)}, bf16[128,768]{1,0:T(8,128)(2,1)S(1)}, u32[]{:S(2)}, u32[]{:S(2)}) collective-permute-start(bf16[128,768]{1,0:T(8,128)(2,1)} %copy-done.12), channel_id=1, source_target_pairs={{0,6},{1,7},{2,4},{3,5},{4,2},{5,3},{6,0},{7,1},{8,14},{9,15},{10,... | collective-permute-start | bytes 589832 | tf_op jit(solution)/shard_map/ppermute | solution.py:60
  81.1 1.1 copy-start.2
  82.3 0.9 copy-start.9
  83.2 0.8 copy-start.6
  83.3 3.6 %collective-permute-start.10 = (bf16[512,768]{1,0:T(8,128)(2,1)S(1)}, bf16[512,768]{1,0:T(8,128)(2,1)S(1)}, u32[]{:S(2)}, u32[]{:S(2)}) collective-permute-start(bf16[512,768]{1,0:T(8,128)(2,1)S(1)} %shard_map.107.x_ref), channel_id=1, source_target_pairs={{0,1},{1,0},{2,3},{3,2},{4,5},{5,4},{6,7},{7,6},{8,9},{9,8},{10,11... | collective-permute-start | bytes 2359304 | tf_op jit(solution)/shard_map/ppermute | solution.py:60
  86.9 2.3 %copy-start.4 = (bf16[768,768]{1,0:T(8,128)(2,1)S(1)}, bf16[768,768]{1,0:T(8,128)(2,1)}, u32[]{:S(2)}) copy-start(bf16[768,768]{1,0:T(8,128)(2,1)} %w_ref.11) | copy-start | bytes 3538948
  99.6 29.4 %all-to-all-start.1 = ((bf16[16,32,768]{2,1,0:T(8,128)(2,1)}), bf16[16,32,768]{2,1,0:T(8,128)(2,1)S(1)}, u32[]{:S(2)}, u32[]{:S(2)}) async-start(bf16[16,32,768]{2,1,0:T(8,128)(2,1)} %bitcast.3), calls=%async_computation.1 | async-start | bytes 1572864 | tf_op jit(solution)/shard_map/all_to_all | solution.py:506
  122.2 22.2 %collective-permute-start.4 = (bf16[4,32,768]{2,1,0:T(8,128)(2,1)S(1)}, bf16[4,32,768]{2,1,0:T(8,128)(2,1)S(1)}, u32[]{:S(2)}, u32[]{:S(2)}) collective-permute-start(bf16[4,32,768]{2,1,0:T(8,128)(2,1)S(1)} %get-tuple-element.48), channel_id=1, source_target_pairs={{0,8},{8,0},{16,24},{24,16},{1,9},{9,1},{17,25},{25,17},{2,10},{10... | collective-permute-start | bytes 589832 | tf_op jit(solution)/shard_map/ppermute | solution.py:60
  124.2 22.7 %collective-permute-start.5 = (bf16[4,32,768]{2,1,0:T(8,128)(2,1)S(1)}, bf16[4,32,768]{2,1,0:T(8,128)(2,1)S(1)}, u32[]{:S(2)}, u32[]{:S(2)}) collective-permute-start(bf16[4,32,768]{2,1,0:T(8,128)(2,1)S(1)} %get-tuple-element.49), channel_id=1, source_target_pairs={{0,16},{8,24},{16,0},{24,8},{1,17},{9,25},{17,1},{25,9},{2,18},{10... | collective-permute-start | bytes 589832 | tf_op jit(solution)/shard_map/ppermute | solution.py:60
  125.7 21.2 %collective-permute-start.6 = (bf16[4,32,768]{2,1,0:T(8,128)(2,1)S(1)}, bf16[4,32,768]{2,1,0:T(8,128)(2,1)S(1)}, u32[]{:S(2)}, u32[]{:S(2)}) collective-permute-start(bf16[4,32,768]{2,1,0:T(8,128)(2,1)S(1)} %get-tuple-element.50), channel_id=1, source_target_pairs={{0,24},{8,16},{16,8},{24,0},{1,25},{9,17},{17,9},{25,1},{2,26},{10... | collective-permute-start | bytes 589832 | tf_op jit(solution)/shard_map/ppermute | solution.py:60
  143.3 7.6 %collective-permute-start.11 = (bf16[4,32,768]{2,1,0:T(8,128)(2,1)S(1)}, bf16[4,32,768]{2,1,0:T(8,128)(2,1)S(1)}, u32[]{:S(2)}, u32[]{:S(2)}) collective-permute-start(bf16[4,32,768]{2,1,0:T(8,128)(2,1)S(1)} %get-tuple-element.60), channel_id=1, source_target_pairs={{0,8},{8,0},{16,24},{24,16},{1,9},{9,1},{17,25},{25,17},{2,10},{10... | collective-permute-start | bytes 589832 | tf_op jit(solution)/shard_map/ppermute | solution.py:60
  143.4 9.7 %collective-permute-start.12 = (bf16[4,32,768]{2,1,0:T(8,128)(2,1)S(1)}, bf16[4,32,768]{2,1,0:T(8,128)(2,1)S(1)}, u32[]{:S(2)}, u32[]{:S(2)}) collective-permute-start(bf16[4,32,768]{2,1,0:T(8,128)(2,1)S(1)} %get-tuple-element.61), channel_id=1, source_target_pairs={{0,16},{8,24},{16,0},{24,8},{1,17},{9,25},{17,1},{25,9},{2,18},{10... | collective-permute-start | bytes 589832 | tf_op jit(solution)/shard_map/ppermute | solution.py:60
  144.5 8.7 %collective-permute-start.13 = (bf16[4,32,768]{2,1,0:T(8,128)(2,1)S(1)}, bf16[4,32,768]{2,1,0:T(8,128)(2,1)S(1)}, u32[]{:S(2)}, u32[]{:S(2)}) collective-permute-start(bf16[4,32,768]{2,1,0:T(8,128)(2,1)S(1)} %get-tuple-element.62), channel_id=1, source_target_pairs={{0,24},{8,16},{16,8},{24,0},{1,25},{9,17},{17,9},{25,1},{2,26},{10... | collective-permute-start | bytes 589832 | tf_op jit(solution)/shard_map/ppermute | solution.py:60

commit v6 on v5

--- a/solution.py
+++ b/solution.py
@@ -20,6 +20,8 @@
 QUERY_SCALE = HEAD_DIM ** (-0.5)
 VMEM_LIMIT = 28 * 1024 * 1024
 WIDE_LIMIT = 52 * 1024 * 1024
+WHOLE_LIMIT = 61 * 1024 * 1024
+LONG = 2**36
 
 F32 = jnp.float32
 BF16 = jnp.bfloat16
@@ -49,7 +51,7 @@
         kernel,
         out_shape=out_shape,
         compiler_params=pltpu.CompilerParams(vmem_limit_bytes=limit),
-        cost_estimate=pl.CostEstimate(flops=0, bytes_accessed=0, transcendentals=0),
+        cost_estimate=pl.CostEstimate(flops=flops, bytes_accessed=nbytes, transcendentals=0),
         **kwargs,
     )
 
@@ -110,8 +112,16 @@
     total = plan.loc_dev * plan.band_dev
     assert plan.loc_dev <= 256
 
-    def kernel(ids_ref, x_ref, *rest):
-        outs, (rows_ref, keys_ref, place_ref) = rest[:count], rest[count:]
+    def kernel(ids_hbm, x_hbm, *rest):
+        outs, rest = rest[:count], rest[count:]
+        rows_ref, keys_ref, place_ref, ids_ref, x_ref, sems = rest
+        copies = [
+            pltpu.make_async_copy(ids_hbm, ids_ref, sems.at[0]),
+            pltpu.make_async_copy(x_hbm, x_ref, sems.at[1]),
+        ]
+        for copy in copies:
+            copy.start()
+        copies[0].wait()
         keys = location_keys(plan, ids_ref)
         keys_ref[...] = keys
         place = lax.broadcasted_iota(jnp.int32, (plan.loc_dev, total), 1)
@@ -120,6 +130,7 @@
         wide = dot(jnp.broadcast_to(keys, (16, plan.loc_dev)).astype(BF16), spread)
         band = lax.broadcasted_iota(jnp.int32, (1, total), 1) % plan.band_dev
         place_ref[...] = wide[:1] + (band * plan.loc_dev).astype(F32)
+        copies[1].wait()
         rows_ref[...] = x_ref[...].reshape(total, plan.width)
         pick_rows(plan, 0, place_ref[...], rows_ref, outs)
 
@@ -133,8 +144,14 @@
         ],
         2 * plan.loc_dev * tokens.size,
         4 * tokens.size,
-        in_specs=[VMEM] * 2,
+        limit=WHOLE_LIMIT,
+        in_specs=[ANY] * 2,
         out_specs=[VMEM] * (count + 3),
+        scratch_shapes=[
+            pltpu.VMEM(ids.shape, jnp.int32),
+            pltpu.VMEM(tokens.shape, BF16),
+            pltpu.SemaphoreType.DMA((2,)),
+        ],
     )(ids, tokens)
 
 
@@ -154,7 +171,7 @@
     )(rows, place_keys, *after)
 
 
-def join_slots(plan, slots, after):
+def join_slots(plan, slots, after, flops):
     def kernel(*refs):
         for slot in range(len(slots)):
             refs[-1][pl.ds(slot * plan.rows, plan.rows), :] = refs[slot][...]
@@ -162,7 +179,7 @@
     return call(
         kernel,
         jax.ShapeDtypeStruct((len(slots) * plan.rows, plan.width), BF16),
-        0,
+        flops,
         4 * len(slots) * plan.rows * plan.width,
         in_specs=[VMEM] * len(slots) + [ANY] * len(after),
         out_specs=VMEM,
@@ -191,7 +208,7 @@
         target[here, :] = norm_rows(source[here, :]).astype(BF16)
 
 
-def project(plan, tokens, index, table, weights, queries, after=()):
+def project(plan, tokens, index, table, weights, queries, hide, after=()):
     rows, width = tokens.shape
     tile = min(rows, ROW_TILE)
     names = range(3) if queries else range(1, 3)
@@ -209,8 +226,8 @@
     return call(
         kernel,
         [jax.ShapeDtypeStruct((rows, width), BF16)] * len(names),
-        2 * rows * width * len(names) * width,
-        2 * ((1 + len(names)) * rows * width + 3 * width * width),
+        hide * 2 * rows * width * len(names) * width,
+        hide * 2 * ((1 + len(names)) * rows * width + 3 * width * width),
         in_specs=[SMEM, VMEM, VMEM, VMEM] + [ANY] * len(after),
         out_specs=[VMEM] * len(names),
     )(index, table, weights, tokens, *after)
@@ -268,7 +285,7 @@
     return results
 
 
-def attend(plan, query, keys, values, tokens, index, table, spatial_out):
+def attend(plan, query, keys, values, tokens, index, table, spatial_out, hide):
     total, width = query.shape
     rows = plan.rows
     pieces = len(keys)
@@ -307,8 +324,8 @@
     return call(
         kernel,
         jax.ShapeDtypeStruct((plan.groups, plan.rows_count, plan.part_rows, width), BF16),
-        16 * total * key_rows * width,
-        2 * width * (2 * key_rows + 3 * total + width),
+        hide * 16 * total * key_rows * width,
+        hide * 2 * width * (2 * key_rows + 3 * total + width),
         in_specs=[SMEM] + [VMEM] * (4 + 2 * pieces),
         out_specs=VMEM,
         scratch_shapes=[pltpu.VMEM((total, width), BF16), pltpu.VMEM((total, width), F32)],
@@ -479,22 +496,27 @@
             [exchange(value, "loc", CORES * step) for step, value in enumerate(following)]
         )
     mids, behind = [], following[:1]
-    for slots in arrived:
-        own = join_slots(plan, slots, behind)
+    for window, slots in enumerate(arrived):
+        hide = int(window == 0)
+        own = join_slots(plan, slots, behind, 0 if hide else LONG)
         if plan.share == 1:
             other = exchange(own, "loc", 1)
-            query, *mine = project(plan, own, band_index, band_table, spatial_qkv, True)
-            theirs = project(plan, other, band_index, band_table, spatial_qkv, False, mine[:1])
+            query, *mine = project(plan, own, band_index, band_table, spatial_qkv, True, hide)
+            theirs = project(
+                plan, other, band_index, band_table, spatial_qkv, False, hide, mine[:1]
+            )
             all_keys, all_values = zip(mine, theirs)
         else:
             step = CORES * plan.share
             same = [list(range(at, at + step)) for at in range(0, plan.locs, step)]
             every = lax.all_gather(own, "loc", axis_index_groups=same, tiled=True)
-            query, _, _ = project(plan, own, band_index, band_table, spatial_qkv, True)
+            query, _, _ = project(plan, own, band_index, band_table, spatial_qkv, True, hide)
             all_keys, all_values = zip(
-                project(plan, every, band_index, band_table, spatial_qkv, False)
+                project(plan, every, band_index, band_table, spatial_qkv, False, hide)
             )
-        mid = attend(plan, query, all_keys, all_values, own, band_index, band_table, spatial_out)
+        mid = attend(
+            plan, query, all_keys, all_values, own, band_index, band_table, spatial_out, hide
+        )
         behind = [mid]
         mids.append(mid)
     same = [

time: 156 us -> 129 us (0.83)
  waiting for transfers between devices: 52.6 us -> 24.4 us
  starting transfers between devices: 32.3 us -> 28.4 us
  Pallas kernels: 65 us -> 68.5 us
    ppermute x14, waiting for transfers between devices: 49.3 us -> 17.6 us  [exchange(): lax.ppermute(value, axis, [(i, i ^ step) for i in range(lax.axis_size(axi...]
    all_to_all x2, starting transfers between devices: 14.9 us -> 9.63 us  [body(): lax.all_to_all(mid.reshape(-1, plan.part_rows, plan.width), ('band', 'loc...]
    all_to_all x2, waiting for transfers between devices: 3.22 us -> 6.82 us  [body(): lax.all_to_all(mid.reshape(-1, plan.part_rows, plan.width), ('band', 'loc...]
    pallas_call x1, Pallas kernels: 1.31 us -> 3.83 us  [arrange_first(): call(kernel, [jax.ShapeDtypeStruct((plan.rows, plan.width), BF16)] * coun...]
    unnamed x30 -> x28, local copies, waits for them, and re-layouts: 5.74 us -> 6.8 us
  transfers between devices with their start and end apart: 16 -> 16, of which waited for: 7 -> 7; matrix products, arithmetic and copies ran while one was open for 0% -> 0% of each run, Pallas kernels for 32% -> 48%
where the time goes in v6:
time: 129 us; the launch traced here: 128 us
  Pallas kernels  68.5 us (53%)
  starting transfers between devices  28.4 us (22%)
  waiting for transfers between devices  24.4 us (19%)
  local copies, waits for them, and re-layouts  6.8 us (5%)
    pallas_call x2, Pallas kernels, channel(): call(kernel, [jax.ShapeDtypeStruct((bands, locations, width), BF16)] * gr...  29.4 us
    pallas_call x2, Pallas kernels, attend(): call(kernel, jax.ShapeDtypeStruct((plan.groups, plan.rows_count, plan.par...  19.8 us
    ppermute x14, starting transfers between devices, exchange(): lax.ppermute(value, axis, [(i, i ^ step) for i in range(lax.axis_size(axi...  18.8 us
    ppermute x14, waiting for transfers between devices, exchange(): lax.ppermute(value, axis, [(i, i ^ step) for i in range(lax.axis_size(axi...  17.6 us
    pallas_call x4, Pallas kernels, project(): call(kernel, [jax.ShapeDtypeStruct((rows, width), BF16)] * len(names), hi...  9.92 us
    all_to_all x2, starting transfers between devices, body(): lax.all_to_all(mid.reshape(-1, plan.part_rows, plan.width), ('band', 'loc...  9.63 us
    all_to_all x2, waiting for transfers between devices, body(): lax.all_to_all(mid.reshape(-1, plan.part_rows, plan.width), ('band', 'loc...  6.82 us
    unnamed x28, local copies, waits for them, and re-layouts  6.8 us
  transfers between devices with their start and end apart: 16, of which 7 were waited for; matrix products, arithmetic and copies ran while one was open for 0% of the time, Pallas kernels for 48%

profile of v6, /device:TPU:0, one launch (start us, length us, event | category | flops | bytes accessed | tf_op | source)
XLA Modules:
  0.0 128.4 jit_solution(5689386280867317730)
XLA Ops:
  0.0 3.8 %shard_map.100 = (bf16[128,768]{1,0:T(8,128)(2,1)}, bf16[128,768]{1,0:T(8,128)(2,1)}, bf16[128,768]{1,0:T(8,128)(2,1)}, bf16[128,768]{1,0:T(8,128)(2,1)}, bf16[1...) custom-call(s32[16,128]{1,0:T(8,128)} %bitcast.7, bf16[256,4,768]{2,1,0:T(4,128)(2,1)} %x_hbm.1), custom_call_target="tpu_custom_call" | custom-call | flops 402653184 | bytes 3145728 | tf_op jit(solution)/shard_map/pallas_call | solution.py:137
  3.8 3.1 %collective-permute-start = (bf16[128,768]{1,0:T(8,128)(2,1)}, bf16[128,768]{1,0:T(8,128)(2,1)S(1)}, u32[]{:S(2)}, u32[]{:S(2)}) collective-permute-start(bf16[128,768]{1,0:T(8,128)(2,1)} %get-tuple-element.36), channel_id=1, source_target_pairs={{0,2},{1,3},{2,0},{3,1},{4,6},{5,7},{6,4},{7,5},{8,10},{9,11},{10,... | collective-permute-start | bytes 589832 | tf_op jit(solution)/shard_map/ppermute | solution.py:62
  6.9 2.6 %collective-permute-start.1 = (bf16[128,768]{1,0:T(8,128)(2,1)}, bf16[128,768]{1,0:T(8,128)(2,1)S(1)}, u32[]{:S(2)}, u32[]{:S(2)}) collective-permute-start(bf16[128,768]{1,0:T(8,128)(2,1)} %get-tuple-element.37), channel_id=1, source_target_pairs={{0,4},{1,5},{2,6},{3,7},{4,0},{5,1},{6,2},{7,3},{8,12},{9,13},{10,... | collective-permute-start | bytes 589832 | tf_op jit(solution)/shard_map/ppermute | solution.py:62
  9.5 6.0 %collective-permute-done.rest_0_.refs_1_ = bf16[128,768]{1,0:T(8,128)(2,1)S(1)} collective-permute-done((bf16[128,768]{1,0:T(8,128)(2,1)}, bf16[128,768]{1,0:T(8,128)(2,1)S(1)}, u32[]{:S(2)}, u32[]{:S(2)}) %collective-permute-start) | collective-permute-done | bytes 196640 | tf_op jit(solution)/shard_map/ppermute | solution.py:62
  15.5 1.4 %copy-done.1 = bf16[1024,768]{1,0:T(8,128)(2,1)S(1)} copy-done((bf16[1024,768]{1,0:T(8,128)(2,1)S(1)}, bf16[1024,768]{1,0:T(8,128)(2,1)}, u32[]{:S(2)}) %copy-start.1) | copy-done | bytes 1572888
  17.6 1.7 %shard_map.101 = (bf16[128,768]{1,0:T(8,128)(2,1)S(1)}, bf16[128,768]{1,0:T(8,128)(2,1)}, bf16[128,768]{1,0:T(8,128)(2,1)}, bf16[128,768]{1,0:T(8,128)(2,1)}) custom-call(bf16[1024,768]{1,0:T(8,128)(2,1)S(1)} %copy-done.1, f32[1,1024]{1,0:T(1,128)S(1)} %copy-done.12, bf16[128,768]{1,0:T(8,128)(2,1)S(1)} %collective-permute-done.rest_0_.refs_1_), custom_call_target="tpu_custom_call" | custom-call | flops 402653184 | bytes 3145728 | tf_op jit(solution)/shard_map/pallas_call | solution.py:164
  19.2 5.0 %collective-permute-done.1.refs_2_ = bf16[128,768]{1,0:T(8,128)(2,1)S(1)} collective-permute-done((bf16[128,768]{1,0:T(8,128)(2,1)}, bf16[128,768]{1,0:T(8,128)(2,1)S(1)}, u32[]{:S(2)}, u32[]{:S(2)}) %collective-permute-start.1) | collective-permute-done | bytes 196640 | tf_op jit(solution)/shard_map/ppermute | solution.py:62
  24.3 0.9 copy-done.10
  25.4 3.4 %collective-permute-start.7 = (bf16[128,768]{1,0:T(8,128)(2,1)}, bf16[128,768]{1,0:T(8,128)(2,1)}, u32[]{:S(2)}, u32[]{:S(2)}) collective-permute-start(bf16[128,768]{1,0:T(8,128)(2,1)} %get-tuple-element.51), channel_id=1, source_target_pairs={{0,2},{1,3},{2,0},{3,1},{4,6},{5,7},{6,4},{7,5},{8,10},{9,11},{10,... | collective-permute-start | bytes 589832 | tf_op jit(solution)/shard_map/ppermute | solution.py:62
  28.8 1.1 collective-permute-start.8
  29.9 1.4 %collective-permute-start.9 = (bf16[128,768]{1,0:T(8,128)(2,1)}, bf16[128,768]{1,0:T(8,128)(2,1)}, u32[]{:S(2)}, u32[]{:S(2)}) collective-permute-start(bf16[128,768]{1,0:T(8,128)(2,1)} %get-tuple-element.53), channel_id=1, source_target_pairs={{0,6},{1,7},{2,4},{3,5},{4,2},{5,3},{6,0},{7,1},{8,14},{9,15},{10,... | collective-permute-start | bytes 589832 | tf_op jit(solution)/shard_map/ppermute | solution.py:62
  32.1 2.8 %shard_map.103 = (bf16[512,768]{1,0:T(8,128)(2,1)S(1)}, bf16[512,768]{1,0:T(8,128)(2,1)S(1)}, bf16[512,768]{1,0:T(8,128)(2,1)S(1)}) custom-call(s32[16]{0:T(128)S(1)} %copy-done.11, f32[16,768]{1,0:T(8,128)S(1)} %copy-done.4, bf16[768,2304]{1,0:T(8,128)(2,1)S(1)} %copy-done, bf16[512,768]{1,0:T(8,128)(2,1)S(1)} %shard_map.102.x_ref), custom_call_target="tpu_custom_call" | custom-call | flops 1811939328 | bytes 6684672 | tf_op jit(solution)/shard_map/pallas_call | solution.py:226
  34.9 2.2 %shard_map.104 = (bf16[512,768]{1,0:T(8,128)(2,1)S(1)}, bf16[512,768]{1,0:T(8,128)(2,1)S(1)}) custom-call(s32[16]{0:T(128)S(1)} %copy-done.11, f32[16,768]{1,0:T(8,128)S(1)} %copy-done.4, bf16[768,2304]{1,0:T(8,128)(2,1)S(1)} %copy-done, bf16[512,768]{1,0:T(8,128)(2,1)S(1)} %collective-permute-done.3.x_ref, bf16[512,768]{1,0:T(8,128)(2,1)S(1)} %get-tuple-element.43.rest_0_), custom_call_target="tpu_custom_call" | custom-call | flops 1207959552 | bytes 5898240 | tf_op jit(solution)/shard_map/pallas_call | solution.py:226
  37.1 9.4 %shard_map.105.refs_4_ = bf16[4,4,32,768]{3,2,1,0:T(8,128)(2,1)S(1)} custom-call(s32[16]{0:T(128)S(1)} %copy-done.11, f32[16,768]{1,0:T(8,128)S(1)} %copy-done.4, bf16[768,768]{1,0:T(8,128)(2,1)S(1)} %copy-done.2, bf16[512,768]{1,0:T(8,128)(2,1)S(1)} %shard_map.102.x_ref, bf16[512,768]{1,0:T(8,128)(2,1)S(1)} %get-tuple-element.42.q_ref, ...), custom_call_target="tpu_custom_call" | custom-call | flops 6442450944 | bytes 6684672 | tf_op jit(solution)/shard_map/pallas_call | solution.py:324
  47.4 5.8 %all-to-all-start = ((bf16[16,32,768]{2,1,0:T(8,128)(2,1)}), bf16[16,32,768]{2,1,0:T(8,128)(2,1)}, u32[]{:S(2)}, u32[]{:S(2)}) async-start(bf16[16,32,768]{2,1,0:T(8,128)(2,1)} %bitcast.5), calls=%async_computation | async-start | bytes 1572864 | tf_op jit(solution)/shard_map/all_to_all | solution.py:528
  53.2 1.1 copy-done.7
  55.3 1.2 shard_map.107.x_ref
  56.6 2.8 %shard_map.108 = (bf16[512,768]{1,0:T(8,128)(2,1)S(1)}, bf16[512,768]{1,0:T(8,128)(2,1)S(1)}, bf16[512,768]{1,0:T(8,128)(2,1)S(1)}) custom-call(s32[16]{0:T(128)S(1)} %copy-done.11, f32[16,768]{1,0:T(8,128)S(1)} %copy-done.5, bf16[768,2304]{1,0:T(8,128)(2,1)S(1)} %copy-done, bf16[512,768]{1,0:T(8,128)(2,1)S(1)} %shard_map.107.x_ref), custom_call_target="tpu_custom_call" | custom-call | tf_op jit(solution)/shard_map/pallas_call | solution.py:226
  59.4 2.2 %shard_map.109 = (bf16[512,768]{1,0:T(8,128)(2,1)S(1)}, bf16[512,768]{1,0:T(8,128)(2,1)S(1)}) custom-call(s32[16]{0:T(128)S(1)} %copy-done.11, f32[16,768]{1,0:T(8,128)S(1)} %copy-done.5, bf16[768,2304]{1,0:T(8,128)(2,1)S(1)} %copy-done, bf16[512,768]{1,0:T(8,128)(2,1)S(1)} %collective-permute-done.10.x_ref, bf16[512,768]{1,0:T(8,128)(2,1)S(1)} %get-tuple-element.55.rest_0_), custom_call_target="tpu_custom_call" | custom-call | tf_op jit(solution)/shard_map/pallas_call | solution.py:226
  61.6 10.4 %shard_map.110 = bf16[4,4,32,768]{3,2,1,0:T(8,128)(2,1)} custom-call(s32[16]{0:T(128)S(1)} %copy-done.11, f32[16,768]{1,0:T(8,128)S(1)} %copy-done.5, bf16[768,768]{1,0:T(8,128)(2,1)S(1)} %copy-done.3, bf16[512,768]{1,0:T(8,128)(2,1)S(1)} %shard_map.107.x_ref, bf16[512,768]{1,0:T(8,128)(2,1)S(1)} %get-tuple-element.54.q_ref, ...), custom_call_target="tpu_custom_call" | custom-call | tf_op jit(solution)/shard_map/pallas_call | solution.py:324
  71.9 3.1 %all-to-all-done = bf16[16,32,768]{2,1,0:T(8,128)(2,1)} async-done(((bf16[16,32,768]{2,1,0:T(8,128)(2,1)}), bf16[16,32,768]{2,1,0:T(8,128)(2,1)}, u32[]{:S(2)}, u32[]{:S(2)}) %all-to-all-start) | async-done | bytes 786464 | tf_op jit(solution)/shard_map/all_to_all | solution.py:528
  75.0 3.9 %all-to-all-start.1 = ((bf16[16,32,768]{2,1,0:T(8,128)(2,1)}), bf16[16,32,768]{2,1,0:T(8,128)(2,1)S(1)}, u32[]{:S(2)}, u32[]{:S(2)}) async-start(bf16[16,32,768]{2,1,0:T(8,128)(2,1)} %bitcast.3), calls=%async_computation.1 | async-start | bytes 1572864 | tf_op jit(solution)/shard_map/all_to_all | solution.py:528
  78.9 15.3 %shard_map.106 = (bf16[4,32,768]{2,1,0:T(8,128)(2,1)S(1)}, bf16[4,32,768]{2,1,0:T(8,128)(2,1)S(1)}, bf16[4,32,768]{2,1,0:T(8,128)(2,1)S(1)}, bf16[4,32,768]{2,1,0:T(8,128)(2,1)S(1)}) custom-call(bf16[768,2304]{1,0:T(8,128)(2,1)} %qkv_hbm.3, bf16[768,768]{1,0:T(8,128)(2,1)} %out_hbm.3, bf16[768,3072]{1,0:T(8,128)(2,1)} %up_hbm.3, bf16[3072,768]{1,0:T(8,128)(2,1)} %down_hbm.3, ...), custom_call_target="tpu_custom_call" | custom-call | flops 7247757312 | bytes 15728640 | tf_op jit(solution)/shard_map/pallas_call | solution.py:430
  94.2 1.9 %collective-permute-start.4 = (bf16[4,32,768]{2,1,0:T(8,128)(2,1)S(1)}, bf16[4,32,768]{2,1,0:T(8,128)(2,1)S(1)}, u32[]{:S(2)}, u32[]{:S(2)}) collective-permute-start(bf16[4,32,768]{2,1,0:T(8,128)(2,1)S(1)} %get-tuple-element.48), channel_id=1, source_target_pairs={{0,8},{8,0},{16,24},{24,16},{1,9},{9,1},{17,25},{25,17},{2,10},{10... | collective-permute-start | bytes 589832 | tf_op jit(solution)/shard_map/ppermute | solution.py:62
  96.1 1.5 %collective-permute-start.5 = (bf16[4,32,768]{2,1,0:T(8,128)(2,1)S(1)}, bf16[4,32,768]{2,1,0:T(8,128)(2,1)S(1)}, u32[]{:S(2)}, u32[]{:S(2)}) collective-permute-start(bf16[4,32,768]{2,1,0:T(8,128)(2,1)S(1)} %get-tuple-element.49), channel_id=1, source_target_pairs={{0,16},{8,24},{16,0},{24,8},{1,17},{9,25},{17,1},{25,9},{2,18},{10... | collective-permute-start | bytes 589832 | tf_op jit(solution)/shard_map/ppermute | solution.py:62
  97.8 3.7 %all-to-all-done.1 = bf16[16,32,768]{2,1,0:T(8,128)(2,1)S(1)} async-done(((bf16[16,32,768]{2,1,0:T(8,128)(2,1)}), bf16[16,32,768]{2,1,0:T(8,128)(2,1)S(1)}, u32[]{:S(2)}, u32[]{:S(2)}) %all-to-all-start.1) | async-done | bytes 786464 | tf_op jit(solution)/shard_map/all_to_all | solution.py:528
  101.5 14.1 %shard_map.111 = (bf16[4,32,768]{2,1,0:T(8,128)(2,1)S(1)}, bf16[4,32,768]{2,1,0:T(8,128)(2,1)S(1)}, bf16[4,32,768]{2,1,0:T(8,128)(2,1)S(1)}, bf16[4,32,768]{2,1,0:T(8,128)(2,1)S(1)}) custom-call(bf16[768,2304]{1,0:T(8,128)(2,1)} %qkv_hbm.3, bf16[768,768]{1,0:T(8,128)(2,1)} %out_hbm.3, bf16[768,3072]{1,0:T(8,128)(2,1)} %up_hbm.3, bf16[3072,768]{1,0:T(8,128)(2,1)} %down_hbm.3, ...), custom_call_target="tpu_custom_call" | custom-call | flops 7247757312 | bytes 15728640 | tf_op jit(solution)/shard_map/pallas_call | solution.py:430
  115.7 1.1 collective-permute-start.12
  116.8 2.4 %collective-permute-start.13 = (bf16[4,32,768]{2,1,0:T(8,128)(2,1)S(1)}, bf16[4,32,768]{2,1,0:T(8,128)(2,1)S(1)}, u32[]{:S(2)}, u32[]{:S(2)}) collective-permute-start(bf16[4,32,768]{2,1,0:T(8,128)(2,1)S(1)} %get-tuple-element.62), channel_id=1, source_target_pairs={{0,24},{8,16},{16,8},{24,0},{1,25},{9,17},{17,9},{25,1},{2,26},{10... | collective-permute-start | bytes 589832 | tf_op jit(solution)/shard_map/ppermute | solution.py:62
  119.2 4.3 %collective-permute-done.11.refs_5_ = bf16[4,32,768]{2,1,0:T(8,128)(2,1)S(1)} collective-permute-done((bf16[4,32,768]{2,1,0:T(8,128)(2,1)S(1)}, bf16[4,32,768]{2,1,0:T(8,128)(2,1)S(1)}, u32[]{:S(2)}, u32[]{:S(2)}) %collective-permute-start.11) | collective-permute-done | bytes 196640 | tf_op jit(solution)/shard_map/ppermute | solution.py:62
  123.6 2.1 %collective-permute-done.13.refs_7_ = bf16[4,32,768]{2,1,0:T(8,128)(2,1)S(1)} collective-permute-done((bf16[4,32,768]{2,1,0:T(8,128)(2,1)S(1)}, bf16[4,32,768]{2,1,0:T(8,128)(2,1)S(1)}, u32[]{:S(2)}, u32[]{:S(2)}) %collective-permute-start.13) | collective-permute-done | bytes 196640 | tf_op jit(solution)/shard_map/ppermute | solution.py:62
  125.7 2.6 %shard_map.112 = bf16[256,4,768]{2,1,0:T(4,128)(2,1)} custom-call(f32[1,256]{1,0:T(1,128)S(1)} %copy-done.13, bf16[4,32,768]{2,1,0:T(8,128)(2,1)S(1)} %get-tuple-element.47.refs_0_, bf16[4,32,768]{2,1,0:T(8,128)(2,1)S(1)} %collective-permute-done.4.refs_1_, bf16[4,32,768]{2,1,0:T(8,128)(2,1)S(1)} %collective-permute-done.5.refs_2_, ...), custom_call_target="tpu_custom_call" | custom-call | flops 402653184 | bytes 3145728 | tf_op jit(solution)/shard_map/pallas_call | solution.py:468
  (41 shorter events, 3.9 us)
Async XLA Ops:
  3.8 11.6 %collective-permute-start = (bf16[128,768]{1,0:T(8,128)(2,1)}, bf16[128,768]{1,0:T(8,128)(2,1)S(1)}, u32[]{:S(2)}, u32[]{:S(2)}) collective-permute-start(bf16[128,768]{1,0:T(8,128)(2,1)} %get-tuple-element.36), channel_id=1, source_target_pairs={{0,2},{1,3},{2,0},{3,1},{4,6},{5,7},{6,4},{7,5},{8,10},{9,11},{10,... | collective-permute-start | bytes 589832 | tf_op jit(solution)/shard_map/ppermute | solution.py:62
  6.9 17.4 %collective-permute-start.1 = (bf16[128,768]{1,0:T(8,128)(2,1)}, bf16[128,768]{1,0:T(8,128)(2,1)S(1)}, u32[]{:S(2)}, u32[]{:S(2)}) collective-permute-start(bf16[128,768]{1,0:T(8,128)(2,1)} %get-tuple-element.37), channel_id=1, source_target_pairs={{0,4},{1,5},{2,6},{3,7},{4,0},{5,1},{6,2},{7,3},{8,12},{9,13},{10,... | collective-permute-start | bytes 589832 | tf_op jit(solution)/shard_map/ppermute | solution.py:62
  9.5 14.8 %collective-permute-start.2 = (bf16[128,768]{1,0:T(8,128)(2,1)}, bf16[128,768]{1,0:T(8,128)(2,1)S(1)}, u32[]{:S(2)}, u32[]{:S(2)}) collective-permute-start(bf16[128,768]{1,0:T(8,128)(2,1)} %get-tuple-element.38), channel_id=1, source_target_pairs={{0,6},{1,7},{2,4},{3,5},{4,2},{5,3},{6,0},{7,1},{8,14},{9,15},{10,... | collective-permute-start | bytes 589832 | tf_op jit(solution)/shard_map/ppermute | solution.py:62
  15.5 15.8 %copy-start.11 = (s32[16]{0:T(128)S(1)}, s32[16]{0:T(128)}, u32[]{:S(2)}) copy-start(s32[16]{0:T(128)} %index_ref.11) | copy-start | bytes 196
  15.5 1.4 %copy-start.1 = (bf16[1024,768]{1,0:T(8,128)(2,1)S(1)}, bf16[1024,768]{1,0:T(8,128)(2,1)}, u32[]{:S(2)}) copy-start(bf16[1024,768]{1,0:T(8,128)(2,1)} %get-tuple-element.39.rows_ref) | copy-start | bytes 4718596
  16.9 0.7 copy-start.12
  17.6 13.7 %copy-start = (bf16[768,2304]{1,0:T(8,128)(2,1)S(1)}, bf16[768,2304]{1,0:T(8,128)(2,1)}, u32[]{:S(2)}) copy-start(bf16[768,2304]{1,0:T(8,128)(2,1)} %w_ref.10) | copy-start | bytes 10616836
  19.2 10.6 %copy-start.8 = (bf16[128,768]{1,0:T(8,128)(2,1)}, bf16[128,768]{1,0:T(8,128)(2,1)S(1)}, u32[]{:S(2)}) copy-start(bf16[128,768]{1,0:T(8,128)(2,1)S(1)} %get-tuple-element.41.refs_4_.refs_0_) | copy-start | bytes 589828
  24.3 0.9 copy-start.10
  25.3 9.6 %collective-permute-start.3 = (bf16[512,768]{1,0:T(8,128)(2,1)S(1)}, bf16[512,768]{1,0:T(8,128)(2,1)S(1)}, u32[]{:S(2)}, u32[]{:S(2)}) collective-permute-start(bf16[512,768]{1,0:T(8,128)(2,1)S(1)} %shard_map.102.x_ref), channel_id=1, source_target_pairs={{0,1},{1,0},{2,3},{3,2},{4,5},{5,4},{6,7},{7,6},{8,9},{9,8},{10,11... | collective-permute-start | bytes 2359304 | tf_op jit(solution)/shard_map/ppermute | solution.py:62
  25.4 27.8 %collective-permute-start.7 = (bf16[128,768]{1,0:T(8,128)(2,1)}, bf16[128,768]{1,0:T(8,128)(2,1)}, u32[]{:S(2)}, u32[]{:S(2)}) collective-permute-start(bf16[128,768]{1,0:T(8,128)(2,1)} %get-tuple-element.51), channel_id=1, source_target_pairs={{0,2},{1,3},{2,0},{3,1},{4,6},{5,7},{6,4},{7,5},{8,10},{9,11},{10,... | collective-permute-start | bytes 589832 | tf_op jit(solution)/shard_map/ppermute | solution.py:62
  28.8 24.4 %collective-permute-start.8 = (bf16[128,768]{1,0:T(8,128)(2,1)}, bf16[128,768]{1,0:T(8,128)(2,1)}, u32[]{:S(2)}, u32[]{:S(2)}) collective-permute-start(bf16[128,768]{1,0:T(8,128)(2,1)} %get-tuple-element.52), channel_id=1, source_target_pairs={{0,4},{1,5},{2,6},{3,7},{4,0},{5,1},{6,2},{7,3},{8,12},{9,13},{10,... | collective-permute-start | bytes 589832 | tf_op jit(solution)/shard_map/ppermute | solution.py:62
  29.9 23.3 %collective-permute-start.9 = (bf16[128,768]{1,0:T(8,128)(2,1)}, bf16[128,768]{1,0:T(8,128)(2,1)}, u32[]{:S(2)}, u32[]{:S(2)}) collective-permute-start(bf16[128,768]{1,0:T(8,128)(2,1)} %get-tuple-element.53), channel_id=1, source_target_pairs={{0,6},{1,7},{2,4},{3,5},{4,2},{5,3},{6,0},{7,1},{8,14},{9,15},{10,... | collective-permute-start | bytes 589832 | tf_op jit(solution)/shard_map/ppermute | solution.py:62
  31.3 0.8 copy-start.4
  34.9 2.2 %copy-start.2 = (bf16[768,768]{1,0:T(8,128)(2,1)S(1)}, bf16[768,768]{1,0:T(8,128)(2,1)}, u32[]{:S(2)}) copy-start(bf16[768,768]{1,0:T(8,128)(2,1)} %w_ref.11) | copy-start | bytes 3538948
  46.5 0.9 copy-start.6
  47.4 27.6 %all-to-all-start = ((bf16[16,32,768]{2,1,0:T(8,128)(2,1)}), bf16[16,32,768]{2,1,0:T(8,128)(2,1)}, u32[]{:S(2)}, u32[]{:S(2)}) async-start(bf16[16,32,768]{2,1,0:T(8,128)(2,1)} %bitcast.5), calls=%async_computation | async-start | bytes 1572864 | tf_op jit(solution)/shard_map/all_to_all | solution.py:528
  53.2 3.4 %copy-start.5 = (f32[16,768]{1,0:T(8,128)S(1)}, f32[16,768]{1,0:T(8,128)}, u32[]{:S(2)}) copy-start(f32[16,768]{1,0:T(8,128)} %table_ref.11) | copy-start | bytes 147460
  53.2 1.2 copy-start.7
  54.4 0.9 copy-start.9
  56.5 2.9 %collective-permute-start.10 = (bf16[512,768]{1,0:T(8,128)(2,1)S(1)}, bf16[512,768]{1,0:T(8,128)(2,1)S(1)}, u32[]{:S(2)}, u32[]{:S(2)}) collective-permute-start(bf16[512,768]{1,0:T(8,128)(2,1)S(1)} %shard_map.107.x_ref), channel_id=1, source_target_pairs={{0,1},{1,0},{2,3},{3,2},{4,5},{5,4},{6,7},{7,6},{8,9},{9,8},{10,11... | collective-permute-start | bytes 2359304 | tf_op jit(solution)/shard_map/ppermute | solution.py:62
  59.4 2.2 %copy-start.3 = (bf16[768,768]{1,0:T(8,128)(2,1)S(1)}, bf16[768,768]{1,0:T(8,128)(2,1)}, u32[]{:S(2)}) copy-start(bf16[768,768]{1,0:T(8,128)(2,1)} %w_ref.11) | copy-start | bytes 3538948
  75.0 26.4 %all-to-all-start.1 = ((bf16[16,32,768]{2,1,0:T(8,128)(2,1)}), bf16[16,32,768]{2,1,0:T(8,128)(2,1)S(1)}, u32[]{:S(2)}, u32[]{:S(2)}) async-start(bf16[16,32,768]{2,1,0:T(8,128)(2,1)} %bitcast.3), calls=%async_computation.1 | async-start | bytes 1572864 | tf_op jit(solution)/shard_map/all_to_all | solution.py:528
  94.2 22.6 %collective-permute-start.4 = (bf16[4,32,768]{2,1,0:T(8,128)(2,1)S(1)}, bf16[4,32,768]{2,1,0:T(8,128)(2,1)S(1)}, u32[]{:S(2)}, u32[]{:S(2)}) collective-permute-start(bf16[4,32,768]{2,1,0:T(8,128)(2,1)S(1)} %get-tuple-element.48), channel_id=1, source_target_pairs={{0,8},{8,0},{16,24},{24,16},{1,9},{9,1},{17,25},{25,17},{2,10},{10... | collective-permute-start | bytes 589832 | tf_op jit(solution)/shard_map/ppermute | solution.py:62
  96.1 23.1 %collective-permute-start.5 = (bf16[4,32,768]{2,1,0:T(8,128)(2,1)S(1)}, bf16[4,32,768]{2,1,0:T(8,128)(2,1)S(1)}, u32[]{:S(2)}, u32[]{:S(2)}) collective-permute-start(bf16[4,32,768]{2,1,0:T(8,128)(2,1)S(1)} %get-tuple-element.49), channel_id=1, source_target_pairs={{0,16},{8,24},{16,0},{24,8},{1,17},{9,25},{17,1},{25,9},{2,18},{10... | collective-permute-start | bytes 589832 | tf_op jit(solution)/shard_map/ppermute | solution.py:62
  97.5 21.6 %collective-permute-start.6 = (bf16[4,32,768]{2,1,0:T(8,128)(2,1)S(1)}, bf16[4,32,768]{2,1,0:T(8,128)(2,1)S(1)}, u32[]{:S(2)}, u32[]{:S(2)}) collective-permute-start(bf16[4,32,768]{2,1,0:T(8,128)(2,1)S(1)} %get-tuple-element.50), channel_id=1, source_target_pairs={{0,24},{8,16},{16,8},{24,0},{1,25},{9,17},{17,9},{25,1},{2,26},{10... | collective-permute-start | bytes 589832 | tf_op jit(solution)/shard_map/ppermute | solution.py:62
  101.5 24.2 %copy-start.13 = (f32[1,256]{1,0:T(1,128)S(1)}, f32[1,256]{1,0:T(1,128)}, u32[]{:S(2)}) copy-start(f32[1,256]{1,0:T(1,128)} %get-tuple-element.34.keys_ref) | copy-start | bytes 3076
  115.6 7.9 %collective-permute-start.11 = (bf16[4,32,768]{2,1,0:T(8,128)(2,1)S(1)}, bf16[4,32,768]{2,1,0:T(8,128)(2,1)S(1)}, u32[]{:S(2)}, u32[]{:S(2)}) collective-permute-start(bf16[4,32,768]{2,1,0:T(8,128)(2,1)S(1)} %get-tuple-element.60), channel_id=1, source_target_pairs={{0,8},{8,0},{16,24},{24,16},{1,9},{9,1},{17,25},{25,17},{2,10},{10... | collective-permute-start | bytes 589832 | tf_op jit(solution)/shard_map/ppermute | solution.py:62
  115.7 7.9 %collective-permute-start.12 = (bf16[4,32,768]{2,1,0:T(8,128)(2,1)S(1)}, bf16[4,32,768]{2,1,0:T(8,128)(2,1)S(1)}, u32[]{:S(2)}, u32[]{:S(2)}) collective-permute-start(bf16[4,32,768]{2,1,0:T(8,128)(2,1)S(1)} %get-tuple-element.61), channel_id=1, source_target_pairs={{0,16},{8,24},{16,0},{24,8},{1,17},{9,25},{17,1},{25,9},{2,18},{10... | collective-permute-start | bytes 589832 | tf_op jit(solution)/shard_map/ppermute | solution.py:62
  116.8 9.0 %collective-permute-start.13 = (bf16[4,32,768]{2,1,0:T(8,128)(2,1)S(1)}, bf16[4,32,768]{2,1,0:T(8,128)(2,1)S(1)}, u32[]{:S(2)}, u32[]{:S(2)}) collective-permute-start(bf16[4,32,768]{2,1,0:T(8,128)(2,1)S(1)} %get-tuple-element.62), channel_id=1, source_target_pairs={{0,24},{8,16},{16,8},{24,0},{1,25},{9,17},{17,9},{25,1},{2,26},{10... | collective-permute-start | bytes 589832 | tf_op jit(solution)/shard_map/ppermute | solution.py:62

commit v7 on v6

--- a/solution.py
+++ b/solution.py
@@ -20,7 +20,6 @@
 QUERY_SCALE = HEAD_DIM ** (-0.5)
 VMEM_LIMIT = 28 * 1024 * 1024
 WIDE_LIMIT = 52 * 1024 * 1024
-WHOLE_LIMIT = 61 * 1024 * 1024
 LONG = 2**36
 
 F32 = jnp.float32
@@ -112,16 +111,8 @@
     total = plan.loc_dev * plan.band_dev
     assert plan.loc_dev <= 256
 
-    def kernel(ids_hbm, x_hbm, *rest):
-        outs, rest = rest[:count], rest[count:]
-        rows_ref, keys_ref, place_ref, ids_ref, x_ref, sems = rest
-        copies = [
-            pltpu.make_async_copy(ids_hbm, ids_ref, sems.at[0]),
-            pltpu.make_async_copy(x_hbm, x_ref, sems.at[1]),
-        ]
-        for copy in copies:
-            copy.start()
-        copies[0].wait()
+    def kernel(ids_ref, x_ref, *rest):
+        outs, (rows_ref, keys_ref, place_ref) = rest[:count], rest[count:]
         keys = location_keys(plan, ids_ref)
         keys_ref[...] = keys
         place = lax.broadcasted_iota(jnp.int32, (plan.loc_dev, total), 1)
@@ -130,7 +121,6 @@
         wide = dot(jnp.broadcast_to(keys, (16, plan.loc_dev)).astype(BF16), spread)
         band = lax.broadcasted_iota(jnp.int32, (1, total), 1) % plan.band_dev
         place_ref[...] = wide[:1] + (band * plan.loc_dev).astype(F32)
-        copies[1].wait()
         rows_ref[...] = x_ref[...].reshape(total, plan.width)
         pick_rows(plan, 0, place_ref[...], rows_ref, outs)
 
@@ -144,14 +134,8 @@
         ],
         2 * plan.loc_dev * tokens.size,
         4 * tokens.size,
-        limit=WHOLE_LIMIT,
-        in_specs=[ANY] * 2,
+        in_specs=[VMEM] * 2,
         out_specs=[VMEM] * (count + 3),
-        scratch_shapes=[
-            pltpu.VMEM(ids.shape, jnp.int32),
-            pltpu.VMEM(tokens.shape, BF16),
-            pltpu.SemaphoreType.DMA((2,)),
-        ],
     )(ids, tokens)
 
 
@@ -318,12 +302,12 @@
             mid = (x_ref[here, :].astype(F32) + embed + added[here, :]).astype(BF16)
             for owner in range(plan.groups):
                 part = mid[owner * plan.part_rows : (owner + 1) * plan.part_rows]
-                out_ref[owner, row ^ slot] = part
+                out_ref[row ^ slot, owner] = part
 
     key_rows = sum(piece.shape[0] for piece in keys)
     return call(
         kernel,
-        jax.ShapeDtypeStruct((plan.groups, plan.rows_count, plan.part_rows, width), BF16),
+        jax.ShapeDtypeStruct((plan.rows_count, plan.groups, plan.part_rows, width), BF16),
         hide * 16 * total * key_rows * width,
         hide * 2 * width * (2 * key_rows + 3 * total + width),
         in_specs=[SMEM] + [VMEM] * (4 + 2 * pieces),
@@ -334,7 +318,7 @@
 
 def channel(plan, parts, channel_qkv, channel_out, up_weight, down_weight):
     groups, width = plan.groups, plan.width
-    _, bands, locations, _ = parts.shape
+    bands, _, locations, _ = parts.shape
     tile, small = TILE_LOCS, GROUP_LOCS
     assert locations % tile == 0
     group_rows = groups * bands * small
@@ -376,7 +360,7 @@
             ]
 
         for owner, band, first in pieces:
-            piece = in_ref[me ^ owner, band, first : first + tile, :].astype(F32)
+            piece = in_ref[band, me ^ owner, first : first + tile, :].astype(F32)
             for number, place in enumerate(places(owner, band, first)):
                 mid[place, :] = piece[number * small : (number + 1) * small]
         norm_into(normed, mid)
@@ -520,7 +504,7 @@
         behind = [mid]
         mids.append(mid)
     same = [
-        [(g * plan.rows_count + r) * CORES + core for g in range(plan.groups) for r in range(plan.rows_count)]
+        [g * plan.locs + r * CORES + core for r in range(plan.rows_count) for g in range(plan.groups)]
         for core in range(CORES)
     ]
     returned = []
@@ -533,7 +517,8 @@
             axis_index_groups=same,
             tiled=True,
         )
-        parts = parts.reshape(plan.groups, plan.band_dev, -1, plan.width)
+        parts = parts.reshape(plan.band_dev, plan.share, plan.groups, plan.part_rows, plan.width)
+        parts = parts.transpose(0, 2, 1, 3, 4).reshape(plan.band_dev, plan.groups, -1, plan.width)
         done = channel(plan, parts, channel_qkv, channel_out, up_weight, down_weight)
         returned.append([exchange(value, "band", step) for step, value in enumerate(done)])
     return restore(plan, keys, returned)

time: 129 us -> 124 us (0.961)
  Pallas kernels: 68.5 us -> 66 us
  waiting for transfers between devices: 24.4 us -> 22.2 us
  starting transfers between devices: 28.4 us -> 30.5 us
  local copies, waits for them, and re-layouts: 6.8 us -> 5.08 us
    all_to_all x2, waiting for transfers between devices: 6.82 us -> 2.23 us  [body(): lax.all_to_all(mid.reshape(-1, plan.part_rows, plan.width), ('band', 'loc...]
    pallas_call x1, Pallas kernels: 3.83 us -> 1.28 us  [arrange_first(): call(kernel, [jax.ShapeDtypeStruct((plan.rows, plan.width), BF16)] * coun...]
    ppermute x14, waiting for transfers between devices: 17.6 us -> 19.9 us  [exchange(): lax.ppermute(value, axis, [(i, i ^ step) for i in range(lax.axis_size(axi...]
    all_to_all x2, starting transfers between devices: 9.63 us -> 11.6 us  [body(): lax.all_to_all(mid.reshape(-1, plan.part_rows, plan.width), ('band', 'loc...]
    unnamed x28 -> x24, local copies, waits for them, and re-layouts: 6.8 us -> 5.08 us
  transfers between devices with their start and end apart: 16 -> 16, of which waited for: 7 -> 7; matrix products, arithmetic and copies ran while one was open for 0% -> 0% of each run, Pallas kernels for 48% -> 50%
where the time goes in v7:
time: 124 us
  Pallas kernels  66 us (53%)
  starting transfers between devices  30.5 us (25%)
  waiting for transfers between devices  22.2 us (18%)
  local copies, waits for them, and re-layouts  5.08 us (4%)
    pallas_call x2, Pallas kernels, channel(): call(kernel, [jax.ShapeDtypeStruct((bands, locations, width), BF16)] * gr...  29.4 us
    ppermute x14, waiting for transfers between devices, exchange(): lax.ppermute(value, axis, [(i, i ^ step) for i in range(lax.axis_size(axi...  19.9 us
    pallas_call x2, Pallas kernels, attend(): call(kernel, jax.ShapeDtypeStruct((plan.rows_count, plan.groups, plan.par...  19.8 us
    ppermute x14, starting transfers between devices, exchange(): lax.ppermute(value, axis, [(i, i ^ step) for i in range(lax.axis_size(axi...  18.8 us
    all_to_all x2, starting transfers between devices, body(): lax.all_to_all(mid.reshape(-1, plan.part_rows, plan.width), ('band', 'loc...  11.6 us
    pallas_call x4, Pallas kernels, project(): call(kernel, [jax.ShapeDtypeStruct((rows, width), BF16)] * len(names), hi...  9.92 us
    unnamed x24, local copies, waits for them, and re-layouts  5.08 us
    pallas_call x1, Pallas kernels, restore(): call(kernel, jax.ShapeDtypeStruct((plan.loc_dev, plan.band_dev, plan.widt...  2.65 us
  transfers between devices with their start and end apart: 16, of which 7 were waited for; matrix products, arithmetic and copies ran while one was open for 0% of the time, Pallas kernels for 50%

profile of v7, /device:TPU:0, one launch (start us, length us, event | category | flops | bytes accessed | tf_op | source)
XLA Modules:
  0.0 123.9 jit_solution(10409259267195993435)
XLA Ops:
  0.0 1.4 %copy-done.1 = bf16[256,4,768]{2,1,0:T(4,128)(2,1)S(1)} copy-done((bf16[256,4,768]{2,1,0:T(4,128)(2,1)S(1)}, bf16[256,4,768]{2,1,0:T(4,128)(2,1)}, u32[]{:S(2)}) %copy-start.1) | copy-done | bytes 1572888
  2.1 1.3 %shard_map.100 = (bf16[128,768]{1,0:T(8,128)(2,1)S(1)}, bf16[128,768]{1,0:T(8,128)(2,1)S(1)}, bf16[128,768]{1,0:T(8,128)(2,1)S(1)}, bf16[128,768]{1,0:T(8,128)(2...) custom-call(s32[16,128]{1,0:T(8,128)S(1)} %bitcast.7, ...), custom_call_target="tpu_custom_call" | custom-call | flops 402653184 | bytes 3145728 | tf_op jit(solution)/shard_map/pallas_call | solution.py:127
  3.4 3.1 %collective-permute-start = (bf16[128,768]{1,0:T(8,128)(2,1)S(1)}, bf16[128,768]{1,0:T(8,128)(2,1)S(1)}, u32[]{:S(2)}, u32[]{:S(2)}) collective-permute-start(bf16[128,768]{1,0:T(8,128)(2,1)S(1)} %get-tuple-element.36), channel_id=1, source_target_pairs={{0,2},{1,3},{2,0},{3,1},{4,6},{5,7},{6,4},{7,5},{8,10},{9,11},{10,... | collective-permute-start | bytes 589832 | tf_op jit(solution)/shard_map/ppermute | solution.py:61
  6.5 2.6 %collective-permute-start.1 = (bf16[128,768]{1,0:T(8,128)(2,1)S(1)}, bf16[128,768]{1,0:T(8,128)(2,1)S(1)}, u32[]{:S(2)}, u32[]{:S(2)}) collective-permute-start(bf16[128,768]{1,0:T(8,128)(2,1)S(1)} %get-tuple-element.37), channel_id=1, source_target_pairs={{0,4},{1,5},{2,6},{3,7},{4,0},{5,1},{6,2},{7,3},{8,12},{9,13},{10,... | collective-permute-start | bytes 589832 | tf_op jit(solution)/shard_map/ppermute | solution.py:61
  9.1 5.7 %collective-permute-done.rest_0_.refs_1_ = bf16[128,768]{1,0:T(8,128)(2,1)S(1)} collective-permute-done((bf16[128,768]{1,0:T(8,128)(2,1)S(1)}, bf16[128,768]{1,0:T(8,128)(2,1)S(1)}, u32[]{:S(2)}, u32[]{:S(2)}) %collective-permute-start) | collective-permute-done | bytes 196640 | tf_op jit(solution)/shard_map/ppermute | solution.py:61
  14.8 1.7 %shard_map.101 = (bf16[128,768]{1,0:T(8,128)(2,1)S(1)}, bf16[128,768]{1,0:T(8,128)(2,1)}, bf16[128,768]{1,0:T(8,128)(2,1)}, bf16[128,768]{1,0:T(8,128)(2,1)}) custom-call(bf16[1024,768]{1,0:T(8,128)(2,1)S(1)} %get-tuple-element.39.rows_ref, f32[1,1024]{1,0:T(1,128)S(1)} %get-tuple-element.40.place_ref, bf16[128,768]{1,0:T(8,128)(2,1)S(1)} %collective-permute-done.rest_0_.refs_1_), custom_call_target="tpu_custom_call" | custom-call | flops 402653184 | bytes 3145728 | tf_op jit(solution)/shard_map/pallas_call | solution.py:148
  16.5 7.2 %collective-permute-done.1.refs_2_ = bf16[128,768]{1,0:T(8,128)(2,1)S(1)} collective-permute-done((bf16[128,768]{1,0:T(8,128)(2,1)S(1)}, bf16[128,768]{1,0:T(8,128)(2,1)S(1)}, u32[]{:S(2)}, u32[]{:S(2)}) %collective-permute-start.1) | collective-permute-done | bytes 196640 | tf_op jit(solution)/shard_map/ppermute | solution.py:61
  23.8 3.4 %collective-permute-start.7 = (bf16[128,768]{1,0:T(8,128)(2,1)}, bf16[128,768]{1,0:T(8,128)(2,1)}, u32[]{:S(2)}, u32[]{:S(2)}) collective-permute-start(bf16[128,768]{1,0:T(8,128)(2,1)} %get-tuple-element.51), channel_id=1, source_target_pairs={{0,2},{1,3},{2,0},{3,1},{4,6},{5,7},{6,4},{7,5},{8,10},{9,11},{10,... | collective-permute-start | bytes 589832 | tf_op jit(solution)/shard_map/ppermute | solution.py:61
  27.2 1.1 collective-permute-start.8
  28.3 1.4 %collective-permute-start.9 = (bf16[128,768]{1,0:T(8,128)(2,1)}, bf16[128,768]{1,0:T(8,128)(2,1)}, u32[]{:S(2)}, u32[]{:S(2)}) collective-permute-start(bf16[128,768]{1,0:T(8,128)(2,1)} %get-tuple-element.53), channel_id=1, source_target_pairs={{0,6},{1,7},{2,4},{3,5},{4,2},{5,3},{6,0},{7,1},{8,14},{9,15},{10,... | collective-permute-start | bytes 589832 | tf_op jit(solution)/shard_map/ppermute | solution.py:61
  29.7 2.8 %shard_map.103 = (bf16[512,768]{1,0:T(8,128)(2,1)S(1)}, bf16[512,768]{1,0:T(8,128)(2,1)S(1)}, bf16[512,768]{1,0:T(8,128)(2,1)S(1)}) custom-call(s32[16]{0:T(128)S(1)} %copy-done.11, f32[16,768]{1,0:T(8,128)S(1)} %copy-done.4, bf16[768,2304]{1,0:T(8,128)(2,1)S(1)} %copy-done, bf16[512,768]{1,0:T(8,128)(2,1)S(1)} %shard_map.102.x_ref), custom_call_target="tpu_custom_call" | custom-call | flops 1811939328 | bytes 6684672 | tf_op jit(solution)/shard_map/pallas_call | solution.py:210
  32.5 2.2 %shard_map.104 = (bf16[512,768]{1,0:T(8,128)(2,1)S(1)}, bf16[512,768]{1,0:T(8,128)(2,1)S(1)}) custom-call(s32[16]{0:T(128)S(1)} %copy-done.11, f32[16,768]{1,0:T(8,128)S(1)} %copy-done.4, bf16[768,2304]{1,0:T(8,128)(2,1)S(1)} %copy-done, bf16[512,768]{1,0:T(8,128)(2,1)S(1)} %collective-permute-done.3.x_ref, bf16[512,768]{1,0:T(8,128)(2,1)S(1)} %get-tuple-element.43.rest_0_), custom_call_target="tpu_custom_call" | custom-call | flops 1207959552 | bytes 5898240 | tf_op jit(solution)/shard_map/pallas_call | solution.py:210
  34.7 9.4 %shard_map.105.refs_4_ = bf16[4,4,32,768]{3,2,1,0:T(8,128)(2,1)S(1)} custom-call(s32[16]{0:T(128)S(1)} %copy-done.11, f32[16,768]{1,0:T(8,128)S(1)} %copy-done.4, bf16[768,768]{1,0:T(8,128)(2,1)S(1)} %copy-done.2, bf16[512,768]{1,0:T(8,128)(2,1)S(1)} %shard_map.102.x_ref, bf16[512,768]{1,0:T(8,128)(2,1)S(1)} %get-tuple-element.42.q_ref, ...), custom_call_target="tpu_custom_call" | custom-call | flops 6442450944 | bytes 6684672 | tf_op jit(solution)/shard_map/pallas_call | solution.py:308
  45.0 5.8 %all-to-all-start = ((bf16[16,32,768]{2,1,0:T(8,128)(2,1)}), bf16[16,32,768]{2,1,0:T(8,128)(2,1)}, u32[]{:S(2)}, u32[]{:S(2)}) async-start(bf16[16,32,768]{2,1,0:T(8,128)(2,1)} %bitcast.5), calls=%async_computation | async-start | bytes 1572864 | tf_op jit(solution)/shard_map/all_to_all | solution.py:512
  50.8 1.1 copy-done.7
  52.9 1.2 shard_map.107.x_ref
  54.2 2.8 %shard_map.108 = (bf16[512,768]{1,0:T(8,128)(2,1)S(1)}, bf16[512,768]{1,0:T(8,128)(2,1)S(1)}, bf16[512,768]{1,0:T(8,128)(2,1)S(1)}) custom-call(s32[16]{0:T(128)S(1)} %copy-done.11, f32[16,768]{1,0:T(8,128)S(1)} %copy-done.5, bf16[768,2304]{1,0:T(8,128)(2,1)S(1)} %copy-done, bf16[512,768]{1,0:T(8,128)(2,1)S(1)} %shard_map.107.x_ref), custom_call_target="tpu_custom_call" | custom-call | tf_op jit(solution)/shard_map/pallas_call | solution.py:210
  57.0 2.2 %shard_map.109 = (bf16[512,768]{1,0:T(8,128)(2,1)S(1)}, bf16[512,768]{1,0:T(8,128)(2,1)S(1)}) custom-call(s32[16]{0:T(128)S(1)} %copy-done.11, f32[16,768]{1,0:T(8,128)S(1)} %copy-done.5, bf16[768,2304]{1,0:T(8,128)(2,1)S(1)} %copy-done, bf16[512,768]{1,0:T(8,128)(2,1)S(1)} %collective-permute-done.10.x_ref, bf16[512,768]{1,0:T(8,128)(2,1)S(1)} %get-tuple-element.55.rest_0_), custom_call_target="tpu_custom_call" | custom-call | tf_op jit(solution)/shard_map/pallas_call | solution.py:210
  59.2 10.4 %shard_map.110 = bf16[4,4,32,768]{3,2,1,0:T(8,128)(2,1)} custom-call(s32[16]{0:T(128)S(1)} %copy-done.11, f32[16,768]{1,0:T(8,128)S(1)} %copy-done.5, bf16[768,768]{1,0:T(8,128)(2,1)S(1)} %copy-done.3, bf16[512,768]{1,0:T(8,128)(2,1)S(1)} %shard_map.107.x_ref, bf16[512,768]{1,0:T(8,128)(2,1)S(1)} %get-tuple-element.54.q_ref, ...), custom_call_target="tpu_custom_call" | custom-call | tf_op jit(solution)/shard_map/pallas_call | solution.py:308
  69.6 1.0 all-to-all-done
  70.5 5.9 %all-to-all-start.1 = ((bf16[16,32,768]{2,1,0:T(8,128)(2,1)}), bf16[16,32,768]{2,1,0:T(8,128)(2,1)S(1)}, u32[]{:S(2)}, u32[]{:S(2)}) async-start(bf16[16,32,768]{2,1,0:T(8,128)(2,1)} %bitcast.3), calls=%async_computation.1 | async-start | bytes 1572864 | tf_op jit(solution)/shard_map/all_to_all | solution.py:512
  76.4 15.3 %shard_map.106 = (bf16[4,32,768]{2,1,0:T(8,128)(2,1)S(1)}, bf16[4,32,768]{2,1,0:T(8,128)(2,1)S(1)}, bf16[4,32,768]{2,1,0:T(8,128)(2,1)S(1)}, bf16[4,32,768]{2,1,0:T(8,128)(2,1)S(1)}) custom-call(bf16[768,2304]{1,0:T(8,128)(2,1)} %qkv_hbm.3, bf16[768,768]{1,0:T(8,128)(2,1)} %out_hbm.3, bf16[768,3072]{1,0:T(8,128)(2,1)} %up_hbm.3, bf16[3072,768]{1,0:T(8,128)(2,1)} %down_hbm.3, ...), custom_call_target="tpu_custom_call" | custom-call | flops 7247757312 | bytes 15728640 | tf_op jit(solution)/shard_map/pallas_call | solution.py:414
  91.7 2.0 %collective-permute-start.4 = (bf16[4,32,768]{2,1,0:T(8,128)(2,1)S(1)}, bf16[4,32,768]{2,1,0:T(8,128)(2,1)S(1)}, u32[]{:S(2)}, u32[]{:S(2)}) collective-permute-start(bf16[4,32,768]{2,1,0:T(8,128)(2,1)S(1)} %get-tuple-element.48), channel_id=1, source_target_pairs={{0,8},{8,0},{16,24},{24,16},{1,9},{9,1},{17,25},{25,17},{2,10},{10... | collective-permute-start | bytes 589832 | tf_op jit(solution)/shard_map/ppermute | solution.py:61
  93.7 1.5 %collective-permute-start.5 = (bf16[4,32,768]{2,1,0:T(8,128)(2,1)S(1)}, bf16[4,32,768]{2,1,0:T(8,128)(2,1)S(1)}, u32[]{:S(2)}, u32[]{:S(2)}) collective-permute-start(bf16[4,32,768]{2,1,0:T(8,128)(2,1)S(1)} %get-tuple-element.49), channel_id=1, source_target_pairs={{0,16},{8,24},{16,0},{24,8},{1,17},{9,25},{17,1},{25,9},{2,18},{10... | collective-permute-start | bytes 589832 | tf_op jit(solution)/shard_map/ppermute | solution.py:61
  95.3 1.2 all-to-all-done.1
  96.5 14.1 %shard_map.111 = (bf16[4,32,768]{2,1,0:T(8,128)(2,1)S(1)}, bf16[4,32,768]{2,1,0:T(8,128)(2,1)S(1)}, bf16[4,32,768]{2,1,0:T(8,128)(2,1)S(1)}, bf16[4,32,768]{2,1,0:T(8,128)(2,1)S(1)}) custom-call(bf16[768,2304]{1,0:T(8,128)(2,1)} %qkv_hbm.3, bf16[768,768]{1,0:T(8,128)(2,1)} %out_hbm.3, bf16[768,3072]{1,0:T(8,128)(2,1)} %up_hbm.3, bf16[3072,768]{1,0:T(8,128)(2,1)} %down_hbm.3, ...), custom_call_target="tpu_custom_call" | custom-call | flops 7247757312 | bytes 15728640 | tf_op jit(solution)/shard_map/pallas_call | solution.py:414
  111.4 1.5 %collective-permute-start.12 = (bf16[4,32,768]{2,1,0:T(8,128)(2,1)S(1)}, bf16[4,32,768]{2,1,0:T(8,128)(2,1)S(1)}, u32[]{:S(2)}, u32[]{:S(2)}) collective-permute-start(bf16[4,32,768]{2,1,0:T(8,128)(2,1)S(1)} %get-tuple-element.61), channel_id=1, source_target_pairs={{0,16},{8,24},{16,0},{24,8},{1,17},{9,25},{17,1},{25,9},{2,18},{10... | collective-permute-start | bytes 589832 | tf_op jit(solution)/shard_map/ppermute | solution.py:61
  112.9 1.3 %collective-permute-start.13 = (bf16[4,32,768]{2,1,0:T(8,128)(2,1)S(1)}, bf16[4,32,768]{2,1,0:T(8,128)(2,1)S(1)}, u32[]{:S(2)}, u32[]{:S(2)}) collective-permute-start(bf16[4,32,768]{2,1,0:T(8,128)(2,1)S(1)} %get-tuple-element.62), channel_id=1, source_target_pairs={{0,24},{8,16},{16,8},{24,0},{1,25},{9,17},{17,9},{25,1},{2,26},{10... | collective-permute-start | bytes 589832 | tf_op jit(solution)/shard_map/ppermute | solution.py:61
  114.2 4.0 %collective-permute-done.11.refs_5_ = bf16[4,32,768]{2,1,0:T(8,128)(2,1)S(1)} collective-permute-done((bf16[4,32,768]{2,1,0:T(8,128)(2,1)S(1)}, bf16[4,32,768]{2,1,0:T(8,128)(2,1)S(1)}, u32[]{:S(2)}, u32[]{:S(2)}) %collective-permute-start.11) | collective-permute-done | bytes 196640 | tf_op jit(solution)/shard_map/ppermute | solution.py:61
  118.2 2.0 %collective-permute-done.12.refs_6_ = bf16[4,32,768]{2,1,0:T(8,128)(2,1)S(1)} collective-permute-done((bf16[4,32,768]{2,1,0:T(8,128)(2,1)S(1)}, bf16[4,32,768]{2,1,0:T(8,128)(2,1)S(1)}, u32[]{:S(2)}, u32[]{:S(2)}) %collective-permute-start.12) | collective-permute-done | bytes 196640 | tf_op jit(solution)/shard_map/ppermute | solution.py:61
  120.2 1.1 collective-permute-done.13.refs_7_
  121.2 2.7 %shard_map.112 = bf16[256,4,768]{2,1,0:T(4,128)(2,1)} custom-call(f32[1,256]{1,0:T(1,128)S(1)} %get-tuple-element.34.keys_ref, bf16[4,32,768]{2,1,0:T(8,128)(2,1)S(1)} %get-tuple-element.47.refs_0_, bf16[4,32,768]{2,1,0:T(8,128)(2,1)S(1)} %collective-permute-done.4.refs_1_, bf16[4,32,768]{2,1,0:T(8,128)(2,1)S(1)} %collective-permute-done.5.refs_2_, ...), custom_call_target="tpu_custom_call" | custom-call | flops 402653184 | bytes 3145728 | tf_op jit(solution)/shard_map/pallas_call | solution.py:452
  (37 shorter events, 3.6 us)
Async XLA Ops:
  0.0 1.4 %copy-start.1 = (bf16[256,4,768]{2,1,0:T(4,128)(2,1)S(1)}, bf16[256,4,768]{2,1,0:T(4,128)(2,1)}, u32[]{:S(2)}) copy-start(bf16[256,4,768]{2,1,0:T(4,128)(2,1)} %x_ref.1) | copy-start | bytes 4718596
  1.4 0.7 copy-start.10
  2.1 27.6 %copy-start.4 = (f32[16,768]{1,0:T(8,128)S(1)}, f32[16,768]{1,0:T(8,128)}, u32[]{:S(2)}) copy-start(f32[16,768]{1,0:T(8,128)} %table_ref.11) | copy-start | bytes 147460
  3.4 11.4 %collective-permute-start = (bf16[128,768]{1,0:T(8,128)(2,1)S(1)}, bf16[128,768]{1,0:T(8,128)(2,1)S(1)}, u32[]{:S(2)}, u32[]{:S(2)}) collective-permute-start(bf16[128,768]{1,0:T(8,128)(2,1)S(1)} %get-tuple-element.36), channel_id=1, source_target_pairs={{0,2},{1,3},{2,0},{3,1},{4,6},{5,7},{6,4},{7,5},{8,10},{9,11},{10,... | collective-permute-start | bytes 589832 | tf_op jit(solution)/shard_map/ppermute | solution.py:61
  6.5 17.2 %collective-permute-start.1 = (bf16[128,768]{1,0:T(8,128)(2,1)S(1)}, bf16[128,768]{1,0:T(8,128)(2,1)S(1)}, u32[]{:S(2)}, u32[]{:S(2)}) collective-permute-start(bf16[128,768]{1,0:T(8,128)(2,1)S(1)} %get-tuple-element.37), channel_id=1, source_target_pairs={{0,4},{1,5},{2,6},{3,7},{4,0},{5,1},{6,2},{7,3},{8,12},{9,13},{10,... | collective-permute-start | bytes 589832 | tf_op jit(solution)/shard_map/ppermute | solution.py:61
  9.1 14.6 %collective-permute-start.2 = (bf16[128,768]{1,0:T(8,128)(2,1)S(1)}, bf16[128,768]{1,0:T(8,128)(2,1)S(1)}, u32[]{:S(2)}, u32[]{:S(2)}) collective-permute-start(bf16[128,768]{1,0:T(8,128)(2,1)S(1)} %get-tuple-element.38), channel_id=1, source_target_pairs={{0,6},{1,7},{2,4},{3,5},{4,2},{5,3},{6,0},{7,1},{8,14},{9,15},{10,... | collective-permute-start | bytes 589832 | tf_op jit(solution)/shard_map/ppermute | solution.py:61
  14.8 14.9 %copy-start = (bf16[768,2304]{1,0:T(8,128)(2,1)S(1)}, bf16[768,2304]{1,0:T(8,128)(2,1)}, u32[]{:S(2)}) copy-start(bf16[768,2304]{1,0:T(8,128)(2,1)} %w_ref.10) | copy-start | bytes 10616836
  14.8 14.9 %copy-start.11 = (s32[16]{0:T(128)S(1)}, s32[16]{0:T(128)}, u32[]{:S(2)}) copy-start(s32[16]{0:T(128)} %index_ref.11) | copy-start | bytes 196
  16.5 11.8 %copy-start.8 = (bf16[128,768]{1,0:T(8,128)(2,1)}, bf16[128,768]{1,0:T(8,128)(2,1)S(1)}, u32[]{:S(2)}) copy-start(bf16[128,768]{1,0:T(8,128)(2,1)S(1)} %get-tuple-element.41.refs_4_.refs_0_) | copy-start | bytes 589828
  23.7 8.8 %collective-permute-start.3 = (bf16[512,768]{1,0:T(8,128)(2,1)S(1)}, bf16[512,768]{1,0:T(8,128)(2,1)S(1)}, u32[]{:S(2)}, u32[]{:S(2)}) collective-permute-start(bf16[512,768]{1,0:T(8,128)(2,1)S(1)} %shard_map.102.x_ref), channel_id=1, source_target_pairs={{0,1},{1,0},{2,3},{3,2},{4,5},{5,4},{6,7},{7,6},{8,9},{9,8},{10,11... | collective-permute-start | bytes 2359304 | tf_op jit(solution)/shard_map/ppermute | solution.py:61
  23.8 27.0 %collective-permute-start.7 = (bf16[128,768]{1,0:T(8,128)(2,1)}, bf16[128,768]{1,0:T(8,128)(2,1)}, u32[]{:S(2)}, u32[]{:S(2)}) collective-permute-start(bf16[128,768]{1,0:T(8,128)(2,1)} %get-tuple-element.51), channel_id=1, source_target_pairs={{0,2},{1,3},{2,0},{3,1},{4,6},{5,7},{6,4},{7,5},{8,10},{9,11},{10,... | collective-permute-start | bytes 589832 | tf_op jit(solution)/shard_map/ppermute | solution.py:61
  27.2 23.6 %collective-permute-start.8 = (bf16[128,768]{1,0:T(8,128)(2,1)}, bf16[128,768]{1,0:T(8,128)(2,1)}, u32[]{:S(2)}, u32[]{:S(2)}) collective-permute-start(bf16[128,768]{1,0:T(8,128)(2,1)} %get-tuple-element.52), channel_id=1, source_target_pairs={{0,4},{1,5},{2,6},{3,7},{4,0},{5,1},{6,2},{7,3},{8,12},{9,13},{10,... | collective-permute-start | bytes 589832 | tf_op jit(solution)/shard_map/ppermute | solution.py:61
  28.3 22.5 %collective-permute-start.9 = (bf16[128,768]{1,0:T(8,128)(2,1)}, bf16[128,768]{1,0:T(8,128)(2,1)}, u32[]{:S(2)}, u32[]{:S(2)}) collective-permute-start(bf16[128,768]{1,0:T(8,128)(2,1)} %get-tuple-element.53), channel_id=1, source_target_pairs={{0,6},{1,7},{2,4},{3,5},{4,2},{5,3},{6,0},{7,1},{8,14},{9,15},{10,... | collective-permute-start | bytes 589832 | tf_op jit(solution)/shard_map/ppermute | solution.py:61
  32.5 2.2 %copy-start.2 = (bf16[768,768]{1,0:T(8,128)(2,1)S(1)}, bf16[768,768]{1,0:T(8,128)(2,1)}, u32[]{:S(2)}) copy-start(bf16[768,768]{1,0:T(8,128)(2,1)} %w_ref.11) | copy-start | bytes 3538948
  44.1 0.9 copy-start.6
  45.0 25.5 %all-to-all-start = ((bf16[16,32,768]{2,1,0:T(8,128)(2,1)}), bf16[16,32,768]{2,1,0:T(8,128)(2,1)}, u32[]{:S(2)}, u32[]{:S(2)}) async-start(bf16[16,32,768]{2,1,0:T(8,128)(2,1)} %bitcast.5), calls=%async_computation | async-start | bytes 1572864 | tf_op jit(solution)/shard_map/all_to_all | solution.py:512
  50.8 3.4 %copy-start.5 = (f32[16,768]{1,0:T(8,128)S(1)}, f32[16,768]{1,0:T(8,128)}, u32[]{:S(2)}) copy-start(f32[16,768]{1,0:T(8,128)} %table_ref.11) | copy-start | bytes 147460
  50.8 1.2 copy-start.7
  52.0 0.9 copy-start.9
  54.1 2.9 %collective-permute-start.10 = (bf16[512,768]{1,0:T(8,128)(2,1)S(1)}, bf16[512,768]{1,0:T(8,128)(2,1)S(1)}, u32[]{:S(2)}, u32[]{:S(2)}) collective-permute-start(bf16[512,768]{1,0:T(8,128)(2,1)S(1)} %shard_map.107.x_ref), channel_id=1, source_target_pairs={{0,1},{1,0},{2,3},{3,2},{4,5},{5,4},{6,7},{7,6},{8,9},{9,8},{10,11... | collective-permute-start | bytes 2359304 | tf_op jit(solution)/shard_map/ppermute | solution.py:61
  57.0 2.2 %copy-start.3 = (bf16[768,768]{1,0:T(8,128)(2,1)S(1)}, bf16[768,768]{1,0:T(8,128)(2,1)}, u32[]{:S(2)}) copy-start(bf16[768,768]{1,0:T(8,128)(2,1)} %w_ref.11) | copy-start | bytes 3538948
  70.5 26.0 %all-to-all-start.1 = ((bf16[16,32,768]{2,1,0:T(8,128)(2,1)}), bf16[16,32,768]{2,1,0:T(8,128)(2,1)S(1)}, u32[]{:S(2)}, u32[]{:S(2)}) async-start(bf16[16,32,768]{2,1,0:T(8,128)(2,1)} %bitcast.3), calls=%async_computation.1 | async-start | bytes 1572864 | tf_op jit(solution)/shard_map/all_to_all | solution.py:512
  91.7 21.2 %collective-permute-start.4 = (bf16[4,32,768]{2,1,0:T(8,128)(2,1)S(1)}, bf16[4,32,768]{2,1,0:T(8,128)(2,1)S(1)}, u32[]{:S(2)}, u32[]{:S(2)}) collective-permute-start(bf16[4,32,768]{2,1,0:T(8,128)(2,1)S(1)} %get-tuple-element.48), channel_id=1, source_target_pairs={{0,8},{8,0},{16,24},{24,16},{1,9},{9,1},{17,25},{25,17},{2,10},{10... | collective-permute-start | bytes 589832 | tf_op jit(solution)/shard_map/ppermute | solution.py:61
  93.7 20.5 %collective-permute-start.5 = (bf16[4,32,768]{2,1,0:T(8,128)(2,1)S(1)}, bf16[4,32,768]{2,1,0:T(8,128)(2,1)S(1)}, u32[]{:S(2)}, u32[]{:S(2)}) collective-permute-start(bf16[4,32,768]{2,1,0:T(8,128)(2,1)S(1)} %get-tuple-element.49), channel_id=1, source_target_pairs={{0,16},{8,24},{16,0},{24,8},{1,17},{9,25},{17,1},{25,9},{2,18},{10... | collective-permute-start | bytes 589832 | tf_op jit(solution)/shard_map/ppermute | solution.py:61
  95.2 19.1 %collective-permute-start.6 = (bf16[4,32,768]{2,1,0:T(8,128)(2,1)S(1)}, bf16[4,32,768]{2,1,0:T(8,128)(2,1)S(1)}, u32[]{:S(2)}, u32[]{:S(2)}) collective-permute-start(bf16[4,32,768]{2,1,0:T(8,128)(2,1)S(1)} %get-tuple-element.50), channel_id=1, source_target_pairs={{0,24},{8,16},{16,8},{24,0},{1,25},{9,17},{17,9},{25,1},{2,26},{10... | collective-permute-start | bytes 589832 | tf_op jit(solution)/shard_map/ppermute | solution.py:61
  110.7 7.5 %collective-permute-start.11 = (bf16[4,32,768]{2,1,0:T(8,128)(2,1)S(1)}, bf16[4,32,768]{2,1,0:T(8,128)(2,1)S(1)}, u32[]{:S(2)}, u32[]{:S(2)}) collective-permute-start(bf16[4,32,768]{2,1,0:T(8,128)(2,1)S(1)} %get-tuple-element.60), channel_id=1, source_target_pairs={{0,8},{8,0},{16,24},{24,16},{1,9},{9,1},{17,25},{25,17},{2,10},{10... | collective-permute-start | bytes 589832 | tf_op jit(solution)/shard_map/ppermute | solution.py:61
  111.4 8.8 %collective-permute-start.12 = (bf16[4,32,768]{2,1,0:T(8,128)(2,1)S(1)}, bf16[4,32,768]{2,1,0:T(8,128)(2,1)S(1)}, u32[]{:S(2)}, u32[]{:S(2)}) collective-permute-start(bf16[4,32,768]{2,1,0:T(8,128)(2,1)S(1)} %get-tuple-element.61), channel_id=1, source_target_pairs={{0,16},{8,24},{16,0},{24,8},{1,17},{9,25},{17,1},{25,9},{2,18},{10... | collective-permute-start | bytes 589832 | tf_op jit(solution)/shard_map/ppermute | solution.py:61
  112.9 8.4 %collective-permute-start.13 = (bf16[4,32,768]{2,1,0:T(8,128)(2,1)S(1)}, bf16[4,32,768]{2,1,0:T(8,128)(2,1)S(1)}, u32[]{:S(2)}, u32[]{:S(2)}) collective-permute-start(bf16[4,32,768]{2,1,0:T(8,128)(2,1)S(1)} %get-tuple-element.62), channel_id=1, source_target_pairs={{0,24},{8,16},{16,8},{24,0},{1,25},{9,17},{17,9},{25,1},{2,26},{10... | collective-permute-start | bytes 589832 | tf_op jit(solution)/shard_map/ppermute | solution.py:61

commit v8 on v7

--- a/solution.py
+++ b/solution.py
@@ -156,17 +156,29 @@
 
 
 def join_slots(plan, slots, after, flops):
+    count, rows = len(slots), plan.rows
+
     def kernel(*refs):
-        for slot in range(len(slots)):
-            refs[-1][pl.ds(slot * plan.rows, plan.rows), :] = refs[slot][...]
-
-    return call(
-        kernel,
-        jax.ShapeDtypeStruct((len(slots) * plan.rows, plan.width), BF16),
+        out_ref, sems = refs[-2:]
+        copies = [
+            pltpu.make_async_copy(
+                refs[slot], out_ref.at[pl.ds(slot * rows, rows), :], sems.at[slot]
+            )
+            for slot in range(count)
+        ]
+        for copy in copies:
+            copy.start()
+        for copy in copies:
+            copy.wait()
+
+    return call(
+        kernel,
+        jax.ShapeDtypeStruct((count * rows, plan.width), BF16),
         flops,
-        4 * len(slots) * plan.rows * plan.width,
-        in_specs=[VMEM] * len(slots) + [ANY] * len(after),
+        0,
+        in_specs=[ANY] * (count + len(after)),
         out_specs=VMEM,
+        scratch_shapes=[pltpu.SemaphoreType.DMA((count,))],
     )(*slots, *after)
 
 
@@ -193,28 +205,33 @@
 
 
 def project(plan, tokens, index, table, weights, queries, hide, after=()):
-    rows, width = tokens.shape
-    tile = min(rows, ROW_TILE)
+    width = plan.width
+    rows = sum(piece.shape[0] for piece in tokens)
     names = range(3) if queries else range(1, 3)
 
-    def kernel(index_ref, table_ref, w_ref, x_ref, *rest):
-        outs = rest[len(after) :]
+    def kernel(index_ref, table_ref, w_ref, *rest):
+        x_refs, outs = rest[: len(tokens)], rest[len(tokens) + len(after) :]
         embed = embed_row(plan, index_ref, table_ref)
-        for first in range(0, rows, tile):
-            here = pl.ds(first, tile)
-            normed = norm_rows(x_ref[here, :].astype(F32) + embed).astype(BF16)
-            for ref, name in zip(outs, names):
-                value = dot(normed, w_ref[:, name * width : (name + 1) * width])
-                ref[here, :] = (value * QUERY_SCALE if name == 0 else value).astype(BF16)
+        at = 0
+        for x_ref in x_refs:
+            count = x_ref.shape[0]
+            tile = min(count, ROW_TILE)
+            for first in range(0, count, tile):
+                normed = norm_rows(x_ref[pl.ds(first, tile), :].astype(F32) + embed).astype(BF16)
+                here = pl.ds(at + first, tile)
+                for ref, name in zip(outs, names):
+                    value = dot(normed, w_ref[:, name * width : (name + 1) * width])
+                    ref[here, :] = (value * QUERY_SCALE if name == 0 else value).astype(BF16)
+            at += count
 
     return call(
         kernel,
         [jax.ShapeDtypeStruct((rows, width), BF16)] * len(names),
         hide * 2 * rows * width * len(names) * width,
         hide * 2 * ((1 + len(names)) * rows * width + 3 * width * width),
-        in_specs=[SMEM, VMEM, VMEM, VMEM] + [ANY] * len(after),
+        in_specs=[SMEM, VMEM, VMEM] + [VMEM] * len(tokens) + [ANY] * len(after),
         out_specs=[VMEM] * len(names),
-    )(index, table, weights, tokens, *after)
+    )(index, table, weights, *tokens, *after)
 
 
 def head_masks(rows):
@@ -270,13 +287,15 @@
 
 
 def attend(plan, query, keys, values, tokens, index, table, spatial_out, hide):
-    total, width = query.shape
-    rows = plan.rows
-    pieces = len(keys)
+    width, rows = plan.width, plan.rows
+    pieces, sources = len(keys), len(query)
+    counts = [piece.shape[0] for piece in query]
+    total = sum(counts)
     pairs = width // LANES
-    unit = min(total, UNIT_ROWS)
-
-    def kernel(index_ref, table_ref, w_ref, x_ref, q_ref, *rest):
+
+    def kernel(index_ref, table_ref, w_ref, *rest):
+        x_refs, rest = rest[:sources], rest[sources:]
+        q_refs, rest = rest[:sources], rest[sources:]
         k_refs, rest = rest[:pieces], rest[pieces:]
         v_refs, (out_ref, result, added) = rest[:pieces], rest[pieces:]
 
@@ -286,10 +305,14 @@
                 here = aligned(number * STEP_PAIRS + i, LANES)
                 pair_keys = [ref[:, here] for ref in k_refs]
                 pair_values = [with_ones(ref[:, here]) for ref in v_refs]
-                for first in range(0, total, unit):
-                    place = (pl.ds(first, unit), here)
-                    units.append((stack_heads(q_ref[place]), pair_keys, pair_values))
-                    places.append(place)
+                at = 0
+                for ref, count in zip(q_refs, counts):
+                    unit = min(count, UNIT_ROWS)
+                    for first in range(0, count, unit):
+                        query_rows = ref[pl.ds(first, unit), here]
+                        units.append((stack_heads(query_rows), pair_keys, pair_values))
+                        places.append((pl.ds(at + first, unit), here))
+                    at += count
             for place, done in zip(places, run_units(units)):
                 result[place] = done
 
@@ -297,12 +320,15 @@
         added[...] = dot(result[...], w_ref[...])
         embed = embed_row(plan, index_ref, table_ref)
         row = lax.axis_index("loc") // CORES
-        for slot in range(plan.rows_count):
-            here = pl.ds(slot * rows, rows)
-            mid = (x_ref[here, :].astype(F32) + embed + added[here, :]).astype(BF16)
-            for owner in range(plan.groups):
-                part = mid[owner * plan.part_rows : (owner + 1) * plan.part_rows]
-                out_ref[row ^ slot, owner] = part
+        slot = 0
+        for ref, count in zip(x_refs, counts):
+            for first in range(0, count, rows):
+                start = ref[pl.ds(first, rows), :].astype(F32) + embed
+                mid = (start + added[pl.ds(slot * rows, rows), :]).astype(BF16)
+                for owner in range(plan.groups):
+                    part = mid[owner * plan.part_rows : (owner + 1) * plan.part_rows]
+                    out_ref[row ^ slot, owner] = part
+                slot += 1
 
     key_rows = sum(piece.shape[0] for piece in keys)
     return call(
@@ -310,10 +336,10 @@
         jax.ShapeDtypeStruct((plan.rows_count, plan.groups, plan.part_rows, width), BF16),
         hide * 16 * total * key_rows * width,
         hide * 2 * width * (2 * key_rows + 3 * total + width),
-        in_specs=[SMEM] + [VMEM] * (4 + 2 * pieces),
+        in_specs=[SMEM] + [VMEM] * (2 + 2 * sources + 2 * pieces),
         out_specs=VMEM,
         scratch_shapes=[pltpu.VMEM((total, width), BF16), pltpu.VMEM((total, width), F32)],
-    )(index, table, spatial_out, tokens, query, *keys, *values)
+    )(index, table, spatial_out, *tokens, *query, *keys, *values)
 
 
 def channel(plan, parts, channel_qkv, channel_out, up_weight, down_weight):
@@ -344,7 +370,7 @@
                         source.at[spot], target.at[spot], sems.at[len(copies)]
                     )
                 )
-        for copy in copies:
+        for copy in copies[: len(columns)]:
             copy.start()
         pieces = [
             (owner, band, first)
@@ -367,6 +393,7 @@
 
         for number, here in enumerate(columns):
             copies[number].wait()
+            copies[number + len(columns)].start()
             factor = QUERY_SCALE if number == 0 else 1.0
             packed[:, here] = (dot(normed[...], qkv_ref[:, here]) * factor).astype(BF16)
         pairs = width // LANES
@@ -471,7 +498,7 @@
 ):
     plan = Plan(tokens)
     ids = window_ids.reshape(-1, LANES)
-    *sent, rows, keys, place_keys = arrange_first(plan, tokens, ids)
+    *sent, rows, location_key, place_keys = arrange_first(plan, tokens, ids)
     arrived = [[exchange(value, "loc", CORES * step) for step, value in enumerate(sent)]]
     following = []
     for window in range(1, WINDOWS):
@@ -479,27 +506,34 @@
         arrived.append(
             [exchange(value, "loc", CORES * step) for step, value in enumerate(following)]
         )
-    mids, behind = [], following[:1]
+    mids, behind = [], []
     for window, slots in enumerate(arrived):
         hide = int(window == 0)
-        own = join_slots(plan, slots, behind, 0 if hide else LONG)
+        half = len(slots) // 2 if hide and plan.share == 1 else len(slots)
+        owns, queries, all_keys, all_values = [], [], [], []
+        tables = (band_index, band_table, spatial_qkv)
+        for first in range(0, len(slots), half):
+            if first > 0:
+                behind = [*following[:1], queries[-1]]
+            own = join_slots(plan, slots[first : first + half], behind, 0 if hide else LONG)
+            query, keys, values = project(plan, [own], *tables, True, hide)
+            owns.append(own)
+            queries.append(query)
+            all_keys.append(keys)
+            all_values.append(values)
         if plan.share == 1:
-            other = exchange(own, "loc", 1)
-            query, *mine = project(plan, own, band_index, band_table, spatial_qkv, True, hide)
-            theirs = project(
-                plan, other, band_index, band_table, spatial_qkv, False, hide, mine[:1]
-            )
-            all_keys, all_values = zip(mine, theirs)
+            others = [exchange(own, "loc", 1) for own in owns]
+            keys, values = project(plan, others, *tables, False, hide, queries[-1:])
+            all_keys.append(keys)
+            all_values.append(values)
         else:
             step = CORES * plan.share
             same = [list(range(at, at + step)) for at in range(0, plan.locs, step)]
-            every = lax.all_gather(own, "loc", axis_index_groups=same, tiled=True)
-            query, _, _ = project(plan, own, band_index, band_table, spatial_qkv, True, hide)
-            all_keys, all_values = zip(
-                project(plan, every, band_index, band_table, spatial_qkv, False, hide)
-            )
+            every = lax.all_gather(owns[0], "loc", axis_index_groups=same, tiled=True)
+            keys, values = project(plan, [every], *tables, False, hide)
+            all_keys, all_values = [keys], [values]
         mid = attend(
-            plan, query, all_keys, all_values, own, band_index, band_table, spatial_out, hide
+            plan, queries, all_keys, all_values, owns, band_index, band_table, spatial_out, hide
         )
         behind = [mid]
         mids.append(mid)
@@ -521,7 +555,7 @@
         parts = parts.transpose(0, 2, 1, 3, 4).reshape(plan.band_dev, plan.groups, -1, plan.width)
         done = channel(plan, parts, channel_qkv, channel_out, up_weight, down_weight)
         returned.append([exchange(value, "band", step) for step, value in enumerate(done)])
-    return restore(plan, keys, returned)
+    return restore(plan, location_key, returned)
 
 
 def solution(mesh):

time: 124 us -> 124 us (level)
  waiting for transfers between devices: 22.2 us -> 19.5 us
  Pallas kernels: 66 us -> 68 us
    ppermute x14 -> x15, waiting for transfers between devices: 19.9 us -> 17.4 us  [exchange(): lax.ppermute(value, axis, [(i, i ^ step) for i in range(lax.axis_size(axi...]
    pallas_call x4 -> x5, Pallas kernels: 9.92 us -> 10.8 us  [project(): call(kernel, [jax.ShapeDtypeStruct((rows, width), BF16)] * len(names), hi...]
    ppermute x14 -> x15, starting transfers between devices: 18.8 us -> 18.9 us  [exchange(): lax.ppermute(value, axis, [(i, i ^ step) for i in range(lax.axis_size(axi...]
  transfers between devices with their start and end apart: 16 -> 17, of which waited for: 7 -> 7; matrix products, arithmetic and copies ran while one was open for 0% -> 0% of each run, Pallas kernels for 50% -> 52%
where the time goes in v8:
time: 124 us
  Pallas kernels  68 us (55%)
  starting transfers between devices  30.7 us (25%)
  waiting for transfers between devices  19.5 us (16%)
  local copies, waits for them, and re-layouts  5.09 us (4%)
    pallas_call x2, Pallas kernels, channel(): call(kernel, [jax.ShapeDtypeStruct((bands, locations, width), BF16)] * gr...  29.4 us
    pallas_call x2, Pallas kernels, attend(): call(kernel, jax.ShapeDtypeStruct((plan.rows_count, plan.groups, plan.par...  19.8 us
    ppermute x15, starting transfers between devices, exchange(): lax.ppermute(value, axis, [(i, i ^ step) for i in range(lax.axis_size(axi...  18.9 us
    ppermute x15, waiting for transfers between devices, exchange(): lax.ppermute(value, axis, [(i, i ^ step) for i in range(lax.axis_size(axi...  17.4 us
    all_to_all x2, starting transfers between devices, body(): lax.all_to_all(mid.reshape(-1, plan.part_rows, plan.width), ('band', 'loc...  11.8 us
    pallas_call x5, Pallas kernels, project(): call(kernel, [jax.ShapeDtypeStruct((rows, width), BF16)] * len(names), hi...  10.8 us
    unnamed x24, local copies, waits for them, and re-layouts  5.09 us
    pallas_call x1, Pallas kernels, restore(): call(kernel, jax.ShapeDtypeStruct((plan.loc_dev, plan.band_dev, plan.widt...  2.65 us
  transfers between devices with their start and end apart: 17, of which 7 were waited for; matrix products, arithmetic and copies ran while one was open for 0% of the time, Pallas kernels for 52%

profile of v8, /device:TPU:0, one launch (start us, length us, event | category | flops | bytes accessed | tf_op | source)
XLA Modules:
  0.0 123.6 jit_solution(16152879194702023786)
XLA Ops:
  0.0 1.4 %copy-done.3 = bf16[256,4,768]{2,1,0:T(4,128)(2,1)S(1)} copy-done((bf16[256,4,768]{2,1,0:T(4,128)(2,1)S(1)}, bf16[256,4,768]{2,1,0:T(4,128)(2,1)}, u32[]{:S(2)}) %copy-start.3) | copy-done | bytes 1572888
  2.1 1.3 %shard_map.100 = (bf16[128,768]{1,0:T(8,128)(2,1)S(1)}, bf16[128,768]{1,0:T(8,128)(2,1)S(1)}, bf16[128,768]{1,0:T(8,128)(2,1)S(1)}, bf16[128,768]{1,0:T(8,128)(2...) custom-call(s32[16,128]{1,0:T(8,128)S(1)} %bitcast.7, ...), custom_call_target="tpu_custom_call" | custom-call | flops 402653184 | bytes 3145728 | tf_op jit(solution)/shard_map/pallas_call | solution.py:127
  3.4 3.1 %collective-permute-start = (bf16[128,768]{1,0:T(8,128)(2,1)S(1)}, bf16[128,768]{1,0:T(8,128)(2,1)S(1)}, u32[]{:S(2)}, u32[]{:S(2)}) collective-permute-start(bf16[128,768]{1,0:T(8,128)(2,1)S(1)} %get-tuple-element.39), channel_id=1, source_target_pairs={{0,2},{1,3},{2,0},{3,1},{4,6},{5,7},{6,4},{7,5},{8,10},{9,11},{10,... | collective-permute-start | bytes 589832 | tf_op jit(solution)/shard_map/ppermute | solution.py:61
  6.5 2.6 %collective-permute-start.1 = (bf16[128,768]{1,0:T(8,128)(2,1)S(1)}, bf16[128,768]{1,0:T(8,128)(2,1)S(1)}, u32[]{:S(2)}, u32[]{:S(2)}) collective-permute-start(bf16[128,768]{1,0:T(8,128)(2,1)S(1)} %get-tuple-element.40), channel_id=1, source_target_pairs={{0,4},{1,5},{2,6},{3,7},{4,0},{5,1},{6,2},{7,3},{8,12},{9,13},{10,... | collective-permute-start | bytes 589832 | tf_op jit(solution)/shard_map/ppermute | solution.py:61
  9.1 5.7 %collective-permute-done.refs_1_.rest_0_ = bf16[128,768]{1,0:T(8,128)(2,1)S(1)} collective-permute-done((bf16[128,768]{1,0:T(8,128)(2,1)S(1)}, bf16[128,768]{1,0:T(8,128)(2,1)S(1)}, u32[]{:S(2)}, u32[]{:S(2)}) %collective-permute-start) | collective-permute-done | bytes 196640 | tf_op jit(solution)/shard_map/ppermute | solution.py:61
  15.4 1.7 %shard_map.102 = (bf16[128,768]{1,0:T(8,128)(2,1)S(1)}, bf16[128,768]{1,0:T(8,128)(2,1)}, bf16[128,768]{1,0:T(8,128)(2,1)}, bf16[128,768]{1,0:T(8,128)(2,1)}) custom-call(bf16[1024,768]{1,0:T(8,128)(2,1)S(1)} %get-tuple-element.42.rows_ref, f32[1,1024]{1,0:T(1,128)S(1)} %get-tuple-element.43.place_ref, bf16[128,768]{1,0:T(8,128)(2,1)S(1)} %collective-permute-done.refs_1_.rest_0_), custom_call_target="tpu_custom_call" | custom-call | flops 402653184 | bytes 3145728 | tf_op jit(solution)/shard_map/pallas_call | solution.py:148
  17.1 1.8 %shard_map.103 = (bf16[256,768]{1,0:T(8,128)(2,1)S(1)}, bf16[256,768]{1,0:T(8,128)(2,1)S(1)}, bf16[256,768]{1,0:T(8,128)(2,1)S(1)}) custom-call(s32[16]{0:T(128)S(1)} %copy-done.10, f32[16,768]{1,0:T(8,128)S(1)} %copy-done.1, bf16[768,2304]{1,0:T(8,128)(2,1)S(1)} %copy-done, bf16[256,768]{1,0:T(8,128)(2,1)S(1)} %shard_map.101.rest_0_), custom_call_target="tpu_custom_call" | custom-call | flops 905969664 | bytes 5111808 | tf_op jit(solution)/shard_map/pallas_call | solution.py:227
  19.0 4.7 %collective-permute-done.1.refs_0_ = bf16[128,768]{1,0:T(8,128)(2,1)S(1)} collective-permute-done((bf16[128,768]{1,0:T(8,128)(2,1)S(1)}, bf16[128,768]{1,0:T(8,128)(2,1)S(1)}, u32[]{:S(2)}, u32[]{:S(2)}) %collective-permute-start.1) | collective-permute-done | bytes 196640 | tf_op jit(solution)/shard_map/ppermute | solution.py:61
  24.3 3.4 %collective-permute-start.8 = (bf16[128,768]{1,0:T(8,128)(2,1)}, bf16[128,768]{1,0:T(8,128)(2,1)}, u32[]{:S(2)}, u32[]{:S(2)}) collective-permute-start(bf16[128,768]{1,0:T(8,128)(2,1)} %get-tuple-element.57), channel_id=1, source_target_pairs={{0,2},{1,3},{2,0},{3,1},{4,6},{5,7},{6,4},{7,5},{8,10},{9,11},{10,... | collective-permute-start | bytes 589832 | tf_op jit(solution)/shard_map/ppermute | solution.py:61
  27.7 1.1 collective-permute-start.9
  28.8 1.4 %collective-permute-start.10 = (bf16[128,768]{1,0:T(8,128)(2,1)}, bf16[128,768]{1,0:T(8,128)(2,1)}, u32[]{:S(2)}, u32[]{:S(2)}) collective-permute-start(bf16[128,768]{1,0:T(8,128)(2,1)} %get-tuple-element.59), channel_id=1, source_target_pairs={{0,6},{1,7},{2,4},{3,5},{4,2},{5,3},{6,0},{7,1},{8,14},{9,15},{10,... | collective-permute-start | bytes 589832 | tf_op jit(solution)/shard_map/ppermute | solution.py:61
  30.1 1.8 %shard_map.105 = (bf16[256,768]{1,0:T(8,128)(2,1)S(1)}, bf16[256,768]{1,0:T(8,128)(2,1)S(1)}, bf16[256,768]{1,0:T(8,128)(2,1)S(1)}) custom-call(s32[16]{0:T(128)S(1)} %copy-done.10, f32[16,768]{1,0:T(8,128)S(1)} %copy-done.1, bf16[768,2304]{1,0:T(8,128)(2,1)S(1)} %copy-done, bf16[256,768]{1,0:T(8,128)(2,1)S(1)} %shard_map.104.rest_0_.rest_1_), custom_call_target="tpu_custom_call" | custom-call | flops 905969664 | bytes 5111808 | tf_op jit(solution)/shard_map/pallas_call | solution.py:227
  32.0 2.2 %shard_map.106 = (bf16[512,768]{1,0:T(8,128)(2,1)S(1)}, bf16[512,768]{1,0:T(8,128)(2,1)S(1)}) custom-call(s32[16]{0:T(128)S(1)} %copy-done.10, f32[16,768]{1,0:T(8,128)S(1)} %copy-done.1, bf16[768,2304]{1,0:T(8,128)(2,1)S(1)} %copy-done, bf16[256,768]{1,0:T(8,128)(2,1)S(1)} %collective-permute-done.3.rest_0_, ...), custom_call_target="tpu_custom_call" | custom-call | flops 1207959552 | bytes 5898240 | tf_op jit(solution)/shard_map/pallas_call | solution.py:227
  34.2 9.5 %shard_map.107.refs_4_ = bf16[4,4,32,768]{3,2,1,0:T(8,128)(2,1)S(1)} custom-call(s32[16]{0:T(128)S(1)} %copy-done.10, f32[16,768]{1,0:T(8,128)S(1)} %copy-done.1, bf16[768,768]{1,0:T(8,128)(2,1)S(1)} %copy-done.4, bf16[256,768]{1,0:T(8,128)(2,1)S(1)} %shard_map.101.rest_0_, bf16[256,768]{1,0:T(8,128)(2,1)S(1)} %shard_map.104.rest_0_.rest_1_, ...), custom_call_target="tpu_custom_call" | custom-call | flops 6442450944 | bytes 6684672 | tf_op jit(solution)/shard_map/pallas_call | solution.py:334
  44.6 5.8 %all-to-all-start = ((bf16[16,32,768]{2,1,0:T(8,128)(2,1)}), bf16[16,32,768]{2,1,0:T(8,128)(2,1)}, u32[]{:S(2)}, u32[]{:S(2)}) async-start(bf16[16,32,768]{2,1,0:T(8,128)(2,1)} %bitcast.5), calls=%async_computation | async-start | bytes 1572864 | tf_op jit(solution)/shard_map/all_to_all | solution.py:546
  50.4 1.1 copy-done.7
  52.5 1.4 %shard_map.109.rest_0_ = bf16[512,768]{1,0:T(8,128)(2,1)S(1)} custom-call(bf16[128,768]{1,0:T(8,128)(2,1)S(1)} %copy-done.9, bf16[128,768]{1,0:T(8,128)(2,1)} %collective-permute-done.8.refs_1_, bf16[128,768]{1,0:T(8,128)(2,1)} %collective-permute-done.9.refs_2_, bf16[128,768]{1,0:T(8,128)(2,1)} %collective-permute-done.10.refs_3_, ...), custom_call_target="tpu_custom_call" | custom-call | flops 68719476736 | tf_op jit(solution)/shard_map/pallas_call | solution.py:174
  53.9 2.8 %shard_map.110 = (bf16[512,768]{1,0:T(8,128)(2,1)S(1)}, bf16[512,768]{1,0:T(8,128)(2,1)S(1)}, bf16[512,768]{1,0:T(8,128)(2,1)S(1)}) custom-call(s32[16]{0:T(128)S(1)} %copy-done.10, f32[16,768]{1,0:T(8,128)S(1)} %copy-done.2, bf16[768,2304]{1,0:T(8,128)(2,1)S(1)} %copy-done, bf16[512,768]{1,0:T(8,128)(2,1)S(1)} %shard_map.109.rest_0_), custom_call_target="tpu_custom_call" | custom-call | tf_op jit(solution)/shard_map/pallas_call | solution.py:227
  56.7 2.2 %shard_map.111 = (bf16[512,768]{1,0:T(8,128)(2,1)S(1)}, bf16[512,768]{1,0:T(8,128)(2,1)S(1)}) custom-call(s32[16]{0:T(128)S(1)} %copy-done.10, f32[16,768]{1,0:T(8,128)S(1)} %copy-done.2, bf16[768,2304]{1,0:T(8,128)(2,1)S(1)} %copy-done, bf16[512,768]{1,0:T(8,128)(2,1)S(1)} %collective-permute-done.11.rest_0_, bf16[512,768]{1,0:T(8,128)(2,1)S(1)} %get-tuple-element.60.rest_1_), custom_call_target="tpu_custom_call" | custom-call | tf_op jit(solution)/shard_map/pallas_call | solution.py:227
  58.9 10.4 %shard_map.112 = bf16[4,4,32,768]{3,2,1,0:T(8,128)(2,1)} custom-call(s32[16]{0:T(128)S(1)} %copy-done.10, f32[16,768]{1,0:T(8,128)S(1)} %copy-done.2, bf16[768,768]{1,0:T(8,128)(2,1)S(1)} %copy-done.5, bf16[512,768]{1,0:T(8,128)(2,1)S(1)} %shard_map.109.rest_0_, bf16[512,768]{1,0:T(8,128)(2,1)S(1)} %get-tuple-element.60.rest_1_, ...), custom_call_target="tpu_custom_call" | custom-call | tf_op jit(solution)/shard_map/pallas_call | solution.py:334
  70.1 6.1 %all-to-all-start.1 = ((bf16[16,32,768]{2,1,0:T(8,128)(2,1)}), bf16[16,32,768]{2,1,0:T(8,128)(2,1)S(1)}, u32[]{:S(2)}, u32[]{:S(2)}) async-start(bf16[16,32,768]{2,1,0:T(8,128)(2,1)} %bitcast.3), calls=%async_computation.1 | async-start | bytes 1572864 | tf_op jit(solution)/shard_map/all_to_all | solution.py:546
  76.2 15.3 %shard_map.108 = (bf16[4,32,768]{2,1,0:T(8,128)(2,1)S(1)}, bf16[4,32,768]{2,1,0:T(8,128)(2,1)S(1)}, bf16[4,32,768]{2,1,0:T(8,128)(2,1)S(1)}, bf16[4,32,768]{2,1,0:T(8,128)(2,1)S(1)}) custom-call(bf16[768,2304]{1,0:T(8,128)(2,1)} %qkv_hbm.3, bf16[768,768]{1,0:T(8,128)(2,1)} %out_hbm.3, bf16[768,3072]{1,0:T(8,128)(2,1)} %up_hbm.3, bf16[3072,768]{1,0:T(8,128)(2,1)} %down_hbm.3, ...), custom_call_target="tpu_custom_call" | custom-call | flops 7247757312 | bytes 15728640 | tf_op jit(solution)/shard_map/pallas_call | solution.py:441
  91.4 2.0 %collective-permute-start.5 = (bf16[4,32,768]{2,1,0:T(8,128)(2,1)S(1)}, bf16[4,32,768]{2,1,0:T(8,128)(2,1)S(1)}, u32[]{:S(2)}, u32[]{:S(2)}) collective-permute-start(bf16[4,32,768]{2,1,0:T(8,128)(2,1)S(1)} %get-tuple-element.54), channel_id=1, source_target_pairs={{0,8},{8,0},{16,24},{24,16},{1,9},{9,1},{17,25},{25,17},{2,10},{10... | collective-permute-start | bytes 589832 | tf_op jit(solution)/shard_map/ppermute | solution.py:61
  93.4 1.4 %collective-permute-start.6 = (bf16[4,32,768]{2,1,0:T(8,128)(2,1)S(1)}, bf16[4,32,768]{2,1,0:T(8,128)(2,1)S(1)}, u32[]{:S(2)}, u32[]{:S(2)}) collective-permute-start(bf16[4,32,768]{2,1,0:T(8,128)(2,1)S(1)} %get-tuple-element.55), channel_id=1, source_target_pairs={{0,16},{8,24},{16,0},{24,8},{1,17},{9,25},{17,1},{25,9},{2,18},{10... | collective-permute-start | bytes 589832 | tf_op jit(solution)/shard_map/ppermute | solution.py:61
  95.0 1.3 %all-to-all-done.1 = bf16[16,32,768]{2,1,0:T(8,128)(2,1)S(1)} async-done(((bf16[16,32,768]{2,1,0:T(8,128)(2,1)}), bf16[16,32,768]{2,1,0:T(8,128)(2,1)S(1)}, u32[]{:S(2)}, u32[]{:S(2)}) %all-to-all-start.1) | async-done | bytes 786464 | tf_op jit(solution)/shard_map/all_to_all | solution.py:546
  96.3 14.1 %shard_map.113 = (bf16[4,32,768]{2,1,0:T(8,128)(2,1)S(1)}, bf16[4,32,768]{2,1,0:T(8,128)(2,1)S(1)}, bf16[4,32,768]{2,1,0:T(8,128)(2,1)S(1)}, bf16[4,32,768]{2,1,0:T(8,128)(2,1)S(1)}) custom-call(bf16[768,2304]{1,0:T(8,128)(2,1)} %qkv_hbm.3, bf16[768,768]{1,0:T(8,128)(2,1)} %out_hbm.3, bf16[768,3072]{1,0:T(8,128)(2,1)} %up_hbm.3, bf16[3072,768]{1,0:T(8,128)(2,1)} %down_hbm.3, ...), custom_call_target="tpu_custom_call" | custom-call | flops 7247757312 | bytes 15728640 | tf_op jit(solution)/shard_map/pallas_call | solution.py:441
  111.1 1.5 %collective-permute-start.13 = (bf16[4,32,768]{2,1,0:T(8,128)(2,1)S(1)}, bf16[4,32,768]{2,1,0:T(8,128)(2,1)S(1)}, u32[]{:S(2)}, u32[]{:S(2)}) collective-permute-start(bf16[4,32,768]{2,1,0:T(8,128)(2,1)S(1)} %get-tuple-element.67), channel_id=1, source_target_pairs={{0,16},{8,24},{16,0},{24,8},{1,17},{9,25},{17,1},{25,9},{2,18},{10... | collective-permute-start | bytes 589832 | tf_op jit(solution)/shard_map/ppermute | solution.py:61
  112.6 1.3 %collective-permute-start.14 = (bf16[4,32,768]{2,1,0:T(8,128)(2,1)S(1)}, bf16[4,32,768]{2,1,0:T(8,128)(2,1)S(1)}, u32[]{:S(2)}, u32[]{:S(2)}) collective-permute-start(bf16[4,32,768]{2,1,0:T(8,128)(2,1)S(1)} %get-tuple-element.68), channel_id=1, source_target_pairs={{0,24},{8,16},{16,8},{24,0},{1,25},{9,17},{17,9},{25,1},{2,26},{10... | collective-permute-start | bytes 589832 | tf_op jit(solution)/shard_map/ppermute | solution.py:61
  114.0 4.0 %collective-permute-done.12.refs_5_ = bf16[4,32,768]{2,1,0:T(8,128)(2,1)S(1)} collective-permute-done((bf16[4,32,768]{2,1,0:T(8,128)(2,1)S(1)}, bf16[4,32,768]{2,1,0:T(8,128)(2,1)S(1)}, u32[]{:S(2)}, u32[]{:S(2)}) %collective-permute-start.12) | collective-permute-done | bytes 196640 | tf_op jit(solution)/shard_map/ppermute | solution.py:61
  117.9 2.0 %collective-permute-done.13.refs_6_ = bf16[4,32,768]{2,1,0:T(8,128)(2,1)S(1)} collective-permute-done((bf16[4,32,768]{2,1,0:T(8,128)(2,1)S(1)}, bf16[4,32,768]{2,1,0:T(8,128)(2,1)S(1)}, u32[]{:S(2)}, u32[]{:S(2)}) %collective-permute-start.13) | collective-permute-done | bytes 196640 | tf_op jit(solution)/shard_map/ppermute | solution.py:61
  120.0 1.0 collective-permute-done.14.refs_7_
  121.0 2.7 %shard_map.114 = bf16[256,4,768]{2,1,0:T(4,128)(2,1)} custom-call(f32[1,256]{1,0:T(1,128)S(1)} %get-tuple-element.37.keys_ref, bf16[4,32,768]{2,1,0:T(8,128)(2,1)S(1)} %get-tuple-element.53.refs_0_, bf16[4,32,768]{2,1,0:T(8,128)(2,1)S(1)} %collective-permute-done.5.refs_1_, bf16[4,32,768]{2,1,0:T(8,128)(2,1)S(1)} %collective-permute-done.6.refs_2_, ...), custom_call_target="tpu_custom_call" | custom-call | flops 402653184 | bytes 3145728 | tf_op jit(solution)/shard_map/pallas_call | solution.py:479
  (41 shorter events, 5.4 us)
Async XLA Ops:
  0.0 1.4 %copy-start.3 = (bf16[256,4,768]{2,1,0:T(4,128)(2,1)S(1)}, bf16[256,4,768]{2,1,0:T(4,128)(2,1)}, u32[]{:S(2)}) copy-start(bf16[256,4,768]{2,1,0:T(4,128)(2,1)} %x_ref.1) | copy-start | bytes 4718596
  1.4 0.7 copy-start.11
  2.1 15.0 %copy-start = (bf16[768,2304]{1,0:T(8,128)(2,1)S(1)}, bf16[768,2304]{1,0:T(8,128)(2,1)}, u32[]{:S(2)}) copy-start(bf16[768,2304]{1,0:T(8,128)(2,1)} %w_ref.12) | copy-start | bytes 10616836
  3.4 13.7 %copy-start.1 = (f32[16,768]{1,0:T(8,128)S(1)}, f32[16,768]{1,0:T(8,128)}, u32[]{:S(2)}) copy-start(f32[16,768]{1,0:T(8,128)} %table_ref.13) | copy-start | bytes 147460
  3.4 13.7 %copy-start.10 = (s32[16]{0:T(128)S(1)}, s32[16]{0:T(128)}, u32[]{:S(2)}) copy-start(s32[16]{0:T(128)} %index_ref.13) | copy-start | bytes 196
  3.4 11.4 %collective-permute-start = (bf16[128,768]{1,0:T(8,128)(2,1)S(1)}, bf16[128,768]{1,0:T(8,128)(2,1)S(1)}, u32[]{:S(2)}, u32[]{:S(2)}) collective-permute-start(bf16[128,768]{1,0:T(8,128)(2,1)S(1)} %get-tuple-element.39), channel_id=1, source_target_pairs={{0,2},{1,3},{2,0},{3,1},{4,6},{5,7},{6,4},{7,5},{8,10},{9,11},{10,... | collective-permute-start | bytes 589832 | tf_op jit(solution)/shard_map/ppermute | solution.py:61
  6.5 17.2 %collective-permute-start.1 = (bf16[128,768]{1,0:T(8,128)(2,1)S(1)}, bf16[128,768]{1,0:T(8,128)(2,1)S(1)}, u32[]{:S(2)}, u32[]{:S(2)}) collective-permute-start(bf16[128,768]{1,0:T(8,128)(2,1)S(1)} %get-tuple-element.40), channel_id=1, source_target_pairs={{0,4},{1,5},{2,6},{3,7},{4,0},{5,1},{6,2},{7,3},{8,12},{9,13},{10,... | collective-permute-start | bytes 589832 | tf_op jit(solution)/shard_map/ppermute | solution.py:61
  9.1 14.6 %collective-permute-start.2 = (bf16[128,768]{1,0:T(8,128)(2,1)S(1)}, bf16[128,768]{1,0:T(8,128)(2,1)S(1)}, u32[]{:S(2)}, u32[]{:S(2)}) collective-permute-start(bf16[128,768]{1,0:T(8,128)(2,1)S(1)} %get-tuple-element.41), channel_id=1, source_target_pairs={{0,6},{1,7},{2,4},{3,5},{4,2},{5,3},{6,0},{7,1},{8,14},{9,15},{10,... | collective-permute-start | bytes 589832 | tf_op jit(solution)/shard_map/ppermute | solution.py:61
  15.3 16.7 %collective-permute-start.3 = (bf16[256,768]{1,0:T(8,128)(2,1)S(1)}, bf16[256,768]{1,0:T(8,128)(2,1)S(1)}, u32[]{:S(2)}, u32[]{:S(2)}) collective-permute-start(bf16[256,768]{1,0:T(8,128)(2,1)S(1)} %shard_map.101.rest_0_), channel_id=1, source_target_pairs={{0,1},{1,0},{2,3},{3,2},{4,5},{5,4},{6,7},{7,6},{8,9},{9,8},{10,11... | collective-permute-start | bytes 1179656 | tf_op jit(solution)/shard_map/ppermute | solution.py:61
  17.1 6.6 %copy-start.8 = (bf16[128,768]{1,0:T(8,128)(2,1)}, bf16[128,768]{1,0:T(8,128)(2,1)S(1)}, u32[]{:S(2)}) copy-start(bf16[128,768]{1,0:T(8,128)(2,1)S(1)} %get-tuple-element.44.refs_2_.refs_0_) | copy-start | bytes 589828
  24.2 7.8 %collective-permute-start.4 = (bf16[256,768]{1,0:T(8,128)(2,1)S(1)}, bf16[256,768]{1,0:T(8,128)(2,1)S(1)}, u32[]{:S(2)}, u32[]{:S(2)}) collective-permute-start(bf16[256,768]{1,0:T(8,128)(2,1)S(1)} %shard_map.104.rest_0_.rest_1_), channel_id=1, source_target_pairs={{0,1},{1,0},{2,3},{3,2},{4,5},{5,4},{6,7},{7,6},{8,9},{9,8},{10,11... | collective-permute-start | bytes 1179656 | tf_op jit(solution)/shard_map/ppermute | solution.py:61
  24.3 26.1 %collective-permute-start.8 = (bf16[128,768]{1,0:T(8,128)(2,1)}, bf16[128,768]{1,0:T(8,128)(2,1)}, u32[]{:S(2)}, u32[]{:S(2)}) collective-permute-start(bf16[128,768]{1,0:T(8,128)(2,1)} %get-tuple-element.57), channel_id=1, source_target_pairs={{0,2},{1,3},{2,0},{3,1},{4,6},{5,7},{6,4},{7,5},{8,10},{9,11},{10,... | collective-permute-start | bytes 589832 | tf_op jit(solution)/shard_map/ppermute | solution.py:61
  27.7 22.7 %collective-permute-start.9 = (bf16[128,768]{1,0:T(8,128)(2,1)}, bf16[128,768]{1,0:T(8,128)(2,1)}, u32[]{:S(2)}, u32[]{:S(2)}) collective-permute-start(bf16[128,768]{1,0:T(8,128)(2,1)} %get-tuple-element.58), channel_id=1, source_target_pairs={{0,4},{1,5},{2,6},{3,7},{4,0},{5,1},{6,2},{7,3},{8,12},{9,13},{10,... | collective-permute-start | bytes 589832 | tf_op jit(solution)/shard_map/ppermute | solution.py:61
  28.8 21.6 %collective-permute-start.10 = (bf16[128,768]{1,0:T(8,128)(2,1)}, bf16[128,768]{1,0:T(8,128)(2,1)}, u32[]{:S(2)}, u32[]{:S(2)}) collective-permute-start(bf16[128,768]{1,0:T(8,128)(2,1)} %get-tuple-element.59), channel_id=1, source_target_pairs={{0,6},{1,7},{2,4},{3,5},{4,2},{5,3},{6,0},{7,1},{8,14},{9,15},{10,... | collective-permute-start | bytes 589832 | tf_op jit(solution)/shard_map/ppermute | solution.py:61
  32.0 2.2 %copy-start.4 = (bf16[768,768]{1,0:T(8,128)(2,1)S(1)}, bf16[768,768]{1,0:T(8,128)(2,1)}, u32[]{:S(2)}) copy-start(bf16[768,768]{1,0:T(8,128)(2,1)} %w_ref.13) | copy-start | bytes 3538948
  43.7 0.9 copy-start.6
  44.6 25.5 %all-to-all-start = ((bf16[16,32,768]{2,1,0:T(8,128)(2,1)}), bf16[16,32,768]{2,1,0:T(8,128)(2,1)}, u32[]{:S(2)}, u32[]{:S(2)}) async-start(bf16[16,32,768]{2,1,0:T(8,128)(2,1)} %bitcast.5), calls=%async_computation | async-start | bytes 1572864 | tf_op jit(solution)/shard_map/all_to_all | solution.py:546
  50.3 3.6 %copy-start.2 = (f32[16,768]{1,0:T(8,128)S(1)}, f32[16,768]{1,0:T(8,128)}, u32[]{:S(2)}) copy-start(f32[16,768]{1,0:T(8,128)} %table_ref.13) | copy-start | bytes 147460
  50.4 1.2 copy-start.7
  51.5 0.9 copy-start.9
  53.8 2.9 %collective-permute-start.11 = (bf16[512,768]{1,0:T(8,128)(2,1)S(1)}, bf16[512,768]{1,0:T(8,128)(2,1)S(1)}, u32[]{:S(2)}, u32[]{:S(2)}) collective-permute-start(bf16[512,768]{1,0:T(8,128)(2,1)S(1)} %shard_map.109.rest_0_), channel_id=1, source_target_pairs={{0,1},{1,0},{2,3},{3,2},{4,5},{5,4},{6,7},{7,6},{8,9},{9,8},{10,11... | collective-permute-start | bytes 2359304 | tf_op jit(solution)/shard_map/ppermute | solution.py:61
  56.7 2.2 %copy-start.5 = (bf16[768,768]{1,0:T(8,128)(2,1)S(1)}, bf16[768,768]{1,0:T(8,128)(2,1)}, u32[]{:S(2)}) copy-start(bf16[768,768]{1,0:T(8,128)(2,1)} %w_ref.13) | copy-start | bytes 3538948
  70.1 26.2 %all-to-all-start.1 = ((bf16[16,32,768]{2,1,0:T(8,128)(2,1)}), bf16[16,32,768]{2,1,0:T(8,128)(2,1)S(1)}, u32[]{:S(2)}, u32[]{:S(2)}) async-start(bf16[16,32,768]{2,1,0:T(8,128)(2,1)} %bitcast.3), calls=%async_computation.1 | async-start | bytes 1572864 | tf_op jit(solution)/shard_map/all_to_all | solution.py:546
  91.4 21.2 %collective-permute-start.5 = (bf16[4,32,768]{2,1,0:T(8,128)(2,1)S(1)}, bf16[4,32,768]{2,1,0:T(8,128)(2,1)S(1)}, u32[]{:S(2)}, u32[]{:S(2)}) collective-permute-start(bf16[4,32,768]{2,1,0:T(8,128)(2,1)S(1)} %get-tuple-element.54), channel_id=1, source_target_pairs={{0,8},{8,0},{16,24},{24,16},{1,9},{9,1},{17,25},{25,17},{2,10},{10... | collective-permute-start | bytes 589832 | tf_op jit(solution)/shard_map/ppermute | solution.py:61
  93.4 20.5 %collective-permute-start.6 = (bf16[4,32,768]{2,1,0:T(8,128)(2,1)S(1)}, bf16[4,32,768]{2,1,0:T(8,128)(2,1)S(1)}, u32[]{:S(2)}, u32[]{:S(2)}) collective-permute-start(bf16[4,32,768]{2,1,0:T(8,128)(2,1)S(1)} %get-tuple-element.55), channel_id=1, source_target_pairs={{0,16},{8,24},{16,0},{24,8},{1,17},{9,25},{17,1},{25,9},{2,18},{10... | collective-permute-start | bytes 589832 | tf_op jit(solution)/shard_map/ppermute | solution.py:61
  94.9 19.1 %collective-permute-start.7 = (bf16[4,32,768]{2,1,0:T(8,128)(2,1)S(1)}, bf16[4,32,768]{2,1,0:T(8,128)(2,1)S(1)}, u32[]{:S(2)}, u32[]{:S(2)}) collective-permute-start(bf16[4,32,768]{2,1,0:T(8,128)(2,1)S(1)} %get-tuple-element.56), channel_id=1, source_target_pairs={{0,24},{8,16},{16,8},{24,0},{1,25},{9,17},{17,9},{25,1},{2,26},{10... | collective-permute-start | bytes 589832 | tf_op jit(solution)/shard_map/ppermute | solution.py:61
  110.4 7.5 %collective-permute-start.12 = (bf16[4,32,768]{2,1,0:T(8,128)(2,1)S(1)}, bf16[4,32,768]{2,1,0:T(8,128)(2,1)S(1)}, u32[]{:S(2)}, u32[]{:S(2)}) collective-permute-start(bf16[4,32,768]{2,1,0:T(8,128)(2,1)S(1)} %get-tuple-element.66), channel_id=1, source_target_pairs={{0,8},{8,0},{16,24},{24,16},{1,9},{9,1},{17,25},{25,17},{2,10},{10... | collective-permute-start | bytes 589832 | tf_op jit(solution)/shard_map/ppermute | solution.py:61
  111.1 8.8 %collective-permute-start.13 = (bf16[4,32,768]{2,1,0:T(8,128)(2,1)S(1)}, bf16[4,32,768]{2,1,0:T(8,128)(2,1)S(1)}, u32[]{:S(2)}, u32[]{:S(2)}) collective-permute-start(bf16[4,32,768]{2,1,0:T(8,128)(2,1)S(1)} %get-tuple-element.67), channel_id=1, source_target_pairs={{0,16},{8,24},{16,0},{24,8},{1,17},{9,25},{17,1},{25,9},{2,18},{10... | collective-permute-start | bytes 589832 | tf_op jit(solution)/shard_map/ppermute | solution.py:61
  112.6 8.3 %collective-permute-start.14 = (bf16[4,32,768]{2,1,0:T(8,128)(2,1)S(1)}, bf16[4,32,768]{2,1,0:T(8,128)(2,1)S(1)}, u32[]{:S(2)}, u32[]{:S(2)}) collective-permute-start(bf16[4,32,768]{2,1,0:T(8,128)(2,1)S(1)} %get-tuple-element.68), channel_id=1, source_target_pairs={{0,24},{8,16},{16,8},{24,0},{1,25},{9,17},{17,9},{25,1},{2,26},{10... | collective-permute-start | bytes 589832 | tf_op jit(solution)/shard_map/ppermute | solution.py:61

commit v9 on v8

--- a/solution.py
+++ b/solution.py
@@ -20,6 +20,7 @@
 QUERY_SCALE = HEAD_DIM ** (-0.5)
 VMEM_LIMIT = 28 * 1024 * 1024
 WIDE_LIMIT = 52 * 1024 * 1024
+HEAD_LIMIT = 52 * 1024 * 1024
 LONG = 2**36
 
 F32 = jnp.float32
@@ -73,6 +74,10 @@
         self.rows = self.block // self.share
         self.part_rows = self.rows // self.groups
         assert self.part_rows * self.groups * self.share * WINDOWS == self.loc_dev
+
+
+def marker():
+    return jax.ShapeDtypeStruct((8, LANES), F32)
 
 
 def location_keys(plan, ids_ref):
@@ -103,16 +108,23 @@
         band, part = peer // plan.share, peer % plan.share
         wanted = place + (band * plan.loc_dev + window * plan.block + part * plan.rows)
         pick = jnp.where(wanted.astype(F32) == place_keys, 1.0, 0.0).astype(BF16)
-        outs[slot][...] = dot(pick, rows[...]).astype(BF16)
-
-
-def arrange_first(plan, tokens, ids):
+        outs[slot][...] = dot(pick, rows).astype(BF16)
+
+
+def arrange(plan, window, tokens, ids, after):
     count = plan.rows_count
     total = plan.loc_dev * plan.band_dev
     assert plan.loc_dev <= 256
 
-    def kernel(ids_ref, x_ref, *rest):
-        outs, (rows_ref, keys_ref, place_ref) = rest[:count], rest[count:]
+    def kernel(ids_hbm, x_hbm, *rest):
+        outs, (keys_ref, ids_ref, x_ref, sems) = rest[len(after) : -4], rest[-4:]
+        copies = [
+            pltpu.make_async_copy(ids_hbm, ids_ref, sems.at[0]),
+            pltpu.make_async_copy(x_hbm, x_ref, sems.at[1]),
+        ]
+        for copy in copies:
+            copy.start()
+        copies[0].wait()
         keys = location_keys(plan, ids_ref)
         keys_ref[...] = keys
         place = lax.broadcasted_iota(jnp.int32, (plan.loc_dev, total), 1)
@@ -120,39 +132,25 @@
         spread = jnp.where(place // plan.band_dev == location, 1.0, 0.0).astype(BF16)
         wide = dot(jnp.broadcast_to(keys, (16, plan.loc_dev)).astype(BF16), spread)
         band = lax.broadcasted_iota(jnp.int32, (1, total), 1) % plan.band_dev
-        place_ref[...] = wide[:1] + (band * plan.loc_dev).astype(F32)
-        rows_ref[...] = x_ref[...].reshape(total, plan.width)
-        pick_rows(plan, 0, place_ref[...], rows_ref, outs)
+        place_keys = wide[:1] + (band * plan.loc_dev).astype(F32)
+        copies[1].wait()
+        pick_rows(plan, window, place_keys, x_ref[...].reshape(total, plan.width), outs)
 
     return call(
         kernel,
         [jax.ShapeDtypeStruct((plan.rows, plan.width), BF16)] * count
-        + [
-            jax.ShapeDtypeStruct((total, plan.width), BF16),
-            jax.ShapeDtypeStruct((1, plan.loc_dev), F32),
-            jax.ShapeDtypeStruct((1, total), F32),
-        ],
+        + [jax.ShapeDtypeStruct((1, plan.loc_dev), F32)],
         2 * plan.loc_dev * tokens.size,
         4 * tokens.size,
-        in_specs=[VMEM] * 2,
-        out_specs=[VMEM] * (count + 3),
-    )(ids, tokens)
-
-
-def arrange_next(plan, window, rows, place_keys, after):
-    count = plan.rows_count
-
-    def kernel(rows_ref, place_ref, *rest):
-        pick_rows(plan, window, place_ref[...], rows_ref, rest[len(after) :])
-
-    return call(
-        kernel,
-        [jax.ShapeDtypeStruct((plan.rows, plan.width), BF16)] * count,
-        2 * plan.loc_dev * rows.size,
-        4 * rows.size,
-        in_specs=[VMEM] * 2 + [ANY] * len(after),
-        out_specs=[VMEM] * count,
-    )(rows, place_keys, *after)
+        limit=HEAD_LIMIT,
+        in_specs=[ANY] * (2 + len(after)),
+        out_specs=[VMEM] * (count + 1),
+        scratch_shapes=[
+            pltpu.VMEM(ids.shape, jnp.int32),
+            pltpu.VMEM(tokens.shape, BF16),
+            pltpu.SemaphoreType.DMA((2,)),
+        ],
+    )(ids, tokens, *after)
 
 
 def join_slots(plan, slots, after, flops):
@@ -297,7 +295,8 @@
         x_refs, rest = rest[:sources], rest[sources:]
         q_refs, rest = rest[:sources], rest[sources:]
         k_refs, rest = rest[:pieces], rest[pieces:]
-        v_refs, (out_ref, result, added) = rest[:pieces], rest[pieces:]
+        v_refs, (out_ref, marker_ref, result, added) = rest[:pieces], rest[pieces:]
+        marker_ref[...] = jnp.zeros_like(marker_ref)
 
         def step(number):
             units, places = [], []
@@ -333,11 +332,14 @@
     key_rows = sum(piece.shape[0] for piece in keys)
     return call(
         kernel,
-        jax.ShapeDtypeStruct((plan.rows_count, plan.groups, plan.part_rows, width), BF16),
+        [
+            jax.ShapeDtypeStruct((plan.rows_count, plan.groups, plan.part_rows, width), BF16),
+            marker(),
+        ],
         hide * 16 * total * key_rows * width,
         hide * 2 * width * (2 * key_rows + 3 * total + width),
         in_specs=[SMEM] + [VMEM] * (2 + 2 * sources + 2 * pieces),
-        out_specs=VMEM,
+        out_specs=[VMEM] * 2,
         scratch_shapes=[pltpu.VMEM((total, width), BF16), pltpu.VMEM((total, width), F32)],
     )(index, table, spatial_out, *tokens, *query, *keys, *values)
 
@@ -498,14 +500,11 @@
 ):
     plan = Plan(tokens)
     ids = window_ids.reshape(-1, LANES)
-    *sent, rows, location_key, place_keys = arrange_first(plan, tokens, ids)
-    arrived = [[exchange(value, "loc", CORES * step) for step, value in enumerate(sent)]]
-    following = []
-    for window in range(1, WINDOWS):
-        following = arrange_next(plan, window, rows, place_keys, arrived[-1][1:2])
-        arrived.append(
-            [exchange(value, "loc", CORES * step) for step, value in enumerate(following)]
-        )
+    arrived, after = [], []
+    for window in range(WINDOWS):
+        *sent, location_key = arrange(plan, window, tokens, ids, after)
+        arrived.append([exchange(value, "loc", CORES * step) for step, value in enumerate(sent)])
+        after = arrived[0][1:2]
     mids, behind = [], []
     for window, slots in enumerate(arrived):
         hide = int(window == 0)
@@ -514,7 +513,7 @@
         tables = (band_index, band_table, spatial_qkv)
         for first in range(0, len(slots), half):
             if first > 0:
-                behind = [*following[:1], queries[-1]]
+                behind = [location_key, queries[-1]]
             own = join_slots(plan, slots[first : first + half], behind, 0 if hide else LONG)
             query, keys, values = project(plan, [own], *tables, True, hide)
             owns.append(own)
@@ -532,10 +531,10 @@
             every = lax.all_gather(owns[0], "loc", axis_index_groups=same, tiled=True)
             keys, values = project(plan, [every], *tables, False, hide)
             all_keys, all_values = [keys], [values]
-        mid = attend(
+        mid, done = attend(
             plan, queries, all_keys, all_values, owns, band_index, band_table, spatial_out, hide
         )
-        behind = [mid]
+        behind = [done]
         mids.append(mid)
     same = [
         [g * plan.locs + r * CORES + core for r in range(plan.rows_count) for g in range(plan.groups)]

time: 124 us -> 123 us (level)
  Pallas kernels: 68 us -> 71.2 us
  waiting for transfers between devices: 19.5 us -> 17.9 us
    pallas_call x4, Pallas kernels: 22.8 us -> 26 us  [the longest x2 19.8 us: attend(): call(kernel, [jax.ShapeDtypeStruct((plan.rows_count, plan.groups, plan.pa...]
    ppermute x15, waiting for transfers between devices: 17.4 us -> 14.7 us  [exchange(): lax.ppermute(value, axis, [(i, i ^ step) for i in range(lax.axis_size(axi...]
  transfers between devices with their start and end apart: 17 -> 17, of which waited for: 7 -> 7; matrix products, arithmetic and copies ran while one was open for 0% -> 0% of each run, Pallas kernels for 52% -> 53%
where the time goes in v9:
time: 123 us
  Pallas kernels  71.2 us (58%)
  starting transfers between devices  29.5 us (24%)
  waiting for transfers between devices  17.9 us (15%)
  local copies, waits for them, and re-layouts  4.01 us (3%)
    pallas_call x2, Pallas kernels, channel(): call(kernel, [jax.ShapeDtypeStruct((bands, locations, width), BF16)] * gr...  29.4 us
    pallas_call x2, Pallas kernels, attend(): call(kernel, [jax.ShapeDtypeStruct((plan.rows_count, plan.groups, plan.pa...  19.8 us
    ppermute x15, starting transfers between devices, exchange(): lax.ppermute(value, axis, [(i, i ^ step) for i in range(lax.axis_size(axi...  18.9 us
    ppermute x15, waiting for transfers between devices, exchange(): lax.ppermute(value, axis, [(i, i ^ step) for i in range(lax.axis_size(axi...  14.7 us
    pallas_call x5, Pallas kernels, project(): call(kernel, [jax.ShapeDtypeStruct((rows, width), BF16)] * len(names), hi...  10.8 us
    all_to_all x2, starting transfers between devices, body(): lax.all_to_all(mid.reshape(-1, plan.part_rows, plan.width), ('band', 'loc...  10.6 us
    pallas_call x2, Pallas kernels, arrange(): call(kernel, [jax.ShapeDtypeStruct((plan.rows, plan.width), BF16)] * coun...  6.25 us
    unnamed x24, local copies, waits for them, and re-layouts  4.01 us
  transfers between devices with their start and end apart: 17, of which 7 were waited for; matrix products, arithmetic and copies ran while one was open for 0% of the time, Pallas kernels for 53%

profile of v9, /device:TPU:0, one launch (start us, length us, event | category | flops | bytes accessed | tf_op | source)
XLA Modules:
  0.0 123.0 jit_solution(3650225488867086977)
XLA Ops:
  0.9 3.1 %shard_map.100 = (bf16[128,768]{1,0:T(8,128)(2,1)S(1)}, bf16[128,768]{1,0:T(8,128)(2,1)S(1)}, bf16[128,768]{1,0:T(8,128)(2,1)S(1)}, bf16[128,768]{1,0:T(8,128)(2,1)S(1)}, f32[1,256]{1,0:T(1,128)}) custom-call(s32[16,128]{1,0:T(8,128)S(1)} %bitcast.7, bf16[256,4,768]{2,1,0:T(4,128)(2,1)} %x_hbm.3), custom_call_target="tpu_custom_call" | custom-call | flops 402653184 | bytes 3145728 | tf_op jit(solution)/shard_map/pallas_call | solution.py:139
  4.0 3.1 %collective-permute-start = (bf16[128,768]{1,0:T(8,128)(2,1)S(1)}, bf16[128,768]{1,0:T(8,128)(2,1)S(1)}, u32[]{:S(2)}, u32[]{:S(2)}) collective-permute-start(bf16[128,768]{1,0:T(8,128)(2,1)S(1)} %get-tuple-element.38), channel_id=1, source_target_pairs={{0,2},{1,3},{2,0},{3,1},{4,6},{5,7},{6,4},{7,5},{8,10},{9,11},{10,... | collective-permute-start | bytes 589832 | tf_op jit(solution)/shard_map/ppermute | solution.py:62
  7.1 2.6 %collective-permute-start.1 = (bf16[128,768]{1,0:T(8,128)(2,1)S(1)}, bf16[128,768]{1,0:T(8,128)(2,1)S(1)}, u32[]{:S(2)}, u32[]{:S(2)}) collective-permute-start(bf16[128,768]{1,0:T(8,128)(2,1)S(1)} %get-tuple-element.41), channel_id=1, source_target_pairs={{0,4},{1,5},{2,6},{3,7},{4,0},{5,1},{6,2},{7,3},{8,12},{9,13},{10,... | collective-permute-start | bytes 589832 | tf_op jit(solution)/shard_map/ppermute | solution.py:62
  9.6 5.7 %collective-permute-done.rest_0_.refs_1_ = bf16[128,768]{1,0:T(8,128)(2,1)S(1)} collective-permute-done((bf16[128,768]{1,0:T(8,128)(2,1)S(1)}, bf16[128,768]{1,0:T(8,128)(2,1)S(1)}, u32[]{:S(2)}, u32[]{:S(2)}) %collective-permute-start) | collective-permute-done | bytes 196640 | tf_op jit(solution)/shard_map/ppermute | solution.py:62
  16.7 3.1 %shard_map.101 = (bf16[128,768]{1,0:T(8,128)(2,1)S(1)}, bf16[128,768]{1,0:T(8,128)(2,1)}, bf16[128,768]{1,0:T(8,128)(2,1)}, bf16[128,768]{1,0:T(8,128)(2,1)}, f32[1,256]{1,0:T(1,128)S(1)}) custom-call(s32[16,128]{1,0:T(8,128)S(1)} %bitcast.8, bf16[256,4,768]{2,1,0:T(4,128)(2,1)} %x_hbm.3, bf16[128,768]{1,0:T(8,128)(2,1)S(1)} %collective-permute-done.rest_0_.refs_1_), custom_call_target="tpu_custom_call" | custom-call | flops 402653184 | bytes 3145728 | tf_op jit(solution)/shard_map/pallas_call | solution.py:139
  20.5 1.8 %shard_map.103 = (bf16[256,768]{1,0:T(8,128)(2,1)S(1)}, bf16[256,768]{1,0:T(8,128)(2,1)S(1)}, bf16[256,768]{1,0:T(8,128)(2,1)S(1)}) custom-call(s32[16]{0:T(128)S(1)} %copy-done.8, f32[16,768]{1,0:T(8,128)S(1)} %copy-done.1, bf16[768,2304]{1,0:T(8,128)(2,1)S(1)} %copy-done, bf16[256,768]{1,0:T(8,128)(2,1)S(1)} %shard_map.102.rest_0_), custom_call_target="tpu_custom_call" | custom-call | flops 905969664 | bytes 5111808 | tf_op jit(solution)/shard_map/pallas_call | solution.py:225
  22.3 1.9 %collective-permute-done.1.refs_0_ = bf16[128,768]{1,0:T(8,128)(2,1)S(1)} collective-permute-done((bf16[128,768]{1,0:T(8,128)(2,1)S(1)}, bf16[128,768]{1,0:T(8,128)(2,1)S(1)}, u32[]{:S(2)}, u32[]{:S(2)}) %collective-permute-start.1) | collective-permute-done | bytes 196640 | tf_op jit(solution)/shard_map/ppermute | solution.py:62
  24.8 3.4 %collective-permute-start.8 = (bf16[128,768]{1,0:T(8,128)(2,1)}, bf16[128,768]{1,0:T(8,128)(2,1)}, u32[]{:S(2)}, u32[]{:S(2)}) collective-permute-start(bf16[128,768]{1,0:T(8,128)(2,1)} %get-tuple-element.57), channel_id=1, source_target_pairs={{0,2},{1,3},{2,0},{3,1},{4,6},{5,7},{6,4},{7,5},{8,10},{9,11},{10,... | collective-permute-start | bytes 589832 | tf_op jit(solution)/shard_map/ppermute | solution.py:62
  28.2 1.1 collective-permute-start.9
  29.3 1.4 %collective-permute-start.10 = (bf16[128,768]{1,0:T(8,128)(2,1)}, bf16[128,768]{1,0:T(8,128)(2,1)}, u32[]{:S(2)}, u32[]{:S(2)}) collective-permute-start(bf16[128,768]{1,0:T(8,128)(2,1)} %get-tuple-element.59), channel_id=1, source_target_pairs={{0,6},{1,7},{2,4},{3,5},{4,2},{5,3},{6,0},{7,1},{8,14},{9,15},{10,... | collective-permute-start | bytes 589832 | tf_op jit(solution)/shard_map/ppermute | solution.py:62
  30.8 1.8 %shard_map.105 = (bf16[256,768]{1,0:T(8,128)(2,1)S(1)}, bf16[256,768]{1,0:T(8,128)(2,1)S(1)}, bf16[256,768]{1,0:T(8,128)(2,1)S(1)}) custom-call(s32[16]{0:T(128)S(1)} %copy-done.9, f32[16,768]{1,0:T(8,128)S(1)} %copy-done.1, bf16[768,2304]{1,0:T(8,128)(2,1)S(1)} %copy-done, bf16[256,768]{1,0:T(8,128)(2,1)S(1)} %shard_map.104.rest_0_.rest_1_), custom_call_target="tpu_custom_call" | custom-call | flops 905969664 | bytes 5111808 | tf_op jit(solution)/shard_map/pallas_call | solution.py:225
  32.6 2.2 %shard_map.106 = (bf16[512,768]{1,0:T(8,128)(2,1)S(1)}, bf16[512,768]{1,0:T(8,128)(2,1)S(1)}) custom-call(s32[16]{0:T(128)S(1)} %copy-done.9, f32[16,768]{1,0:T(8,128)S(1)} %copy-done.1, bf16[768,2304]{1,0:T(8,128)(2,1)S(1)} %copy-done, bf16[256,768]{1,0:T(8,128)(2,1)S(1)} %collective-permute-done.3.rest_0_, ...), custom_call_target="tpu_custom_call" | custom-call | flops 1207959552 | bytes 5898240 | tf_op jit(solution)/shard_map/pallas_call | solution.py:225
  34.8 9.4 %shard_map.107 = (bf16[4,4,32,768]{3,2,1,0:T(8,128)(2,1)S(1)}, f32[8,128]{1,0:T(8,128)S(1)}) custom-call(s32[16]{0:T(128)S(1)} %copy-done.9, f32[16,768]{1,0:T(8,128)S(1)} %copy-done.1, bf16[768,768]{1,0:T(8,128)(2,1)S(1)} %copy-done.3, bf16[256,768]{1,0:T(8,128)(2,1)S(1)} %shard_map.102.rest_0_, bf16[256,768]{1,0:T(8,128)(2,1)S(1)} %shard_map.104.rest_0_.rest_1_, ...), custom_call_target="tpu_custom_call" | custom-call | flops 6442450944 | bytes 6684672 | tf_op jit(solution)/shard_map/pallas_call | solution.py:333
  45.1 5.7 %all-to-all-start = ((bf16[16,32,768]{2,1,0:T(8,128)(2,1)}), bf16[16,32,768]{2,1,0:T(8,128)(2,1)}, u32[]{:S(2)}, u32[]{:S(2)}) async-start(bf16[16,32,768]{2,1,0:T(8,128)(2,1)} %bitcast.5), calls=%async_computation | async-start | bytes 1572864 | tf_op jit(solution)/shard_map/all_to_all | solution.py:545
  50.9 0.9 copy-done.11
  51.8 1.4 %shard_map.109.rest_0_ = bf16[512,768]{1,0:T(8,128)(2,1)S(1)} custom-call(bf16[128,768]{1,0:T(8,128)(2,1)S(1)} %copy-done.11, bf16[128,768]{1,0:T(8,128)(2,1)} %collective-permute-done.8.refs_1_, bf16[128,768]{1,0:T(8,128)(2,1)} %collective-permute-done.9.refs_2_, bf16[128,768]{1,0:T(8,128)(2,1)} %collective-permute-done.10.refs_3_, ...), custom_call_target="tpu_custom_call" | custom-call | flops 68719476736 | tf_op jit(solution)/shard_map/pallas_call | solution.py:172
  53.3 2.8 %shard_map.110 = (bf16[512,768]{1,0:T(8,128)(2,1)S(1)}, bf16[512,768]{1,0:T(8,128)(2,1)S(1)}, bf16[512,768]{1,0:T(8,128)(2,1)S(1)}) custom-call(s32[16]{0:T(128)S(1)} %copy-done.9, f32[16,768]{1,0:T(8,128)S(1)} %copy-done.2, bf16[768,2304]{1,0:T(8,128)(2,1)S(1)} %copy-done, bf16[512,768]{1,0:T(8,128)(2,1)S(1)} %shard_map.109.rest_0_), custom_call_target="tpu_custom_call" | custom-call | tf_op jit(solution)/shard_map/pallas_call | solution.py:225
  56.1 2.2 %shard_map.111 = (bf16[512,768]{1,0:T(8,128)(2,1)S(1)}, bf16[512,768]{1,0:T(8,128)(2,1)S(1)}) custom-call(s32[16]{0:T(128)S(1)} %copy-done.9, f32[16,768]{1,0:T(8,128)S(1)} %copy-done.2, bf16[768,2304]{1,0:T(8,128)(2,1)S(1)} %copy-done, bf16[512,768]{1,0:T(8,128)(2,1)S(1)} %collective-permute-done.11.rest_0_, bf16[512,768]{1,0:T(8,128)(2,1)S(1)} %get-tuple-element.61.rest_1_), custom_call_target="tpu_custom_call" | custom-call | tf_op jit(solution)/shard_map/pallas_call | solution.py:225
  58.3 10.3 %shard_map.112 = (bf16[4,4,32,768]{3,2,1,0:T(8,128)(2,1)}, f32[8,128]{1,0:T(8,128)}) custom-call(s32[16]{0:T(128)S(1)} %copy-done.9, f32[16,768]{1,0:T(8,128)S(1)} %copy-done.2, bf16[768,768]{1,0:T(8,128)(2,1)S(1)} %copy-done.4, bf16[512,768]{1,0:T(8,128)(2,1)S(1)} %shard_map.109.rest_0_, bf16[512,768]{1,0:T(8,128)(2,1)S(1)} %get-tuple-element.61.rest_1_, ...), custom_call_target="tpu_custom_call" | custom-call | tf_op jit(solution)/shard_map/pallas_call | solution.py:333
  68.6 2.0 %all-to-all-done = bf16[16,32,768]{2,1,0:T(8,128)(2,1)} async-done(((bf16[16,32,768]{2,1,0:T(8,128)(2,1)}), bf16[16,32,768]{2,1,0:T(8,128)(2,1)}, u32[]{:S(2)}, u32[]{:S(2)}) %all-to-all-start) | async-done | bytes 786464 | tf_op jit(solution)/shard_map/all_to_all | solution.py:545
  70.6 4.9 %all-to-all-start.1 = ((bf16[16,32,768]{2,1,0:T(8,128)(2,1)}), bf16[16,32,768]{2,1,0:T(8,128)(2,1)S(1)}, u32[]{:S(2)}, u32[]{:S(2)}) async-start(bf16[16,32,768]{2,1,0:T(8,128)(2,1)} %bitcast.3), calls=%async_computation.1 | async-start | bytes 1572864 | tf_op jit(solution)/shard_map/all_to_all | solution.py:545
  75.5 15.3 %shard_map.108 = (bf16[4,32,768]{2,1,0:T(8,128)(2,1)S(1)}, bf16[4,32,768]{2,1,0:T(8,128)(2,1)S(1)}, bf16[4,32,768]{2,1,0:T(8,128)(2,1)S(1)}, bf16[4,32,768]{2,1,0:T(8,128)(2,1)S(1)}) custom-call(bf16[768,2304]{1,0:T(8,128)(2,1)} %qkv_hbm.3, bf16[768,768]{1,0:T(8,128)(2,1)} %out_hbm.3, bf16[768,3072]{1,0:T(8,128)(2,1)} %up_hbm.3, bf16[3072,768]{1,0:T(8,128)(2,1)} %down_hbm.3, ...), custom_call_target="tpu_custom_call" | custom-call | flops 7247757312 | bytes 15728640 | tf_op jit(solution)/shard_map/pallas_call | solution.py:443
  90.8 2.0 %collective-permute-start.5 = (bf16[4,32,768]{2,1,0:T(8,128)(2,1)S(1)}, bf16[4,32,768]{2,1,0:T(8,128)(2,1)S(1)}, u32[]{:S(2)}, u32[]{:S(2)}) collective-permute-start(bf16[4,32,768]{2,1,0:T(8,128)(2,1)S(1)} %get-tuple-element.53), channel_id=1, source_target_pairs={{0,8},{8,0},{16,24},{24,16},{1,9},{9,1},{17,25},{25,17},{2,10},{10... | collective-permute-start | bytes 589832 | tf_op jit(solution)/shard_map/ppermute | solution.py:62
  92.8 1.4 %collective-permute-start.6 = (bf16[4,32,768]{2,1,0:T(8,128)(2,1)S(1)}, bf16[4,32,768]{2,1,0:T(8,128)(2,1)S(1)}, u32[]{:S(2)}, u32[]{:S(2)}) collective-permute-start(bf16[4,32,768]{2,1,0:T(8,128)(2,1)S(1)} %get-tuple-element.54), channel_id=1, source_target_pairs={{0,16},{8,24},{16,0},{24,8},{1,17},{9,25},{17,1},{25,9},{2,18},{10... | collective-permute-start | bytes 589832 | tf_op jit(solution)/shard_map/ppermute | solution.py:62
  94.3 1.3 %all-to-all-done.1 = bf16[16,32,768]{2,1,0:T(8,128)(2,1)S(1)} async-done(((bf16[16,32,768]{2,1,0:T(8,128)(2,1)}), bf16[16,32,768]{2,1,0:T(8,128)(2,1)S(1)}, u32[]{:S(2)}, u32[]{:S(2)}) %all-to-all-start.1) | async-done | bytes 786464 | tf_op jit(solution)/shard_map/all_to_all | solution.py:545
  95.6 14.1 %shard_map.113 = (bf16[4,32,768]{2,1,0:T(8,128)(2,1)S(1)}, bf16[4,32,768]{2,1,0:T(8,128)(2,1)S(1)}, bf16[4,32,768]{2,1,0:T(8,128)(2,1)S(1)}, bf16[4,32,768]{2,1,0:T(8,128)(2,1)S(1)}) custom-call(bf16[768,2304]{1,0:T(8,128)(2,1)} %qkv_hbm.3, bf16[768,768]{1,0:T(8,128)(2,1)} %out_hbm.3, bf16[768,3072]{1,0:T(8,128)(2,1)} %up_hbm.3, bf16[3072,768]{1,0:T(8,128)(2,1)} %down_hbm.3, ...), custom_call_target="tpu_custom_call" | custom-call | flops 7247757312 | bytes 15728640 | tf_op jit(solution)/shard_map/pallas_call | solution.py:443
  110.5 1.5 %collective-permute-start.13 = (bf16[4,32,768]{2,1,0:T(8,128)(2,1)S(1)}, bf16[4,32,768]{2,1,0:T(8,128)(2,1)S(1)}, u32[]{:S(2)}, u32[]{:S(2)}) collective-permute-start(bf16[4,32,768]{2,1,0:T(8,128)(2,1)S(1)} %get-tuple-element.69), channel_id=1, source_target_pairs={{0,16},{8,24},{16,0},{24,8},{1,17},{9,25},{17,1},{25,9},{2,18},{10... | collective-permute-start | bytes 589832 | tf_op jit(solution)/shard_map/ppermute | solution.py:62
  112.0 1.3 %collective-permute-start.14 = (bf16[4,32,768]{2,1,0:T(8,128)(2,1)S(1)}, bf16[4,32,768]{2,1,0:T(8,128)(2,1)S(1)}, u32[]{:S(2)}, u32[]{:S(2)}) collective-permute-start(bf16[4,32,768]{2,1,0:T(8,128)(2,1)S(1)} %get-tuple-element.70), channel_id=1, source_target_pairs={{0,24},{8,16},{16,8},{24,0},{1,25},{9,17},{17,9},{25,1},{2,26},{10... | collective-permute-start | bytes 589832 | tf_op jit(solution)/shard_map/ppermute | solution.py:62
  113.3 4.0 %collective-permute-done.12.refs_5_ = bf16[4,32,768]{2,1,0:T(8,128)(2,1)S(1)} collective-permute-done((bf16[4,32,768]{2,1,0:T(8,128)(2,1)S(1)}, bf16[4,32,768]{2,1,0:T(8,128)(2,1)S(1)}, u32[]{:S(2)}, u32[]{:S(2)}) %collective-permute-start.12) | collective-permute-done | bytes 196640 | tf_op jit(solution)/shard_map/ppermute | solution.py:62
  117.3 2.0 %collective-permute-done.13.refs_6_ = bf16[4,32,768]{2,1,0:T(8,128)(2,1)S(1)} collective-permute-done((bf16[4,32,768]{2,1,0:T(8,128)(2,1)S(1)}, bf16[4,32,768]{2,1,0:T(8,128)(2,1)S(1)}, u32[]{:S(2)}, u32[]{:S(2)}) %collective-permute-start.13) | collective-permute-done | bytes 196640 | tf_op jit(solution)/shard_map/ppermute | solution.py:62
  119.3 1.0 collective-permute-done.14.refs_7_
  120.3 2.6 %shard_map.114 = bf16[256,4,768]{2,1,0:T(4,128)(2,1)} custom-call(f32[1,256]{1,0:T(1,128)S(1)} %get-tuple-element.39.refs_2_.keys_ref, bf16[4,32,768]{2,1,0:T(8,128)(2,1)S(1)} %get-tuple-element.52.refs_0_, bf16[4,32,768]{2,1,0:T(8,128)(2,1)S(1)} %collective-permute-done.5.refs_1_, bf16[4,32,768]{2,1,0:T(8,128)(2,1)S(1)} %collective-permute-done.6.refs_2_, ...), custom_call_target="tpu_custom_call" | custom-call | flops 402653184 | bytes 3145728 | tf_op jit(solution)/shard_map/pallas_call | solution.py:481
  (41 shorter events, 5.2 us)
Async XLA Ops:
  0.0 19.8 %copy-start.1 = (f32[16,768]{1,0:T(8,128)S(1)}, f32[16,768]{1,0:T(8,128)}, u32[]{:S(2)}) copy-start(f32[16,768]{1,0:T(8,128)} %table_ref.13) | copy-start | bytes 147460
  0.0 19.8 %copy-start = (bf16[768,2304]{1,0:T(8,128)(2,1)S(1)}, bf16[768,2304]{1,0:T(8,128)(2,1)}, u32[]{:S(2)}) copy-start(bf16[768,2304]{1,0:T(8,128)(2,1)} %w_ref.12) | copy-start | bytes 10616836
  0.0 0.8 copy-start.6
  4.0 11.4 %collective-permute-start = (bf16[128,768]{1,0:T(8,128)(2,1)S(1)}, bf16[128,768]{1,0:T(8,128)(2,1)S(1)}, u32[]{:S(2)}, u32[]{:S(2)}) collective-permute-start(bf16[128,768]{1,0:T(8,128)(2,1)S(1)} %get-tuple-element.38), channel_id=1, source_target_pairs={{0,2},{1,3},{2,0},{3,1},{4,6},{5,7},{6,4},{7,5},{8,10},{9,11},{10,... | collective-permute-start | bytes 589832 | tf_op jit(solution)/shard_map/ppermute | solution.py:62
  7.1 17.2 %collective-permute-start.1 = (bf16[128,768]{1,0:T(8,128)(2,1)S(1)}, bf16[128,768]{1,0:T(8,128)(2,1)S(1)}, u32[]{:S(2)}, u32[]{:S(2)}) collective-permute-start(bf16[128,768]{1,0:T(8,128)(2,1)S(1)} %get-tuple-element.41), channel_id=1, source_target_pairs={{0,4},{1,5},{2,6},{3,7},{4,0},{5,1},{6,2},{7,3},{8,12},{9,13},{10,... | collective-permute-start | bytes 589832 | tf_op jit(solution)/shard_map/ppermute | solution.py:62
  9.6 14.6 %collective-permute-start.2 = (bf16[128,768]{1,0:T(8,128)(2,1)S(1)}, bf16[128,768]{1,0:T(8,128)(2,1)S(1)}, u32[]{:S(2)}, u32[]{:S(2)}) collective-permute-start(bf16[128,768]{1,0:T(8,128)(2,1)S(1)} %get-tuple-element.42), channel_id=1, source_target_pairs={{0,6},{1,7},{2,4},{3,5},{4,2},{5,3},{6,0},{7,1},{8,14},{9,15},{10,... | collective-permute-start | bytes 589832 | tf_op jit(solution)/shard_map/ppermute | solution.py:62
  15.9 16.7 %collective-permute-start.3 = (bf16[256,768]{1,0:T(8,128)(2,1)S(1)}, bf16[256,768]{1,0:T(8,128)(2,1)S(1)}, u32[]{:S(2)}, u32[]{:S(2)}) collective-permute-start(bf16[256,768]{1,0:T(8,128)(2,1)S(1)} %shard_map.102.rest_0_), channel_id=1, source_target_pairs={{0,1},{1,0},{2,3},{3,2},{4,5},{5,4},{6,7},{7,6},{8,9},{9,8},{10,11... | collective-permute-start | bytes 1179656 | tf_op jit(solution)/shard_map/ppermute | solution.py:62
  16.0 0.7 copy-start.7
  16.7 14.1 %copy-start.9 = (s32[16]{0:T(128)S(1)}, s32[16]{0:T(128)}, u32[]{:S(2)}) copy-start(s32[16]{0:T(128)} %index_ref.13) | copy-start | bytes 196
  19.8 0.7 copy-start.8
  20.5 8.8 %copy-start.10 = (bf16[128,768]{1,0:T(8,128)(2,1)}, bf16[128,768]{1,0:T(8,128)(2,1)S(1)}, u32[]{:S(2)}) copy-start(bf16[128,768]{1,0:T(8,128)(2,1)S(1)} %get-tuple-element.56.refs_0_) | copy-start | bytes 589828
  24.7 7.9 %collective-permute-start.4 = (bf16[256,768]{1,0:T(8,128)(2,1)S(1)}, bf16[256,768]{1,0:T(8,128)(2,1)S(1)}, u32[]{:S(2)}, u32[]{:S(2)}) collective-permute-start(bf16[256,768]{1,0:T(8,128)(2,1)S(1)} %shard_map.104.rest_0_.rest_1_), channel_id=1, source_target_pairs={{0,1},{1,0},{2,3},{3,2},{4,5},{5,4},{6,7},{7,6},{8,9},{9,8},{10,11... | collective-permute-start | bytes 1179656 | tf_op jit(solution)/shard_map/ppermute | solution.py:62
  24.8 26.0 %collective-permute-start.8 = (bf16[128,768]{1,0:T(8,128)(2,1)}, bf16[128,768]{1,0:T(8,128)(2,1)}, u32[]{:S(2)}, u32[]{:S(2)}) collective-permute-start(bf16[128,768]{1,0:T(8,128)(2,1)} %get-tuple-element.57), channel_id=1, source_target_pairs={{0,2},{1,3},{2,0},{3,1},{4,6},{5,7},{6,4},{7,5},{8,10},{9,11},{10,... | collective-permute-start | bytes 589832 | tf_op jit(solution)/shard_map/ppermute | solution.py:62
  28.2 22.6 %collective-permute-start.9 = (bf16[128,768]{1,0:T(8,128)(2,1)}, bf16[128,768]{1,0:T(8,128)(2,1)}, u32[]{:S(2)}, u32[]{:S(2)}) collective-permute-start(bf16[128,768]{1,0:T(8,128)(2,1)} %get-tuple-element.58), channel_id=1, source_target_pairs={{0,4},{1,5},{2,6},{3,7},{4,0},{5,1},{6,2},{7,3},{8,12},{9,13},{10,... | collective-permute-start | bytes 589832 | tf_op jit(solution)/shard_map/ppermute | solution.py:62
  29.3 5.5 %copy-start.3 = (bf16[768,768]{1,0:T(8,128)(2,1)S(1)}, bf16[768,768]{1,0:T(8,128)(2,1)}, u32[]{:S(2)}) copy-start(bf16[768,768]{1,0:T(8,128)(2,1)} %w_ref.13) | copy-start | bytes 3538948
  29.3 21.6 %collective-permute-start.10 = (bf16[128,768]{1,0:T(8,128)(2,1)}, bf16[128,768]{1,0:T(8,128)(2,1)}, u32[]{:S(2)}, u32[]{:S(2)}) collective-permute-start(bf16[128,768]{1,0:T(8,128)(2,1)} %get-tuple-element.59), channel_id=1, source_target_pairs={{0,6},{1,7},{2,4},{3,5},{4,2},{5,3},{6,0},{7,1},{8,14},{9,15},{10,... | collective-permute-start | bytes 589832 | tf_op jit(solution)/shard_map/ppermute | solution.py:62
  44.3 0.9 copy-start.5
  45.1 25.5 %all-to-all-start = ((bf16[16,32,768]{2,1,0:T(8,128)(2,1)}), bf16[16,32,768]{2,1,0:T(8,128)(2,1)}, u32[]{:S(2)}, u32[]{:S(2)}) async-start(bf16[16,32,768]{2,1,0:T(8,128)(2,1)} %bitcast.5), calls=%async_computation | async-start | bytes 1572864 | tf_op jit(solution)/shard_map/all_to_all | solution.py:545
  50.9 0.9 copy-start.11
  51.8 1.5 %copy-start.2 = (f32[16,768]{1,0:T(8,128)S(1)}, f32[16,768]{1,0:T(8,128)}, u32[]{:S(2)}) copy-start(f32[16,768]{1,0:T(8,128)} %table_ref.13) | copy-start | bytes 147460
  53.2 2.9 %collective-permute-start.11 = (bf16[512,768]{1,0:T(8,128)(2,1)S(1)}, bf16[512,768]{1,0:T(8,128)(2,1)S(1)}, u32[]{:S(2)}, u32[]{:S(2)}) collective-permute-start(bf16[512,768]{1,0:T(8,128)(2,1)S(1)} %shard_map.109.rest_0_), channel_id=1, source_target_pairs={{0,1},{1,0},{2,3},{3,2},{4,5},{5,4},{6,7},{7,6},{8,9},{9,8},{10,11... | collective-permute-start | bytes 2359304 | tf_op jit(solution)/shard_map/ppermute | solution.py:62
  56.1 2.2 %copy-start.4 = (bf16[768,768]{1,0:T(8,128)(2,1)S(1)}, bf16[768,768]{1,0:T(8,128)(2,1)}, u32[]{:S(2)}) copy-start(bf16[768,768]{1,0:T(8,128)(2,1)} %w_ref.13) | copy-start | bytes 3538948
  70.6 25.0 %all-to-all-start.1 = ((bf16[16,32,768]{2,1,0:T(8,128)(2,1)}), bf16[16,32,768]{2,1,0:T(8,128)(2,1)S(1)}, u32[]{:S(2)}, u32[]{:S(2)}) async-start(bf16[16,32,768]{2,1,0:T(8,128)(2,1)} %bitcast.3), calls=%async_computation.1 | async-start | bytes 1572864 | tf_op jit(solution)/shard_map/all_to_all | solution.py:545
  90.8 21.2 %collective-permute-start.5 = (bf16[4,32,768]{2,1,0:T(8,128)(2,1)S(1)}, bf16[4,32,768]{2,1,0:T(8,128)(2,1)S(1)}, u32[]{:S(2)}, u32[]{:S(2)}) collective-permute-start(bf16[4,32,768]{2,1,0:T(8,128)(2,1)S(1)} %get-tuple-element.53), channel_id=1, source_target_pairs={{0,8},{8,0},{16,24},{24,16},{1,9},{9,1},{17,25},{25,17},{2,10},{10... | collective-permute-start | bytes 589832 | tf_op jit(solution)/shard_map/ppermute | solution.py:62
  92.8 20.5 %collective-permute-start.6 = (bf16[4,32,768]{2,1,0:T(8,128)(2,1)S(1)}, bf16[4,32,768]{2,1,0:T(8,128)(2,1)S(1)}, u32[]{:S(2)}, u32[]{:S(2)}) collective-permute-start(bf16[4,32,768]{2,1,0:T(8,128)(2,1)S(1)} %get-tuple-element.54), channel_id=1, source_target_pairs={{0,16},{8,24},{16,0},{24,8},{1,17},{9,25},{17,1},{25,9},{2,18},{10... | collective-permute-start | bytes 589832 | tf_op jit(solution)/shard_map/ppermute | solution.py:62
  94.2 19.1 %collective-permute-start.7 = (bf16[4,32,768]{2,1,0:T(8,128)(2,1)S(1)}, bf16[4,32,768]{2,1,0:T(8,128)(2,1)S(1)}, u32[]{:S(2)}, u32[]{:S(2)}) collective-permute-start(bf16[4,32,768]{2,1,0:T(8,128)(2,1)S(1)} %get-tuple-element.55), channel_id=1, source_target_pairs={{0,24},{8,16},{16,8},{24,0},{1,25},{9,17},{17,9},{25,1},{2,26},{10... | collective-permute-start | bytes 589832 | tf_op jit(solution)/shard_map/ppermute | solution.py:62
  109.7 7.6 %collective-permute-start.12 = (bf16[4,32,768]{2,1,0:T(8,128)(2,1)S(1)}, bf16[4,32,768]{2,1,0:T(8,128)(2,1)S(1)}, u32[]{:S(2)}, u32[]{:S(2)}) collective-permute-start(bf16[4,32,768]{2,1,0:T(8,128)(2,1)S(1)} %get-tuple-element.68), channel_id=1, source_target_pairs={{0,8},{8,0},{16,24},{24,16},{1,9},{9,1},{17,25},{25,17},{2,10},{10... | collective-permute-start | bytes 589832 | tf_op jit(solution)/shard_map/ppermute | solution.py:62
  110.5 8.8 %collective-permute-start.13 = (bf16[4,32,768]{2,1,0:T(8,128)(2,1)S(1)}, bf16[4,32,768]{2,1,0:T(8,128)(2,1)S(1)}, u32[]{:S(2)}, u32[]{:S(2)}) collective-permute-start(bf16[4,32,768]{2,1,0:T(8,128)(2,1)S(1)} %get-tuple-element.69), channel_id=1, source_target_pairs={{0,16},{8,24},{16,0},{24,8},{1,17},{9,25},{17,1},{25,9},{2,18},{10... | collective-permute-start | bytes 589832 | tf_op jit(solution)/shard_map/ppermute | solution.py:62
  112.0 8.3 %collective-permute-start.14 = (bf16[4,32,768]{2,1,0:T(8,128)(2,1)S(1)}, bf16[4,32,768]{2,1,0:T(8,128)(2,1)S(1)}, u32[]{:S(2)}, u32[]{:S(2)}) collective-permute-start(bf16[4,32,768]{2,1,0:T(8,128)(2,1)S(1)} %get-tuple-element.70), channel_id=1, source_target_pairs={{0,24},{8,16},{16,8},{24,0},{1,25},{9,17},{17,9},{25,1},{2,26},{10... | collective-permute-start | bytes 589832 | tf_op jit(solution)/shard_map/ppermute | solution.py:62

commit v10 on v8

--- a/solution.py
+++ b/solution.py
@@ -75,6 +75,10 @@
         assert self.part_rows * self.groups * self.share * WINDOWS == self.loc_dev
 
 
+def marker():
+    return jax.ShapeDtypeStruct((8, LANES), F32)
+
+
 def location_keys(plan, ids_ref):
     size = plan.loc_dev
     lines = size // LANES
@@ -143,15 +147,17 @@
     count = plan.rows_count
 
     def kernel(rows_ref, place_ref, *rest):
-        pick_rows(plan, window, place_ref[...], rows_ref, rest[len(after) :])
-
-    return call(
-        kernel,
-        [jax.ShapeDtypeStruct((plan.rows, plan.width), BF16)] * count,
+        outs = rest[len(after) :]
+        outs[-1][...] = jnp.zeros_like(outs[-1])
+        pick_rows(plan, window, place_ref[...], rows_ref, outs[:-1])
+
+    return call(
+        kernel,
+        [jax.ShapeDtypeStruct((plan.rows, plan.width), BF16)] * count + [marker()],
         2 * plan.loc_dev * rows.size,
         4 * rows.size,
         in_specs=[VMEM] * 2 + [ANY] * len(after),
-        out_specs=[VMEM] * count,
+        out_specs=[VMEM] * (count + 1),
     )(rows, place_keys, *after)
 
 
@@ -198,7 +204,7 @@
 
 def norm_into(target, source):
     rows = source.shape[0]
-    tile = min(rows, ROW_TILE)
+    tile = rows // pl.cdiv(rows, ROW_TILE)
     for first in range(0, rows, tile):
         here = pl.ds(first, tile)
         target[here, :] = norm_rows(source[here, :]).astype(BF16)
@@ -297,7 +303,8 @@
         x_refs, rest = rest[:sources], rest[sources:]
         q_refs, rest = rest[:sources], rest[sources:]
         k_refs, rest = rest[:pieces], rest[pieces:]
-        v_refs, (out_ref, result, added) = rest[:pieces], rest[pieces:]
+        v_refs, (out_ref, marker_ref, result, added) = rest[:pieces], rest[pieces:]
+        marker_ref[...] = jnp.zeros_like(marker_ref)
 
         def step(number):
             units, places = [], []
@@ -333,27 +340,128 @@
     key_rows = sum(piece.shape[0] for piece in keys)
     return call(
         kernel,
-        jax.ShapeDtypeStruct((plan.rows_count, plan.groups, plan.part_rows, width), BF16),
+        [
+            jax.ShapeDtypeStruct((plan.rows_count, plan.groups, plan.part_rows, width), BF16),
+            marker(),
+        ],
         hide * 16 * total * key_rows * width,
         hide * 2 * width * (2 * key_rows + 3 * total + width),
         in_specs=[SMEM] + [VMEM] * (2 + 2 * sources + 2 * pieces),
-        out_specs=VMEM,
+        out_specs=[VMEM] * 2,
         scratch_shapes=[pltpu.VMEM((total, width), BF16), pltpu.VMEM((total, width), F32)],
     )(index, table, spatial_out, *tokens, *query, *keys, *values)
 
 
-def channel(plan, parts, channel_qkv, channel_out, up_weight, down_weight):
+def piece_places(owners, bands, locations):
+    stride = len(owners) * bands * GROUP_LOCS
+    places = {}
+    for position, owner in enumerate(owners):
+        for band in range(bands):
+            for first in range(0, locations, TILE_LOCS):
+                places[owner, band, first] = [
+                    pl.ds(at // GROUP_LOCS * stride + (position * bands + band) * GROUP_LOCS, GROUP_LOCS)
+                    for at in range(first, first + TILE_LOCS, GROUP_LOCS)
+                ]
+    return places
+
+
+def mlp_into(mid, normed, up_ref, down_ref, waits=()):
+    rows, width = mid.shape
+    row_tile = rows // pl.cdiv(rows, ROW_TILE)
+    tiles = [pl.ds(first, row_tile) for first in range(0, rows, row_tile)]
+    norm_into(normed, mid)
+
+    def step(here):
+        raised = [dot(normed[mine, :], up_ref[:, here]) for mine in tiles]
+        for mine, value in zip(tiles, raised):
+            mid[mine, :] += dot(gelu(value).astype(BF16), down_ref[here, :])
+
+    blocks = up_ref.shape[1] // width
+    if waits:
+        for block in range(blocks):
+            waits[block]()
+            step(pl.ds(block * width, width))
+    else:
+        loop(blocks, lambda block: step(aligned(block, width)))
+
+
+def write_pieces(mid, outs, owners, bands, locations):
+    for (owner, band, first), places in piece_places(owners, bands, locations).items():
+        piece = jnp.concatenate([mid[place, :] for place in places], axis=0)
+        outs[owners.index(owner)][band, first : first + TILE_LOCS, :] = piece.astype(BF16)
+
+
+def finish(plan, rest, owners, bands, up_weight, down_weight):
+    rows, width = rest.shape
+    locations = rows // (len(owners) * bands)
+    blocks = up_weight.shape[1] // width
+
+    def kernel(up_hbm, down_hbm, rest_ref, *refs):
+        outs, refs = refs[: len(owners)], refs[len(owners) :]
+        mid, normed, up_ref, down_ref, sems = refs
+        pairs = []
+        for block in range(blocks):
+            here = pl.ds(block * width, width)
+            pairs.append(
+                [
+                    pltpu.make_async_copy(
+                        up_hbm.at[:, here], up_ref.at[:, here], sems.at[2 * block]
+                    ),
+                    pltpu.make_async_copy(
+                        down_hbm.at[here, :], down_ref.at[here, :], sems.at[2 * block + 1]
+                    ),
+                ]
+            )
+
+        def start(block):
+            for copy in pairs[block]:
+                copy.start()
+
+        def wait(block):
+            for copy in pairs[block]:
+                copy.wait()
+            if block + 2 < blocks:
+                start(block + 2)
+
+        for block in range(min(2, blocks)):
+            start(block)
+        mid[...] = rest_ref[...]
+        waits = [functools.partial(wait, block) for block in range(blocks)]
+        mlp_into(mid, normed, up_ref, down_ref, waits)
+        write_pieces(mid, outs, owners, bands, locations)
+
+    return call(
+        kernel,
+        [jax.ShapeDtypeStruct((bands, locations, width), BF16)] * len(owners),
+        4 * rows * up_weight.size,
+        2 * 2 * up_weight.size,
+        limit=WIDE_LIMIT,
+        in_specs=[ANY] * 2 + [VMEM],
+        out_specs=[VMEM] * len(owners),
+        scratch_shapes=[
+            pltpu.VMEM((rows, width), F32),
+            pltpu.VMEM((rows, width), BF16),
+            pltpu.VMEM(up_weight.shape, BF16),
+            pltpu.VMEM(down_weight.shape, BF16),
+            pltpu.SemaphoreType.DMA((2 * blocks,)),
+        ],
+    )(up_weight, down_weight, rest)
+
+
+def channel(plan, parts, now, later, channel_qkv, channel_out, up_weight, down_weight):
     groups, width = plan.groups, plan.width
     bands, _, locations, _ = parts.shape
-    tile, small = TILE_LOCS, GROUP_LOCS
-    assert locations % tile == 0
+    small = GROUP_LOCS
+    assert locations % TILE_LOCS == 0
+    owners = [*now, *later]
     group_rows = groups * bands * small
     rows = groups * bands * locations
-    row_tile = min(rows, ROW_TILE)
+    now_rows = rows * len(now) // groups
+    count = len(now) + (len(later) > 0)
 
     def kernel(qkv_hbm, out_hbm, up_hbm, down_hbm, *refs):
         in_ref, *refs = refs
-        outs, refs = refs[:groups], refs[groups:]
+        outs, refs = refs[:count], refs[count:]
         mid, normed, packed, attended, qkv_ref, out_ref, up_ref, down_ref, sems = refs
         me = lax.axis_index("band")
         columns = [pl.ds(first, width) for first in range(0, 3 * width, width)]
@@ -372,22 +480,9 @@
                 )
         for copy in copies[: len(columns)]:
             copy.start()
-        pieces = [
-            (owner, band, first)
-            for owner in range(groups)
-            for band in range(bands)
-            for first in range(0, locations, tile)
-        ]
-
-        def places(owner, band, first):
-            return [
-                pl.ds((at // small) * group_rows + (owner * bands + band) * small, small)
-                for at in range(first, first + tile, small)
-            ]
-
-        for owner, band, first in pieces:
-            piece = in_ref[band, me ^ owner, first : first + tile, :].astype(F32)
-            for number, place in enumerate(places(owner, band, first)):
+        for (owner, band, first), places in piece_places(owners, bands, locations).items():
+            piece = in_ref[band, me ^ owner, first : first + TILE_LOCS, :].astype(F32)
+            for number, place in enumerate(places):
                 mid[place, :] = piece[number * small : (number + 1) * small]
         norm_into(normed, mid)
 
@@ -417,35 +512,31 @@
         loop(pairs, attention_step, unroll=3)
         copies[3].wait()
         mid[...] += dot(attended[...], out_ref[...])
-        norm_into(normed, mid)
-
         copies[4].wait()
         copies[5].wait()
-
-        def mlp_step(block):
-            here = aligned(block, width)
-            tiles = [pl.ds(first, row_tile) for first in range(0, rows, row_tile)]
-            raised = [dot(normed[mine, :], up_ref[:, here]) for mine in tiles]
-            for mine, value in zip(tiles, raised):
-                mid[mine, :] += dot(gelu(value).astype(BF16), down_ref[here, :])
-
-        loop(up_weight.shape[1] // width, mlp_step)
-        for owner, band, first in pieces:
-            piece = jnp.concatenate(
-                [mid[place, :] for place in places(owner, band, first)], axis=0
-            )
-            outs[owner][band, first : first + tile, :] = piece.astype(BF16)
+        if later:
+            head = len(now) * bands * small
+            tail = group_rows - head
+            for group in range(rows // group_rows):
+                at = group * group_rows
+                outs[-1][pl.ds(group * tail, tail), :] = mid[pl.ds(at + head, tail), :]
+                if group > 0:
+                    mid[pl.ds(group * head, head), :] = mid[pl.ds(at, head), :]
+        mine = pl.ds(0, now_rows)
+        mlp_into(mid.at[mine, :], normed.at[mine, :], up_ref, down_ref)
+        write_pieces(mid, outs, now, bands, locations)
 
     weights = [channel_qkv, channel_out, up_weight, down_weight]
     size = sum(weight.size for weight in weights)
     return call(
         kernel,
-        [jax.ShapeDtypeStruct((bands, locations, width), BF16)] * groups,
+        [jax.ShapeDtypeStruct((bands, locations, width), BF16)] * len(now)
+        + [jax.ShapeDtypeStruct((rows - now_rows, width), F32)] * (count - len(now)),
         2 * rows * size,
         2 * (2 * rows * width + size),
         limit=WIDE_LIMIT,
         in_specs=[ANY] * 4 + [VMEM],
-        out_specs=[VMEM] * groups,
+        out_specs=[VMEM] * count,
         scratch_shapes=[
             pltpu.VMEM((rows, width), F32),
             pltpu.VMEM((rows, width), BF16),
@@ -500,12 +591,10 @@
     ids = window_ids.reshape(-1, LANES)
     *sent, rows, location_key, place_keys = arrange_first(plan, tokens, ids)
     arrived = [[exchange(value, "loc", CORES * step) for step, value in enumerate(sent)]]
-    following = []
+    arranged = None
     for window in range(1, WINDOWS):
-        following = arrange_next(plan, window, rows, place_keys, arrived[-1][1:2])
-        arrived.append(
-            [exchange(value, "loc", CORES * step) for step, value in enumerate(following)]
-        )
+        *sent, arranged = arrange_next(plan, window, rows, place_keys, arrived[0][1:2])
+        arrived.append([exchange(value, "loc", CORES * step) for step, value in enumerate(sent)])
     mids, behind = [], []
     for window, slots in enumerate(arrived):
         hide = int(window == 0)
@@ -514,7 +603,7 @@
         tables = (band_index, band_table, spatial_qkv)
         for first in range(0, len(slots), half):
             if first > 0:
-                behind = [*following[:1], queries[-1]]
+                behind = [arranged, queries[-1]]
             own = join_slots(plan, slots[first : first + half], behind, 0 if hide else LONG)
             query, keys, values = project(plan, [own], *tables, True, hide)
             owns.append(own)
@@ -532,10 +621,10 @@
             every = lax.all_gather(owns[0], "loc", axis_index_groups=same, tiled=True)
             keys, values = project(plan, [every], *tables, False, hide)
             all_keys, all_values = [keys], [values]
-        mid = attend(
+        mid, done = attend(
             plan, queries, all_keys, all_values, owns, band_index, band_table, spatial_out, hide
         )
-        behind = [mid]
+        behind = [done]
         mids.append(mid)
     same = [
         [g * plan.locs + r * CORES + core for r in range(plan.rows_count) for g in range(plan.groups)]
@@ -553,8 +642,16 @@
         )
         parts = parts.reshape(plan.band_dev, plan.share, plan.groups, plan.part_rows, plan.width)
         parts = parts.transpose(0, 2, 1, 3, 4).reshape(plan.band_dev, plan.groups, -1, plan.width)
-        done = channel(plan, parts, channel_qkv, channel_out, up_weight, down_weight)
-        returned.append([exchange(value, "band", step) for step, value in enumerate(done)])
+        weights = (channel_qkv, channel_out, up_weight, down_weight)
+        now, later = list(range(plan.groups)), []
+        if mid is mids[-1] and plan.groups > 1:
+            now, later = now[1:], now[:1]
+        done = channel(plan, parts, now, later, *weights)
+        if later:
+            *done, rest = done
+            done += finish(plan, rest, later, plan.band_dev, up_weight, down_weight)
+        done = dict(zip([*now, *later], done))
+        returned.append([exchange(done[step], "band", step) for step in range(plan.groups)])
     return restore(plan, location_key, returned)
 
 

time: 124 us -> 122 us (0.984)
  Pallas kernels: 68 us -> 72.1 us
  waiting for transfers between devices: 19.5 us -> 15.8 us
    ppermute x15, waiting for transfers between devices: 17.4 us -> 12.6 us  [exchange(): lax.ppermute(value, axis, [(i, i ^ step) for i in range(lax.axis_size(axi...]
    pallas_call x4 -> x5, Pallas kernels: 49.2 us -> 53.2 us  [the longest x2 28.6 us: channel(): call(kernel, [jax.ShapeDtypeStruct((bands, locations, width), BF16)] * le...]
    unnamed x24 -> x22, local copies, waits for them, and re-layouts: 5.09 us -> 3.93 us
  transfers between devices with their start and end apart: 17 -> 17, of which waited for: 7 -> 6; matrix products, arithmetic and copies ran while one was open for 0% -> 0% of each run, Pallas kernels for 52% -> 56%
where the time goes in v10:
time: 122 us
  Pallas kernels  72.1 us (59%)
  starting transfers between devices  29.5 us (24%)
  waiting for transfers between devices  15.8 us (13%)
  local copies, waits for them, and re-layouts  3.93 us (3%)
    pallas_call x2, Pallas kernels, channel(): call(kernel, [jax.ShapeDtypeStruct((bands, locations, width), BF16)] * le...  28.6 us
    pallas_call x2, Pallas kernels, attend(): call(kernel, [jax.ShapeDtypeStruct((plan.rows_count, plan.groups, plan.pa...  19.8 us
    ppermute x15, starting transfers between devices, exchange(): lax.ppermute(value, axis, [(i, i ^ step) for i in range(lax.axis_size(axi...  18.9 us
    ppermute x15, waiting for transfers between devices, exchange(): lax.ppermute(value, axis, [(i, i ^ step) for i in range(lax.axis_size(axi...  12.6 us
    pallas_call x5, Pallas kernels, project(): call(kernel, [jax.ShapeDtypeStruct((rows, width), BF16)] * len(names), hi...  10.8 us
    all_to_all x2, starting transfers between devices, body(): lax.all_to_all(mid.reshape(-1, plan.part_rows, plan.width), ('band', 'loc...  10.7 us
    pallas_call x1, Pallas kernels, finish(): call(kernel, [jax.ShapeDtypeStruct((bands, locations, width), BF16)] * le...  4.84 us
    unnamed x22, local copies, waits for them, and re-layouts  3.93 us
  transfers between devices with their start and end apart: 17, of which 6 were waited for; matrix products, arithmetic and copies ran while one was open for 0% of the time, Pallas kernels for 56%

profile of v10, /device:TPU:0, one launch (start us, length us, event | category | flops | bytes accessed | tf_op | source)
XLA Modules:
  0.0 121.6 jit_solution(6125154331152417528)
XLA Ops:
  0.0 1.4 %copy-done.3 = bf16[256,4,768]{2,1,0:T(4,128)(2,1)S(1)} copy-done((bf16[256,4,768]{2,1,0:T(4,128)(2,1)S(1)}, bf16[256,4,768]{2,1,0:T(4,128)(2,1)}, u32[]{:S(2)}) %copy-start.3) | copy-done | bytes 1572888
  2.1 1.3 %shard_map.100 = (bf16[128,768]{1,0:T(8,128)(2,1)S(1)}, bf16[128,768]{1,0:T(8,128)(2,1)S(1)}, bf16[128,768]{1,0:T(8,128)(2,1)S(1)}, bf16[128,768]{1,0:T(8,128)(2...) custom-call(s32[16,128]{1,0:T(8,128)S(1)} %bitcast.7, ...), custom_call_target="tpu_custom_call" | custom-call | flops 402653184 | bytes 3145728 | tf_op jit(solution)/shard_map/pallas_call | solution.py:131
  3.4 3.1 %collective-permute-start = (bf16[128,768]{1,0:T(8,128)(2,1)S(1)}, bf16[128,768]{1,0:T(8,128)(2,1)S(1)}, u32[]{:S(2)}, u32[]{:S(2)}) collective-permute-start(bf16[128,768]{1,0:T(8,128)(2,1)S(1)} %get-tuple-element.43), channel_id=1, source_target_pairs={{0,2},{1,3},{2,0},{3,1},{4,6},{5,7},{6,4},{7,5},{8,10},{9,11},{10,... | collective-permute-start | bytes 589832 | tf_op jit(solution)/shard_map/ppermute | solution.py:61
  6.5 2.6 %collective-permute-start.1 = (bf16[128,768]{1,0:T(8,128)(2,1)S(1)}, bf16[128,768]{1,0:T(8,128)(2,1)S(1)}, u32[]{:S(2)}, u32[]{:S(2)}) collective-permute-start(bf16[128,768]{1,0:T(8,128)(2,1)S(1)} %get-tuple-element.44), channel_id=1, source_target_pairs={{0,4},{1,5},{2,6},{3,7},{4,0},{5,1},{6,2},{7,3},{8,12},{9,13},{10,... | collective-permute-start | bytes 589832 | tf_op jit(solution)/shard_map/ppermute | solution.py:61
  9.1 5.7 %collective-permute-done.refs_1_.rest_0_ = bf16[128,768]{1,0:T(8,128)(2,1)S(1)} collective-permute-done((bf16[128,768]{1,0:T(8,128)(2,1)S(1)}, bf16[128,768]{1,0:T(8,128)(2,1)S(1)}, u32[]{:S(2)}, u32[]{:S(2)}) %collective-permute-start) | collective-permute-done | bytes 196640 | tf_op jit(solution)/shard_map/ppermute | solution.py:61
  15.4 1.7 %shard_map.102 = (bf16[128,768]{1,0:T(8,128)(2,1)S(1)}, bf16[128,768]{1,0:T(8,128)(2,1)}, bf16[128,768]{1,0:T(8,128)(2,1)}, bf16[128,768]{1,0:T(8,128)(2,1)}, f32[8,128]{1,0:T(8,128)S(1)}) custom-call(bf16[1024,768]{1,0:T(8,128)(2,1)S(1)} %get-tuple-element.46.rows_ref, f32[1,1024]{1,0:T(1,128)S(1)} %get-tuple-element.47.place_ref, ...), custom_call_target="tpu_custom_call" | custom-call | flops 402653184 | bytes 3145728 | tf_op jit(solution)/shard_map/pallas_call | solution.py:154
  17.1 1.8 %shard_map.103 = (bf16[256,768]{1,0:T(8,128)(2,1)S(1)}, bf16[256,768]{1,0:T(8,128)(2,1)S(1)}, bf16[256,768]{1,0:T(8,128)(2,1)S(1)}) custom-call(s32[16]{0:T(128)S(1)} %copy-done.7, f32[16,768]{1,0:T(8,128)S(1)} %copy-done.1, bf16[768,2304]{1,0:T(8,128)(2,1)S(1)} %copy-done, bf16[256,768]{1,0:T(8,128)(2,1)S(1)} %shard_map.101.rest_0_), custom_call_target="tpu_custom_call" | custom-call | flops 905969664 | bytes 5111808 | tf_op jit(solution)/shard_map/pallas_call | solution.py:233
  19.0 4.7 %collective-permute-done.1.refs_0_ = bf16[128,768]{1,0:T(8,128)(2,1)S(1)} collective-permute-done((bf16[128,768]{1,0:T(8,128)(2,1)S(1)}, bf16[128,768]{1,0:T(8,128)(2,1)S(1)}, u32[]{:S(2)}, u32[]{:S(2)}) %collective-permute-start.1) | collective-permute-done | bytes 196640 | tf_op jit(solution)/shard_map/ppermute | solution.py:61
  24.3 3.4 %collective-permute-start.8 = (bf16[128,768]{1,0:T(8,128)(2,1)}, bf16[128,768]{1,0:T(8,128)(2,1)}, u32[]{:S(2)}, u32[]{:S(2)}) collective-permute-start(bf16[128,768]{1,0:T(8,128)(2,1)} %get-tuple-element.63), channel_id=1, source_target_pairs={{0,2},{1,3},{2,0},{3,1},{4,6},{5,7},{6,4},{7,5},{8,10},{9,11},{10,... | collective-permute-start | bytes 589832 | tf_op jit(solution)/shard_map/ppermute | solution.py:61
  27.7 1.1 collective-permute-start.9
  28.8 1.4 %collective-permute-start.10 = (bf16[128,768]{1,0:T(8,128)(2,1)}, bf16[128,768]{1,0:T(8,128)(2,1)}, u32[]{:S(2)}, u32[]{:S(2)}) collective-permute-start(bf16[128,768]{1,0:T(8,128)(2,1)} %get-tuple-element.65), channel_id=1, source_target_pairs={{0,6},{1,7},{2,4},{3,5},{4,2},{5,3},{6,0},{7,1},{8,14},{9,15},{10,... | collective-permute-start | bytes 589832 | tf_op jit(solution)/shard_map/ppermute | solution.py:61
  30.1 1.8 %shard_map.105 = (bf16[256,768]{1,0:T(8,128)(2,1)S(1)}, bf16[256,768]{1,0:T(8,128)(2,1)S(1)}, bf16[256,768]{1,0:T(8,128)(2,1)S(1)}) custom-call(s32[16]{0:T(128)S(1)} %copy-done.7, f32[16,768]{1,0:T(8,128)S(1)} %copy-done.1, bf16[768,2304]{1,0:T(8,128)(2,1)S(1)} %copy-done, bf16[256,768]{1,0:T(8,128)(2,1)S(1)} %shard_map.104.rest_0_.rest_1_), custom_call_target="tpu_custom_call" | custom-call | flops 905969664 | bytes 5111808 | tf_op jit(solution)/shard_map/pallas_call | solution.py:233
  32.0 2.2 %shard_map.106 = (bf16[512,768]{1,0:T(8,128)(2,1)S(1)}, bf16[512,768]{1,0:T(8,128)(2,1)S(1)}) custom-call(s32[16]{0:T(128)S(1)} %copy-done.7, f32[16,768]{1,0:T(8,128)S(1)} %copy-done.1, bf16[768,2304]{1,0:T(8,128)(2,1)S(1)} %copy-done, bf16[256,768]{1,0:T(8,128)(2,1)S(1)} %collective-permute-done.3.rest_0_, ...), custom_call_target="tpu_custom_call" | custom-call | flops 1207959552 | bytes 5898240 | tf_op jit(solution)/shard_map/pallas_call | solution.py:233
  34.2 9.4 %shard_map.107 = (bf16[4,4,32,768]{3,2,1,0:T(8,128)(2,1)S(1)}, f32[8,128]{1,0:T(8,128)S(1)}) custom-call(s32[16]{0:T(128)S(1)} %copy-done.7, f32[16,768]{1,0:T(8,128)S(1)} %copy-done.1, bf16[768,768]{1,0:T(8,128)(2,1)S(1)} %copy-done.4, bf16[256,768]{1,0:T(8,128)(2,1)S(1)} %shard_map.101.rest_0_, bf16[256,768]{1,0:T(8,128)(2,1)S(1)} %shard_map.104.rest_0_.rest_1_, ...), custom_call_target="tpu_custom_call" | custom-call | flops 6442450944 | bytes 6684672 | tf_op jit(solution)/shard_map/pallas_call | solution.py:341
  44.5 5.8 %all-to-all-start = ((bf16[16,32,768]{2,1,0:T(8,128)(2,1)}), bf16[16,32,768]{2,1,0:T(8,128)(2,1)}, u32[]{:S(2)}, u32[]{:S(2)}) async-start(bf16[16,32,768]{2,1,0:T(8,128)(2,1)} %bitcast.5), calls=%async_computation | async-start | bytes 1572864 | tf_op jit(solution)/shard_map/all_to_all | solution.py:635
  51.3 1.4 %shard_map.109.rest_0_ = bf16[512,768]{1,0:T(8,128)(2,1)S(1)} custom-call(bf16[128,768]{1,0:T(8,128)(2,1)S(1)} %copy-done.10, bf16[128,768]{1,0:T(8,128)(2,1)} %collective-permute-done.8.refs_1_, bf16[128,768]{1,0:T(8,128)(2,1)} %collective-permute-done.9.refs_2_, bf16[128,768]{1,0:T(8,128)(2,1)} %collective-permute-done.10.refs_3_, ...), custom_call_target="tpu_custom_call" | custom-call | flops 68719476736 | tf_op jit(solution)/shard_map/pallas_call | solution.py:180
  52.7 2.8 %shard_map.110 = (bf16[512,768]{1,0:T(8,128)(2,1)S(1)}, bf16[512,768]{1,0:T(8,128)(2,1)S(1)}, bf16[512,768]{1,0:T(8,128)(2,1)S(1)}) custom-call(s32[16]{0:T(128)S(1)} %copy-done.7, f32[16,768]{1,0:T(8,128)S(1)} %copy-done.2, bf16[768,2304]{1,0:T(8,128)(2,1)S(1)} %copy-done, bf16[512,768]{1,0:T(8,128)(2,1)S(1)} %shard_map.109.rest_0_), custom_call_target="tpu_custom_call" | custom-call | tf_op jit(solution)/shard_map/pallas_call | solution.py:233
  55.6 2.2 %shard_map.111 = (bf16[512,768]{1,0:T(8,128)(2,1)S(1)}, bf16[512,768]{1,0:T(8,128)(2,1)S(1)}) custom-call(s32[16]{0:T(128)S(1)} %copy-done.7, f32[16,768]{1,0:T(8,128)S(1)} %copy-done.2, bf16[768,2304]{1,0:T(8,128)(2,1)S(1)} %copy-done, bf16[512,768]{1,0:T(8,128)(2,1)S(1)} %collective-permute-done.11.rest_0_, bf16[512,768]{1,0:T(8,128)(2,1)S(1)} %get-tuple-element.67.rest_1_), custom_call_target="tpu_custom_call" | custom-call | tf_op jit(solution)/shard_map/pallas_call | solution.py:233
  57.7 10.3 %shard_map.112 = (bf16[4,4,32,768]{3,2,1,0:T(8,128)(2,1)}, f32[8,128]{1,0:T(8,128)}) custom-call(s32[16]{0:T(128)S(1)} %copy-done.7, f32[16,768]{1,0:T(8,128)S(1)} %copy-done.2, bf16[768,768]{1,0:T(8,128)(2,1)S(1)} %copy-done.5, bf16[512,768]{1,0:T(8,128)(2,1)S(1)} %shard_map.109.rest_0_, bf16[512,768]{1,0:T(8,128)(2,1)S(1)} %get-tuple-element.67.rest_1_, ...), custom_call_target="tpu_custom_call" | custom-call | tf_op jit(solution)/shard_map/pallas_call | solution.py:341
  68.1 2.0 %all-to-all-done = bf16[16,32,768]{2,1,0:T(8,128)(2,1)} async-done(((bf16[16,32,768]{2,1,0:T(8,128)(2,1)}), bf16[16,32,768]{2,1,0:T(8,128)(2,1)}, u32[]{:S(2)}, u32[]{:S(2)}) %all-to-all-start) | async-done | bytes 786464 | tf_op jit(solution)/shard_map/all_to_all | solution.py:635
  70.1 4.9 %all-to-all-start.1 = ((bf16[16,32,768]{2,1,0:T(8,128)(2,1)}), bf16[16,32,768]{2,1,0:T(8,128)(2,1)S(1)}, u32[]{:S(2)}, u32[]{:S(2)}) async-start(bf16[16,32,768]{2,1,0:T(8,128)(2,1)} %bitcast.3), calls=%async_computation.1 | async-start | bytes 1572864 | tf_op jit(solution)/shard_map/all_to_all | solution.py:635
  75.0 15.3 %shard_map.108 = (bf16[4,32,768]{2,1,0:T(8,128)(2,1)S(1)}, bf16[4,32,768]{2,1,0:T(8,128)(2,1)S(1)}, bf16[4,32,768]{2,1,0:T(8,128)(2,1)S(1)}, bf16[4,32,768]{2,1,0:T(8,128)(2,1)S(1)}) custom-call(bf16[768,2304]{1,0:T(8,128)(2,1)} %qkv_hbm.3, bf16[768,768]{1,0:T(8,128)(2,1)} %out_hbm.3, bf16[768,3072]{1,0:T(8,128)(2,1)} %up_hbm.5, bf16[3072,768]{1,0:T(8,128)(2,1)} %down_hbm.5, ...), custom_call_target="tpu_custom_call" | custom-call | flops 7247757312 | bytes 15728640 | tf_op jit(solution)/shard_map/pallas_call | solution.py:531
  90.3 2.0 %collective-permute-start.5 = (bf16[4,32,768]{2,1,0:T(8,128)(2,1)S(1)}, bf16[4,32,768]{2,1,0:T(8,128)(2,1)S(1)}, u32[]{:S(2)}, u32[]{:S(2)}) collective-permute-start(bf16[4,32,768]{2,1,0:T(8,128)(2,1)S(1)} %get-tuple-element.59), channel_id=1, source_target_pairs={{0,8},{8,0},{16,24},{24,16},{1,9},{9,1},{17,25},{25,17},{2,10},{10... | collective-permute-start | bytes 589832 | tf_op jit(solution)/shard_map/ppermute | solution.py:61
  92.3 1.5 %collective-permute-start.6 = (bf16[4,32,768]{2,1,0:T(8,128)(2,1)S(1)}, bf16[4,32,768]{2,1,0:T(8,128)(2,1)S(1)}, u32[]{:S(2)}, u32[]{:S(2)}) collective-permute-start(bf16[4,32,768]{2,1,0:T(8,128)(2,1)S(1)} %get-tuple-element.60), channel_id=1, source_target_pairs={{0,16},{8,24},{16,0},{24,8},{1,17},{9,25},{17,1},{25,9},{2,18},{10... | collective-permute-start | bytes 589832 | tf_op jit(solution)/shard_map/ppermute | solution.py:61
  93.9 1.2 all-to-all-done.1
  95.0 13.3 %shard_map.113 = (bf16[4,32,768]{2,1,0:T(8,128)(2,1)S(1)}, bf16[4,32,768]{2,1,0:T(8,128)(2,1)S(1)}, bf16[4,32,768]{2,1,0:T(8,128)(2,1)S(1)}, f32[128,768]{1,0:T(8,128)S(1)}) custom-call(bf16[768,2304]{1,0:T(8,128)(2,1)} %qkv_hbm.3, bf16[768,768]{1,0:T(8,128)(2,1)} %out_hbm.3, bf16[768,3072]{1,0:T(8,128)(2,1)} %up_hbm.5, bf16[3072,768]{1,0:T(8,128)(2,1)} %down_hbm.5, ...), custom_call_target="tpu_custom_call" | custom-call | flops 7247757312 | bytes 15728640 | tf_op jit(solution)/shard_map/pallas_call | solution.py:531
  109.1 1.5 %collective-permute-start.13 = (bf16[4,32,768]{2,1,0:T(8,128)(2,1)S(1)}, bf16[4,32,768]{2,1,0:T(8,128)(2,1)S(1)}, u32[]{:S(2)}, u32[]{:S(2)}) collective-permute-start(bf16[4,32,768]{2,1,0:T(8,128)(2,1)S(1)} %get-tuple-element.75), channel_id=1, source_target_pairs={{0,16},{8,24},{16,0},{24,8},{1,17},{9,25},{17,1},{25,9},{2,18},{10... | collective-permute-start | bytes 589832 | tf_op jit(solution)/shard_map/ppermute | solution.py:61
  110.6 1.3 %collective-permute-start.14 = (bf16[4,32,768]{2,1,0:T(8,128)(2,1)S(1)}, bf16[4,32,768]{2,1,0:T(8,128)(2,1)S(1)}, u32[]{:S(2)}, u32[]{:S(2)}) collective-permute-start(bf16[4,32,768]{2,1,0:T(8,128)(2,1)S(1)} %get-tuple-element.76), channel_id=1, source_target_pairs={{0,24},{8,16},{16,8},{24,0},{1,25},{9,17},{17,9},{25,1},{2,26},{10... | collective-permute-start | bytes 589832 | tf_op jit(solution)/shard_map/ppermute | solution.py:61
  111.9 4.8 %shard_map.114.refs_4_ = bf16[4,32,768]{2,1,0:T(8,128)(2,1)S(1)} custom-call(bf16[768,3072]{1,0:T(8,128)(2,1)} %up_hbm.5, bf16[3072,768]{1,0:T(8,128)(2,1)} %down_hbm.5, f32[128,768]{1,0:T(8,128)S(1)} %get-tuple-element.73.rest_ref), custom_call_target="tpu_custom_call" | custom-call | flops 1207959552 | bytes 9437184 | tf_op jit(solution)/shard_map/pallas_call | solution.py:433
  116.8 1.2 collective-permute-done.13.refs_6_
  117.9 1.0 collective-permute-done.14.refs_7_
  118.9 2.7 %shard_map.115 = bf16[256,4,768]{2,1,0:T(4,128)(2,1)} custom-call(f32[1,256]{1,0:T(1,128)S(1)} %get-tuple-element.41.keys_ref, bf16[4,32,768]{2,1,0:T(8,128)(2,1)S(1)} %get-tuple-element.58.refs_0_, bf16[4,32,768]{2,1,0:T(8,128)(2,1)S(1)} %collective-permute-done.5.refs_1_, bf16[4,32,768]{2,1,0:T(8,128)(2,1)S(1)} %collective-permute-done.6.refs_2_, ...), custom_call_target="tpu_custom_call" | custom-call | flops 402653184 | bytes 3145728 | tf_op jit(solution)/shard_map/pallas_call | solution.py:570
  (40 shorter events, 4.7 us)
Async XLA Ops:
  0.0 1.4 %copy-start.3 = (bf16[256,4,768]{2,1,0:T(4,128)(2,1)S(1)}, bf16[256,4,768]{2,1,0:T(4,128)(2,1)}, u32[]{:S(2)}) copy-start(bf16[256,4,768]{2,1,0:T(4,128)(2,1)} %x_ref.1) | copy-start | bytes 4718596
  1.4 0.7 copy-start.8
  2.1 15.0 %copy-start = (bf16[768,2304]{1,0:T(8,128)(2,1)S(1)}, bf16[768,2304]{1,0:T(8,128)(2,1)}, u32[]{:S(2)}) copy-start(bf16[768,2304]{1,0:T(8,128)(2,1)} %w_ref.12) | copy-start | bytes 10616836
  3.4 13.7 %copy-start.1 = (f32[16,768]{1,0:T(8,128)S(1)}, f32[16,768]{1,0:T(8,128)}, u32[]{:S(2)}) copy-start(f32[16,768]{1,0:T(8,128)} %table_ref.13) | copy-start | bytes 147460
  3.4 13.7 %copy-start.7 = (s32[16]{0:T(128)S(1)}, s32[16]{0:T(128)}, u32[]{:S(2)}) copy-start(s32[16]{0:T(128)} %index_ref.13) | copy-start | bytes 196
  3.4 11.4 %collective-permute-start = (bf16[128,768]{1,0:T(8,128)(2,1)S(1)}, bf16[128,768]{1,0:T(8,128)(2,1)S(1)}, u32[]{:S(2)}, u32[]{:S(2)}) collective-permute-start(bf16[128,768]{1,0:T(8,128)(2,1)S(1)} %get-tuple-element.43), channel_id=1, source_target_pairs={{0,2},{1,3},{2,0},{3,1},{4,6},{5,7},{6,4},{7,5},{8,10},{9,11},{10,... | collective-permute-start | bytes 589832 | tf_op jit(solution)/shard_map/ppermute | solution.py:61
  6.5 17.2 %collective-permute-start.1 = (bf16[128,768]{1,0:T(8,128)(2,1)S(1)}, bf16[128,768]{1,0:T(8,128)(2,1)S(1)}, u32[]{:S(2)}, u32[]{:S(2)}) collective-permute-start(bf16[128,768]{1,0:T(8,128)(2,1)S(1)} %get-tuple-element.44), channel_id=1, source_target_pairs={{0,4},{1,5},{2,6},{3,7},{4,0},{5,1},{6,2},{7,3},{8,12},{9,13},{10,... | collective-permute-start | bytes 589832 | tf_op jit(solution)/shard_map/ppermute | solution.py:61
  9.1 14.6 %collective-permute-start.2 = (bf16[128,768]{1,0:T(8,128)(2,1)S(1)}, bf16[128,768]{1,0:T(8,128)(2,1)S(1)}, u32[]{:S(2)}, u32[]{:S(2)}) collective-permute-start(bf16[128,768]{1,0:T(8,128)(2,1)S(1)} %get-tuple-element.45), channel_id=1, source_target_pairs={{0,6},{1,7},{2,4},{3,5},{4,2},{5,3},{6,0},{7,1},{8,14},{9,15},{10,... | collective-permute-start | bytes 589832 | tf_op jit(solution)/shard_map/ppermute | solution.py:61
  15.3 16.7 %collective-permute-start.3 = (bf16[256,768]{1,0:T(8,128)(2,1)S(1)}, bf16[256,768]{1,0:T(8,128)(2,1)S(1)}, u32[]{:S(2)}, u32[]{:S(2)}) collective-permute-start(bf16[256,768]{1,0:T(8,128)(2,1)S(1)} %shard_map.101.rest_0_), channel_id=1, source_target_pairs={{0,1},{1,0},{2,3},{3,2},{4,5},{5,4},{6,7},{7,6},{8,9},{9,8},{10,11... | collective-permute-start | bytes 1179656 | tf_op jit(solution)/shard_map/ppermute | solution.py:61
  17.1 1.9 %copy-start.9 = (bf16[128,768]{1,0:T(8,128)(2,1)}, bf16[128,768]{1,0:T(8,128)(2,1)S(1)}, u32[]{:S(2)}) copy-start(bf16[128,768]{1,0:T(8,128)(2,1)S(1)} %get-tuple-element.62.refs_0_) | copy-start | bytes 589828
  24.2 7.8 %collective-permute-start.4 = (bf16[256,768]{1,0:T(8,128)(2,1)S(1)}, bf16[256,768]{1,0:T(8,128)(2,1)S(1)}, u32[]{:S(2)}, u32[]{:S(2)}) collective-permute-start(bf16[256,768]{1,0:T(8,128)(2,1)S(1)} %shard_map.104.rest_0_.rest_1_), channel_id=1, source_target_pairs={{0,1},{1,0},{2,3},{3,2},{4,5},{5,4},{6,7},{7,6},{8,9},{9,8},{10,11... | collective-permute-start | bytes 1179656 | tf_op jit(solution)/shard_map/ppermute | solution.py:61
  24.3 26.1 %collective-permute-start.8 = (bf16[128,768]{1,0:T(8,128)(2,1)}, bf16[128,768]{1,0:T(8,128)(2,1)}, u32[]{:S(2)}, u32[]{:S(2)}) collective-permute-start(bf16[128,768]{1,0:T(8,128)(2,1)} %get-tuple-element.63), channel_id=1, source_target_pairs={{0,2},{1,3},{2,0},{3,1},{4,6},{5,7},{6,4},{7,5},{8,10},{9,11},{10,... | collective-permute-start | bytes 589832 | tf_op jit(solution)/shard_map/ppermute | solution.py:61
  27.7 22.7 %collective-permute-start.9 = (bf16[128,768]{1,0:T(8,128)(2,1)}, bf16[128,768]{1,0:T(8,128)(2,1)}, u32[]{:S(2)}, u32[]{:S(2)}) collective-permute-start(bf16[128,768]{1,0:T(8,128)(2,1)} %get-tuple-element.64), channel_id=1, source_target_pairs={{0,4},{1,5},{2,6},{3,7},{4,0},{5,1},{6,2},{7,3},{8,12},{9,13},{10,... | collective-permute-start | bytes 589832 | tf_op jit(solution)/shard_map/ppermute | solution.py:61
  28.8 21.6 %collective-permute-start.10 = (bf16[128,768]{1,0:T(8,128)(2,1)}, bf16[128,768]{1,0:T(8,128)(2,1)}, u32[]{:S(2)}, u32[]{:S(2)}) collective-permute-start(bf16[128,768]{1,0:T(8,128)(2,1)} %get-tuple-element.65), channel_id=1, source_target_pairs={{0,6},{1,7},{2,4},{3,5},{4,2},{5,3},{6,0},{7,1},{8,14},{9,15},{10,... | collective-permute-start | bytes 589832 | tf_op jit(solution)/shard_map/ppermute | solution.py:61
  32.0 2.2 %copy-start.4 = (bf16[768,768]{1,0:T(8,128)(2,1)S(1)}, bf16[768,768]{1,0:T(8,128)(2,1)}, u32[]{:S(2)}) copy-start(bf16[768,768]{1,0:T(8,128)(2,1)} %w_ref.13) | copy-start | bytes 3538948
  43.7 0.9 copy-start.6
  44.5 25.5 %all-to-all-start = ((bf16[16,32,768]{2,1,0:T(8,128)(2,1)}), bf16[16,32,768]{2,1,0:T(8,128)(2,1)}, u32[]{:S(2)}, u32[]{:S(2)}) async-start(bf16[16,32,768]{2,1,0:T(8,128)(2,1)} %bitcast.5), calls=%async_computation | async-start | bytes 1572864 | tf_op jit(solution)/shard_map/all_to_all | solution.py:635
  50.3 0.9 copy-start.10
  51.3 1.5 %copy-start.2 = (f32[16,768]{1,0:T(8,128)S(1)}, f32[16,768]{1,0:T(8,128)}, u32[]{:S(2)}) copy-start(f32[16,768]{1,0:T(8,128)} %table_ref.13) | copy-start | bytes 147460
  52.7 2.9 %collective-permute-start.11 = (bf16[512,768]{1,0:T(8,128)(2,1)S(1)}, bf16[512,768]{1,0:T(8,128)(2,1)S(1)}, u32[]{:S(2)}, u32[]{:S(2)}) collective-permute-start(bf16[512,768]{1,0:T(8,128)(2,1)S(1)} %shard_map.109.rest_0_), channel_id=1, source_target_pairs={{0,1},{1,0},{2,3},{3,2},{4,5},{5,4},{6,7},{7,6},{8,9},{9,8},{10,11... | collective-permute-start | bytes 2359304 | tf_op jit(solution)/shard_map/ppermute | solution.py:61
  55.5 2.2 %copy-start.5 = (bf16[768,768]{1,0:T(8,128)(2,1)S(1)}, bf16[768,768]{1,0:T(8,128)(2,1)}, u32[]{:S(2)}) copy-start(bf16[768,768]{1,0:T(8,128)(2,1)} %w_ref.13) | copy-start | bytes 3538948
  70.1 25.0 %all-to-all-start.1 = ((bf16[16,32,768]{2,1,0:T(8,128)(2,1)}), bf16[16,32,768]{2,1,0:T(8,128)(2,1)S(1)}, u32[]{:S(2)}, u32[]{:S(2)}) async-start(bf16[16,32,768]{2,1,0:T(8,128)(2,1)} %bitcast.3), calls=%async_computation.1 | async-start | bytes 1572864 | tf_op jit(solution)/shard_map/all_to_all | solution.py:635
  90.3 20.3 %collective-permute-start.5 = (bf16[4,32,768]{2,1,0:T(8,128)(2,1)S(1)}, bf16[4,32,768]{2,1,0:T(8,128)(2,1)S(1)}, u32[]{:S(2)}, u32[]{:S(2)}) collective-permute-start(bf16[4,32,768]{2,1,0:T(8,128)(2,1)S(1)} %get-tuple-element.59), channel_id=1, source_target_pairs={{0,8},{8,0},{16,24},{24,16},{1,9},{9,1},{17,25},{25,17},{2,10},{10... | collective-permute-start | bytes 589832 | tf_op jit(solution)/shard_map/ppermute | solution.py:61
  92.3 24.4 %collective-permute-start.6 = (bf16[4,32,768]{2,1,0:T(8,128)(2,1)S(1)}, bf16[4,32,768]{2,1,0:T(8,128)(2,1)S(1)}, u32[]{:S(2)}, u32[]{:S(2)}) collective-permute-start(bf16[4,32,768]{2,1,0:T(8,128)(2,1)S(1)} %get-tuple-element.60), channel_id=1, source_target_pairs={{0,16},{8,24},{16,0},{24,8},{1,17},{9,25},{17,1},{25,9},{2,18},{10... | collective-permute-start | bytes 589832 | tf_op jit(solution)/shard_map/ppermute | solution.py:61
  93.8 23.0 %collective-permute-start.7 = (bf16[4,32,768]{2,1,0:T(8,128)(2,1)S(1)}, bf16[4,32,768]{2,1,0:T(8,128)(2,1)S(1)}, u32[]{:S(2)}, u32[]{:S(2)}) collective-permute-start(bf16[4,32,768]{2,1,0:T(8,128)(2,1)S(1)} %get-tuple-element.61), channel_id=1, source_target_pairs={{0,24},{8,16},{16,8},{24,0},{1,25},{9,17},{17,9},{25,1},{2,26},{10... | collective-permute-start | bytes 589832 | tf_op jit(solution)/shard_map/ppermute | solution.py:61
  108.3 8.4 %collective-permute-start.12 = (bf16[4,32,768]{2,1,0:T(8,128)(2,1)S(1)}, bf16[4,32,768]{2,1,0:T(8,128)(2,1)S(1)}, u32[]{:S(2)}, u32[]{:S(2)}) collective-permute-start(bf16[4,32,768]{2,1,0:T(8,128)(2,1)S(1)} %get-tuple-element.74), channel_id=1, source_target_pairs={{0,8},{8,0},{16,24},{24,16},{1,9},{9,1},{17,25},{25,17},{2,10},{10... | collective-permute-start | bytes 589832 | tf_op jit(solution)/shard_map/ppermute | solution.py:61
  109.1 8.8 %collective-permute-start.13 = (bf16[4,32,768]{2,1,0:T(8,128)(2,1)S(1)}, bf16[4,32,768]{2,1,0:T(8,128)(2,1)S(1)}, u32[]{:S(2)}, u32[]{:S(2)}) collective-permute-start(bf16[4,32,768]{2,1,0:T(8,128)(2,1)S(1)} %get-tuple-element.75), channel_id=1, source_target_pairs={{0,16},{8,24},{16,0},{24,8},{1,17},{9,25},{17,1},{25,9},{2,18},{10... | collective-permute-start | bytes 589832 | tf_op jit(solution)/shard_map/ppermute | solution.py:61
  110.6 8.3 %collective-permute-start.14 = (bf16[4,32,768]{2,1,0:T(8,128)(2,1)S(1)}, bf16[4,32,768]{2,1,0:T(8,128)(2,1)S(1)}, u32[]{:S(2)}, u32[]{:S(2)}) collective-permute-start(bf16[4,32,768]{2,1,0:T(8,128)(2,1)S(1)} %get-tuple-element.76), channel_id=1, source_target_pairs={{0,24},{8,16},{16,8},{24,0},{1,25},{9,17},{17,9},{25,1},{2,26},{10... | collective-permute-start | bytes 589832 | tf_op jit(solution)/shard_map/ppermute | solution.py:61

commit v11 on v10

--- a/solution.py
+++ b/solution.py
@@ -155,7 +155,7 @@
         kernel,
         [jax.ShapeDtypeStruct((plan.rows, plan.width), BF16)] * count + [marker()],
         2 * plan.loc_dev * rows.size,
-        4 * rows.size,
+        0,
         in_specs=[VMEM] * 2 + [ANY] * len(after),
         out_specs=[VMEM] * (count + 1),
     )(rows, place_keys, *after)
@@ -345,7 +345,7 @@
             marker(),
         ],
         hide * 16 * total * key_rows * width,
-        hide * 2 * width * (2 * key_rows + 3 * total + width),
+        0,
         in_specs=[SMEM] + [VMEM] * (2 + 2 * sources + 2 * pieces),
         out_specs=[VMEM] * 2,
         scratch_shapes=[pltpu.VMEM((total, width), BF16), pltpu.VMEM((total, width), F32)],
@@ -448,7 +448,7 @@
     )(up_weight, down_weight, rest)
 
 
-def channel(plan, parts, now, later, channel_qkv, channel_out, up_weight, down_weight):
+def channel(plan, parts, now, later, fetch, channel_qkv, channel_out, up_weight, down_weight):
     groups, width = plan.groups, plan.width
     bands, _, locations, _ = parts.shape
     small = GROUP_LOCS
@@ -462,7 +462,11 @@
     def kernel(qkv_hbm, out_hbm, up_hbm, down_hbm, *refs):
         in_ref, *refs = refs
         outs, refs = refs[:count], refs[count:]
-        mid, normed, packed, attended, qkv_ref, out_ref, up_ref, down_ref, sems = refs
+        mid, normed, packed, attended, qkv_ref, out_ref, up_ref, down_ref, sems, *held = refs
+        if held:
+            load = pltpu.make_async_copy(in_ref, held[0], sems.at[6])
+            load.start()
+            in_ref = held[0]
         me = lax.axis_index("band")
         columns = [pl.ds(first, width) for first in range(0, 3 * width, width)]
         copies = []
@@ -480,6 +484,8 @@
                 )
         for copy in copies[: len(columns)]:
             copy.start()
+        if held:
+            load.wait()
         for (owner, band, first), places in piece_places(owners, bands, locations).items():
             piece = in_ref[band, me ^ owner, first : first + TILE_LOCS, :].astype(F32)
             for number, place in enumerate(places):
@@ -535,7 +541,7 @@
         2 * rows * size,
         2 * (2 * rows * width + size),
         limit=WIDE_LIMIT,
-        in_specs=[ANY] * 4 + [VMEM],
+        in_specs=[ANY] * 4 + [ANY if fetch else VMEM],
         out_specs=[VMEM] * count,
         scratch_shapes=[
             pltpu.VMEM((rows, width), F32),
@@ -544,7 +550,8 @@
             pltpu.VMEM((rows, width), BF16),
         ]
         + [pltpu.VMEM(weight.shape, BF16) for weight in weights]
-        + [pltpu.SemaphoreType.DMA((6,))],
+        + [pltpu.SemaphoreType.DMA((7,))]
+        + [pltpu.VMEM(parts.shape, BF16)] * fetch,
     )(*weights, parts)
 
 
@@ -646,7 +653,7 @@
         now, later = list(range(plan.groups)), []
         if mid is mids[-1] and plan.groups > 1:
             now, later = now[1:], now[:1]
-        done = channel(plan, parts, now, later, *weights)
+        done = channel(plan, parts, now, later, mid is not mids[-1], *weights)
         if later:
             *done, rest = done
             done += finish(plan, rest, later, plan.band_dev, up_weight, down_weight)

time: 122 us -> 122 us (level)
  transfers between devices with their start and end apart: 17 -> 17, of which waited for: 6 -> 6; matrix products, arithmetic and copies ran while one was open for 0% -> 0% of each run, Pallas kernels for 56% -> 55%
where the time goes in v11:
time: 122 us
  Pallas kernels  71.2 us (58%)
  starting transfers between devices  29.5 us (24%)
  waiting for transfers between devices  16.6 us (14%)
  local copies, waits for them, and re-layouts  3.93 us (3%)
    pallas_call x2, Pallas kernels, channel(): call(kernel, [jax.ShapeDtypeStruct((bands, locations, width), BF16)] * le...  27.7 us
    pallas_call x2, Pallas kernels, attend(): call(kernel, [jax.ShapeDtypeStruct((plan.rows_count, plan.groups, plan.pa...  19.8 us
    ppermute x15, starting transfers between devices, exchange(): lax.ppermute(value, axis, [(i, i ^ step) for i in range(lax.axis_size(axi...  18.9 us
    ppermute x15, waiting for transfers between devices, exchange(): lax.ppermute(value, axis, [(i, i ^ step) for i in range(lax.axis_size(axi...  12.6 us
    pallas_call x5, Pallas kernels, project(): call(kernel, [jax.ShapeDtypeStruct((rows, width), BF16)] * len(names), hi...  10.8 us
    all_to_all x2, starting transfers between devices, body(): lax.all_to_all(mid.reshape(-1, plan.part_rows, plan.width), ('band', 'loc...  10.7 us
    pallas_call x1, Pallas kernels, finish(): call(kernel, [jax.ShapeDtypeStruct((bands, locations, width), BF16)] * le...  4.84 us
    all_to_all x2, waiting for transfers between devices, body(): lax.all_to_all(mid.reshape(-1, plan.part_rows, plan.width), ('band', 'loc...  4.03 us
  transfers between devices with their start and end apart: 17, of which 6 were waited for; matrix products, arithmetic and copies ran while one was open for 0% of the time, Pallas kernels for 55%

profile of v11, /device:TPU:0, one launch (start us, length us, event | category | flops | bytes accessed | tf_op | source)
XLA Modules:
  0.0 121.6 jit_solution(6866339747058899543)
XLA Ops:
  0.0 1.4 %copy-done.3 = bf16[256,4,768]{2,1,0:T(4,128)(2,1)S(1)} copy-done((bf16[256,4,768]{2,1,0:T(4,128)(2,1)S(1)}, bf16[256,4,768]{2,1,0:T(4,128)(2,1)}, u32[]{:S(2)}) %copy-start.3) | copy-done | bytes 1572888
  2.1 1.3 %shard_map.100 = (bf16[128,768]{1,0:T(8,128)(2,1)S(1)}, bf16[128,768]{1,0:T(8,128)(2,1)S(1)}, bf16[128,768]{1,0:T(8,128)(2,1)S(1)}, bf16[128,768]{1,0:T(8,128)(2...) custom-call(s32[16,128]{1,0:T(8,128)S(1)} %bitcast.7, ...), custom_call_target="tpu_custom_call" | custom-call | flops 402653184 | bytes 3145728 | tf_op jit(solution)/shard_map/pallas_call | solution.py:131
  3.4 3.1 %collective-permute-start = (bf16[128,768]{1,0:T(8,128)(2,1)S(1)}, bf16[128,768]{1,0:T(8,128)(2,1)S(1)}, u32[]{:S(2)}, u32[]{:S(2)}) collective-permute-start(bf16[128,768]{1,0:T(8,128)(2,1)S(1)} %get-tuple-element.43), channel_id=1, source_target_pairs={{0,2},{1,3},{2,0},{3,1},{4,6},{5,7},{6,4},{7,5},{8,10},{9,11},{10,... | collective-permute-start | bytes 589832 | tf_op jit(solution)/shard_map/ppermute | solution.py:61
  6.5 2.6 %collective-permute-start.1 = (bf16[128,768]{1,0:T(8,128)(2,1)S(1)}, bf16[128,768]{1,0:T(8,128)(2,1)S(1)}, u32[]{:S(2)}, u32[]{:S(2)}) collective-permute-start(bf16[128,768]{1,0:T(8,128)(2,1)S(1)} %get-tuple-element.44), channel_id=1, source_target_pairs={{0,4},{1,5},{2,6},{3,7},{4,0},{5,1},{6,2},{7,3},{8,12},{9,13},{10,... | collective-permute-start | bytes 589832 | tf_op jit(solution)/shard_map/ppermute | solution.py:61
  9.1 5.7 %collective-permute-done.refs_1_.rest_0_ = bf16[128,768]{1,0:T(8,128)(2,1)S(1)} collective-permute-done((bf16[128,768]{1,0:T(8,128)(2,1)S(1)}, bf16[128,768]{1,0:T(8,128)(2,1)S(1)}, u32[]{:S(2)}, u32[]{:S(2)}) %collective-permute-start) | collective-permute-done | bytes 196640 | tf_op jit(solution)/shard_map/ppermute | solution.py:61
  15.4 1.7 %shard_map.102 = (bf16[128,768]{1,0:T(8,128)(2,1)S(1)}, bf16[128,768]{1,0:T(8,128)(2,1)}, bf16[128,768]{1,0:T(8,128)(2,1)}, bf16[128,768]{1,0:T(8,128)(2,1)}, f32[8,128]{1,0:T(8,128)S(1)}) custom-call(bf16[1024,768]{1,0:T(8,128)(2,1)S(1)} %get-tuple-element.46.rows_ref, f32[1,1024]{1,0:T(1,128)S(1)} %get-tuple-element.47.place_ref, ...), custom_call_target="tpu_custom_call" | custom-call | flops 402653184 | tf_op jit(solution)/shard_map/pallas_call | solution.py:154
  17.1 1.8 %shard_map.103 = (bf16[256,768]{1,0:T(8,128)(2,1)S(1)}, bf16[256,768]{1,0:T(8,128)(2,1)S(1)}, bf16[256,768]{1,0:T(8,128)(2,1)S(1)}) custom-call(s32[16]{0:T(128)S(1)} %copy-done.7, f32[16,768]{1,0:T(8,128)S(1)} %copy-done.1, bf16[768,2304]{1,0:T(8,128)(2,1)S(1)} %copy-done, bf16[256,768]{1,0:T(8,128)(2,1)S(1)} %shard_map.101.rest_0_), custom_call_target="tpu_custom_call" | custom-call | flops 905969664 | bytes 5111808 | tf_op jit(solution)/shard_map/pallas_call | solution.py:233
  19.0 4.7 %collective-permute-done.1.refs_0_ = bf16[128,768]{1,0:T(8,128)(2,1)S(1)} collective-permute-done((bf16[128,768]{1,0:T(8,128)(2,1)S(1)}, bf16[128,768]{1,0:T(8,128)(2,1)S(1)}, u32[]{:S(2)}, u32[]{:S(2)}) %collective-permute-start.1) | collective-permute-done | bytes 196640 | tf_op jit(solution)/shard_map/ppermute | solution.py:61
  24.3 3.4 %collective-permute-start.8 = (bf16[128,768]{1,0:T(8,128)(2,1)}, bf16[128,768]{1,0:T(8,128)(2,1)}, u32[]{:S(2)}, u32[]{:S(2)}) collective-permute-start(bf16[128,768]{1,0:T(8,128)(2,1)} %get-tuple-element.63), channel_id=1, source_target_pairs={{0,2},{1,3},{2,0},{3,1},{4,6},{5,7},{6,4},{7,5},{8,10},{9,11},{10,... | collective-permute-start | bytes 589832 | tf_op jit(solution)/shard_map/ppermute | solution.py:61
  27.7 1.1 collective-permute-start.9
  28.8 1.4 %collective-permute-start.10 = (bf16[128,768]{1,0:T(8,128)(2,1)}, bf16[128,768]{1,0:T(8,128)(2,1)}, u32[]{:S(2)}, u32[]{:S(2)}) collective-permute-start(bf16[128,768]{1,0:T(8,128)(2,1)} %get-tuple-element.65), channel_id=1, source_target_pairs={{0,6},{1,7},{2,4},{3,5},{4,2},{5,3},{6,0},{7,1},{8,14},{9,15},{10,... | collective-permute-start | bytes 589832 | tf_op jit(solution)/shard_map/ppermute | solution.py:61
  30.1 1.8 %shard_map.105 = (bf16[256,768]{1,0:T(8,128)(2,1)S(1)}, bf16[256,768]{1,0:T(8,128)(2,1)S(1)}, bf16[256,768]{1,0:T(8,128)(2,1)S(1)}) custom-call(s32[16]{0:T(128)S(1)} %copy-done.7, f32[16,768]{1,0:T(8,128)S(1)} %copy-done.1, bf16[768,2304]{1,0:T(8,128)(2,1)S(1)} %copy-done, bf16[256,768]{1,0:T(8,128)(2,1)S(1)} %shard_map.104.rest_0_.rest_1_), custom_call_target="tpu_custom_call" | custom-call | flops 905969664 | bytes 5111808 | tf_op jit(solution)/shard_map/pallas_call | solution.py:233
  32.0 2.2 %shard_map.106 = (bf16[512,768]{1,0:T(8,128)(2,1)S(1)}, bf16[512,768]{1,0:T(8,128)(2,1)S(1)}) custom-call(s32[16]{0:T(128)S(1)} %copy-done.7, f32[16,768]{1,0:T(8,128)S(1)} %copy-done.1, bf16[768,2304]{1,0:T(8,128)(2,1)S(1)} %copy-done, bf16[256,768]{1,0:T(8,128)(2,1)S(1)} %collective-permute-done.3.rest_0_, ...), custom_call_target="tpu_custom_call" | custom-call | flops 1207959552 | bytes 5898240 | tf_op jit(solution)/shard_map/pallas_call | solution.py:233
  34.2 9.4 %shard_map.107 = (bf16[4,4,32,768]{3,2,1,0:T(8,128)(2,1)S(1)}, f32[8,128]{1,0:T(8,128)S(1)}) custom-call(s32[16]{0:T(128)S(1)} %copy-done.7, f32[16,768]{1,0:T(8,128)S(1)} %copy-done.1, bf16[768,768]{1,0:T(8,128)(2,1)S(1)} %copy-done.4, bf16[256,768]{1,0:T(8,128)(2,1)S(1)} %shard_map.101.rest_0_, bf16[256,768]{1,0:T(8,128)(2,1)S(1)} %shard_map.104.rest_0_.rest_1_, ...), custom_call_target="tpu_custom_call" | custom-call | flops 6442450944 | tf_op jit(solution)/shard_map/pallas_call | solution.py:341
  44.5 5.8 %all-to-all-start = ((bf16[16,32,768]{2,1,0:T(8,128)(2,1)}), bf16[16,32,768]{2,1,0:T(8,128)(2,1)}, u32[]{:S(2)}, u32[]{:S(2)}) async-start(bf16[16,32,768]{2,1,0:T(8,128)(2,1)} %bitcast.5), calls=%async_computation | async-start | bytes 1572864 | tf_op jit(solution)/shard_map/all_to_all | solution.py:642
  50.3 0.9 copy-done.10
  51.3 1.4 %shard_map.109.rest_0_ = bf16[512,768]{1,0:T(8,128)(2,1)S(1)} custom-call(bf16[128,768]{1,0:T(8,128)(2,1)S(1)} %copy-done.10, bf16[128,768]{1,0:T(8,128)(2,1)} %collective-permute-done.8.refs_1_, bf16[128,768]{1,0:T(8,128)(2,1)} %collective-permute-done.9.refs_2_, bf16[128,768]{1,0:T(8,128)(2,1)} %collective-permute-done.10.refs_3_, ...), custom_call_target="tpu_custom_call" | custom-call | flops 68719476736 | tf_op jit(solution)/shard_map/pallas_call | solution.py:180
  52.7 2.8 %shard_map.110 = (bf16[512,768]{1,0:T(8,128)(2,1)S(1)}, bf16[512,768]{1,0:T(8,128)(2,1)S(1)}, bf16[512,768]{1,0:T(8,128)(2,1)S(1)}) custom-call(s32[16]{0:T(128)S(1)} %copy-done.7, f32[16,768]{1,0:T(8,128)S(1)} %copy-done.2, bf16[768,2304]{1,0:T(8,128)(2,1)S(1)} %copy-done, bf16[512,768]{1,0:T(8,128)(2,1)S(1)} %shard_map.109.rest_0_), custom_call_target="tpu_custom_call" | custom-call | tf_op jit(solution)/shard_map/pallas_call | solution.py:233
  55.6 2.2 %shard_map.111 = (bf16[512,768]{1,0:T(8,128)(2,1)S(1)}, bf16[512,768]{1,0:T(8,128)(2,1)S(1)}) custom-call(s32[16]{0:T(128)S(1)} %copy-done.7, f32[16,768]{1,0:T(8,128)S(1)} %copy-done.2, bf16[768,2304]{1,0:T(8,128)(2,1)S(1)} %copy-done, bf16[512,768]{1,0:T(8,128)(2,1)S(1)} %collective-permute-done.11.rest_0_, bf16[512,768]{1,0:T(8,128)(2,1)S(1)} %get-tuple-element.67.rest_1_), custom_call_target="tpu_custom_call" | custom-call | tf_op jit(solution)/shard_map/pallas_call | solution.py:233
  57.7 10.3 %shard_map.112 = (bf16[4,4,32,768]{3,2,1,0:T(8,128)(2,1)}, f32[8,128]{1,0:T(8,128)}) custom-call(s32[16]{0:T(128)S(1)} %copy-done.7, f32[16,768]{1,0:T(8,128)S(1)} %copy-done.2, bf16[768,768]{1,0:T(8,128)(2,1)S(1)} %copy-done.5, bf16[512,768]{1,0:T(8,128)(2,1)S(1)} %shard_map.109.rest_0_, bf16[512,768]{1,0:T(8,128)(2,1)S(1)} %get-tuple-element.67.rest_1_, ...), custom_call_target="tpu_custom_call" | custom-call | tf_op jit(solution)/shard_map/pallas_call | solution.py:341
  68.1 2.0 %all-to-all-done = bf16[16,32,768]{2,1,0:T(8,128)(2,1)} async-done(((bf16[16,32,768]{2,1,0:T(8,128)(2,1)}), bf16[16,32,768]{2,1,0:T(8,128)(2,1)}, u32[]{:S(2)}, u32[]{:S(2)}) %all-to-all-start) | async-done | bytes 786464 | tf_op jit(solution)/shard_map/all_to_all | solution.py:642
  70.1 4.9 %all-to-all-start.1 = ((bf16[16,32,768]{2,1,0:T(8,128)(2,1)}), bf16[16,32,768]{2,1,0:T(8,128)(2,1)S(1)}, u32[]{:S(2)}, u32[]{:S(2)}) async-start(bf16[16,32,768]{2,1,0:T(8,128)(2,1)} %bitcast.3), calls=%async_computation.1 | async-start | bytes 1572864 | tf_op jit(solution)/shard_map/all_to_all | solution.py:642
  75.0 14.5 %shard_map.108 = (bf16[4,32,768]{2,1,0:T(8,128)(2,1)S(1)}, bf16[4,32,768]{2,1,0:T(8,128)(2,1)S(1)}, bf16[4,32,768]{2,1,0:T(8,128)(2,1)S(1)}, bf16[4,32,768]{2,1,0:T(8,128)(2,1)S(1)}) custom-call(bf16[768,2304]{1,0:T(8,128)(2,1)} %qkv_hbm.3, bf16[768,768]{1,0:T(8,128)(2,1)} %out_hbm.3, bf16[768,3072]{1,0:T(8,128)(2,1)} %up_hbm.5, bf16[3072,768]{1,0:T(8,128)(2,1)} %down_hbm.5, ...), custom_call_target="tpu_custom_call" | custom-call | flops 7247757312 | bytes 15728640 | tf_op jit(solution)/shard_map/pallas_call | solution.py:537
  89.4 2.0 %collective-permute-start.5 = (bf16[4,32,768]{2,1,0:T(8,128)(2,1)S(1)}, bf16[4,32,768]{2,1,0:T(8,128)(2,1)S(1)}, u32[]{:S(2)}, u32[]{:S(2)}) collective-permute-start(bf16[4,32,768]{2,1,0:T(8,128)(2,1)S(1)} %get-tuple-element.59), channel_id=1, source_target_pairs={{0,8},{8,0},{16,24},{24,16},{1,9},{9,1},{17,25},{25,17},{2,10},{10... | collective-permute-start | bytes 589832 | tf_op jit(solution)/shard_map/ppermute | solution.py:61
  91.4 1.5 %collective-permute-start.6 = (bf16[4,32,768]{2,1,0:T(8,128)(2,1)S(1)}, bf16[4,32,768]{2,1,0:T(8,128)(2,1)S(1)}, u32[]{:S(2)}, u32[]{:S(2)}) collective-permute-start(bf16[4,32,768]{2,1,0:T(8,128)(2,1)S(1)} %get-tuple-element.60), channel_id=1, source_target_pairs={{0,16},{8,24},{16,0},{24,8},{1,17},{9,25},{17,1},{25,9},{2,18},{10... | collective-permute-start | bytes 589832 | tf_op jit(solution)/shard_map/ppermute | solution.py:61
  93.0 2.1 %all-to-all-done.1 = bf16[16,32,768]{2,1,0:T(8,128)(2,1)S(1)} async-done(((bf16[16,32,768]{2,1,0:T(8,128)(2,1)}), bf16[16,32,768]{2,1,0:T(8,128)(2,1)S(1)}, u32[]{:S(2)}, u32[]{:S(2)}) %all-to-all-start.1) | async-done | bytes 786464 | tf_op jit(solution)/shard_map/all_to_all | solution.py:642
  95.0 13.3 %shard_map.113 = (bf16[4,32,768]{2,1,0:T(8,128)(2,1)S(1)}, bf16[4,32,768]{2,1,0:T(8,128)(2,1)S(1)}, bf16[4,32,768]{2,1,0:T(8,128)(2,1)S(1)}, f32[128,768]{1,0:T(8,128)S(1)}) custom-call(bf16[768,2304]{1,0:T(8,128)(2,1)} %qkv_hbm.3, bf16[768,768]{1,0:T(8,128)(2,1)} %out_hbm.3, bf16[768,3072]{1,0:T(8,128)(2,1)} %up_hbm.5, bf16[3072,768]{1,0:T(8,128)(2,1)} %down_hbm.5, ...), custom_call_target="tpu_custom_call" | custom-call | flops 7247757312 | bytes 15728640 | tf_op jit(solution)/shard_map/pallas_call | solution.py:537
  109.0 1.6 %collective-permute-start.13 = (bf16[4,32,768]{2,1,0:T(8,128)(2,1)S(1)}, bf16[4,32,768]{2,1,0:T(8,128)(2,1)S(1)}, u32[]{:S(2)}, u32[]{:S(2)}) collective-permute-start(bf16[4,32,768]{2,1,0:T(8,128)(2,1)S(1)} %get-tuple-element.75), channel_id=1, source_target_pairs={{0,16},{8,24},{16,0},{24,8},{1,17},{9,25},{17,1},{25,9},{2,18},{10... | collective-permute-start | bytes 589832 | tf_op jit(solution)/shard_map/ppermute | solution.py:61
  110.6 1.3 %collective-permute-start.14 = (bf16[4,32,768]{2,1,0:T(8,128)(2,1)S(1)}, bf16[4,32,768]{2,1,0:T(8,128)(2,1)S(1)}, u32[]{:S(2)}, u32[]{:S(2)}) collective-permute-start(bf16[4,32,768]{2,1,0:T(8,128)(2,1)S(1)} %get-tuple-element.76), channel_id=1, source_target_pairs={{0,24},{8,16},{16,8},{24,0},{1,25},{9,17},{17,9},{25,1},{2,26},{10... | collective-permute-start | bytes 589832 | tf_op jit(solution)/shard_map/ppermute | solution.py:61
  111.9 4.8 %shard_map.114.refs_4_ = bf16[4,32,768]{2,1,0:T(8,128)(2,1)S(1)} custom-call(bf16[768,3072]{1,0:T(8,128)(2,1)} %up_hbm.5, bf16[3072,768]{1,0:T(8,128)(2,1)} %down_hbm.5, f32[128,768]{1,0:T(8,128)S(1)} %get-tuple-element.73.rest_ref), custom_call_target="tpu_custom_call" | custom-call | flops 1207959552 | bytes 9437184 | tf_op jit(solution)/shard_map/pallas_call | solution.py:433
  117.3 1.6 %collective-permute-done.14.refs_7_ = bf16[4,32,768]{2,1,0:T(8,128)(2,1)S(1)} collective-permute-done((bf16[4,32,768]{2,1,0:T(8,128)(2,1)S(1)}, bf16[4,32,768]{2,1,0:T(8,128)(2,1)S(1)}, u32[]{:S(2)}, u32[]{:S(2)}) %collective-permute-start.14) | collective-permute-done | bytes 196640 | tf_op jit(solution)/shard_map/ppermute | solution.py:61
  118.9 2.7 %shard_map.115 = bf16[256,4,768]{2,1,0:T(4,128)(2,1)} custom-call(f32[1,256]{1,0:T(1,128)S(1)} %get-tuple-element.41.keys_ref, bf16[4,32,768]{2,1,0:T(8,128)(2,1)S(1)} %get-tuple-element.58.refs_0_, bf16[4,32,768]{2,1,0:T(8,128)(2,1)S(1)} %collective-permute-done.5.refs_1_, bf16[4,32,768]{2,1,0:T(8,128)(2,1)S(1)} %collective-permute-done.6.refs_2_, ...), custom_call_target="tpu_custom_call" | custom-call | flops 402653184 | bytes 3145728 | tf_op jit(solution)/shard_map/pallas_call | solution.py:577
  (40 shorter events, 4.1 us)
Async XLA Ops:
  0.0 1.4 %copy-start.3 = (bf16[256,4,768]{2,1,0:T(4,128)(2,1)S(1)}, bf16[256,4,768]{2,1,0:T(4,128)(2,1)}, u32[]{:S(2)}) copy-start(bf16[256,4,768]{2,1,0:T(4,128)(2,1)} %x_ref.1) | copy-start | bytes 4718596
  1.4 0.7 copy-start.8
  2.1 15.0 %copy-start = (bf16[768,2304]{1,0:T(8,128)(2,1)S(1)}, bf16[768,2304]{1,0:T(8,128)(2,1)}, u32[]{:S(2)}) copy-start(bf16[768,2304]{1,0:T(8,128)(2,1)} %w_ref.12) | copy-start | bytes 10616836
  3.4 13.7 %copy-start.1 = (f32[16,768]{1,0:T(8,128)S(1)}, f32[16,768]{1,0:T(8,128)}, u32[]{:S(2)}) copy-start(f32[16,768]{1,0:T(8,128)} %table_ref.13) | copy-start | bytes 147460
  3.4 13.7 %copy-start.7 = (s32[16]{0:T(128)S(1)}, s32[16]{0:T(128)}, u32[]{:S(2)}) copy-start(s32[16]{0:T(128)} %index_ref.13) | copy-start | bytes 196
  3.4 11.4 %collective-permute-start = (bf16[128,768]{1,0:T(8,128)(2,1)S(1)}, bf16[128,768]{1,0:T(8,128)(2,1)S(1)}, u32[]{:S(2)}, u32[]{:S(2)}) collective-permute-start(bf16[128,768]{1,0:T(8,128)(2,1)S(1)} %get-tuple-element.43), channel_id=1, source_target_pairs={{0,2},{1,3},{2,0},{3,1},{4,6},{5,7},{6,4},{7,5},{8,10},{9,11},{10,... | collective-permute-start | bytes 589832 | tf_op jit(solution)/shard_map/ppermute | solution.py:61
  6.5 17.2 %collective-permute-start.1 = (bf16[128,768]{1,0:T(8,128)(2,1)S(1)}, bf16[128,768]{1,0:T(8,128)(2,1)S(1)}, u32[]{:S(2)}, u32[]{:S(2)}) collective-permute-start(bf16[128,768]{1,0:T(8,128)(2,1)S(1)} %get-tuple-element.44), channel_id=1, source_target_pairs={{0,4},{1,5},{2,6},{3,7},{4,0},{5,1},{6,2},{7,3},{8,12},{9,13},{10,... | collective-permute-start | bytes 589832 | tf_op jit(solution)/shard_map/ppermute | solution.py:61
  9.1 14.6 %collective-permute-start.2 = (bf16[128,768]{1,0:T(8,128)(2,1)S(1)}, bf16[128,768]{1,0:T(8,128)(2,1)S(1)}, u32[]{:S(2)}, u32[]{:S(2)}) collective-permute-start(bf16[128,768]{1,0:T(8,128)(2,1)S(1)} %get-tuple-element.45), channel_id=1, source_target_pairs={{0,6},{1,7},{2,4},{3,5},{4,2},{5,3},{6,0},{7,1},{8,14},{9,15},{10,... | collective-permute-start | bytes 589832 | tf_op jit(solution)/shard_map/ppermute | solution.py:61
  15.3 16.7 %collective-permute-start.3 = (bf16[256,768]{1,0:T(8,128)(2,1)S(1)}, bf16[256,768]{1,0:T(8,128)(2,1)S(1)}, u32[]{:S(2)}, u32[]{:S(2)}) collective-permute-start(bf16[256,768]{1,0:T(8,128)(2,1)S(1)} %shard_map.101.rest_0_), channel_id=1, source_target_pairs={{0,1},{1,0},{2,3},{3,2},{4,5},{5,4},{6,7},{7,6},{8,9},{9,8},{10,11... | collective-permute-start | bytes 1179656 | tf_op jit(solution)/shard_map/ppermute | solution.py:61
  17.1 1.9 %copy-start.9 = (bf16[128,768]{1,0:T(8,128)(2,1)}, bf16[128,768]{1,0:T(8,128)(2,1)S(1)}, u32[]{:S(2)}) copy-start(bf16[128,768]{1,0:T(8,128)(2,1)S(1)} %get-tuple-element.62.refs_0_) | copy-start | bytes 589828
  24.2 7.8 %collective-permute-start.4 = (bf16[256,768]{1,0:T(8,128)(2,1)S(1)}, bf16[256,768]{1,0:T(8,128)(2,1)S(1)}, u32[]{:S(2)}, u32[]{:S(2)}) collective-permute-start(bf16[256,768]{1,0:T(8,128)(2,1)S(1)} %shard_map.104.rest_0_.rest_1_), channel_id=1, source_target_pairs={{0,1},{1,0},{2,3},{3,2},{4,5},{5,4},{6,7},{7,6},{8,9},{9,8},{10,11... | collective-permute-start | bytes 1179656 | tf_op jit(solution)/shard_map/ppermute | solution.py:61
  24.3 26.1 %collective-permute-start.8 = (bf16[128,768]{1,0:T(8,128)(2,1)}, bf16[128,768]{1,0:T(8,128)(2,1)}, u32[]{:S(2)}, u32[]{:S(2)}) collective-permute-start(bf16[128,768]{1,0:T(8,128)(2,1)} %get-tuple-element.63), channel_id=1, source_target_pairs={{0,2},{1,3},{2,0},{3,1},{4,6},{5,7},{6,4},{7,5},{8,10},{9,11},{10,... | collective-permute-start | bytes 589832 | tf_op jit(solution)/shard_map/ppermute | solution.py:61
  27.7 22.7 %collective-permute-start.9 = (bf16[128,768]{1,0:T(8,128)(2,1)}, bf16[128,768]{1,0:T(8,128)(2,1)}, u32[]{:S(2)}, u32[]{:S(2)}) collective-permute-start(bf16[128,768]{1,0:T(8,128)(2,1)} %get-tuple-element.64), channel_id=1, source_target_pairs={{0,4},{1,5},{2,6},{3,7},{4,0},{5,1},{6,2},{7,3},{8,12},{9,13},{10,... | collective-permute-start | bytes 589832 | tf_op jit(solution)/shard_map/ppermute | solution.py:61
  28.8 21.6 %collective-permute-start.10 = (bf16[128,768]{1,0:T(8,128)(2,1)}, bf16[128,768]{1,0:T(8,128)(2,1)}, u32[]{:S(2)}, u32[]{:S(2)}) collective-permute-start(bf16[128,768]{1,0:T(8,128)(2,1)} %get-tuple-element.65), channel_id=1, source_target_pairs={{0,6},{1,7},{2,4},{3,5},{4,2},{5,3},{6,0},{7,1},{8,14},{9,15},{10,... | collective-permute-start | bytes 589832 | tf_op jit(solution)/shard_map/ppermute | solution.py:61
  32.0 2.2 %copy-start.4 = (bf16[768,768]{1,0:T(8,128)(2,1)S(1)}, bf16[768,768]{1,0:T(8,128)(2,1)}, u32[]{:S(2)}) copy-start(bf16[768,768]{1,0:T(8,128)(2,1)} %w_ref.13) | copy-start | bytes 3538948
  43.7 0.9 copy-start.6
  44.5 25.5 %all-to-all-start = ((bf16[16,32,768]{2,1,0:T(8,128)(2,1)}), bf16[16,32,768]{2,1,0:T(8,128)(2,1)}, u32[]{:S(2)}, u32[]{:S(2)}) async-start(bf16[16,32,768]{2,1,0:T(8,128)(2,1)} %bitcast.5), calls=%async_computation | async-start | bytes 1572864 | tf_op jit(solution)/shard_map/all_to_all | solution.py:642
  50.3 0.9 copy-start.10
  51.3 1.5 %copy-start.2 = (f32[16,768]{1,0:T(8,128)S(1)}, f32[16,768]{1,0:T(8,128)}, u32[]{:S(2)}) copy-start(f32[16,768]{1,0:T(8,128)} %table_ref.13) | copy-start | bytes 147460
  52.7 2.9 %collective-permute-start.11 = (bf16[512,768]{1,0:T(8,128)(2,1)S(1)}, bf16[512,768]{1,0:T(8,128)(2,1)S(1)}, u32[]{:S(2)}, u32[]{:S(2)}) collective-permute-start(bf16[512,768]{1,0:T(8,128)(2,1)S(1)} %shard_map.109.rest_0_), channel_id=1, source_target_pairs={{0,1},{1,0},{2,3},{3,2},{4,5},{5,4},{6,7},{7,6},{8,9},{9,8},{10,11... | collective-permute-start | bytes 2359304 | tf_op jit(solution)/shard_map/ppermute | solution.py:61
  55.5 2.2 %copy-start.5 = (bf16[768,768]{1,0:T(8,128)(2,1)S(1)}, bf16[768,768]{1,0:T(8,128)(2,1)}, u32[]{:S(2)}) copy-start(bf16[768,768]{1,0:T(8,128)(2,1)} %w_ref.13) | copy-start | bytes 3538948
  70.1 25.0 %all-to-all-start.1 = ((bf16[16,32,768]{2,1,0:T(8,128)(2,1)}), bf16[16,32,768]{2,1,0:T(8,128)(2,1)S(1)}, u32[]{:S(2)}, u32[]{:S(2)}) async-start(bf16[16,32,768]{2,1,0:T(8,128)(2,1)} %bitcast.3), calls=%async_computation.1 | async-start | bytes 1572864 | tf_op jit(solution)/shard_map/all_to_all | solution.py:642
  89.4 21.2 %collective-permute-start.5 = (bf16[4,32,768]{2,1,0:T(8,128)(2,1)S(1)}, bf16[4,32,768]{2,1,0:T(8,128)(2,1)S(1)}, u32[]{:S(2)}, u32[]{:S(2)}) collective-permute-start(bf16[4,32,768]{2,1,0:T(8,128)(2,1)S(1)} %get-tuple-element.59), channel_id=1, source_target_pairs={{0,8},{8,0},{16,24},{24,16},{1,9},{9,1},{17,25},{25,17},{2,10},{10... | collective-permute-start | bytes 589832 | tf_op jit(solution)/shard_map/ppermute | solution.py:61
  91.4 25.3 %collective-permute-start.6 = (bf16[4,32,768]{2,1,0:T(8,128)(2,1)S(1)}, bf16[4,32,768]{2,1,0:T(8,128)(2,1)S(1)}, u32[]{:S(2)}, u32[]{:S(2)}) collective-permute-start(bf16[4,32,768]{2,1,0:T(8,128)(2,1)S(1)} %get-tuple-element.60), channel_id=1, source_target_pairs={{0,16},{8,24},{16,0},{24,8},{1,17},{9,25},{17,1},{25,9},{2,18},{10... | collective-permute-start | bytes 589832 | tf_op jit(solution)/shard_map/ppermute | solution.py:61
  92.9 23.9 %collective-permute-start.7 = (bf16[4,32,768]{2,1,0:T(8,128)(2,1)S(1)}, bf16[4,32,768]{2,1,0:T(8,128)(2,1)S(1)}, u32[]{:S(2)}, u32[]{:S(2)}) collective-permute-start(bf16[4,32,768]{2,1,0:T(8,128)(2,1)S(1)} %get-tuple-element.61), channel_id=1, source_target_pairs={{0,24},{8,16},{16,8},{24,0},{1,25},{9,17},{17,9},{25,1},{2,26},{10... | collective-permute-start | bytes 589832 | tf_op jit(solution)/shard_map/ppermute | solution.py:61
  108.3 8.4 %collective-permute-start.12 = (bf16[4,32,768]{2,1,0:T(8,128)(2,1)S(1)}, bf16[4,32,768]{2,1,0:T(8,128)(2,1)S(1)}, u32[]{:S(2)}, u32[]{:S(2)}) collective-permute-start(bf16[4,32,768]{2,1,0:T(8,128)(2,1)S(1)} %get-tuple-element.74), channel_id=1, source_target_pairs={{0,8},{8,0},{16,24},{24,16},{1,9},{9,1},{17,25},{25,17},{2,10},{10... | collective-permute-start | bytes 589832 | tf_op jit(solution)/shard_map/ppermute | solution.py:61
  109.0 8.3 %collective-permute-start.13 = (bf16[4,32,768]{2,1,0:T(8,128)(2,1)S(1)}, bf16[4,32,768]{2,1,0:T(8,128)(2,1)S(1)}, u32[]{:S(2)}, u32[]{:S(2)}) collective-permute-start(bf16[4,32,768]{2,1,0:T(8,128)(2,1)S(1)} %get-tuple-element.75), channel_id=1, source_target_pairs={{0,16},{8,24},{16,0},{24,8},{1,17},{9,25},{17,1},{25,9},{2,18},{10... | collective-permute-start | bytes 589832 | tf_op jit(solution)/shard_map/ppermute | solution.py:61
  110.6 8.3 %collective-permute-start.14 = (bf16[4,32,768]{2,1,0:T(8,128)(2,1)S(1)}, bf16[4,32,768]{2,1,0:T(8,128)(2,1)S(1)}, u32[]{:S(2)}, u32[]{:S(2)}) collective-permute-start(bf16[4,32,768]{2,1,0:T(8,128)(2,1)S(1)} %get-tuple-element.76), channel_id=1, source_target_pairs={{0,24},{8,16},{16,8},{24,0},{1,25},{9,17},{17,9},{25,1},{2,26},{10... | collective-permute-start | bytes 589832 | tf_op jit(solution)/shard_map/ppermute | solution.py:61

commit v12 on v11

--- a/solution.py
+++ b/solution.py
@@ -73,6 +73,13 @@
         self.rows = self.block // self.share
         self.part_rows = self.rows // self.groups
         assert self.part_rows * self.groups * self.share * WINDOWS == self.loc_dev
+        self.row_bits = self.rows_count.bit_length() - 1 if self.share == 1 else 0
+
+    def spot(self, row):
+        if self.row_bits == 0:
+            return row
+        bits = range(self.row_bits)
+        return sum(((row >> bit) & 1) << (self.row_bits - 1 - bit) for bit in bits)
 
 
 def marker():
@@ -334,7 +341,7 @@
                 mid = (start + added[pl.ds(slot * rows, rows), :]).astype(BF16)
                 for owner in range(plan.groups):
                     part = mid[owner * plan.part_rows : (owner + 1) * plan.part_rows]
-                    out_ref[row ^ slot, owner] = part
+                    out_ref[plan.spot(row ^ slot), owner] = part
                 slot += 1
 
     key_rows = sum(piece.shape[0] for piece in keys)
@@ -567,7 +574,7 @@
         wanted = window * plan.block + part * plan.rows + owner * plan.part_rows + inner
         pick = jnp.where(wanted.astype(F32) == keys_ref[...], 1.0, 0.0).astype(BF16)
         for band in range(plan.band_dev):
-            rows = jnp.concatenate([ref[band] for ref in ins], axis=0)
+            rows = jnp.concatenate([ref[plan.spot(band)] for ref in ins], axis=0)
             out_ref[:, band, :] = lax.dot_general(
                 pick, rows, (((0,), (0,)), ((), ())), preferred_element_type=F32
             ).astype(BF16)
@@ -634,7 +641,11 @@
         behind = [done]
         mids.append(mid)
     same = [
-        [g * plan.locs + r * CORES + core for r in range(plan.rows_count) for g in range(plan.groups)]
+        [
+            g * plan.locs + plan.spot(r) * CORES + core
+            for r in range(plan.rows_count)
+            for g in range(plan.groups)
+        ]
         for core in range(CORES)
     ]
     returned = []

time: 122 us -> 124 us (1.016)
  waiting for transfers between devices: 16.6 us -> 19.6 us
    all_to_all x2, waiting for transfers between devices: 4.03 us -> 6.09 us  [body(): lax.all_to_all(mid.reshape(-1, plan.part_rows, plan.width), ('band', 'loc...]
  transfers between devices with their start and end apart: 17 -> 17, of which waited for: 6 -> 6; matrix products, arithmetic and copies ran while one was open for 0% -> 0% of each run, Pallas kernels for 55% -> 54%
where the time goes in v12:
time: 124 us
  Pallas kernels  71.2 us (57%)
  starting transfers between devices  28.6 us (23%)
  waiting for transfers between devices  19.6 us (16%)
  local copies, waits for them, and re-layouts  3.93 us (3%)
    pallas_call x2, Pallas kernels, channel(): call(kernel, [jax.ShapeDtypeStruct((bands, locations, width), BF16)] * le...  27.7 us
    pallas_call x2, Pallas kernels, attend(): call(kernel, [jax.ShapeDtypeStruct((plan.rows_count, plan.groups, plan.pa...  19.8 us
    ppermute x15, starting transfers between devices, exchange(): lax.ppermute(value, axis, [(i, i ^ step) for i in range(lax.axis_size(axi...  19 us
    ppermute x15, waiting for transfers between devices, exchange(): lax.ppermute(value, axis, [(i, i ^ step) for i in range(lax.axis_size(axi...  13.5 us
    pallas_call x5, Pallas kernels, project(): call(kernel, [jax.ShapeDtypeStruct((rows, width), BF16)] * len(names), hi...  10.8 us
    all_to_all x2, starting transfers between devices, body(): lax.all_to_all(mid.reshape(-1, plan.part_rows, plan.width), ('band', 'loc...  9.64 us
    all_to_all x2, waiting for transfers between devices, body(): lax.all_to_all(mid.reshape(-1, plan.part_rows, plan.width), ('band', 'loc...  6.09 us
    pallas_call x1, Pallas kernels, finish(): call(kernel, [jax.ShapeDtypeStruct((bands, locations, width), BF16)] * le...  4.84 us
  transfers between devices with their start and end apart: 17, of which 6 were waited for; matrix products, arithmetic and copies ran while one was open for 0% of the time, Pallas kernels for 54%

profile of v12, /device:TPU:0, one launch (start us, length us, event | category | flops | bytes accessed | tf_op | source)
XLA Modules:
  0.0 123.6 jit_solution(17220348652826238635)
XLA Ops:
  0.0 1.4 %copy-done.3 = bf16[256,4,768]{2,1,0:T(4,128)(2,1)S(1)} copy-done((bf16[256,4,768]{2,1,0:T(4,128)(2,1)S(1)}, bf16[256,4,768]{2,1,0:T(4,128)(2,1)}, u32[]{:S(2)}) %copy-start.3) | copy-done | bytes 1572888
  2.1 1.3 %shard_map.100 = (bf16[128,768]{1,0:T(8,128)(2,1)S(1)}, bf16[128,768]{1,0:T(8,128)(2,1)S(1)}, bf16[128,768]{1,0:T(8,128)(2,1)S(1)}, bf16[128,768]{1,0:T(8,128)(2...) custom-call(s32[16,128]{1,0:T(8,128)S(1)} %bitcast.7, ...), custom_call_target="tpu_custom_call" | custom-call | flops 402653184 | bytes 3145728 | tf_op jit(solution)/shard_map/pallas_call | solution.py:138
  3.4 3.1 %collective-permute-start = (bf16[128,768]{1,0:T(8,128)(2,1)S(1)}, bf16[128,768]{1,0:T(8,128)(2,1)S(1)}, u32[]{:S(2)}, u32[]{:S(2)}) collective-permute-start(bf16[128,768]{1,0:T(8,128)(2,1)S(1)} %get-tuple-element.43), channel_id=1, source_target_pairs={{0,2},{1,3},{2,0},{3,1},{4,6},{5,7},{6,4},{7,5},{8,10},{9,11},{10,... | collective-permute-start | bytes 589832 | tf_op jit(solution)/shard_map/ppermute | solution.py:61
  6.5 2.6 %collective-permute-start.1 = (bf16[128,768]{1,0:T(8,128)(2,1)S(1)}, bf16[128,768]{1,0:T(8,128)(2,1)S(1)}, u32[]{:S(2)}, u32[]{:S(2)}) collective-permute-start(bf16[128,768]{1,0:T(8,128)(2,1)S(1)} %get-tuple-element.44), channel_id=1, source_target_pairs={{0,4},{1,5},{2,6},{3,7},{4,0},{5,1},{6,2},{7,3},{8,12},{9,13},{10,... | collective-permute-start | bytes 589832 | tf_op jit(solution)/shard_map/ppermute | solution.py:61
  9.1 5.7 %collective-permute-done.refs_1_.rest_0_ = bf16[128,768]{1,0:T(8,128)(2,1)S(1)} collective-permute-done((bf16[128,768]{1,0:T(8,128)(2,1)S(1)}, bf16[128,768]{1,0:T(8,128)(2,1)S(1)}, u32[]{:S(2)}, u32[]{:S(2)}) %collective-permute-start) | collective-permute-done | bytes 196640 | tf_op jit(solution)/shard_map/ppermute | solution.py:61
  15.4 1.7 %shard_map.102 = (bf16[128,768]{1,0:T(8,128)(2,1)S(1)}, bf16[128,768]{1,0:T(8,128)(2,1)}, bf16[128,768]{1,0:T(8,128)(2,1)}, bf16[128,768]{1,0:T(8,128)(2,1)}, f32[8,128]{1,0:T(8,128)S(1)}) custom-call(bf16[1024,768]{1,0:T(8,128)(2,1)S(1)} %get-tuple-element.46.rows_ref, f32[1,1024]{1,0:T(1,128)S(1)} %get-tuple-element.47.place_ref, ...), custom_call_target="tpu_custom_call" | custom-call | flops 402653184 | tf_op jit(solution)/shard_map/pallas_call | solution.py:161
  17.1 1.8 %shard_map.103 = (bf16[256,768]{1,0:T(8,128)(2,1)S(1)}, bf16[256,768]{1,0:T(8,128)(2,1)S(1)}, bf16[256,768]{1,0:T(8,128)(2,1)S(1)}) custom-call(s32[16]{0:T(128)S(1)} %copy-done.7, f32[16,768]{1,0:T(8,128)S(1)} %copy-done.1, bf16[768,2304]{1,0:T(8,128)(2,1)S(1)} %copy-done, bf16[256,768]{1,0:T(8,128)(2,1)S(1)} %shard_map.101.rest_0_), custom_call_target="tpu_custom_call" | custom-call | flops 905969664 | bytes 5111808 | tf_op jit(solution)/shard_map/pallas_call | solution.py:240
  19.0 4.7 %collective-permute-done.1.refs_0_ = bf16[128,768]{1,0:T(8,128)(2,1)S(1)} collective-permute-done((bf16[128,768]{1,0:T(8,128)(2,1)S(1)}, bf16[128,768]{1,0:T(8,128)(2,1)S(1)}, u32[]{:S(2)}, u32[]{:S(2)}) %collective-permute-start.1) | collective-permute-done | bytes 196640 | tf_op jit(solution)/shard_map/ppermute | solution.py:61
  24.3 3.4 %collective-permute-start.8 = (bf16[128,768]{1,0:T(8,128)(2,1)}, bf16[128,768]{1,0:T(8,128)(2,1)}, u32[]{:S(2)}, u32[]{:S(2)}) collective-permute-start(bf16[128,768]{1,0:T(8,128)(2,1)} %get-tuple-element.63), channel_id=1, source_target_pairs={{0,2},{1,3},{2,0},{3,1},{4,6},{5,7},{6,4},{7,5},{8,10},{9,11},{10,... | collective-permute-start | bytes 589832 | tf_op jit(solution)/shard_map/ppermute | solution.py:61
  27.7 1.1 collective-permute-start.9
  28.8 1.4 %collective-permute-start.10 = (bf16[128,768]{1,0:T(8,128)(2,1)}, bf16[128,768]{1,0:T(8,128)(2,1)}, u32[]{:S(2)}, u32[]{:S(2)}) collective-permute-start(bf16[128,768]{1,0:T(8,128)(2,1)} %get-tuple-element.65), channel_id=1, source_target_pairs={{0,6},{1,7},{2,4},{3,5},{4,2},{5,3},{6,0},{7,1},{8,14},{9,15},{10,... | collective-permute-start | bytes 589832 | tf_op jit(solution)/shard_map/ppermute | solution.py:61
  30.1 1.8 %shard_map.105 = (bf16[256,768]{1,0:T(8,128)(2,1)S(1)}, bf16[256,768]{1,0:T(8,128)(2,1)S(1)}, bf16[256,768]{1,0:T(8,128)(2,1)S(1)}) custom-call(s32[16]{0:T(128)S(1)} %copy-done.7, f32[16,768]{1,0:T(8,128)S(1)} %copy-done.1, bf16[768,2304]{1,0:T(8,128)(2,1)S(1)} %copy-done, bf16[256,768]{1,0:T(8,128)(2,1)S(1)} %shard_map.104.rest_0_.rest_1_), custom_call_target="tpu_custom_call" | custom-call | flops 905969664 | bytes 5111808 | tf_op jit(solution)/shard_map/pallas_call | solution.py:240
  32.0 2.2 %shard_map.106 = (bf16[512,768]{1,0:T(8,128)(2,1)S(1)}, bf16[512,768]{1,0:T(8,128)(2,1)S(1)}) custom-call(s32[16]{0:T(128)S(1)} %copy-done.7, f32[16,768]{1,0:T(8,128)S(1)} %copy-done.1, bf16[768,2304]{1,0:T(8,128)(2,1)S(1)} %copy-done, bf16[256,768]{1,0:T(8,128)(2,1)S(1)} %collective-permute-done.3.rest_0_, ...), custom_call_target="tpu_custom_call" | custom-call | flops 1207959552 | bytes 5898240 | tf_op jit(solution)/shard_map/pallas_call | solution.py:240
  34.2 9.4 %shard_map.107 = (bf16[4,4,32,768]{3,2,1,0:T(8,128)(2,1)S(1)}, f32[8,128]{1,0:T(8,128)S(1)}) custom-call(s32[16]{0:T(128)S(1)} %copy-done.7, f32[16,768]{1,0:T(8,128)S(1)} %copy-done.1, bf16[768,768]{1,0:T(8,128)(2,1)S(1)} %copy-done.4, bf16[256,768]{1,0:T(8,128)(2,1)S(1)} %shard_map.101.rest_0_, bf16[256,768]{1,0:T(8,128)(2,1)S(1)} %shard_map.104.rest_0_.rest_1_, ...), custom_call_target="tpu_custom_call" | custom-call | flops 6442450944 | tf_op jit(solution)/shard_map/pallas_call | solution.py:348
  44.5 5.8 %all-to-all-start = ((bf16[16,32,768]{2,1,0:T(8,128)(2,1)}), bf16[16,32,768]{2,1,0:T(8,128)(2,1)}, u32[]{:S(2)}, u32[]{:S(2)}) async-start(bf16[16,32,768]{2,1,0:T(8,128)(2,1)} %bitcast.5), calls=%async_computation | async-start | bytes 1572864 | tf_op jit(solution)/shard_map/all_to_all | solution.py:653
  50.3 0.9 copy-done.10
  51.3 1.4 %shard_map.109.rest_0_ = bf16[512,768]{1,0:T(8,128)(2,1)S(1)} custom-call(bf16[128,768]{1,0:T(8,128)(2,1)S(1)} %copy-done.10, bf16[128,768]{1,0:T(8,128)(2,1)} %collective-permute-done.8.refs_1_, bf16[128,768]{1,0:T(8,128)(2,1)} %collective-permute-done.9.refs_2_, bf16[128,768]{1,0:T(8,128)(2,1)} %collective-permute-done.10.refs_3_, ...), custom_call_target="tpu_custom_call" | custom-call | flops 68719476736 | tf_op jit(solution)/shard_map/pallas_call | solution.py:187
  52.7 2.8 %shard_map.110 = (bf16[512,768]{1,0:T(8,128)(2,1)S(1)}, bf16[512,768]{1,0:T(8,128)(2,1)S(1)}, bf16[512,768]{1,0:T(8,128)(2,1)S(1)}) custom-call(s32[16]{0:T(128)S(1)} %copy-done.7, f32[16,768]{1,0:T(8,128)S(1)} %copy-done.2, bf16[768,2304]{1,0:T(8,128)(2,1)S(1)} %copy-done, bf16[512,768]{1,0:T(8,128)(2,1)S(1)} %shard_map.109.rest_0_), custom_call_target="tpu_custom_call" | custom-call | tf_op jit(solution)/shard_map/pallas_call | solution.py:240
  55.6 2.2 %shard_map.111 = (bf16[512,768]{1,0:T(8,128)(2,1)S(1)}, bf16[512,768]{1,0:T(8,128)(2,1)S(1)}) custom-call(s32[16]{0:T(128)S(1)} %copy-done.7, f32[16,768]{1,0:T(8,128)S(1)} %copy-done.2, bf16[768,2304]{1,0:T(8,128)(2,1)S(1)} %copy-done, bf16[512,768]{1,0:T(8,128)(2,1)S(1)} %collective-permute-done.11.rest_0_, bf16[512,768]{1,0:T(8,128)(2,1)S(1)} %get-tuple-element.67.rest_1_), custom_call_target="tpu_custom_call" | custom-call | tf_op jit(solution)/shard_map/pallas_call | solution.py:240
  57.7 10.3 %shard_map.112 = (bf16[4,4,32,768]{3,2,1,0:T(8,128)(2,1)}, f32[8,128]{1,0:T(8,128)}) custom-call(s32[16]{0:T(128)S(1)} %copy-done.7, f32[16,768]{1,0:T(8,128)S(1)} %copy-done.2, bf16[768,768]{1,0:T(8,128)(2,1)S(1)} %copy-done.5, bf16[512,768]{1,0:T(8,128)(2,1)S(1)} %shard_map.109.rest_0_, bf16[512,768]{1,0:T(8,128)(2,1)S(1)} %get-tuple-element.67.rest_1_, ...), custom_call_target="tpu_custom_call" | custom-call | tf_op jit(solution)/shard_map/pallas_call | solution.py:348
  68.1 3.0 %all-to-all-done = bf16[16,32,768]{2,1,0:T(8,128)(2,1)} async-done(((bf16[16,32,768]{2,1,0:T(8,128)(2,1)}), bf16[16,32,768]{2,1,0:T(8,128)(2,1)}, u32[]{:S(2)}, u32[]{:S(2)}) %all-to-all-start) | async-done | bytes 786464 | tf_op jit(solution)/shard_map/all_to_all | solution.py:653
  71.1 3.9 %all-to-all-start.1 = ((bf16[16,32,768]{2,1,0:T(8,128)(2,1)}), bf16[16,32,768]{2,1,0:T(8,128)(2,1)S(1)}, u32[]{:S(2)}, u32[]{:S(2)}) async-start(bf16[16,32,768]{2,1,0:T(8,128)(2,1)} %bitcast.3), calls=%async_computation.1 | async-start | bytes 1572864 | tf_op jit(solution)/shard_map/all_to_all | solution.py:653
  75.0 14.5 %shard_map.108 = (bf16[4,32,768]{2,1,0:T(8,128)(2,1)S(1)}, bf16[4,32,768]{2,1,0:T(8,128)(2,1)S(1)}, bf16[4,32,768]{2,1,0:T(8,128)(2,1)S(1)}, bf16[4,32,768]{2,1,0:T(8,128)(2,1)S(1)}) custom-call(bf16[768,2304]{1,0:T(8,128)(2,1)} %qkv_hbm.3, bf16[768,768]{1,0:T(8,128)(2,1)} %out_hbm.3, bf16[768,3072]{1,0:T(8,128)(2,1)} %up_hbm.5, bf16[3072,768]{1,0:T(8,128)(2,1)} %down_hbm.5, ...), custom_call_target="tpu_custom_call" | custom-call | flops 7247757312 | bytes 15728640 | tf_op jit(solution)/shard_map/pallas_call | solution.py:544
  89.5 1.9 %collective-permute-start.5 = (bf16[4,32,768]{2,1,0:T(8,128)(2,1)S(1)}, bf16[4,32,768]{2,1,0:T(8,128)(2,1)S(1)}, u32[]{:S(2)}, u32[]{:S(2)}) collective-permute-start(bf16[4,32,768]{2,1,0:T(8,128)(2,1)S(1)} %get-tuple-element.59), channel_id=1, source_target_pairs={{0,8},{8,0},{16,24},{24,16},{1,9},{9,1},{17,25},{25,17},{2,10},{10... | collective-permute-start | bytes 589832 | tf_op jit(solution)/shard_map/ppermute | solution.py:61
  91.4 1.5 %collective-permute-start.6 = (bf16[4,32,768]{2,1,0:T(8,128)(2,1)S(1)}, bf16[4,32,768]{2,1,0:T(8,128)(2,1)S(1)}, u32[]{:S(2)}, u32[]{:S(2)}) collective-permute-start(bf16[4,32,768]{2,1,0:T(8,128)(2,1)S(1)} %get-tuple-element.60), channel_id=1, source_target_pairs={{0,16},{8,24},{16,0},{24,8},{1,17},{9,25},{17,1},{25,9},{2,18},{10... | collective-permute-start | bytes 589832 | tf_op jit(solution)/shard_map/ppermute | solution.py:61
  93.0 3.0 %all-to-all-done.1 = bf16[16,32,768]{2,1,0:T(8,128)(2,1)S(1)} async-done(((bf16[16,32,768]{2,1,0:T(8,128)(2,1)}), bf16[16,32,768]{2,1,0:T(8,128)(2,1)S(1)}, u32[]{:S(2)}, u32[]{:S(2)}) %all-to-all-start.1) | async-done | bytes 786464 | tf_op jit(solution)/shard_map/all_to_all | solution.py:653
  96.1 13.3 %shard_map.113 = (bf16[4,32,768]{2,1,0:T(8,128)(2,1)S(1)}, bf16[4,32,768]{2,1,0:T(8,128)(2,1)S(1)}, bf16[4,32,768]{2,1,0:T(8,128)(2,1)S(1)}, f32[128,768]{1,0:T(8,128)S(1)}) custom-call(bf16[768,2304]{1,0:T(8,128)(2,1)} %qkv_hbm.3, bf16[768,768]{1,0:T(8,128)(2,1)} %out_hbm.3, bf16[768,3072]{1,0:T(8,128)(2,1)} %up_hbm.5, bf16[3072,768]{1,0:T(8,128)(2,1)} %down_hbm.5, ...), custom_call_target="tpu_custom_call" | custom-call | flops 7247757312 | bytes 15728640 | tf_op jit(solution)/shard_map/pallas_call | solution.py:544
  110.0 2.1 %collective-permute-start.13 = (bf16[4,32,768]{2,1,0:T(8,128)(2,1)S(1)}, bf16[4,32,768]{2,1,0:T(8,128)(2,1)S(1)}, u32[]{:S(2)}, u32[]{:S(2)}) collective-permute-start(bf16[4,32,768]{2,1,0:T(8,128)(2,1)S(1)} %get-tuple-element.75), channel_id=1, source_target_pairs={{0,16},{8,24},{16,0},{24,8},{1,17},{9,25},{17,1},{25,9},{2,18},{10... | collective-permute-start | bytes 589832 | tf_op jit(solution)/shard_map/ppermute | solution.py:61
  113.0 4.8 %shard_map.114.refs_4_ = bf16[4,32,768]{2,1,0:T(8,128)(2,1)S(1)} custom-call(bf16[768,3072]{1,0:T(8,128)(2,1)} %up_hbm.5, bf16[3072,768]{1,0:T(8,128)(2,1)} %down_hbm.5, f32[128,768]{1,0:T(8,128)S(1)} %get-tuple-element.73.rest_ref), custom_call_target="tpu_custom_call" | custom-call | flops 1207959552 | bytes 9437184 | tf_op jit(solution)/shard_map/pallas_call | solution.py:440
  117.9 1.4 %collective-permute-done.13.refs_6_ = bf16[4,32,768]{2,1,0:T(8,128)(2,1)S(1)} collective-permute-done((bf16[4,32,768]{2,1,0:T(8,128)(2,1)S(1)}, bf16[4,32,768]{2,1,0:T(8,128)(2,1)S(1)}, u32[]{:S(2)}, u32[]{:S(2)}) %collective-permute-start.13) | collective-permute-done | bytes 196640 | tf_op jit(solution)/shard_map/ppermute | solution.py:61
  119.3 1.6 %collective-permute-done.14.refs_7_ = bf16[4,32,768]{2,1,0:T(8,128)(2,1)S(1)} collective-permute-done((bf16[4,32,768]{2,1,0:T(8,128)(2,1)S(1)}, bf16[4,32,768]{2,1,0:T(8,128)(2,1)S(1)}, u32[]{:S(2)}, u32[]{:S(2)}) %collective-permute-start.14) | collective-permute-done | bytes 196640 | tf_op jit(solution)/shard_map/ppermute | solution.py:61
  121.0 2.7 %shard_map.115 = bf16[256,4,768]{2,1,0:T(4,128)(2,1)} custom-call(f32[1,256]{1,0:T(1,128)S(1)} %get-tuple-element.41.keys_ref, bf16[4,32,768]{2,1,0:T(8,128)(2,1)S(1)} %get-tuple-element.58.refs_0_, bf16[4,32,768]{2,1,0:T(8,128)(2,1)S(1)} %collective-permute-done.5.refs_1_, bf16[4,32,768]{2,1,0:T(8,128)(2,1)S(1)} %collective-permute-done.6.refs_2_, ...), custom_call_target="tpu_custom_call" | custom-call | flops 402653184 | bytes 3145728 | tf_op jit(solution)/shard_map/pallas_call | solution.py:584
  (40 shorter events, 4.5 us)
Async XLA Ops:
  0.0 1.4 %copy-start.3 = (bf16[256,4,768]{2,1,0:T(4,128)(2,1)S(1)}, bf16[256,4,768]{2,1,0:T(4,128)(2,1)}, u32[]{:S(2)}) copy-start(bf16[256,4,768]{2,1,0:T(4,128)(2,1)} %x_ref.1) | copy-start | bytes 4718596
  1.4 0.7 copy-start.8
  2.1 15.0 %copy-start = (bf16[768,2304]{1,0:T(8,128)(2,1)S(1)}, bf16[768,2304]{1,0:T(8,128)(2,1)}, u32[]{:S(2)}) copy-start(bf16[768,2304]{1,0:T(8,128)(2,1)} %w_ref.12) | copy-start | bytes 10616836
  3.4 13.7 %copy-start.1 = (f32[16,768]{1,0:T(8,128)S(1)}, f32[16,768]{1,0:T(8,128)}, u32[]{:S(2)}) copy-start(f32[16,768]{1,0:T(8,128)} %table_ref.13) | copy-start | bytes 147460
  3.4 13.7 %copy-start.7 = (s32[16]{0:T(128)S(1)}, s32[16]{0:T(128)}, u32[]{:S(2)}) copy-start(s32[16]{0:T(128)} %index_ref.13) | copy-start | bytes 196
  3.4 11.4 %collective-permute-start = (bf16[128,768]{1,0:T(8,128)(2,1)S(1)}, bf16[128,768]{1,0:T(8,128)(2,1)S(1)}, u32[]{:S(2)}, u32[]{:S(2)}) collective-permute-start(bf16[128,768]{1,0:T(8,128)(2,1)S(1)} %get-tuple-element.43), channel_id=1, source_target_pairs={{0,2},{1,3},{2,0},{3,1},{4,6},{5,7},{6,4},{7,5},{8,10},{9,11},{10,... | collective-permute-start | bytes 589832 | tf_op jit(solution)/shard_map/ppermute | solution.py:61
  6.5 17.2 %collective-permute-start.1 = (bf16[128,768]{1,0:T(8,128)(2,1)S(1)}, bf16[128,768]{1,0:T(8,128)(2,1)S(1)}, u32[]{:S(2)}, u32[]{:S(2)}) collective-permute-start(bf16[128,768]{1,0:T(8,128)(2,1)S(1)} %get-tuple-element.44), channel_id=1, source_target_pairs={{0,4},{1,5},{2,6},{3,7},{4,0},{5,1},{6,2},{7,3},{8,12},{9,13},{10,... | collective-permute-start | bytes 589832 | tf_op jit(solution)/shard_map/ppermute | solution.py:61
  9.1 14.6 %collective-permute-start.2 = (bf16[128,768]{1,0:T(8,128)(2,1)S(1)}, bf16[128,768]{1,0:T(8,128)(2,1)S(1)}, u32[]{:S(2)}, u32[]{:S(2)}) collective-permute-start(bf16[128,768]{1,0:T(8,128)(2,1)S(1)} %get-tuple-element.45), channel_id=1, source_target_pairs={{0,6},{1,7},{2,4},{3,5},{4,2},{5,3},{6,0},{7,1},{8,14},{9,15},{10,... | collective-permute-start | bytes 589832 | tf_op jit(solution)/shard_map/ppermute | solution.py:61
  15.3 16.7 %collective-permute-start.3 = (bf16[256,768]{1,0:T(8,128)(2,1)S(1)}, bf16[256,768]{1,0:T(8,128)(2,1)S(1)}, u32[]{:S(2)}, u32[]{:S(2)}) collective-permute-start(bf16[256,768]{1,0:T(8,128)(2,1)S(1)} %shard_map.101.rest_0_), channel_id=1, source_target_pairs={{0,1},{1,0},{2,3},{3,2},{4,5},{5,4},{6,7},{7,6},{8,9},{9,8},{10,11... | collective-permute-start | bytes 1179656 | tf_op jit(solution)/shard_map/ppermute | solution.py:61
  17.1 1.9 %copy-start.9 = (bf16[128,768]{1,0:T(8,128)(2,1)}, bf16[128,768]{1,0:T(8,128)(2,1)S(1)}, u32[]{:S(2)}) copy-start(bf16[128,768]{1,0:T(8,128)(2,1)S(1)} %get-tuple-element.62.refs_0_) | copy-start | bytes 589828
  24.2 7.8 %collective-permute-start.4 = (bf16[256,768]{1,0:T(8,128)(2,1)S(1)}, bf16[256,768]{1,0:T(8,128)(2,1)S(1)}, u32[]{:S(2)}, u32[]{:S(2)}) collective-permute-start(bf16[256,768]{1,0:T(8,128)(2,1)S(1)} %shard_map.104.rest_0_.rest_1_), channel_id=1, source_target_pairs={{0,1},{1,0},{2,3},{3,2},{4,5},{5,4},{6,7},{7,6},{8,9},{9,8},{10,11... | collective-permute-start | bytes 1179656 | tf_op jit(solution)/shard_map/ppermute | solution.py:61
  24.3 26.1 %collective-permute-start.8 = (bf16[128,768]{1,0:T(8,128)(2,1)}, bf16[128,768]{1,0:T(8,128)(2,1)}, u32[]{:S(2)}, u32[]{:S(2)}) collective-permute-start(bf16[128,768]{1,0:T(8,128)(2,1)} %get-tuple-element.63), channel_id=1, source_target_pairs={{0,2},{1,3},{2,0},{3,1},{4,6},{5,7},{6,4},{7,5},{8,10},{9,11},{10,... | collective-permute-start | bytes 589832 | tf_op jit(solution)/shard_map/ppermute | solution.py:61
  27.7 22.7 %collective-permute-start.9 = (bf16[128,768]{1,0:T(8,128)(2,1)}, bf16[128,768]{1,0:T(8,128)(2,1)}, u32[]{:S(2)}, u32[]{:S(2)}) collective-permute-start(bf16[128,768]{1,0:T(8,128)(2,1)} %get-tuple-element.64), channel_id=1, source_target_pairs={{0,4},{1,5},{2,6},{3,7},{4,0},{5,1},{6,2},{7,3},{8,12},{9,13},{10,... | collective-permute-start | bytes 589832 | tf_op jit(solution)/shard_map/ppermute | solution.py:61
  28.8 21.6 %collective-permute-start.10 = (bf16[128,768]{1,0:T(8,128)(2,1)}, bf16[128,768]{1,0:T(8,128)(2,1)}, u32[]{:S(2)}, u32[]{:S(2)}) collective-permute-start(bf16[128,768]{1,0:T(8,128)(2,1)} %get-tuple-element.65), channel_id=1, source_target_pairs={{0,6},{1,7},{2,4},{3,5},{4,2},{5,3},{6,0},{7,1},{8,14},{9,15},{10,... | collective-permute-start | bytes 589832 | tf_op jit(solution)/shard_map/ppermute | solution.py:61
  32.0 2.2 %copy-start.4 = (bf16[768,768]{1,0:T(8,128)(2,1)S(1)}, bf16[768,768]{1,0:T(8,128)(2,1)}, u32[]{:S(2)}) copy-start(bf16[768,768]{1,0:T(8,128)(2,1)} %w_ref.13) | copy-start | bytes 3538948
  43.7 0.9 copy-start.6
  44.5 26.6 %all-to-all-start = ((bf16[16,32,768]{2,1,0:T(8,128)(2,1)}), bf16[16,32,768]{2,1,0:T(8,128)(2,1)}, u32[]{:S(2)}, u32[]{:S(2)}) async-start(bf16[16,32,768]{2,1,0:T(8,128)(2,1)} %bitcast.5), calls=%async_computation | async-start | bytes 1572864 | tf_op jit(solution)/shard_map/all_to_all | solution.py:653
  50.3 0.9 copy-start.10
  51.3 1.5 %copy-start.2 = (f32[16,768]{1,0:T(8,128)S(1)}, f32[16,768]{1,0:T(8,128)}, u32[]{:S(2)}) copy-start(f32[16,768]{1,0:T(8,128)} %table_ref.13) | copy-start | bytes 147460
  52.7 2.9 %collective-permute-start.11 = (bf16[512,768]{1,0:T(8,128)(2,1)S(1)}, bf16[512,768]{1,0:T(8,128)(2,1)S(1)}, u32[]{:S(2)}, u32[]{:S(2)}) collective-permute-start(bf16[512,768]{1,0:T(8,128)(2,1)S(1)} %shard_map.109.rest_0_), channel_id=1, source_target_pairs={{0,1},{1,0},{2,3},{3,2},{4,5},{5,4},{6,7},{7,6},{8,9},{9,8},{10,11... | collective-permute-start | bytes 2359304 | tf_op jit(solution)/shard_map/ppermute | solution.py:61
  55.5 2.2 %copy-start.5 = (bf16[768,768]{1,0:T(8,128)(2,1)S(1)}, bf16[768,768]{1,0:T(8,128)(2,1)}, u32[]{:S(2)}) copy-start(bf16[768,768]{1,0:T(8,128)(2,1)} %w_ref.13) | copy-start | bytes 3538948
  71.1 25.0 %all-to-all-start.1 = ((bf16[16,32,768]{2,1,0:T(8,128)(2,1)}), bf16[16,32,768]{2,1,0:T(8,128)(2,1)S(1)}, u32[]{:S(2)}, u32[]{:S(2)}) async-start(bf16[16,32,768]{2,1,0:T(8,128)(2,1)} %bitcast.3), calls=%async_computation.1 | async-start | bytes 1572864 | tf_op jit(solution)/shard_map/all_to_all | solution.py:653
  89.5 22.6 %collective-permute-start.5 = (bf16[4,32,768]{2,1,0:T(8,128)(2,1)S(1)}, bf16[4,32,768]{2,1,0:T(8,128)(2,1)S(1)}, u32[]{:S(2)}, u32[]{:S(2)}) collective-permute-start(bf16[4,32,768]{2,1,0:T(8,128)(2,1)S(1)} %get-tuple-element.59), channel_id=1, source_target_pairs={{0,8},{8,0},{16,24},{24,16},{1,9},{9,1},{17,25},{25,17},{2,10},{10... | collective-permute-start | bytes 589832 | tf_op jit(solution)/shard_map/ppermute | solution.py:61
  91.4 26.4 %collective-permute-start.6 = (bf16[4,32,768]{2,1,0:T(8,128)(2,1)S(1)}, bf16[4,32,768]{2,1,0:T(8,128)(2,1)S(1)}, u32[]{:S(2)}, u32[]{:S(2)}) collective-permute-start(bf16[4,32,768]{2,1,0:T(8,128)(2,1)S(1)} %get-tuple-element.60), channel_id=1, source_target_pairs={{0,16},{8,24},{16,0},{24,8},{1,17},{9,25},{17,1},{25,9},{2,18},{10... | collective-permute-start | bytes 589832 | tf_op jit(solution)/shard_map/ppermute | solution.py:61
  92.9 25.0 %collective-permute-start.7 = (bf16[4,32,768]{2,1,0:T(8,128)(2,1)S(1)}, bf16[4,32,768]{2,1,0:T(8,128)(2,1)S(1)}, u32[]{:S(2)}, u32[]{:S(2)}) collective-permute-start(bf16[4,32,768]{2,1,0:T(8,128)(2,1)S(1)} %get-tuple-element.61), channel_id=1, source_target_pairs={{0,24},{8,16},{16,8},{24,0},{1,25},{9,17},{17,9},{25,1},{2,26},{10... | collective-permute-start | bytes 589832 | tf_op jit(solution)/shard_map/ppermute | solution.py:61
  109.4 8.5 %collective-permute-start.12 = (bf16[4,32,768]{2,1,0:T(8,128)(2,1)S(1)}, bf16[4,32,768]{2,1,0:T(8,128)(2,1)S(1)}, u32[]{:S(2)}, u32[]{:S(2)}) collective-permute-start(bf16[4,32,768]{2,1,0:T(8,128)(2,1)S(1)} %get-tuple-element.74), channel_id=1, source_target_pairs={{0,8},{8,0},{16,24},{24,16},{1,9},{9,1},{17,25},{25,17},{2,10},{10... | collective-permute-start | bytes 589832 | tf_op jit(solution)/shard_map/ppermute | solution.py:61
  110.0 9.3 %collective-permute-start.13 = (bf16[4,32,768]{2,1,0:T(8,128)(2,1)S(1)}, bf16[4,32,768]{2,1,0:T(8,128)(2,1)S(1)}, u32[]{:S(2)}, u32[]{:S(2)}) collective-permute-start(bf16[4,32,768]{2,1,0:T(8,128)(2,1)S(1)} %get-tuple-element.75), channel_id=1, source_target_pairs={{0,16},{8,24},{16,0},{24,8},{1,17},{9,25},{17,1},{25,9},{2,18},{10... | collective-permute-start | bytes 589832 | tf_op jit(solution)/shard_map/ppermute | solution.py:61
  112.1 8.8 %collective-permute-start.14 = (bf16[4,32,768]{2,1,0:T(8,128)(2,1)S(1)}, bf16[4,32,768]{2,1,0:T(8,128)(2,1)S(1)}, u32[]{:S(2)}, u32[]{:S(2)}) collective-permute-start(bf16[4,32,768]{2,1,0:T(8,128)(2,1)S(1)} %get-tuple-element.76), channel_id=1, source_target_pairs={{0,24},{8,16},{16,8},{24,0},{1,25},{9,17},{17,9},{25,1},{2,26},{10... | collective-permute-start | bytes 589832 | tf_op jit(solution)/shard_map/ppermute | solution.py:61

commit v13 on v12

--- a/solution.py
+++ b/solution.py
@@ -73,13 +73,13 @@
         self.rows = self.block // self.share
         self.part_rows = self.rows // self.groups
         assert self.part_rows * self.groups * self.share * WINDOWS == self.loc_dev
-        self.row_bits = self.rows_count.bit_length() - 1 if self.share == 1 else 0
+        self.turn = 1 if self.share == 1 else 0
+
+    def row_at(self, spot):
+        return (spot + self.turn) % self.rows_count
 
     def spot(self, row):
-        if self.row_bits == 0:
-            return row
-        bits = range(self.row_bits)
-        return sum(((row >> bit) & 1) << (self.row_bits - 1 - bit) for bit in bits)
+        return (row + self.rows_count - self.turn) % self.rows_count
 
 
 def marker():
@@ -642,8 +642,8 @@
         mids.append(mid)
     same = [
         [
-            g * plan.locs + plan.spot(r) * CORES + core
-            for r in range(plan.rows_count)
+            g * plan.locs + plan.row_at(spot) * CORES + core
+            for spot in range(plan.rows_count)
             for g in range(plan.groups)
         ]
         for core in range(CORES)

time: 124 us -> 120 us (0.968)
  waiting for transfers between devices: 19.6 us -> 13.8 us
  starting transfers between devices: 28.6 us -> 30.7 us
    all_to_all x2, waiting for transfers between devices: 6.09 us -> 1.31 us  [body(): lax.all_to_all(mid.reshape(-1, plan.part_rows, plan.width), ('band', 'loc...]
    all_to_all x2, starting transfers between devices: 9.64 us -> 11.8 us  [body(): lax.all_to_all(mid.reshape(-1, plan.part_rows, plan.width), ('band', 'loc...]
  transfers between devices with their start and end apart: 17 -> 17, of which waited for: 6 -> 6; matrix products, arithmetic and copies ran while one was open for 0% -> 0% of each run, Pallas kernels for 54% -> 56%
where the time goes in v13:
time: 120 us
  Pallas kernels  71.2 us (59%)
  starting transfers between devices  30.7 us (26%)
  waiting for transfers between devices  13.8 us (12%)
  local copies, waits for them, and re-layouts  3.93 us (3%)
    pallas_call x2, Pallas kernels, channel(): call(kernel, [jax.ShapeDtypeStruct((bands, locations, width), BF16)] * le...  27.7 us
    pallas_call x2, Pallas kernels, attend(): call(kernel, [jax.ShapeDtypeStruct((plan.rows_count, plan.groups, plan.pa...  19.8 us
    ppermute x15, starting transfers between devices, exchange(): lax.ppermute(value, axis, [(i, i ^ step) for i in range(lax.axis_size(axi...  18.9 us
    ppermute x15, waiting for transfers between devices, exchange(): lax.ppermute(value, axis, [(i, i ^ step) for i in range(lax.axis_size(axi...  12.5 us
    all_to_all x2, starting transfers between devices, body(): lax.all_to_all(mid.reshape(-1, plan.part_rows, plan.width), ('band', 'loc...  11.8 us
    pallas_call x5, Pallas kernels, project(): call(kernel, [jax.ShapeDtypeStruct((rows, width), BF16)] * len(names), hi...  10.8 us
    pallas_call x1, Pallas kernels, finish(): call(kernel, [jax.ShapeDtypeStruct((bands, locations, width), BF16)] * le...  4.84 us
    unnamed x22, local copies, waits for them, and re-layouts  3.93 us
  transfers between devices with their start and end apart: 17, of which 6 were waited for; matrix products, arithmetic and copies ran while one was open for 0% of the time, Pallas kernels for 56%

profile of v13, /device:TPU:0, one launch (start us, length us, event | category | flops | bytes accessed | tf_op | source)
XLA Modules:
  0.0 119.9 jit_solution(11383547048477418171)
XLA Ops:
  0.0 1.4 %copy-done.3 = bf16[256,4,768]{2,1,0:T(4,128)(2,1)S(1)} copy-done((bf16[256,4,768]{2,1,0:T(4,128)(2,1)S(1)}, bf16[256,4,768]{2,1,0:T(4,128)(2,1)}, u32[]{:S(2)}) %copy-start.3) | copy-done | bytes 1572888
  2.1 1.3 %shard_map.100 = (bf16[128,768]{1,0:T(8,128)(2,1)S(1)}, bf16[128,768]{1,0:T(8,128)(2,1)S(1)}, bf16[128,768]{1,0:T(8,128)(2,1)S(1)}, bf16[128,768]{1,0:T(8,128)(2...) custom-call(s32[16,128]{1,0:T(8,128)S(1)} %bitcast.7, ...), custom_call_target="tpu_custom_call" | custom-call | flops 402653184 | bytes 3145728 | tf_op jit(solution)/shard_map/pallas_call | solution.py:138
  3.4 3.1 %collective-permute-start = (bf16[128,768]{1,0:T(8,128)(2,1)S(1)}, bf16[128,768]{1,0:T(8,128)(2,1)S(1)}, u32[]{:S(2)}, u32[]{:S(2)}) collective-permute-start(bf16[128,768]{1,0:T(8,128)(2,1)S(1)} %get-tuple-element.43), channel_id=1, source_target_pairs={{0,2},{1,3},{2,0},{3,1},{4,6},{5,7},{6,4},{7,5},{8,10},{9,11},{10,... | collective-permute-start | bytes 589832 | tf_op jit(solution)/shard_map/ppermute | solution.py:61
  6.5 2.6 %collective-permute-start.1 = (bf16[128,768]{1,0:T(8,128)(2,1)S(1)}, bf16[128,768]{1,0:T(8,128)(2,1)S(1)}, u32[]{:S(2)}, u32[]{:S(2)}) collective-permute-start(bf16[128,768]{1,0:T(8,128)(2,1)S(1)} %get-tuple-element.44), channel_id=1, source_target_pairs={{0,4},{1,5},{2,6},{3,7},{4,0},{5,1},{6,2},{7,3},{8,12},{9,13},{10,... | collective-permute-start | bytes 589832 | tf_op jit(solution)/shard_map/ppermute | solution.py:61
  9.1 5.7 %collective-permute-done.refs_1_.rest_0_ = bf16[128,768]{1,0:T(8,128)(2,1)S(1)} collective-permute-done((bf16[128,768]{1,0:T(8,128)(2,1)S(1)}, bf16[128,768]{1,0:T(8,128)(2,1)S(1)}, u32[]{:S(2)}, u32[]{:S(2)}) %collective-permute-start) | collective-permute-done | bytes 196640 | tf_op jit(solution)/shard_map/ppermute | solution.py:61
  15.4 1.7 %shard_map.102 = (bf16[128,768]{1,0:T(8,128)(2,1)S(1)}, bf16[128,768]{1,0:T(8,128)(2,1)}, bf16[128,768]{1,0:T(8,128)(2,1)}, bf16[128,768]{1,0:T(8,128)(2,1)}, f32[8,128]{1,0:T(8,128)S(1)}) custom-call(bf16[1024,768]{1,0:T(8,128)(2,1)S(1)} %get-tuple-element.46.rows_ref, f32[1,1024]{1,0:T(1,128)S(1)} %get-tuple-element.47.place_ref, ...), custom_call_target="tpu_custom_call" | custom-call | flops 402653184 | tf_op jit(solution)/shard_map/pallas_call | solution.py:161
  17.1 1.8 %shard_map.103 = (bf16[256,768]{1,0:T(8,128)(2,1)S(1)}, bf16[256,768]{1,0:T(8,128)(2,1)S(1)}, bf16[256,768]{1,0:T(8,128)(2,1)S(1)}) custom-call(s32[16]{0:T(128)S(1)} %copy-done.7, f32[16,768]{1,0:T(8,128)S(1)} %copy-done.1, bf16[768,2304]{1,0:T(8,128)(2,1)S(1)} %copy-done, bf16[256,768]{1,0:T(8,128)(2,1)S(1)} %shard_map.101.rest_0_), custom_call_target="tpu_custom_call" | custom-call | flops 905969664 | bytes 5111808 | tf_op jit(solution)/shard_map/pallas_call | solution.py:240
  19.0 4.7 %collective-permute-done.1.refs_0_ = bf16[128,768]{1,0:T(8,128)(2,1)S(1)} collective-permute-done((bf16[128,768]{1,0:T(8,128)(2,1)S(1)}, bf16[128,768]{1,0:T(8,128)(2,1)S(1)}, u32[]{:S(2)}, u32[]{:S(2)}) %collective-permute-start.1) | collective-permute-done | bytes 196640 | tf_op jit(solution)/shard_map/ppermute | solution.py:61
  24.3 3.4 %collective-permute-start.8 = (bf16[128,768]{1,0:T(8,128)(2,1)}, bf16[128,768]{1,0:T(8,128)(2,1)}, u32[]{:S(2)}, u32[]{:S(2)}) collective-permute-start(bf16[128,768]{1,0:T(8,128)(2,1)} %get-tuple-element.63), channel_id=1, source_target_pairs={{0,2},{1,3},{2,0},{3,1},{4,6},{5,7},{6,4},{7,5},{8,10},{9,11},{10,... | collective-permute-start | bytes 589832 | tf_op jit(solution)/shard_map/ppermute | solution.py:61
  27.7 1.1 collective-permute-start.9
  28.8 1.4 %collective-permute-start.10 = (bf16[128,768]{1,0:T(8,128)(2,1)}, bf16[128,768]{1,0:T(8,128)(2,1)}, u32[]{:S(2)}, u32[]{:S(2)}) collective-permute-start(bf16[128,768]{1,0:T(8,128)(2,1)} %get-tuple-element.65), channel_id=1, source_target_pairs={{0,6},{1,7},{2,4},{3,5},{4,2},{5,3},{6,0},{7,1},{8,14},{9,15},{10,... | collective-permute-start | bytes 589832 | tf_op jit(solution)/shard_map/ppermute | solution.py:61
  30.1 1.8 %shard_map.105 = (bf16[256,768]{1,0:T(8,128)(2,1)S(1)}, bf16[256,768]{1,0:T(8,128)(2,1)S(1)}, bf16[256,768]{1,0:T(8,128)(2,1)S(1)}) custom-call(s32[16]{0:T(128)S(1)} %copy-done.7, f32[16,768]{1,0:T(8,128)S(1)} %copy-done.1, bf16[768,2304]{1,0:T(8,128)(2,1)S(1)} %copy-done, bf16[256,768]{1,0:T(8,128)(2,1)S(1)} %shard_map.104.rest_0_.rest_1_), custom_call_target="tpu_custom_call" | custom-call | flops 905969664 | bytes 5111808 | tf_op jit(solution)/shard_map/pallas_call | solution.py:240
  32.0 2.2 %shard_map.106 = (bf16[512,768]{1,0:T(8,128)(2,1)S(1)}, bf16[512,768]{1,0:T(8,128)(2,1)S(1)}) custom-call(s32[16]{0:T(128)S(1)} %copy-done.7, f32[16,768]{1,0:T(8,128)S(1)} %copy-done.1, bf16[768,2304]{1,0:T(8,128)(2,1)S(1)} %copy-done, bf16[256,768]{1,0:T(8,128)(2,1)S(1)} %collective-permute-done.3.rest_0_, ...), custom_call_target="tpu_custom_call" | custom-call | flops 1207959552 | bytes 5898240 | tf_op jit(solution)/shard_map/pallas_call | solution.py:240
  34.2 9.4 %shard_map.107 = (bf16[4,4,32,768]{3,2,1,0:T(8,128)(2,1)S(1)}, f32[8,128]{1,0:T(8,128)S(1)}) custom-call(s32[16]{0:T(128)S(1)} %copy-done.7, f32[16,768]{1,0:T(8,128)S(1)} %copy-done.1, bf16[768,768]{1,0:T(8,128)(2,1)S(1)} %copy-done.4, bf16[256,768]{1,0:T(8,128)(2,1)S(1)} %shard_map.101.rest_0_, bf16[256,768]{1,0:T(8,128)(2,1)S(1)} %shard_map.104.rest_0_.rest_1_, ...), custom_call_target="tpu_custom_call" | custom-call | flops 6442450944 | tf_op jit(solution)/shard_map/pallas_call | solution.py:348
  44.5 6.2 %all-to-all-start = ((bf16[16,32,768]{2,1,0:T(8,128)(2,1)}), bf16[16,32,768]{2,1,0:T(8,128)(2,1)}, u32[]{:S(2)}, u32[]{:S(2)}) async-start(bf16[16,32,768]{2,1,0:T(8,128)(2,1)} %bitcast.5), calls=%async_computation | async-start | bytes 1572864 | tf_op jit(solution)/shard_map/all_to_all | solution.py:653
  50.8 0.9 copy-done.10
  51.7 1.4 %shard_map.109.rest_0_ = bf16[512,768]{1,0:T(8,128)(2,1)S(1)} custom-call(bf16[128,768]{1,0:T(8,128)(2,1)S(1)} %copy-done.10, bf16[128,768]{1,0:T(8,128)(2,1)} %collective-permute-done.8.refs_1_, bf16[128,768]{1,0:T(8,128)(2,1)} %collective-permute-done.9.refs_2_, bf16[128,768]{1,0:T(8,128)(2,1)} %collective-permute-done.10.refs_3_, ...), custom_call_target="tpu_custom_call" | custom-call | flops 68719476736 | tf_op jit(solution)/shard_map/pallas_call | solution.py:187
  53.1 2.8 %shard_map.110 = (bf16[512,768]{1,0:T(8,128)(2,1)S(1)}, bf16[512,768]{1,0:T(8,128)(2,1)S(1)}, bf16[512,768]{1,0:T(8,128)(2,1)S(1)}) custom-call(s32[16]{0:T(128)S(1)} %copy-done.7, f32[16,768]{1,0:T(8,128)S(1)} %copy-done.2, bf16[768,2304]{1,0:T(8,128)(2,1)S(1)} %copy-done, bf16[512,768]{1,0:T(8,128)(2,1)S(1)} %shard_map.109.rest_0_), custom_call_target="tpu_custom_call" | custom-call | tf_op jit(solution)/shard_map/pallas_call | solution.py:240
  56.0 2.2 %shard_map.111 = (bf16[512,768]{1,0:T(8,128)(2,1)S(1)}, bf16[512,768]{1,0:T(8,128)(2,1)S(1)}) custom-call(s32[16]{0:T(128)S(1)} %copy-done.7, f32[16,768]{1,0:T(8,128)S(1)} %copy-done.2, bf16[768,2304]{1,0:T(8,128)(2,1)S(1)} %copy-done, bf16[512,768]{1,0:T(8,128)(2,1)S(1)} %collective-permute-done.11.rest_0_, bf16[512,768]{1,0:T(8,128)(2,1)S(1)} %get-tuple-element.67.rest_1_), custom_call_target="tpu_custom_call" | custom-call | tf_op jit(solution)/shard_map/pallas_call | solution.py:240
  58.2 10.3 %shard_map.112 = (bf16[4,4,32,768]{3,2,1,0:T(8,128)(2,1)}, f32[8,128]{1,0:T(8,128)}) custom-call(s32[16]{0:T(128)S(1)} %copy-done.7, f32[16,768]{1,0:T(8,128)S(1)} %copy-done.2, bf16[768,768]{1,0:T(8,128)(2,1)S(1)} %copy-done.5, bf16[512,768]{1,0:T(8,128)(2,1)S(1)} %shard_map.109.rest_0_, bf16[512,768]{1,0:T(8,128)(2,1)S(1)} %get-tuple-element.67.rest_1_, ...), custom_call_target="tpu_custom_call" | custom-call | tf_op jit(solution)/shard_map/pallas_call | solution.py:348
  69.2 5.6 %all-to-all-start.1 = ((bf16[16,32,768]{2,1,0:T(8,128)(2,1)}), bf16[16,32,768]{2,1,0:T(8,128)(2,1)S(1)}, u32[]{:S(2)}, u32[]{:S(2)}) async-start(bf16[16,32,768]{2,1,0:T(8,128)(2,1)} %bitcast.3), calls=%async_computation.1 | async-start | bytes 1572864 | tf_op jit(solution)/shard_map/all_to_all | solution.py:653
  74.8 14.4 %shard_map.108 = (bf16[4,32,768]{2,1,0:T(8,128)(2,1)S(1)}, bf16[4,32,768]{2,1,0:T(8,128)(2,1)S(1)}, bf16[4,32,768]{2,1,0:T(8,128)(2,1)S(1)}, bf16[4,32,768]{2,1,0:T(8,128)(2,1)S(1)}) custom-call(bf16[768,2304]{1,0:T(8,128)(2,1)} %qkv_hbm.3, bf16[768,768]{1,0:T(8,128)(2,1)} %out_hbm.3, bf16[768,3072]{1,0:T(8,128)(2,1)} %up_hbm.5, bf16[3072,768]{1,0:T(8,128)(2,1)} %down_hbm.5, ...), custom_call_target="tpu_custom_call" | custom-call | flops 7247757312 | bytes 15728640 | tf_op jit(solution)/shard_map/pallas_call | solution.py:544
  89.2 1.5 %collective-permute-start.5 = (bf16[4,32,768]{2,1,0:T(8,128)(2,1)S(1)}, bf16[4,32,768]{2,1,0:T(8,128)(2,1)S(1)}, u32[]{:S(2)}, u32[]{:S(2)}) collective-permute-start(bf16[4,32,768]{2,1,0:T(8,128)(2,1)S(1)} %get-tuple-element.59), channel_id=1, source_target_pairs={{0,8},{8,0},{16,24},{24,16},{1,9},{9,1},{17,25},{25,17},{2,10},{10... | collective-permute-start | bytes 589832 | tf_op jit(solution)/shard_map/ppermute | solution.py:61
  90.8 1.5 %collective-permute-start.6 = (bf16[4,32,768]{2,1,0:T(8,128)(2,1)S(1)}, bf16[4,32,768]{2,1,0:T(8,128)(2,1)S(1)}, u32[]{:S(2)}, u32[]{:S(2)}) collective-permute-start(bf16[4,32,768]{2,1,0:T(8,128)(2,1)S(1)} %get-tuple-element.60), channel_id=1, source_target_pairs={{0,16},{8,24},{16,0},{24,8},{1,17},{9,25},{17,1},{25,9},{2,18},{10... | collective-permute-start | bytes 589832 | tf_op jit(solution)/shard_map/ppermute | solution.py:61
  93.4 13.3 %shard_map.113 = (bf16[4,32,768]{2,1,0:T(8,128)(2,1)S(1)}, bf16[4,32,768]{2,1,0:T(8,128)(2,1)S(1)}, bf16[4,32,768]{2,1,0:T(8,128)(2,1)S(1)}, f32[128,768]{1,0:T(8,128)S(1)}) custom-call(bf16[768,2304]{1,0:T(8,128)(2,1)} %qkv_hbm.3, bf16[768,768]{1,0:T(8,128)(2,1)} %out_hbm.3, bf16[768,3072]{1,0:T(8,128)(2,1)} %up_hbm.5, bf16[3072,768]{1,0:T(8,128)(2,1)} %down_hbm.5, ...), custom_call_target="tpu_custom_call" | custom-call | flops 7247757312 | bytes 15728640 | tf_op jit(solution)/shard_map/pallas_call | solution.py:544
  106.7 0.9 collective-permute-start.12
  107.6 1.5 %collective-permute-start.13 = (bf16[4,32,768]{2,1,0:T(8,128)(2,1)S(1)}, bf16[4,32,768]{2,1,0:T(8,128)(2,1)S(1)}, u32[]{:S(2)}, u32[]{:S(2)}) collective-permute-start(bf16[4,32,768]{2,1,0:T(8,128)(2,1)S(1)} %get-tuple-element.75), channel_id=1, source_target_pairs={{0,16},{8,24},{16,0},{24,8},{1,17},{9,25},{17,1},{25,9},{2,18},{10... | collective-permute-start | bytes 589832 | tf_op jit(solution)/shard_map/ppermute | solution.py:61
  109.1 1.2 collective-permute-start.14
  110.3 4.8 %shard_map.114.refs_4_ = bf16[4,32,768]{2,1,0:T(8,128)(2,1)S(1)} custom-call(bf16[768,3072]{1,0:T(8,128)(2,1)} %up_hbm.5, bf16[3072,768]{1,0:T(8,128)(2,1)} %down_hbm.5, f32[128,768]{1,0:T(8,128)S(1)} %get-tuple-element.73.rest_ref), custom_call_target="tpu_custom_call" | custom-call | flops 1207959552 | bytes 9437184 | tf_op jit(solution)/shard_map/pallas_call | solution.py:440
  115.2 1.0 collective-permute-done.13.refs_6_
  116.2 1.0 collective-permute-done.14.refs_7_
  117.2 2.7 %shard_map.115 = bf16[256,4,768]{2,1,0:T(4,128)(2,1)} custom-call(f32[1,256]{1,0:T(1,128)S(1)} %get-tuple-element.41.keys_ref, bf16[4,32,768]{2,1,0:T(8,128)(2,1)S(1)} %get-tuple-element.58.refs_0_, bf16[4,32,768]{2,1,0:T(8,128)(2,1)S(1)} %collective-permute-done.5.refs_1_, bf16[4,32,768]{2,1,0:T(8,128)(2,1)S(1)} %collective-permute-done.6.refs_2_, ...), custom_call_target="tpu_custom_call" | custom-call | flops 402653184 | bytes 3145728 | tf_op jit(solution)/shard_map/pallas_call | solution.py:584
  (40 shorter events, 4.7 us)
Async XLA Ops:
  0.0 1.4 %copy-start.3 = (bf16[256,4,768]{2,1,0:T(4,128)(2,1)S(1)}, bf16[256,4,768]{2,1,0:T(4,128)(2,1)}, u32[]{:S(2)}) copy-start(bf16[256,4,768]{2,1,0:T(4,128)(2,1)} %x_ref.1) | copy-start | bytes 4718596
  1.4 0.7 copy-start.8
  2.1 15.0 %copy-start = (bf16[768,2304]{1,0:T(8,128)(2,1)S(1)}, bf16[768,2304]{1,0:T(8,128)(2,1)}, u32[]{:S(2)}) copy-start(bf16[768,2304]{1,0:T(8,128)(2,1)} %w_ref.12) | copy-start | bytes 10616836
  3.4 13.7 %copy-start.1 = (f32[16,768]{1,0:T(8,128)S(1)}, f32[16,768]{1,0:T(8,128)}, u32[]{:S(2)}) copy-start(f32[16,768]{1,0:T(8,128)} %table_ref.13) | copy-start | bytes 147460
  3.4 13.7 %copy-start.7 = (s32[16]{0:T(128)S(1)}, s32[16]{0:T(128)}, u32[]{:S(2)}) copy-start(s32[16]{0:T(128)} %index_ref.13) | copy-start | bytes 196
  3.4 11.4 %collective-permute-start = (bf16[128,768]{1,0:T(8,128)(2,1)S(1)}, bf16[128,768]{1,0:T(8,128)(2,1)S(1)}, u32[]{:S(2)}, u32[]{:S(2)}) collective-permute-start(bf16[128,768]{1,0:T(8,128)(2,1)S(1)} %get-tuple-element.43), channel_id=1, source_target_pairs={{0,2},{1,3},{2,0},{3,1},{4,6},{5,7},{6,4},{7,5},{8,10},{9,11},{10,... | collective-permute-start | bytes 589832 | tf_op jit(solution)/shard_map/ppermute | solution.py:61
  6.5 17.2 %collective-permute-start.1 = (bf16[128,768]{1,0:T(8,128)(2,1)S(1)}, bf16[128,768]{1,0:T(8,128)(2,1)S(1)}, u32[]{:S(2)}, u32[]{:S(2)}) collective-permute-start(bf16[128,768]{1,0:T(8,128)(2,1)S(1)} %get-tuple-element.44), channel_id=1, source_target_pairs={{0,4},{1,5},{2,6},{3,7},{4,0},{5,1},{6,2},{7,3},{8,12},{9,13},{10,... | collective-permute-start | bytes 589832 | tf_op jit(solution)/shard_map/ppermute | solution.py:61
  9.1 14.6 %collective-permute-start.2 = (bf16[128,768]{1,0:T(8,128)(2,1)S(1)}, bf16[128,768]{1,0:T(8,128)(2,1)S(1)}, u32[]{:S(2)}, u32[]{:S(2)}) collective-permute-start(bf16[128,768]{1,0:T(8,128)(2,1)S(1)} %get-tuple-element.45), channel_id=1, source_target_pairs={{0,6},{1,7},{2,4},{3,5},{4,2},{5,3},{6,0},{7,1},{8,14},{9,15},{10,... | collective-permute-start | bytes 589832 | tf_op jit(solution)/shard_map/ppermute | solution.py:61
  15.3 16.7 %collective-permute-start.3 = (bf16[256,768]{1,0:T(8,128)(2,1)S(1)}, bf16[256,768]{1,0:T(8,128)(2,1)S(1)}, u32[]{:S(2)}, u32[]{:S(2)}) collective-permute-start(bf16[256,768]{1,0:T(8,128)(2,1)S(1)} %shard_map.101.rest_0_), channel_id=1, source_target_pairs={{0,1},{1,0},{2,3},{3,2},{4,5},{5,4},{6,7},{7,6},{8,9},{9,8},{10,11... | collective-permute-start | bytes 1179656 | tf_op jit(solution)/shard_map/ppermute | solution.py:61
  17.1 1.9 %copy-start.9 = (bf16[128,768]{1,0:T(8,128)(2,1)}, bf16[128,768]{1,0:T(8,128)(2,1)S(1)}, u32[]{:S(2)}) copy-start(bf16[128,768]{1,0:T(8,128)(2,1)S(1)} %get-tuple-element.62.refs_0_) | copy-start | bytes 589828
  24.2 7.8 %collective-permute-start.4 = (bf16[256,768]{1,0:T(8,128)(2,1)S(1)}, bf16[256,768]{1,0:T(8,128)(2,1)S(1)}, u32[]{:S(2)}, u32[]{:S(2)}) collective-permute-start(bf16[256,768]{1,0:T(8,128)(2,1)S(1)} %shard_map.104.rest_0_.rest_1_), channel_id=1, source_target_pairs={{0,1},{1,0},{2,3},{3,2},{4,5},{5,4},{6,7},{7,6},{8,9},{9,8},{10,11... | collective-permute-start | bytes 1179656 | tf_op jit(solution)/shard_map/ppermute | solution.py:61
  24.3 26.5 %collective-permute-start.8 = (bf16[128,768]{1,0:T(8,128)(2,1)}, bf16[128,768]{1,0:T(8,128)(2,1)}, u32[]{:S(2)}, u32[]{:S(2)}) collective-permute-start(bf16[128,768]{1,0:T(8,128)(2,1)} %get-tuple-element.63), channel_id=1, source_target_pairs={{0,2},{1,3},{2,0},{3,1},{4,6},{5,7},{6,4},{7,5},{8,10},{9,11},{10,... | collective-permute-start | bytes 589832 | tf_op jit(solution)/shard_map/ppermute | solution.py:61
  27.7 23.1 %collective-permute-start.9 = (bf16[128,768]{1,0:T(8,128)(2,1)}, bf16[128,768]{1,0:T(8,128)(2,1)}, u32[]{:S(2)}, u32[]{:S(2)}) collective-permute-start(bf16[128,768]{1,0:T(8,128)(2,1)} %get-tuple-element.64), channel_id=1, source_target_pairs={{0,4},{1,5},{2,6},{3,7},{4,0},{5,1},{6,2},{7,3},{8,12},{9,13},{10,... | collective-permute-start | bytes 589832 | tf_op jit(solution)/shard_map/ppermute | solution.py:61
  28.8 22.0 %collective-permute-start.10 = (bf16[128,768]{1,0:T(8,128)(2,1)}, bf16[128,768]{1,0:T(8,128)(2,1)}, u32[]{:S(2)}, u32[]{:S(2)}) collective-permute-start(bf16[128,768]{1,0:T(8,128)(2,1)} %get-tuple-element.65), channel_id=1, source_target_pairs={{0,6},{1,7},{2,4},{3,5},{4,2},{5,3},{6,0},{7,1},{8,14},{9,15},{10,... | collective-permute-start | bytes 589832 | tf_op jit(solution)/shard_map/ppermute | solution.py:61
  32.0 2.2 %copy-start.4 = (bf16[768,768]{1,0:T(8,128)(2,1)S(1)}, bf16[768,768]{1,0:T(8,128)(2,1)}, u32[]{:S(2)}) copy-start(bf16[768,768]{1,0:T(8,128)(2,1)} %w_ref.13) | copy-start | bytes 3538948
  43.7 0.9 copy-start.6
  44.5 24.6 %all-to-all-start = ((bf16[16,32,768]{2,1,0:T(8,128)(2,1)}), bf16[16,32,768]{2,1,0:T(8,128)(2,1)}, u32[]{:S(2)}, u32[]{:S(2)}) async-start(bf16[16,32,768]{2,1,0:T(8,128)(2,1)} %bitcast.5), calls=%async_computation | async-start | bytes 1572864 | tf_op jit(solution)/shard_map/all_to_all | solution.py:653
  50.7 0.9 copy-start.10
  51.7 1.5 %copy-start.2 = (f32[16,768]{1,0:T(8,128)S(1)}, f32[16,768]{1,0:T(8,128)}, u32[]{:S(2)}) copy-start(f32[16,768]{1,0:T(8,128)} %table_ref.13) | copy-start | bytes 147460
  53.1 2.9 %collective-permute-start.11 = (bf16[512,768]{1,0:T(8,128)(2,1)S(1)}, bf16[512,768]{1,0:T(8,128)(2,1)S(1)}, u32[]{:S(2)}, u32[]{:S(2)}) collective-permute-start(bf16[512,768]{1,0:T(8,128)(2,1)S(1)} %shard_map.109.rest_0_), channel_id=1, source_target_pairs={{0,1},{1,0},{2,3},{3,2},{4,5},{5,4},{6,7},{7,6},{8,9},{9,8},{10,11... | collective-permute-start | bytes 2359304 | tf_op jit(solution)/shard_map/ppermute | solution.py:61
  56.0 2.2 %copy-start.5 = (bf16[768,768]{1,0:T(8,128)(2,1)S(1)}, bf16[768,768]{1,0:T(8,128)(2,1)}, u32[]{:S(2)}) copy-start(bf16[768,768]{1,0:T(8,128)(2,1)} %w_ref.13) | copy-start | bytes 3538948
  69.2 24.3 %all-to-all-start.1 = ((bf16[16,32,768]{2,1,0:T(8,128)(2,1)}), bf16[16,32,768]{2,1,0:T(8,128)(2,1)S(1)}, u32[]{:S(2)}, u32[]{:S(2)}) async-start(bf16[16,32,768]{2,1,0:T(8,128)(2,1)} %bitcast.3), calls=%async_computation.1 | async-start | bytes 1572864 | tf_op jit(solution)/shard_map/all_to_all | solution.py:653
  89.2 19.9 %collective-permute-start.5 = (bf16[4,32,768]{2,1,0:T(8,128)(2,1)S(1)}, bf16[4,32,768]{2,1,0:T(8,128)(2,1)S(1)}, u32[]{:S(2)}, u32[]{:S(2)}) collective-permute-start(bf16[4,32,768]{2,1,0:T(8,128)(2,1)S(1)} %get-tuple-element.59), channel_id=1, source_target_pairs={{0,8},{8,0},{16,24},{24,16},{1,9},{9,1},{17,25},{25,17},{2,10},{10... | collective-permute-start | bytes 589832 | tf_op jit(solution)/shard_map/ppermute | solution.py:61
  90.8 24.4 %collective-permute-start.6 = (bf16[4,32,768]{2,1,0:T(8,128)(2,1)S(1)}, bf16[4,32,768]{2,1,0:T(8,128)(2,1)S(1)}, u32[]{:S(2)}, u32[]{:S(2)}) collective-permute-start(bf16[4,32,768]{2,1,0:T(8,128)(2,1)S(1)} %get-tuple-element.60), channel_id=1, source_target_pairs={{0,16},{8,24},{16,0},{24,8},{1,17},{9,25},{17,1},{25,9},{2,18},{10... | collective-permute-start | bytes 589832 | tf_op jit(solution)/shard_map/ppermute | solution.py:61
  92.3 22.9 %collective-permute-start.7 = (bf16[4,32,768]{2,1,0:T(8,128)(2,1)S(1)}, bf16[4,32,768]{2,1,0:T(8,128)(2,1)S(1)}, u32[]{:S(2)}, u32[]{:S(2)}) collective-permute-start(bf16[4,32,768]{2,1,0:T(8,128)(2,1)S(1)} %get-tuple-element.61), channel_id=1, source_target_pairs={{0,24},{8,16},{16,8},{24,0},{1,25},{9,17},{17,9},{25,1},{2,26},{10... | collective-permute-start | bytes 589832 | tf_op jit(solution)/shard_map/ppermute | solution.py:61
  106.7 8.4 %collective-permute-start.12 = (bf16[4,32,768]{2,1,0:T(8,128)(2,1)S(1)}, bf16[4,32,768]{2,1,0:T(8,128)(2,1)S(1)}, u32[]{:S(2)}, u32[]{:S(2)}) collective-permute-start(bf16[4,32,768]{2,1,0:T(8,128)(2,1)S(1)} %get-tuple-element.74), channel_id=1, source_target_pairs={{0,8},{8,0},{16,24},{24,16},{1,9},{9,1},{17,25},{25,17},{2,10},{10... | collective-permute-start | bytes 589832 | tf_op jit(solution)/shard_map/ppermute | solution.py:61
  107.6 8.5 %collective-permute-start.13 = (bf16[4,32,768]{2,1,0:T(8,128)(2,1)S(1)}, bf16[4,32,768]{2,1,0:T(8,128)(2,1)S(1)}, u32[]{:S(2)}, u32[]{:S(2)}) collective-permute-start(bf16[4,32,768]{2,1,0:T(8,128)(2,1)S(1)} %get-tuple-element.75), channel_id=1, source_target_pairs={{0,16},{8,24},{16,0},{24,8},{1,17},{9,25},{17,1},{25,9},{2,18},{10... | collective-permute-start | bytes 589832 | tf_op jit(solution)/shard_map/ppermute | solution.py:61
  109.1 8.1 %collective-permute-start.14 = (bf16[4,32,768]{2,1,0:T(8,128)(2,1)S(1)}, bf16[4,32,768]{2,1,0:T(8,128)(2,1)S(1)}, u32[]{:S(2)}, u32[]{:S(2)}) collective-permute-start(bf16[4,32,768]{2,1,0:T(8,128)(2,1)S(1)} %get-tuple-element.76), channel_id=1, source_target_pairs={{0,24},{8,16},{16,8},{24,0},{1,25},{9,17},{17,9},{25,1},{2,26},{10... | collective-permute-start | bytes 589832 | tf_op jit(solution)/shard_map/ppermute | solution.py:61

commit v14 on v11

--- a/solution.py
+++ b/solution.py
@@ -73,6 +73,13 @@
         self.rows = self.block // self.share
         self.part_rows = self.rows // self.groups
         assert self.part_rows * self.groups * self.share * WINDOWS == self.loc_dev
+
+    def spot(self, row, group):
+        if self.share > 1:
+            return row * self.groups + group
+        place = (row + self.rows_count - 1) % self.rows_count
+        turn = (group + self.rows_count * self.groups - place) % self.groups
+        return turn * self.rows_count + place
 
 
 def marker():
@@ -334,14 +341,14 @@
                 mid = (start + added[pl.ds(slot * rows, rows), :]).astype(BF16)
                 for owner in range(plan.groups):
                     part = mid[owner * plan.part_rows : (owner + 1) * plan.part_rows]
-                    out_ref[row ^ slot, owner] = part
+                    out_ref[plan.spot(row ^ slot, owner)] = part
                 slot += 1
 
     key_rows = sum(piece.shape[0] for piece in keys)
     return call(
         kernel,
         [
-            jax.ShapeDtypeStruct((plan.rows_count, plan.groups, plan.part_rows, width), BF16),
+            jax.ShapeDtypeStruct((plan.rows_count * plan.groups, plan.part_rows, width), BF16),
             marker(),
         ],
         hide * 16 * total * key_rows * width,
@@ -450,7 +457,7 @@
 
 def channel(plan, parts, now, later, fetch, channel_qkv, channel_out, up_weight, down_weight):
     groups, width = plan.groups, plan.width
-    bands, _, locations, _ = parts.shape
+    bands, locations = plan.band_dev, parts.shape[1]
     small = GROUP_LOCS
     assert locations % TILE_LOCS == 0
     owners = [*now, *later]
@@ -487,7 +494,7 @@
         if held:
             load.wait()
         for (owner, band, first), places in piece_places(owners, bands, locations).items():
-            piece = in_ref[band, me ^ owner, first : first + TILE_LOCS, :].astype(F32)
+            piece = in_ref[plan.spot(band, me ^ owner), first : first + TILE_LOCS, :].astype(F32)
             for number, place in enumerate(places):
                 mid[place, :] = piece[number * small : (number + 1) * small]
         norm_into(normed, mid)
@@ -633,22 +640,23 @@
         )
         behind = [done]
         mids.append(mid)
-    same = [
-        [g * plan.locs + r * CORES + core for r in range(plan.rows_count) for g in range(plan.groups)]
-        for core in range(CORES)
-    ]
+    listed = [(r, g) for r in range(plan.rows_count) for g in range(plan.groups)]
+    listed.sort(key=lambda device: plan.spot(*device))
+    same = [[g * plan.locs + r * CORES + core for r, g in listed] for core in range(CORES)]
     returned = []
     for mid in mids:
         parts = lax.all_to_all(
-            mid.reshape(-1, plan.part_rows, plan.width),
+            mid,
             ("band", "loc"),
             0,
             0,
             axis_index_groups=same,
             tiled=True,
         )
-        parts = parts.reshape(plan.band_dev, plan.share, plan.groups, plan.part_rows, plan.width)
-        parts = parts.transpose(0, 2, 1, 3, 4).reshape(plan.band_dev, plan.groups, -1, plan.width)
+        if plan.share > 1:
+            shape = (plan.band_dev, plan.share, plan.groups, plan.part_rows, plan.width)
+            parts = parts.reshape(shape).transpose(0, 2, 1, 3, 4)
+            parts = parts.reshape(plan.band_dev * plan.groups, -1, plan.width)
         weights = (channel_qkv, channel_out, up_weight, down_weight)
         now, later = list(range(plan.groups)), []
         if mid is mids[-1] and plan.groups > 1:

time: 122 us -> 122 us (level)
  transfers between devices with their start and end apart: 17 -> 17, of which waited for: 6 -> 5; matrix products, arithmetic and copies ran while one was open for 0% -> 0% of each run, Pallas kernels for 55% -> 55%
where the time goes in v14:
time: 122 us
  Pallas kernels  71.2 us (58%)
  starting transfers between devices  29.3 us (24%)
  waiting for transfers between devices  17.3 us (14%)
  local copies, waits for them, and re-layouts  3.93 us (3%)
    pallas_call x2, Pallas kernels, channel(): call(kernel, [jax.ShapeDtypeStruct((bands, locations, width), BF16)] * le...  27.8 us
    pallas_call x2, Pallas kernels, attend(): call(kernel, [jax.ShapeDtypeStruct((plan.rows_count * plan.groups, plan.p...  19.8 us
    ppermute x15, starting transfers between devices, exchange(): lax.ppermute(value, axis, [(i, i ^ step) for i in range(lax.axis_size(axi...  18.9 us
    ppermute x15, waiting for transfers between devices, exchange(): lax.ppermute(value, axis, [(i, i ^ step) for i in range(lax.axis_size(axi...  13.2 us
    pallas_call x5, Pallas kernels, project(): call(kernel, [jax.ShapeDtypeStruct((rows, width), BF16)] * len(names), hi...  10.8 us
    all_to_all x2, starting transfers between devices, body(): lax.all_to_all(mid, ('band', 'loc'), 0, 0, axis_index_groups=same, tiled=...  10.4 us
    pallas_call x1, Pallas kernels, finish(): call(kernel, [jax.ShapeDtypeStruct((bands, locations, width), BF16)] * le...  4.84 us
    all_to_all x2, waiting for transfers between devices, body(): lax.all_to_all(mid, ('band', 'loc'), 0, 0, axis_index_groups=same, tiled=...  4.13 us
  transfers between devices with their start and end apart: 17, of which 5 were waited for; matrix products, arithmetic and copies ran while one was open for 0% of the time, Pallas kernels for 55%

profile of v14, /device:TPU:0, one launch (start us, length us, event | category | flops | bytes accessed | tf_op | source)
XLA Modules:
  0.0 122.0 jit_solution(6162895428141116169)
XLA Ops:
  0.0 1.4 %copy-done.3 = bf16[256,4,768]{2,1,0:T(4,128)(2,1)S(1)} copy-done((bf16[256,4,768]{2,1,0:T(4,128)(2,1)S(1)}, bf16[256,4,768]{2,1,0:T(4,128)(2,1)}, u32[]{:S(2)}) %copy-start.3) | copy-done | bytes 1572888
  2.1 1.3 %shard_map.100 = (bf16[128,768]{1,0:T(8,128)(2,1)S(1)}, bf16[128,768]{1,0:T(8,128)(2,1)S(1)}, bf16[128,768]{1,0:T(8,128)(2,1)S(1)}, bf16[128,768]{1,0:T(8,128)(2...) custom-call(s32[16,128]{1,0:T(8,128)S(1)} %bitcast.1, ...), custom_call_target="tpu_custom_call" | custom-call | flops 402653184 | bytes 3145728 | tf_op jit(solution)/shard_map/pallas_call | solution.py:138
  3.4 3.1 %collective-permute-start = (bf16[128,768]{1,0:T(8,128)(2,1)S(1)}, bf16[128,768]{1,0:T(8,128)(2,1)S(1)}, u32[]{:S(2)}, u32[]{:S(2)}) collective-permute-start(bf16[128,768]{1,0:T(8,128)(2,1)S(1)} %get-tuple-element.43), channel_id=1, source_target_pairs={{0,2},{1,3},{2,0},{3,1},{4,6},{5,7},{6,4},{7,5},{8,10},{9,11},{10,... | collective-permute-start | bytes 589832 | tf_op jit(solution)/shard_map/ppermute | solution.py:61
  6.5 2.6 %collective-permute-start.1 = (bf16[128,768]{1,0:T(8,128)(2,1)S(1)}, bf16[128,768]{1,0:T(8,128)(2,1)S(1)}, u32[]{:S(2)}, u32[]{:S(2)}) collective-permute-start(bf16[128,768]{1,0:T(8,128)(2,1)S(1)} %get-tuple-element.44), channel_id=1, source_target_pairs={{0,4},{1,5},{2,6},{3,7},{4,0},{5,1},{6,2},{7,3},{8,12},{9,13},{10,... | collective-permute-start | bytes 589832 | tf_op jit(solution)/shard_map/ppermute | solution.py:61
  9.1 5.7 %collective-permute-done.refs_1_.rest_0_ = bf16[128,768]{1,0:T(8,128)(2,1)S(1)} collective-permute-done((bf16[128,768]{1,0:T(8,128)(2,1)S(1)}, bf16[128,768]{1,0:T(8,128)(2,1)S(1)}, u32[]{:S(2)}, u32[]{:S(2)}) %collective-permute-start) | collective-permute-done | bytes 196640 | tf_op jit(solution)/shard_map/ppermute | solution.py:61
  15.4 1.7 %shard_map.102 = (bf16[128,768]{1,0:T(8,128)(2,1)S(1)}, bf16[128,768]{1,0:T(8,128)(2,1)}, bf16[128,768]{1,0:T(8,128)(2,1)}, bf16[128,768]{1,0:T(8,128)(2,1)}, f32[8,128]{1,0:T(8,128)S(1)}) custom-call(bf16[1024,768]{1,0:T(8,128)(2,1)S(1)} %get-tuple-element.46.rows_ref, f32[1,1024]{1,0:T(1,128)S(1)} %get-tuple-element.47.place_ref, ...), custom_call_target="tpu_custom_call" | custom-call | flops 402653184 | tf_op jit(solution)/shard_map/pallas_call | solution.py:161
  17.1 1.8 %shard_map.103 = (bf16[256,768]{1,0:T(8,128)(2,1)S(1)}, bf16[256,768]{1,0:T(8,128)(2,1)S(1)}, bf16[256,768]{1,0:T(8,128)(2,1)S(1)}) custom-call(s32[16]{0:T(128)S(1)} %copy-done.7, f32[16,768]{1,0:T(8,128)S(1)} %copy-done.1, bf16[768,2304]{1,0:T(8,128)(2,1)S(1)} %copy-done, bf16[256,768]{1,0:T(8,128)(2,1)S(1)} %shard_map.101.rest_0_), custom_call_target="tpu_custom_call" | custom-call | flops 905969664 | bytes 5111808 | tf_op jit(solution)/shard_map/pallas_call | solution.py:240
  19.0 4.7 %collective-permute-done.1.refs_0_ = bf16[128,768]{1,0:T(8,128)(2,1)S(1)} collective-permute-done((bf16[128,768]{1,0:T(8,128)(2,1)S(1)}, bf16[128,768]{1,0:T(8,128)(2,1)S(1)}, u32[]{:S(2)}, u32[]{:S(2)}) %collective-permute-start.1) | collective-permute-done | bytes 196640 | tf_op jit(solution)/shard_map/ppermute | solution.py:61
  24.3 3.4 %collective-permute-start.8 = (bf16[128,768]{1,0:T(8,128)(2,1)}, bf16[128,768]{1,0:T(8,128)(2,1)}, u32[]{:S(2)}, u32[]{:S(2)}) collective-permute-start(bf16[128,768]{1,0:T(8,128)(2,1)} %get-tuple-element.63), channel_id=1, source_target_pairs={{0,2},{1,3},{2,0},{3,1},{4,6},{5,7},{6,4},{7,5},{8,10},{9,11},{10,... | collective-permute-start | bytes 589832 | tf_op jit(solution)/shard_map/ppermute | solution.py:61
  27.7 1.1 collective-permute-start.9
  28.8 1.4 %collective-permute-start.10 = (bf16[128,768]{1,0:T(8,128)(2,1)}, bf16[128,768]{1,0:T(8,128)(2,1)}, u32[]{:S(2)}, u32[]{:S(2)}) collective-permute-start(bf16[128,768]{1,0:T(8,128)(2,1)} %get-tuple-element.65), channel_id=1, source_target_pairs={{0,6},{1,7},{2,4},{3,5},{4,2},{5,3},{6,0},{7,1},{8,14},{9,15},{10,... | collective-permute-start | bytes 589832 | tf_op jit(solution)/shard_map/ppermute | solution.py:61
  30.1 1.8 %shard_map.105 = (bf16[256,768]{1,0:T(8,128)(2,1)S(1)}, bf16[256,768]{1,0:T(8,128)(2,1)S(1)}, bf16[256,768]{1,0:T(8,128)(2,1)S(1)}) custom-call(s32[16]{0:T(128)S(1)} %copy-done.7, f32[16,768]{1,0:T(8,128)S(1)} %copy-done.1, bf16[768,2304]{1,0:T(8,128)(2,1)S(1)} %copy-done, bf16[256,768]{1,0:T(8,128)(2,1)S(1)} %shard_map.104.rest_0_.rest_1_), custom_call_target="tpu_custom_call" | custom-call | flops 905969664 | bytes 5111808 | tf_op jit(solution)/shard_map/pallas_call | solution.py:240
  32.0 2.2 %shard_map.106 = (bf16[512,768]{1,0:T(8,128)(2,1)S(1)}, bf16[512,768]{1,0:T(8,128)(2,1)S(1)}) custom-call(s32[16]{0:T(128)S(1)} %copy-done.7, f32[16,768]{1,0:T(8,128)S(1)} %copy-done.1, bf16[768,2304]{1,0:T(8,128)(2,1)S(1)} %copy-done, bf16[256,768]{1,0:T(8,128)(2,1)S(1)} %collective-permute-done.3.rest_0_, ...), custom_call_target="tpu_custom_call" | custom-call | flops 1207959552 | bytes 5898240 | tf_op jit(solution)/shard_map/pallas_call | solution.py:240
  34.2 9.4 %shard_map.107 = (bf16[16,32,768]{2,1,0:T(8,128)(2,1)S(1)}, f32[8,128]{1,0:T(8,128)S(1)}) custom-call(s32[16]{0:T(128)S(1)} %copy-done.7, f32[16,768]{1,0:T(8,128)S(1)} %copy-done.1, bf16[768,768]{1,0:T(8,128)(2,1)S(1)} %copy-done.4, bf16[256,768]{1,0:T(8,128)(2,1)S(1)} %shard_map.101.rest_0_, bf16[256,768]{1,0:T(8,128)(2,1)S(1)} %shard_map.104.rest_0_.rest_1_, ...), custom_call_target="tpu_custom_call" | custom-call | flops 6442450944 | tf_op jit(solution)/shard_map/pallas_call | solution.py:348
  44.5 6.2 %all-to-all-start = ((bf16[16,32,768]{2,1,0:T(8,128)(2,1)}), bf16[16,32,768]{2,1,0:T(8,128)(2,1)}, u32[]{:S(2)}, u32[]{:S(2)}) async-start(bf16[16,32,768]{2,1,0:T(8,128)(2,1)} %copy-done.6), calls=%async_computation | async-start | bytes 1572864 | tf_op jit(solution)/shard_map/all_to_all | solution.py:648
  50.8 0.9 copy-done.10
  51.7 1.4 %shard_map.109.rest_0_ = bf16[512,768]{1,0:T(8,128)(2,1)S(1)} custom-call(bf16[128,768]{1,0:T(8,128)(2,1)S(1)} %copy-done.10, bf16[128,768]{1,0:T(8,128)(2,1)} %collective-permute-done.8.refs_1_, bf16[128,768]{1,0:T(8,128)(2,1)} %collective-permute-done.9.refs_2_, bf16[128,768]{1,0:T(8,128)(2,1)} %collective-permute-done.10.refs_3_, ...), custom_call_target="tpu_custom_call" | custom-call | flops 68719476736 | tf_op jit(solution)/shard_map/pallas_call | solution.py:187
  53.1 2.8 %shard_map.110 = (bf16[512,768]{1,0:T(8,128)(2,1)S(1)}, bf16[512,768]{1,0:T(8,128)(2,1)S(1)}, bf16[512,768]{1,0:T(8,128)(2,1)S(1)}) custom-call(s32[16]{0:T(128)S(1)} %copy-done.7, f32[16,768]{1,0:T(8,128)S(1)} %copy-done.2, bf16[768,2304]{1,0:T(8,128)(2,1)S(1)} %copy-done, bf16[512,768]{1,0:T(8,128)(2,1)S(1)} %shard_map.109.rest_0_), custom_call_target="tpu_custom_call" | custom-call | tf_op jit(solution)/shard_map/pallas_call | solution.py:240
  56.0 2.2 %shard_map.111 = (bf16[512,768]{1,0:T(8,128)(2,1)S(1)}, bf16[512,768]{1,0:T(8,128)(2,1)S(1)}) custom-call(s32[16]{0:T(128)S(1)} %copy-done.7, f32[16,768]{1,0:T(8,128)S(1)} %copy-done.2, bf16[768,2304]{1,0:T(8,128)(2,1)S(1)} %copy-done, bf16[512,768]{1,0:T(8,128)(2,1)S(1)} %collective-permute-done.11.rest_0_, bf16[512,768]{1,0:T(8,128)(2,1)S(1)} %get-tuple-element.67.rest_1_), custom_call_target="tpu_custom_call" | custom-call | tf_op jit(solution)/shard_map/pallas_call | solution.py:240
  58.2 10.3 %shard_map.112 = (bf16[16,32,768]{2,1,0:T(8,128)(2,1)}, f32[8,128]{1,0:T(8,128)}) custom-call(s32[16]{0:T(128)S(1)} %copy-done.7, f32[16,768]{1,0:T(8,128)S(1)} %copy-done.2, bf16[768,768]{1,0:T(8,128)(2,1)S(1)} %copy-done.5, bf16[512,768]{1,0:T(8,128)(2,1)S(1)} %shard_map.109.rest_0_, bf16[512,768]{1,0:T(8,128)(2,1)S(1)} %get-tuple-element.67.rest_1_, ...), custom_call_target="tpu_custom_call" | custom-call | tf_op jit(solution)/shard_map/pallas_call | solution.py:348
  68.5 1.9 %all-to-all-done.refs_0_ = bf16[16,32,768]{2,1,0:T(8,128)(2,1)} async-done(((bf16[16,32,768]{2,1,0:T(8,128)(2,1)}), bf16[16,32,768]{2,1,0:T(8,128)(2,1)}, u32[]{:S(2)}, u32[]{:S(2)}) %all-to-all-start) | async-done | bytes 786464 | tf_op jit(solution)/shard_map/all_to_all | solution.py:648
  70.4 4.2 %all-to-all-start.1 = ((bf16[16,32,768]{2,1,0:T(8,128)(2,1)}), bf16[16,32,768]{2,1,0:T(8,128)(2,1)S(1)}, u32[]{:S(2)}, u32[]{:S(2)}) async-start(bf16[16,32,768]{2,1,0:T(8,128)(2,1)} %get-tuple-element.72), calls=%async_computation.1 | async-start | bytes 1572864 | tf_op jit(solution)/shard_map/all_to_all | solution.py:648
  74.6 14.5 %shard_map.108 = (bf16[4,32,768]{2,1,0:T(8,128)(2,1)S(1)}, bf16[4,32,768]{2,1,0:T(8,128)(2,1)S(1)}, bf16[4,32,768]{2,1,0:T(8,128)(2,1)S(1)}, bf16[4,32,768]{2,1,0:T(8,128)(2,1)S(1)}) custom-call(bf16[768,2304]{1,0:T(8,128)(2,1)} %qkv_hbm.3, bf16[768,768]{1,0:T(8,128)(2,1)} %out_hbm.3, bf16[768,3072]{1,0:T(8,128)(2,1)} %up_hbm.5, bf16[3072,768]{1,0:T(8,128)(2,1)} %down_hbm.5, ...), custom_call_target="tpu_custom_call" | custom-call | flops 7247757312 | bytes 15728640 | tf_op jit(solution)/shard_map/pallas_call | solution.py:544
  89.1 1.5 %collective-permute-start.5 = (bf16[4,32,768]{2,1,0:T(8,128)(2,1)S(1)}, bf16[4,32,768]{2,1,0:T(8,128)(2,1)S(1)}, u32[]{:S(2)}, u32[]{:S(2)}) collective-permute-start(bf16[4,32,768]{2,1,0:T(8,128)(2,1)S(1)} %get-tuple-element.59), channel_id=1, source_target_pairs={{0,8},{8,0},{16,24},{24,16},{1,9},{9,1},{17,25},{25,17},{2,10},{10... | collective-permute-start | bytes 589832 | tf_op jit(solution)/shard_map/ppermute | solution.py:61
  90.6 1.5 %collective-permute-start.6 = (bf16[4,32,768]{2,1,0:T(8,128)(2,1)S(1)}, bf16[4,32,768]{2,1,0:T(8,128)(2,1)S(1)}, u32[]{:S(2)}, u32[]{:S(2)}) collective-permute-start(bf16[4,32,768]{2,1,0:T(8,128)(2,1)S(1)} %get-tuple-element.60), channel_id=1, source_target_pairs={{0,16},{8,24},{16,0},{24,8},{1,17},{9,25},{17,1},{25,9},{2,18},{10... | collective-permute-start | bytes 589832 | tf_op jit(solution)/shard_map/ppermute | solution.py:61
  92.6 2.2 %all-to-all-done.1.refs_0_ = bf16[16,32,768]{2,1,0:T(8,128)(2,1)S(1)} async-done(((bf16[16,32,768]{2,1,0:T(8,128)(2,1)}), bf16[16,32,768]{2,1,0:T(8,128)(2,1)S(1)}, u32[]{:S(2)}, u32[]{:S(2)}) %all-to-all-start.1) | async-done | bytes 786464 | tf_op jit(solution)/shard_map/all_to_all | solution.py:648
  94.8 13.4 %shard_map.113 = (bf16[4,32,768]{2,1,0:T(8,128)(2,1)S(1)}, bf16[4,32,768]{2,1,0:T(8,128)(2,1)S(1)}, bf16[4,32,768]{2,1,0:T(8,128)(2,1)S(1)}, f32[128,768]{1,0:T(8,128)S(1)}) custom-call(bf16[768,2304]{1,0:T(8,128)(2,1)} %qkv_hbm.3, bf16[768,768]{1,0:T(8,128)(2,1)} %out_hbm.3, bf16[768,3072]{1,0:T(8,128)(2,1)} %up_hbm.5, bf16[3072,768]{1,0:T(8,128)(2,1)} %down_hbm.5, ...), custom_call_target="tpu_custom_call" | custom-call | flops 7247757312 | bytes 15728640 | tf_op jit(solution)/shard_map/pallas_call | solution.py:544
  108.2 1.5 %collective-permute-start.12 = (bf16[4,32,768]{2,1,0:T(8,128)(2,1)S(1)}, bf16[4,32,768]{2,1,0:T(8,128)(2,1)S(1)}, u32[]{:S(2)}, u32[]{:S(2)}) collective-permute-start(bf16[4,32,768]{2,1,0:T(8,128)(2,1)S(1)} %get-tuple-element.74), channel_id=1, source_target_pairs={{0,8},{8,0},{16,24},{24,16},{1,9},{9,1},{17,25},{25,17},{2,10},{10... | collective-permute-start | bytes 589832 | tf_op jit(solution)/shard_map/ppermute | solution.py:61
  110.3 1.5 %collective-permute-start.14 = (bf16[4,32,768]{2,1,0:T(8,128)(2,1)S(1)}, bf16[4,32,768]{2,1,0:T(8,128)(2,1)S(1)}, u32[]{:S(2)}, u32[]{:S(2)}) collective-permute-start(bf16[4,32,768]{2,1,0:T(8,128)(2,1)S(1)} %get-tuple-element.76), channel_id=1, source_target_pairs={{0,24},{8,16},{16,8},{24,0},{1,25},{9,17},{17,9},{25,1},{2,26},{10... | collective-permute-start | bytes 589832 | tf_op jit(solution)/shard_map/ppermute | solution.py:61
  111.8 4.8 %shard_map.114.refs_4_ = bf16[4,32,768]{2,1,0:T(8,128)(2,1)S(1)} custom-call(bf16[768,3072]{1,0:T(8,128)(2,1)} %up_hbm.5, bf16[3072,768]{1,0:T(8,128)(2,1)} %down_hbm.5, f32[128,768]{1,0:T(8,128)S(1)} %get-tuple-element.73.rest_ref), custom_call_target="tpu_custom_call" | custom-call | flops 1207959552 | bytes 9437184 | tf_op jit(solution)/shard_map/pallas_call | solution.py:440
  116.7 2.7 %collective-permute-done.13.refs_6_ = bf16[4,32,768]{2,1,0:T(8,128)(2,1)S(1)} collective-permute-done((bf16[4,32,768]{2,1,0:T(8,128)(2,1)S(1)}, bf16[4,32,768]{2,1,0:T(8,128)(2,1)S(1)}, u32[]{:S(2)}, u32[]{:S(2)}) %collective-permute-start.13) | collective-permute-done | bytes 196640 | tf_op jit(solution)/shard_map/ppermute | solution.py:61
  119.4 2.7 %shard_map.115 = bf16[256,4,768]{2,1,0:T(4,128)(2,1)} custom-call(f32[1,256]{1,0:T(1,128)S(1)} %get-tuple-element.41.keys_ref, bf16[4,32,768]{2,1,0:T(8,128)(2,1)S(1)} %get-tuple-element.58.refs_0_, bf16[4,32,768]{2,1,0:T(8,128)(2,1)S(1)} %collective-permute-done.5.refs_1_, bf16[4,32,768]{2,1,0:T(8,128)(2,1)S(1)} %collective-permute-done.6.refs_2_, ...), custom_call_target="tpu_custom_call" | custom-call | flops 402653184 | bytes 3145728 | tf_op jit(solution)/shard_map/pallas_call | solution.py:584
  (40 shorter events, 4.0 us)
Async XLA Ops:
  0.0 1.4 %copy-start.3 = (bf16[256,4,768]{2,1,0:T(4,128)(2,1)S(1)}, bf16[256,4,768]{2,1,0:T(4,128)(2,1)}, u32[]{:S(2)}) copy-start(bf16[256,4,768]{2,1,0:T(4,128)(2,1)} %x_ref.1) | copy-start | bytes 4718596
  1.4 0.7 copy-start.8
  2.1 15.0 %copy-start = (bf16[768,2304]{1,0:T(8,128)(2,1)S(1)}, bf16[768,2304]{1,0:T(8,128)(2,1)}, u32[]{:S(2)}) copy-start(bf16[768,2304]{1,0:T(8,128)(2,1)} %w_ref.12) | copy-start | bytes 10616836
  3.4 13.7 %copy-start.1 = (f32[16,768]{1,0:T(8,128)S(1)}, f32[16,768]{1,0:T(8,128)}, u32[]{:S(2)}) copy-start(f32[16,768]{1,0:T(8,128)} %table_ref.13) | copy-start | bytes 147460
  3.4 13.7 %copy-start.7 = (s32[16]{0:T(128)S(1)}, s32[16]{0:T(128)}, u32[]{:S(2)}) copy-start(s32[16]{0:T(128)} %index_ref.13) | copy-start | bytes 196
  3.4 11.4 %collective-permute-start = (bf16[128,768]{1,0:T(8,128)(2,1)S(1)}, bf16[128,768]{1,0:T(8,128)(2,1)S(1)}, u32[]{:S(2)}, u32[]{:S(2)}) collective-permute-start(bf16[128,768]{1,0:T(8,128)(2,1)S(1)} %get-tuple-element.43), channel_id=1, source_target_pairs={{0,2},{1,3},{2,0},{3,1},{4,6},{5,7},{6,4},{7,5},{8,10},{9,11},{10,... | collective-permute-start | bytes 589832 | tf_op jit(solution)/shard_map/ppermute | solution.py:61
  6.5 17.2 %collective-permute-start.1 = (bf16[128,768]{1,0:T(8,128)(2,1)S(1)}, bf16[128,768]{1,0:T(8,128)(2,1)S(1)}, u32[]{:S(2)}, u32[]{:S(2)}) collective-permute-start(bf16[128,768]{1,0:T(8,128)(2,1)S(1)} %get-tuple-element.44), channel_id=1, source_target_pairs={{0,4},{1,5},{2,6},{3,7},{4,0},{5,1},{6,2},{7,3},{8,12},{9,13},{10,... | collective-permute-start | bytes 589832 | tf_op jit(solution)/shard_map/ppermute | solution.py:61
  9.1 14.6 %collective-permute-start.2 = (bf16[128,768]{1,0:T(8,128)(2,1)S(1)}, bf16[128,768]{1,0:T(8,128)(2,1)S(1)}, u32[]{:S(2)}, u32[]{:S(2)}) collective-permute-start(bf16[128,768]{1,0:T(8,128)(2,1)S(1)} %get-tuple-element.45), channel_id=1, source_target_pairs={{0,6},{1,7},{2,4},{3,5},{4,2},{5,3},{6,0},{7,1},{8,14},{9,15},{10,... | collective-permute-start | bytes 589832 | tf_op jit(solution)/shard_map/ppermute | solution.py:61
  15.3 16.7 %collective-permute-start.3 = (bf16[256,768]{1,0:T(8,128)(2,1)S(1)}, bf16[256,768]{1,0:T(8,128)(2,1)S(1)}, u32[]{:S(2)}, u32[]{:S(2)}) collective-permute-start(bf16[256,768]{1,0:T(8,128)(2,1)S(1)} %shard_map.101.rest_0_), channel_id=1, source_target_pairs={{0,1},{1,0},{2,3},{3,2},{4,5},{5,4},{6,7},{7,6},{8,9},{9,8},{10,11... | collective-permute-start | bytes 1179656 | tf_op jit(solution)/shard_map/ppermute | solution.py:61
  17.1 1.9 %copy-start.9 = (bf16[128,768]{1,0:T(8,128)(2,1)}, bf16[128,768]{1,0:T(8,128)(2,1)S(1)}, u32[]{:S(2)}) copy-start(bf16[128,768]{1,0:T(8,128)(2,1)S(1)} %get-tuple-element.62.refs_0_) | copy-start | bytes 589828
  24.2 7.8 %collective-permute-start.4 = (bf16[256,768]{1,0:T(8,128)(2,1)S(1)}, bf16[256,768]{1,0:T(8,128)(2,1)S(1)}, u32[]{:S(2)}, u32[]{:S(2)}) collective-permute-start(bf16[256,768]{1,0:T(8,128)(2,1)S(1)} %shard_map.104.rest_0_.rest_1_), channel_id=1, source_target_pairs={{0,1},{1,0},{2,3},{3,2},{4,5},{5,4},{6,7},{7,6},{8,9},{9,8},{10,11... | collective-permute-start | bytes 1179656 | tf_op jit(solution)/shard_map/ppermute | solution.py:61
  24.3 26.5 %collective-permute-start.8 = (bf16[128,768]{1,0:T(8,128)(2,1)}, bf16[128,768]{1,0:T(8,128)(2,1)}, u32[]{:S(2)}, u32[]{:S(2)}) collective-permute-start(bf16[128,768]{1,0:T(8,128)(2,1)} %get-tuple-element.63), channel_id=1, source_target_pairs={{0,2},{1,3},{2,0},{3,1},{4,6},{5,7},{6,4},{7,5},{8,10},{9,11},{10,... | collective-permute-start | bytes 589832 | tf_op jit(solution)/shard_map/ppermute | solution.py:61
  27.7 23.1 %collective-permute-start.9 = (bf16[128,768]{1,0:T(8,128)(2,1)}, bf16[128,768]{1,0:T(8,128)(2,1)}, u32[]{:S(2)}, u32[]{:S(2)}) collective-permute-start(bf16[128,768]{1,0:T(8,128)(2,1)} %get-tuple-element.64), channel_id=1, source_target_pairs={{0,4},{1,5},{2,6},{3,7},{4,0},{5,1},{6,2},{7,3},{8,12},{9,13},{10,... | collective-permute-start | bytes 589832 | tf_op jit(solution)/shard_map/ppermute | solution.py:61
  28.8 22.0 %collective-permute-start.10 = (bf16[128,768]{1,0:T(8,128)(2,1)}, bf16[128,768]{1,0:T(8,128)(2,1)}, u32[]{:S(2)}, u32[]{:S(2)}) collective-permute-start(bf16[128,768]{1,0:T(8,128)(2,1)} %get-tuple-element.65), channel_id=1, source_target_pairs={{0,6},{1,7},{2,4},{3,5},{4,2},{5,3},{6,0},{7,1},{8,14},{9,15},{10,... | collective-permute-start | bytes 589832 | tf_op jit(solution)/shard_map/ppermute | solution.py:61
  32.0 2.2 %copy-start.4 = (bf16[768,768]{1,0:T(8,128)(2,1)S(1)}, bf16[768,768]{1,0:T(8,128)(2,1)}, u32[]{:S(2)}) copy-start(bf16[768,768]{1,0:T(8,128)(2,1)} %w_ref.13) | copy-start | bytes 3538948
  43.7 0.9 copy-start.6
  44.5 25.8 %all-to-all-start = ((bf16[16,32,768]{2,1,0:T(8,128)(2,1)}), bf16[16,32,768]{2,1,0:T(8,128)(2,1)}, u32[]{:S(2)}, u32[]{:S(2)}) async-start(bf16[16,32,768]{2,1,0:T(8,128)(2,1)} %copy-done.6), calls=%async_computation | async-start | bytes 1572864 | tf_op jit(solution)/shard_map/all_to_all | solution.py:648
  50.7 0.9 copy-start.10
  51.7 1.5 %copy-start.2 = (f32[16,768]{1,0:T(8,128)S(1)}, f32[16,768]{1,0:T(8,128)}, u32[]{:S(2)}) copy-start(f32[16,768]{1,0:T(8,128)} %table_ref.13) | copy-start | bytes 147460
  53.1 2.9 %collective-permute-start.11 = (bf16[512,768]{1,0:T(8,128)(2,1)S(1)}, bf16[512,768]{1,0:T(8,128)(2,1)S(1)}, u32[]{:S(2)}, u32[]{:S(2)}) collective-permute-start(bf16[512,768]{1,0:T(8,128)(2,1)S(1)} %shard_map.109.rest_0_), channel_id=1, source_target_pairs={{0,1},{1,0},{2,3},{3,2},{4,5},{5,4},{6,7},{7,6},{8,9},{9,8},{10,11... | collective-permute-start | bytes 2359304 | tf_op jit(solution)/shard_map/ppermute | solution.py:61
  55.9 2.2 %copy-start.5 = (bf16[768,768]{1,0:T(8,128)(2,1)S(1)}, bf16[768,768]{1,0:T(8,128)(2,1)}, u32[]{:S(2)}) copy-start(bf16[768,768]{1,0:T(8,128)(2,1)} %w_ref.13) | copy-start | bytes 3538948
  70.4 24.5 %all-to-all-start.1 = ((bf16[16,32,768]{2,1,0:T(8,128)(2,1)}), bf16[16,32,768]{2,1,0:T(8,128)(2,1)S(1)}, u32[]{:S(2)}, u32[]{:S(2)}) async-start(bf16[16,32,768]{2,1,0:T(8,128)(2,1)} %get-tuple-element.72), calls=%async_computation.1 | async-start | bytes 1572864 | tf_op jit(solution)/shard_map/all_to_all | solution.py:648
  89.1 21.2 %collective-permute-start.5 = (bf16[4,32,768]{2,1,0:T(8,128)(2,1)S(1)}, bf16[4,32,768]{2,1,0:T(8,128)(2,1)S(1)}, u32[]{:S(2)}, u32[]{:S(2)}) collective-permute-start(bf16[4,32,768]{2,1,0:T(8,128)(2,1)S(1)} %get-tuple-element.59), channel_id=1, source_target_pairs={{0,8},{8,0},{16,24},{24,16},{1,9},{9,1},{17,25},{25,17},{2,10},{10... | collective-permute-start | bytes 589832 | tf_op jit(solution)/shard_map/ppermute | solution.py:61
  90.6 26.0 %collective-permute-start.6 = (bf16[4,32,768]{2,1,0:T(8,128)(2,1)S(1)}, bf16[4,32,768]{2,1,0:T(8,128)(2,1)S(1)}, u32[]{:S(2)}, u32[]{:S(2)}) collective-permute-start(bf16[4,32,768]{2,1,0:T(8,128)(2,1)S(1)} %get-tuple-element.60), channel_id=1, source_target_pairs={{0,16},{8,24},{16,0},{24,8},{1,17},{9,25},{17,1},{25,9},{2,18},{10... | collective-permute-start | bytes 589832 | tf_op jit(solution)/shard_map/ppermute | solution.py:61
  92.0 24.6 %collective-permute-start.7 = (bf16[4,32,768]{2,1,0:T(8,128)(2,1)S(1)}, bf16[4,32,768]{2,1,0:T(8,128)(2,1)S(1)}, u32[]{:S(2)}, u32[]{:S(2)}) collective-permute-start(bf16[4,32,768]{2,1,0:T(8,128)(2,1)S(1)} %get-tuple-element.61), channel_id=1, source_target_pairs={{0,24},{8,16},{16,8},{24,0},{1,25},{9,17},{17,9},{25,1},{2,26},{10... | collective-permute-start | bytes 589832 | tf_op jit(solution)/shard_map/ppermute | solution.py:61
  108.2 8.4 %collective-permute-start.12 = (bf16[4,32,768]{2,1,0:T(8,128)(2,1)S(1)}, bf16[4,32,768]{2,1,0:T(8,128)(2,1)S(1)}, u32[]{:S(2)}, u32[]{:S(2)}) collective-permute-start(bf16[4,32,768]{2,1,0:T(8,128)(2,1)S(1)} %get-tuple-element.74), channel_id=1, source_target_pairs={{0,8},{8,0},{16,24},{24,16},{1,9},{9,1},{17,25},{25,17},{2,10},{10... | collective-permute-start | bytes 589832 | tf_op jit(solution)/shard_map/ppermute | solution.py:61
  109.7 9.6 %collective-permute-start.13 = (bf16[4,32,768]{2,1,0:T(8,128)(2,1)S(1)}, bf16[4,32,768]{2,1,0:T(8,128)(2,1)S(1)}, u32[]{:S(2)}, u32[]{:S(2)}) collective-permute-start(bf16[4,32,768]{2,1,0:T(8,128)(2,1)S(1)} %get-tuple-element.75), channel_id=1, source_target_pairs={{0,16},{8,24},{16,0},{24,8},{1,17},{9,25},{17,1},{25,9},{2,18},{10... | collective-permute-start | bytes 589832 | tf_op jit(solution)/shard_map/ppermute | solution.py:61
  110.3 9.1 %collective-permute-start.14 = (bf16[4,32,768]{2,1,0:T(8,128)(2,1)S(1)}, bf16[4,32,768]{2,1,0:T(8,128)(2,1)S(1)}, u32[]{:S(2)}, u32[]{:S(2)}) collective-permute-start(bf16[4,32,768]{2,1,0:T(8,128)(2,1)S(1)} %get-tuple-element.76), channel_id=1, source_target_pairs={{0,24},{8,16},{16,8},{24,0},{1,25},{9,17},{17,9},{25,1},{2,26},{10... | collective-permute-start | bytes 589832 | tf_op jit(solution)/shard_map/ppermute | solution.py:61

commit v15 on v14

--- a/solution.py
+++ b/solution.py
@@ -78,7 +78,8 @@
         if self.share > 1:
             return row * self.groups + group
         place = (row + self.rows_count - 1) % self.rows_count
-        turn = (group + self.rows_count * self.groups - place) % self.groups
+        last = self.rows_count + self.groups - 2
+        turn = (group + self.rows_count * self.groups + last - place) % self.groups
         return turn * self.rows_count + place
 
 

time: 122 us -> 122 us (level)
  waiting for transfers between devices: 17.3 us -> 15.6 us
    all_to_all x2, waiting for transfers between devices: 4.13 us -> 2.28 us  [body(): lax.all_to_all(mid, ('band', 'loc'), 0, 0, axis_index_groups=same, tiled=...]
  transfers between devices with their start and end apart: 17 -> 17, of which waited for: 5 -> 5; matrix products, arithmetic and copies ran while one was open for 0% -> 0% of each run, Pallas kernels for 55% -> 56%
where the time goes in v15:
time: 122 us; the launch traced here: 121 us
  Pallas kernels  71.2 us (58%)
  starting transfers between devices  30.2 us (25%)
  waiting for transfers between devices  15.6 us (13%)
  local copies, waits for them, and re-layouts  3.93 us (3%)
    pallas_call x2, Pallas kernels, channel(): call(kernel, [jax.ShapeDtypeStruct((bands, locations, width), BF16)] * le...  27.8 us
    pallas_call x2, Pallas kernels, attend(): call(kernel, [jax.ShapeDtypeStruct((plan.rows_count * plan.groups, plan.p...  19.8 us
    ppermute x15, starting transfers between devices, exchange(): lax.ppermute(value, axis, [(i, i ^ step) for i in range(lax.axis_size(axi...  18.9 us
    ppermute x15, waiting for transfers between devices, exchange(): lax.ppermute(value, axis, [(i, i ^ step) for i in range(lax.axis_size(axi...  13.3 us
    all_to_all x2, starting transfers between devices, body(): lax.all_to_all(mid, ('band', 'loc'), 0, 0, axis_index_groups=same, tiled=...  11.3 us
    pallas_call x5, Pallas kernels, project(): call(kernel, [jax.ShapeDtypeStruct((rows, width), BF16)] * len(names), hi...  10.8 us
    pallas_call x1, Pallas kernels, finish(): call(kernel, [jax.ShapeDtypeStruct((bands, locations, width), BF16)] * le...  4.84 us
    unnamed x22, local copies, waits for them, and re-layouts  3.93 us
  transfers between devices with their start and end apart: 17, of which 5 were waited for; matrix products, arithmetic and copies ran while one was open for 0% of the time, Pallas kernels for 56%

profile of v15, /device:TPU:0, one launch (start us, length us, event | category | flops | bytes accessed | tf_op | source)
XLA Modules:
  0.0 121.2 jit_solution(3855321933808698316)
XLA Ops:
  0.0 1.4 %copy-done.3 = bf16[256,4,768]{2,1,0:T(4,128)(2,1)S(1)} copy-done((bf16[256,4,768]{2,1,0:T(4,128)(2,1)S(1)}, bf16[256,4,768]{2,1,0:T(4,128)(2,1)}, u32[]{:S(2)}) %copy-start.3) | copy-done | bytes 1572888
  2.1 1.3 %shard_map.100 = (bf16[128,768]{1,0:T(8,128)(2,1)S(1)}, bf16[128,768]{1,0:T(8,128)(2,1)S(1)}, bf16[128,768]{1,0:T(8,128)(2,1)S(1)}, bf16[128,768]{1,0:T(8,128)(2...) custom-call(s32[16,128]{1,0:T(8,128)S(1)} %bitcast.1, ...), custom_call_target="tpu_custom_call" | custom-call | flops 402653184 | bytes 3145728 | tf_op jit(solution)/shard_map/pallas_call | solution.py:139
  3.4 3.1 %collective-permute-start = (bf16[128,768]{1,0:T(8,128)(2,1)S(1)}, bf16[128,768]{1,0:T(8,128)(2,1)S(1)}, u32[]{:S(2)}, u32[]{:S(2)}) collective-permute-start(bf16[128,768]{1,0:T(8,128)(2,1)S(1)} %get-tuple-element.43), channel_id=1, source_target_pairs={{0,2},{1,3},{2,0},{3,1},{4,6},{5,7},{6,4},{7,5},{8,10},{9,11},{10,... | collective-permute-start | bytes 589832 | tf_op jit(solution)/shard_map/ppermute | solution.py:61
  6.5 2.6 %collective-permute-start.1 = (bf16[128,768]{1,0:T(8,128)(2,1)S(1)}, bf16[128,768]{1,0:T(8,128)(2,1)S(1)}, u32[]{:S(2)}, u32[]{:S(2)}) collective-permute-start(bf16[128,768]{1,0:T(8,128)(2,1)S(1)} %get-tuple-element.44), channel_id=1, source_target_pairs={{0,4},{1,5},{2,6},{3,7},{4,0},{5,1},{6,2},{7,3},{8,12},{9,13},{10,... | collective-permute-start | bytes 589832 | tf_op jit(solution)/shard_map/ppermute | solution.py:61
  9.1 5.7 %collective-permute-done.refs_1_.rest_0_ = bf16[128,768]{1,0:T(8,128)(2,1)S(1)} collective-permute-done((bf16[128,768]{1,0:T(8,128)(2,1)S(1)}, bf16[128,768]{1,0:T(8,128)(2,1)S(1)}, u32[]{:S(2)}, u32[]{:S(2)}) %collective-permute-start) | collective-permute-done | bytes 196640 | tf_op jit(solution)/shard_map/ppermute | solution.py:61
  15.4 1.7 %shard_map.102 = (bf16[128,768]{1,0:T(8,128)(2,1)S(1)}, bf16[128,768]{1,0:T(8,128)(2,1)}, bf16[128,768]{1,0:T(8,128)(2,1)}, bf16[128,768]{1,0:T(8,128)(2,1)}, f32[8,128]{1,0:T(8,128)S(1)}) custom-call(bf16[1024,768]{1,0:T(8,128)(2,1)S(1)} %get-tuple-element.46.rows_ref, f32[1,1024]{1,0:T(1,128)S(1)} %get-tuple-element.47.place_ref, ...), custom_call_target="tpu_custom_call" | custom-call | flops 402653184 | tf_op jit(solution)/shard_map/pallas_call | solution.py:162
  17.1 1.8 %shard_map.103 = (bf16[256,768]{1,0:T(8,128)(2,1)S(1)}, bf16[256,768]{1,0:T(8,128)(2,1)S(1)}, bf16[256,768]{1,0:T(8,128)(2,1)S(1)}) custom-call(s32[16]{0:T(128)S(1)} %copy-done.7, f32[16,768]{1,0:T(8,128)S(1)} %copy-done.1, bf16[768,2304]{1,0:T(8,128)(2,1)S(1)} %copy-done, bf16[256,768]{1,0:T(8,128)(2,1)S(1)} %shard_map.101.rest_0_), custom_call_target="tpu_custom_call" | custom-call | flops 905969664 | bytes 5111808 | tf_op jit(solution)/shard_map/pallas_call | solution.py:241
  19.0 4.7 %collective-permute-done.1.refs_0_ = bf16[128,768]{1,0:T(8,128)(2,1)S(1)} collective-permute-done((bf16[128,768]{1,0:T(8,128)(2,1)S(1)}, bf16[128,768]{1,0:T(8,128)(2,1)S(1)}, u32[]{:S(2)}, u32[]{:S(2)}) %collective-permute-start.1) | collective-permute-done | bytes 196640 | tf_op jit(solution)/shard_map/ppermute | solution.py:61
  24.3 3.4 %collective-permute-start.8 = (bf16[128,768]{1,0:T(8,128)(2,1)}, bf16[128,768]{1,0:T(8,128)(2,1)}, u32[]{:S(2)}, u32[]{:S(2)}) collective-permute-start(bf16[128,768]{1,0:T(8,128)(2,1)} %get-tuple-element.63), channel_id=1, source_target_pairs={{0,2},{1,3},{2,0},{3,1},{4,6},{5,7},{6,4},{7,5},{8,10},{9,11},{10,... | collective-permute-start | bytes 589832 | tf_op jit(solution)/shard_map/ppermute | solution.py:61
  27.7 1.1 collective-permute-start.9
  28.8 1.4 %collective-permute-start.10 = (bf16[128,768]{1,0:T(8,128)(2,1)}, bf16[128,768]{1,0:T(8,128)(2,1)}, u32[]{:S(2)}, u32[]{:S(2)}) collective-permute-start(bf16[128,768]{1,0:T(8,128)(2,1)} %get-tuple-element.65), channel_id=1, source_target_pairs={{0,6},{1,7},{2,4},{3,5},{4,2},{5,3},{6,0},{7,1},{8,14},{9,15},{10,... | collective-permute-start | bytes 589832 | tf_op jit(solution)/shard_map/ppermute | solution.py:61
  30.1 1.8 %shard_map.105 = (bf16[256,768]{1,0:T(8,128)(2,1)S(1)}, bf16[256,768]{1,0:T(8,128)(2,1)S(1)}, bf16[256,768]{1,0:T(8,128)(2,1)S(1)}) custom-call(s32[16]{0:T(128)S(1)} %copy-done.7, f32[16,768]{1,0:T(8,128)S(1)} %copy-done.1, bf16[768,2304]{1,0:T(8,128)(2,1)S(1)} %copy-done, bf16[256,768]{1,0:T(8,128)(2,1)S(1)} %shard_map.104.rest_0_.rest_1_), custom_call_target="tpu_custom_call" | custom-call | flops 905969664 | bytes 5111808 | tf_op jit(solution)/shard_map/pallas_call | solution.py:241
  32.0 2.2 %shard_map.106 = (bf16[512,768]{1,0:T(8,128)(2,1)S(1)}, bf16[512,768]{1,0:T(8,128)(2,1)S(1)}) custom-call(s32[16]{0:T(128)S(1)} %copy-done.7, f32[16,768]{1,0:T(8,128)S(1)} %copy-done.1, bf16[768,2304]{1,0:T(8,128)(2,1)S(1)} %copy-done, bf16[256,768]{1,0:T(8,128)(2,1)S(1)} %collective-permute-done.3.rest_0_, ...), custom_call_target="tpu_custom_call" | custom-call | flops 1207959552 | bytes 5898240 | tf_op jit(solution)/shard_map/pallas_call | solution.py:241
  34.2 9.4 %shard_map.107 = (bf16[16,32,768]{2,1,0:T(8,128)(2,1)S(1)}, f32[8,128]{1,0:T(8,128)S(1)}) custom-call(s32[16]{0:T(128)S(1)} %copy-done.7, f32[16,768]{1,0:T(8,128)S(1)} %copy-done.1, bf16[768,768]{1,0:T(8,128)(2,1)S(1)} %copy-done.4, bf16[256,768]{1,0:T(8,128)(2,1)S(1)} %shard_map.101.rest_0_, bf16[256,768]{1,0:T(8,128)(2,1)S(1)} %shard_map.104.rest_0_.rest_1_, ...), custom_call_target="tpu_custom_call" | custom-call | flops 6442450944 | tf_op jit(solution)/shard_map/pallas_call | solution.py:349
  44.5 6.2 %all-to-all-start = ((bf16[16,32,768]{2,1,0:T(8,128)(2,1)}), bf16[16,32,768]{2,1,0:T(8,128)(2,1)}, u32[]{:S(2)}, u32[]{:S(2)}) async-start(bf16[16,32,768]{2,1,0:T(8,128)(2,1)} %copy-done.6), calls=%async_computation | async-start | bytes 1572864 | tf_op jit(solution)/shard_map/all_to_all | solution.py:649
  50.8 0.9 copy-done.10
  51.7 1.4 %shard_map.109.rest_0_ = bf16[512,768]{1,0:T(8,128)(2,1)S(1)} custom-call(bf16[128,768]{1,0:T(8,128)(2,1)S(1)} %copy-done.10, bf16[128,768]{1,0:T(8,128)(2,1)} %collective-permute-done.8.refs_1_, bf16[128,768]{1,0:T(8,128)(2,1)} %collective-permute-done.9.refs_2_, bf16[128,768]{1,0:T(8,128)(2,1)} %collective-permute-done.10.refs_3_, ...), custom_call_target="tpu_custom_call" | custom-call | flops 68719476736 | tf_op jit(solution)/shard_map/pallas_call | solution.py:188
  53.2 2.8 %shard_map.110 = (bf16[512,768]{1,0:T(8,128)(2,1)S(1)}, bf16[512,768]{1,0:T(8,128)(2,1)S(1)}, bf16[512,768]{1,0:T(8,128)(2,1)S(1)}) custom-call(s32[16]{0:T(128)S(1)} %copy-done.7, f32[16,768]{1,0:T(8,128)S(1)} %copy-done.2, bf16[768,2304]{1,0:T(8,128)(2,1)S(1)} %copy-done, bf16[512,768]{1,0:T(8,128)(2,1)S(1)} %shard_map.109.rest_0_), custom_call_target="tpu_custom_call" | custom-call | tf_op jit(solution)/shard_map/pallas_call | solution.py:241
  56.0 2.2 %shard_map.111 = (bf16[512,768]{1,0:T(8,128)(2,1)S(1)}, bf16[512,768]{1,0:T(8,128)(2,1)S(1)}) custom-call(s32[16]{0:T(128)S(1)} %copy-done.7, f32[16,768]{1,0:T(8,128)S(1)} %copy-done.2, bf16[768,2304]{1,0:T(8,128)(2,1)S(1)} %copy-done, bf16[512,768]{1,0:T(8,128)(2,1)S(1)} %collective-permute-done.11.rest_0_, bf16[512,768]{1,0:T(8,128)(2,1)S(1)} %get-tuple-element.67.rest_1_), custom_call_target="tpu_custom_call" | custom-call | tf_op jit(solution)/shard_map/pallas_call | solution.py:241
  58.2 10.3 %shard_map.112 = (bf16[16,32,768]{2,1,0:T(8,128)(2,1)}, f32[8,128]{1,0:T(8,128)}) custom-call(s32[16]{0:T(128)S(1)} %copy-done.7, f32[16,768]{1,0:T(8,128)S(1)} %copy-done.2, bf16[768,768]{1,0:T(8,128)(2,1)S(1)} %copy-done.5, bf16[512,768]{1,0:T(8,128)(2,1)S(1)} %shard_map.109.rest_0_, bf16[512,768]{1,0:T(8,128)(2,1)S(1)} %get-tuple-element.67.rest_1_, ...), custom_call_target="tpu_custom_call" | custom-call | tf_op jit(solution)/shard_map/pallas_call | solution.py:349
  68.5 1.0 all-to-all-done.refs_0_
  69.5 5.1 %all-to-all-start.1 = ((bf16[16,32,768]{2,1,0:T(8,128)(2,1)}), bf16[16,32,768]{2,1,0:T(8,128)(2,1)S(1)}, u32[]{:S(2)}, u32[]{:S(2)}) async-start(bf16[16,32,768]{2,1,0:T(8,128)(2,1)} %get-tuple-element.72), calls=%async_computation.1 | async-start | bytes 1572864 | tf_op jit(solution)/shard_map/all_to_all | solution.py:649
  74.6 14.5 %shard_map.108 = (bf16[4,32,768]{2,1,0:T(8,128)(2,1)S(1)}, bf16[4,32,768]{2,1,0:T(8,128)(2,1)S(1)}, bf16[4,32,768]{2,1,0:T(8,128)(2,1)S(1)}, bf16[4,32,768]{2,1,0:T(8,128)(2,1)S(1)}) custom-call(bf16[768,2304]{1,0:T(8,128)(2,1)} %qkv_hbm.3, bf16[768,768]{1,0:T(8,128)(2,1)} %out_hbm.3, bf16[768,3072]{1,0:T(8,128)(2,1)} %up_hbm.5, bf16[3072,768]{1,0:T(8,128)(2,1)} %down_hbm.5, ...), custom_call_target="tpu_custom_call" | custom-call | flops 7247757312 | bytes 15728640 | tf_op jit(solution)/shard_map/pallas_call | solution.py:545
  89.1 1.5 %collective-permute-start.5 = (bf16[4,32,768]{2,1,0:T(8,128)(2,1)S(1)}, bf16[4,32,768]{2,1,0:T(8,128)(2,1)S(1)}, u32[]{:S(2)}, u32[]{:S(2)}) collective-permute-start(bf16[4,32,768]{2,1,0:T(8,128)(2,1)S(1)} %get-tuple-element.59), channel_id=1, source_target_pairs={{0,8},{8,0},{16,24},{24,16},{1,9},{9,1},{17,25},{25,17},{2,10},{10... | collective-permute-start | bytes 589832 | tf_op jit(solution)/shard_map/ppermute | solution.py:61
  91.2 1.4 %collective-permute-start.7 = (bf16[4,32,768]{2,1,0:T(8,128)(2,1)S(1)}, bf16[4,32,768]{2,1,0:T(8,128)(2,1)S(1)}, u32[]{:S(2)}, u32[]{:S(2)}) collective-permute-start(bf16[4,32,768]{2,1,0:T(8,128)(2,1)S(1)} %get-tuple-element.61), channel_id=1, source_target_pairs={{0,24},{8,16},{16,8},{24,0},{1,25},{9,17},{17,9},{25,1},{2,26},{10... | collective-permute-start | bytes 589832 | tf_op jit(solution)/shard_map/ppermute | solution.py:61
  92.6 1.3 %all-to-all-done.1.refs_0_ = bf16[16,32,768]{2,1,0:T(8,128)(2,1)S(1)} async-done(((bf16[16,32,768]{2,1,0:T(8,128)(2,1)}), bf16[16,32,768]{2,1,0:T(8,128)(2,1)S(1)}, u32[]{:S(2)}, u32[]{:S(2)}) %all-to-all-start.1) | async-done | bytes 786464 | tf_op jit(solution)/shard_map/all_to_all | solution.py:649
  93.9 13.4 %shard_map.113 = (bf16[4,32,768]{2,1,0:T(8,128)(2,1)S(1)}, bf16[4,32,768]{2,1,0:T(8,128)(2,1)S(1)}, bf16[4,32,768]{2,1,0:T(8,128)(2,1)S(1)}, f32[128,768]{1,0:T(8,128)S(1)}) custom-call(bf16[768,2304]{1,0:T(8,128)(2,1)} %qkv_hbm.3, bf16[768,768]{1,0:T(8,128)(2,1)} %out_hbm.3, bf16[768,3072]{1,0:T(8,128)(2,1)} %up_hbm.5, bf16[3072,768]{1,0:T(8,128)(2,1)} %down_hbm.5, ...), custom_call_target="tpu_custom_call" | custom-call | flops 7247757312 | bytes 15728640 | tf_op jit(solution)/shard_map/pallas_call | solution.py:545
  107.3 1.6 %collective-permute-start.12 = (bf16[4,32,768]{2,1,0:T(8,128)(2,1)S(1)}, bf16[4,32,768]{2,1,0:T(8,128)(2,1)S(1)}, u32[]{:S(2)}, u32[]{:S(2)}) collective-permute-start(bf16[4,32,768]{2,1,0:T(8,128)(2,1)S(1)} %get-tuple-element.74), channel_id=1, source_target_pairs={{0,8},{8,0},{16,24},{24,16},{1,9},{9,1},{17,25},{25,17},{2,10},{10... | collective-permute-start | bytes 589832 | tf_op jit(solution)/shard_map/ppermute | solution.py:61
  108.8 1.5 %collective-permute-start.13 = (bf16[4,32,768]{2,1,0:T(8,128)(2,1)S(1)}, bf16[4,32,768]{2,1,0:T(8,128)(2,1)S(1)}, u32[]{:S(2)}, u32[]{:S(2)}) collective-permute-start(bf16[4,32,768]{2,1,0:T(8,128)(2,1)S(1)} %get-tuple-element.75), channel_id=1, source_target_pairs={{0,16},{8,24},{16,0},{24,8},{1,17},{9,25},{17,1},{25,9},{2,18},{10... | collective-permute-start | bytes 589832 | tf_op jit(solution)/shard_map/ppermute | solution.py:61
  110.8 4.8 %shard_map.114.refs_4_ = bf16[4,32,768]{2,1,0:T(8,128)(2,1)S(1)} custom-call(bf16[768,3072]{1,0:T(8,128)(2,1)} %up_hbm.5, bf16[3072,768]{1,0:T(8,128)(2,1)} %down_hbm.5, f32[128,768]{1,0:T(8,128)S(1)} %get-tuple-element.73.rest_ref), custom_call_target="tpu_custom_call" | custom-call | flops 1207959552 | bytes 9437184 | tf_op jit(solution)/shard_map/pallas_call | solution.py:441
  115.7 2.9 %collective-permute-done.13.refs_6_ = bf16[4,32,768]{2,1,0:T(8,128)(2,1)S(1)} collective-permute-done((bf16[4,32,768]{2,1,0:T(8,128)(2,1)S(1)}, bf16[4,32,768]{2,1,0:T(8,128)(2,1)S(1)}, u32[]{:S(2)}, u32[]{:S(2)}) %collective-permute-start.13) | collective-permute-done | bytes 196640 | tf_op jit(solution)/shard_map/ppermute | solution.py:61
  118.6 2.7 %shard_map.115 = bf16[256,4,768]{2,1,0:T(4,128)(2,1)} custom-call(f32[1,256]{1,0:T(1,128)S(1)} %get-tuple-element.41.keys_ref, bf16[4,32,768]{2,1,0:T(8,128)(2,1)S(1)} %get-tuple-element.58.refs_0_, bf16[4,32,768]{2,1,0:T(8,128)(2,1)S(1)} %collective-permute-done.5.refs_1_, bf16[4,32,768]{2,1,0:T(8,128)(2,1)S(1)} %collective-permute-done.6.refs_2_, ...), custom_call_target="tpu_custom_call" | custom-call | flops 402653184 | bytes 3145728 | tf_op jit(solution)/shard_map/pallas_call | solution.py:585
  (40 shorter events, 4.0 us)
Async XLA Ops:
  0.0 1.4 %copy-start.3 = (bf16[256,4,768]{2,1,0:T(4,128)(2,1)S(1)}, bf16[256,4,768]{2,1,0:T(4,128)(2,1)}, u32[]{:S(2)}) copy-start(bf16[256,4,768]{2,1,0:T(4,128)(2,1)} %x_ref.1) | copy-start | bytes 4718596
  1.4 0.7 copy-start.8
  2.1 15.0 %copy-start = (bf16[768,2304]{1,0:T(8,128)(2,1)S(1)}, bf16[768,2304]{1,0:T(8,128)(2,1)}, u32[]{:S(2)}) copy-start(bf16[768,2304]{1,0:T(8,128)(2,1)} %w_ref.12) | copy-start | bytes 10616836
  3.4 13.7 %copy-start.1 = (f32[16,768]{1,0:T(8,128)S(1)}, f32[16,768]{1,0:T(8,128)}, u32[]{:S(2)}) copy-start(f32[16,768]{1,0:T(8,128)} %table_ref.13) | copy-start | bytes 147460
  3.4 13.7 %copy-start.7 = (s32[16]{0:T(128)S(1)}, s32[16]{0:T(128)}, u32[]{:S(2)}) copy-start(s32[16]{0:T(128)} %index_ref.13) | copy-start | bytes 196
  3.4 11.4 %collective-permute-start = (bf16[128,768]{1,0:T(8,128)(2,1)S(1)}, bf16[128,768]{1,0:T(8,128)(2,1)S(1)}, u32[]{:S(2)}, u32[]{:S(2)}) collective-permute-start(bf16[128,768]{1,0:T(8,128)(2,1)S(1)} %get-tuple-element.43), channel_id=1, source_target_pairs={{0,2},{1,3},{2,0},{3,1},{4,6},{5,7},{6,4},{7,5},{8,10},{9,11},{10,... | collective-permute-start | bytes 589832 | tf_op jit(solution)/shard_map/ppermute | solution.py:61
  6.5 17.2 %collective-permute-start.1 = (bf16[128,768]{1,0:T(8,128)(2,1)S(1)}, bf16[128,768]{1,0:T(8,128)(2,1)S(1)}, u32[]{:S(2)}, u32[]{:S(2)}) collective-permute-start(bf16[128,768]{1,0:T(8,128)(2,1)S(1)} %get-tuple-element.44), channel_id=1, source_target_pairs={{0,4},{1,5},{2,6},{3,7},{4,0},{5,1},{6,2},{7,3},{8,12},{9,13},{10,... | collective-permute-start | bytes 589832 | tf_op jit(solution)/shard_map/ppermute | solution.py:61
  9.1 14.6 %collective-permute-start.2 = (bf16[128,768]{1,0:T(8,128)(2,1)S(1)}, bf16[128,768]{1,0:T(8,128)(2,1)S(1)}, u32[]{:S(2)}, u32[]{:S(2)}) collective-permute-start(bf16[128,768]{1,0:T(8,128)(2,1)S(1)} %get-tuple-element.45), channel_id=1, source_target_pairs={{0,6},{1,7},{2,4},{3,5},{4,2},{5,3},{6,0},{7,1},{8,14},{9,15},{10,... | collective-permute-start | bytes 589832 | tf_op jit(solution)/shard_map/ppermute | solution.py:61
  15.3 16.7 %collective-permute-start.3 = (bf16[256,768]{1,0:T(8,128)(2,1)S(1)}, bf16[256,768]{1,0:T(8,128)(2,1)S(1)}, u32[]{:S(2)}, u32[]{:S(2)}) collective-permute-start(bf16[256,768]{1,0:T(8,128)(2,1)S(1)} %shard_map.101.rest_0_), channel_id=1, source_target_pairs={{0,1},{1,0},{2,3},{3,2},{4,5},{5,4},{6,7},{7,6},{8,9},{9,8},{10,11... | collective-permute-start | bytes 1179656 | tf_op jit(solution)/shard_map/ppermute | solution.py:61
  17.1 1.9 %copy-start.9 = (bf16[128,768]{1,0:T(8,128)(2,1)}, bf16[128,768]{1,0:T(8,128)(2,1)S(1)}, u32[]{:S(2)}) copy-start(bf16[128,768]{1,0:T(8,128)(2,1)S(1)} %get-tuple-element.62.refs_0_) | copy-start | bytes 589828
  24.2 7.8 %collective-permute-start.4 = (bf16[256,768]{1,0:T(8,128)(2,1)S(1)}, bf16[256,768]{1,0:T(8,128)(2,1)S(1)}, u32[]{:S(2)}, u32[]{:S(2)}) collective-permute-start(bf16[256,768]{1,0:T(8,128)(2,1)S(1)} %shard_map.104.rest_0_.rest_1_), channel_id=1, source_target_pairs={{0,1},{1,0},{2,3},{3,2},{4,5},{5,4},{6,7},{7,6},{8,9},{9,8},{10,11... | collective-permute-start | bytes 1179656 | tf_op jit(solution)/shard_map/ppermute | solution.py:61
  24.3 26.5 %collective-permute-start.8 = (bf16[128,768]{1,0:T(8,128)(2,1)}, bf16[128,768]{1,0:T(8,128)(2,1)}, u32[]{:S(2)}, u32[]{:S(2)}) collective-permute-start(bf16[128,768]{1,0:T(8,128)(2,1)} %get-tuple-element.63), channel_id=1, source_target_pairs={{0,2},{1,3},{2,0},{3,1},{4,6},{5,7},{6,4},{7,5},{8,10},{9,11},{10,... | collective-permute-start | bytes 589832 | tf_op jit(solution)/shard_map/ppermute | solution.py:61
  27.7 23.1 %collective-permute-start.9 = (bf16[128,768]{1,0:T(8,128)(2,1)}, bf16[128,768]{1,0:T(8,128)(2,1)}, u32[]{:S(2)}, u32[]{:S(2)}) collective-permute-start(bf16[128,768]{1,0:T(8,128)(2,1)} %get-tuple-element.64), channel_id=1, source_target_pairs={{0,4},{1,5},{2,6},{3,7},{4,0},{5,1},{6,2},{7,3},{8,12},{9,13},{10,... | collective-permute-start | bytes 589832 | tf_op jit(solution)/shard_map/ppermute | solution.py:61
  28.8 22.0 %collective-permute-start.10 = (bf16[128,768]{1,0:T(8,128)(2,1)}, bf16[128,768]{1,0:T(8,128)(2,1)}, u32[]{:S(2)}, u32[]{:S(2)}) collective-permute-start(bf16[128,768]{1,0:T(8,128)(2,1)} %get-tuple-element.65), channel_id=1, source_target_pairs={{0,6},{1,7},{2,4},{3,5},{4,2},{5,3},{6,0},{7,1},{8,14},{9,15},{10,... | collective-permute-start | bytes 589832 | tf_op jit(solution)/shard_map/ppermute | solution.py:61
  32.0 2.2 %copy-start.4 = (bf16[768,768]{1,0:T(8,128)(2,1)S(1)}, bf16[768,768]{1,0:T(8,128)(2,1)}, u32[]{:S(2)}) copy-start(bf16[768,768]{1,0:T(8,128)(2,1)} %w_ref.13) | copy-start | bytes 3538948
  43.7 0.9 copy-start.6
  44.5 24.9 %all-to-all-start = ((bf16[16,32,768]{2,1,0:T(8,128)(2,1)}), bf16[16,32,768]{2,1,0:T(8,128)(2,1)}, u32[]{:S(2)}, u32[]{:S(2)}) async-start(bf16[16,32,768]{2,1,0:T(8,128)(2,1)} %copy-done.6), calls=%async_computation | async-start | bytes 1572864 | tf_op jit(solution)/shard_map/all_to_all | solution.py:649
  50.7 0.9 copy-start.10
  51.7 1.5 %copy-start.2 = (f32[16,768]{1,0:T(8,128)S(1)}, f32[16,768]{1,0:T(8,128)}, u32[]{:S(2)}) copy-start(f32[16,768]{1,0:T(8,128)} %table_ref.13) | copy-start | bytes 147460
  53.1 2.9 %collective-permute-start.11 = (bf16[512,768]{1,0:T(8,128)(2,1)S(1)}, bf16[512,768]{1,0:T(8,128)(2,1)S(1)}, u32[]{:S(2)}, u32[]{:S(2)}) collective-permute-start(bf16[512,768]{1,0:T(8,128)(2,1)S(1)} %shard_map.109.rest_0_), channel_id=1, source_target_pairs={{0,1},{1,0},{2,3},{3,2},{4,5},{5,4},{6,7},{7,6},{8,9},{9,8},{10,11... | collective-permute-start | bytes 2359304 | tf_op jit(solution)/shard_map/ppermute | solution.py:61
  56.0 2.2 %copy-start.5 = (bf16[768,768]{1,0:T(8,128)(2,1)S(1)}, bf16[768,768]{1,0:T(8,128)(2,1)}, u32[]{:S(2)}) copy-start(bf16[768,768]{1,0:T(8,128)(2,1)} %w_ref.13) | copy-start | bytes 3538948
  69.5 24.4 %all-to-all-start.1 = ((bf16[16,32,768]{2,1,0:T(8,128)(2,1)}), bf16[16,32,768]{2,1,0:T(8,128)(2,1)S(1)}, u32[]{:S(2)}, u32[]{:S(2)}) async-start(bf16[16,32,768]{2,1,0:T(8,128)(2,1)} %get-tuple-element.72), calls=%async_computation.1 | async-start | bytes 1572864 | tf_op jit(solution)/shard_map/all_to_all | solution.py:649
  89.1 21.2 %collective-permute-start.5 = (bf16[4,32,768]{2,1,0:T(8,128)(2,1)S(1)}, bf16[4,32,768]{2,1,0:T(8,128)(2,1)S(1)}, u32[]{:S(2)}, u32[]{:S(2)}) collective-permute-start(bf16[4,32,768]{2,1,0:T(8,128)(2,1)S(1)} %get-tuple-element.59), channel_id=1, source_target_pairs={{0,8},{8,0},{16,24},{24,16},{1,9},{9,1},{17,25},{25,17},{2,10},{10... | collective-permute-start | bytes 589832 | tf_op jit(solution)/shard_map/ppermute | solution.py:61
  90.6 25.1 %collective-permute-start.6 = (bf16[4,32,768]{2,1,0:T(8,128)(2,1)S(1)}, bf16[4,32,768]{2,1,0:T(8,128)(2,1)S(1)}, u32[]{:S(2)}, u32[]{:S(2)}) collective-permute-start(bf16[4,32,768]{2,1,0:T(8,128)(2,1)S(1)} %get-tuple-element.60), channel_id=1, source_target_pairs={{0,16},{8,24},{16,0},{24,8},{1,17},{9,25},{17,1},{25,9},{2,18},{10... | collective-permute-start | bytes 589832 | tf_op jit(solution)/shard_map/ppermute | solution.py:61
  91.2 24.5 %collective-permute-start.7 = (bf16[4,32,768]{2,1,0:T(8,128)(2,1)S(1)}, bf16[4,32,768]{2,1,0:T(8,128)(2,1)S(1)}, u32[]{:S(2)}, u32[]{:S(2)}) collective-permute-start(bf16[4,32,768]{2,1,0:T(8,128)(2,1)S(1)} %get-tuple-element.61), channel_id=1, source_target_pairs={{0,24},{8,16},{16,8},{24,0},{1,25},{9,17},{17,9},{25,1},{2,26},{10... | collective-permute-start | bytes 589832 | tf_op jit(solution)/shard_map/ppermute | solution.py:61
  107.3 8.4 %collective-permute-start.12 = (bf16[4,32,768]{2,1,0:T(8,128)(2,1)S(1)}, bf16[4,32,768]{2,1,0:T(8,128)(2,1)S(1)}, u32[]{:S(2)}, u32[]{:S(2)}) collective-permute-start(bf16[4,32,768]{2,1,0:T(8,128)(2,1)S(1)} %get-tuple-element.74), channel_id=1, source_target_pairs={{0,8},{8,0},{16,24},{24,16},{1,9},{9,1},{17,25},{25,17},{2,10},{10... | collective-permute-start | bytes 589832 | tf_op jit(solution)/shard_map/ppermute | solution.py:61
  108.8 9.7 %collective-permute-start.13 = (bf16[4,32,768]{2,1,0:T(8,128)(2,1)S(1)}, bf16[4,32,768]{2,1,0:T(8,128)(2,1)S(1)}, u32[]{:S(2)}, u32[]{:S(2)}) collective-permute-start(bf16[4,32,768]{2,1,0:T(8,128)(2,1)S(1)} %get-tuple-element.75), channel_id=1, source_target_pairs={{0,16},{8,24},{16,0},{24,8},{1,17},{9,25},{17,1},{25,9},{2,18},{10... | collective-permute-start | bytes 589832 | tf_op jit(solution)/shard_map/ppermute | solution.py:61
  110.3 8.3 %collective-permute-start.14 = (bf16[4,32,768]{2,1,0:T(8,128)(2,1)S(1)}, bf16[4,32,768]{2,1,0:T(8,128)(2,1)S(1)}, u32[]{:S(2)}, u32[]{:S(2)}) collective-permute-start(bf16[4,32,768]{2,1,0:T(8,128)(2,1)S(1)} %get-tuple-element.76), channel_id=1, source_target_pairs={{0,24},{8,16},{16,8},{24,0},{1,25},{9,17},{17,9},{25,1},{2,26},{10... | collective-permute-start | bytes 589832 | tf_op jit(solution)/shard_map/ppermute | solution.py:61
